TPU v7x, 32 devices: a whole 2x2x4 slice. The times are simulated.
32 devices in a mesh: dp: 16 (over z, x, core), chan: 2 (over y).
Axes of the slice: x: 2, y: 2, z: 4, core: 2. Of those that a mesh axis runs over, the one named last changes fastest.
Arguments:
- inputs: bfloat16 [16, 2048, 1152], P('dp', 'chan'), may hold values from -6 to 6
- weight: bfloat16 [2048, 9, 256], P('chan'), may hold values from -0.046875 to 0.046875
- cotangent: bfloat16 [16, 256, 1152], P('dp', 'chan'), may hold values from -6 to 6
Outputs:
- result: bfloat16 [16, 256, 1152], P('dp', 'chan')
- input_grad: bfloat16 [16, 2048, 1152], P('dp', 'chan')
- weight_grad: float32 [2048, 9, 256], P('chan')
All inputs are finite; a program needn't handle non-finite values.
Results may differ from a plain program's by a relative error of at most 0.001.
Values may be sent and summed in bfloat16 or wider, within the bound.
No kernel may reach another device: no remote copies, remote signals or barrier semaphores. Data moves between devices by JAX's collectives and lax.ppermute only.
A program may use at most 64 MiB of HBM per device.

v0:
```python
import jax
import jax.numpy as jnp
from jax import lax
from jax.sharding import PartitionSpec as P

DILATION_RATE = 12
MAP_HEIGHT = 16
MAP_WIDTH = 72


def translated_input(receptive_field, row_shift, column_shift, reach):
    height, width = (receptive_field.shape[1], receptive_field.shape[2])
    bordered_input = jnp.pad(receptive_field, ((0, 0), (reach, reach), (reach, reach)))
    return bordered_input[
        :,
        reach + row_shift : reach + row_shift + height,
        reach + column_shift : reach + column_shift + width,
    ]


def on_device(inputs, weight, cotangent):
    input_channels_local = inputs.shape[1]
    cout_local = cotangent.shape[1]
    tap_locations = MAP_HEIGHT * MAP_WIDTH
    feature_map = inputs[0].reshape(input_channels_local, MAP_HEIGHT, MAP_WIDTH)
    tap_list = weight.shape[1]
    output_channels_total = weight.shape[2]
    tap_shifts = [
        (DILATION_RATE * (tap_index // 3 - 1), DILATION_RATE * (tap_index % 3 - 1))
        for tap_index in range(tap_list)
    ]
    displaced_input = [
        translated_input(feature_map, first_operand, second_operand, DILATION_RATE).reshape(
            input_channels_local, tap_locations
        )
        for first_operand, second_operand in tap_shifts
    ]
    contract_rows = (((0,), (0,)), ((), ()))
    total = jnp.zeros((cout_local * lax.axis_size("chan"), tap_locations), jnp.float32)
    for tap_index in range(tap_list):
        columns = weight[:, tap_index, :]
        total = total + lax.dot_general(
            columns, displaced_input[tap_index], contract_rows, preferred_element_type=jnp.float32
        )
    owned = lax.psum_scatter(total, "chan", scatter_dimension=0, tiled=True)
    result = owned.astype(jnp.bfloat16).reshape(1, cout_local, tap_locations)
    flat_grads = lax.all_gather(cotangent[0], "chan", axis=0, tiled=True)
    collected_input = flat_grads.reshape(output_channels_total, MAP_HEIGHT, MAP_WIDTH)
    back_sum = jnp.zeros((input_channels_local, tap_locations), jnp.float32)
    for tap_index in range(tap_list):
        row_shift, column_shift = tap_shifts[tap_index]
        displaced_gradient = translated_input(
            collected_input, -row_shift, -column_shift, DILATION_RATE
        ).reshape(output_channels_total, tap_locations)
        back_sum = back_sum + jnp.dot(
            weight[:, tap_index, :], displaced_gradient, preferred_element_type=jnp.float32
        )
    input_grad = back_sum.astype(jnp.bfloat16).reshape(1, input_channels_local, tap_locations)
    contract_cols = (((1,), (1,)), ((), ()))
    local_grad = jnp.stack(
        [
            lax.dot_general(
                displaced_input[tap_index],
                flat_grads,
                contract_cols,
                preferred_element_type=jnp.float32,
            )
            for tap_index in range(tap_list)
        ],
        axis=1,
    )
    summed_grad = lax.psum(local_grad, "dp")
    weight_grad = summed_grad / jnp.float32(lax.axis_size("dp"))
    return (result, input_grad, weight_grad)


def solution(mesh):
    placed = (P("dp", "chan", None), P("chan", None, None), P("dp", "chan", None))
    return jax.shard_map(
        on_device,
        mesh=mesh,
        in_specs=placed,
        out_specs=(P("dp", "chan", None), P("dp", "chan", None), P("chan", None, None)),
        check_vma=False,
    )
```

profile of v0, /device:TPU:0, one launch (start us, length us, event | category | flops | bytes accessed | tf_op | source)
XLA Modules:
  0.0 268.8 jit_solution(9408169461751972447)
XLA Ops:
  8.0 0.0 reduce-scatter.2.cloned.1.call-start
  8.0 4.3 %copy.10 = bf16[1,1024,1152]{1,2,0:T(8,128)(2,1)} copy(bf16[1,1024,1152]{2,1,0:T(8,128)(2,1)} %param.3) | data formatting | bytes 4718592 | tf_op args[0]
  12.3 8.4 %pad_slice_fusion.4 = (bf16[1024,16,72]{0,2,1:T(8,128)(2,1)S(1)}, bf16[1024,16,72]{0,2,1:T(8,128)(2,1)S(1)}, bf16[1024,16,72]{0,2,1:T(8,128)(2,1)S(1)}, bf16[102...) fusion(bf16[1024,16,72]{0,2,1:T(8,128)(2,1)} %bitcast.193), kind=kLoop, calls=%fused_computation.4 | loop fusion | bytes 21233664 | tf_op jit(solution)/shard_map/slice | solution.py:14
  20.8 0.0 copy-start.2
  20.8 4.2 %convolution_bitcast_fusion.3 = f32[256,1152]{0,1:T(8,128)S(1)} fusion(bf16[1024,1152]{0,1:T(8,128)(2,1)} %bitcast.209, bf16[1024,9,256]{2,0,1:T(8,128)(2,1)S(1)} %copy-done.4), kind=kOutput, calls=%fused_computation.38 | convolution fusion | flops 603979776 | bytes 4063232 | tf_op jit(solution)/shard_map/dot_general | solution.py:42
  25.0 0.8 convolution_bitcast_fusion.2
  25.8 0.0 copy-done.9
  25.8 0.8 convolution_bitcast_fusion.1
  26.6 0.8 convolution_bitcast_fusion
  27.4 0.9 copy-done.14
  28.3 0.8 fusion.57
  29.1 0.8 convolution_add_fusion.7
  29.9 0.8 convolution_add_fusion.6
  30.7 0.0 copy-start.5
  30.7 0.8 fusion.8
  31.5 0.8 copy-done.5
  32.3 2.3 fusion.7
  34.7 0.0 reduce-scatter.2.cloned.1.call-update
  34.7 0.0 all-reduce.4.cloned.1.call-start
  34.8 0.2 copy.12
  35.0 12.9 %all-gather = bf16[1,256,1152]{1,2,0:T(8,128)(2,1)S(1)} all-gather(bf16[1,128,1152]{1,2,0:T(8,128)(2,1)S(1)} %copy.12), channel_id=2, replica_groups=mesh['dp'=16,'chan'=2] {'chan'}, dimensions={1}, use_global_device_ids=true | all-gather | bytes 884736 | tf_op jit(solution)/shard_map/all_gather | solution.py:47
  47.9 3.7 %fusion.25 = f32[1024,9,256]{2,0,1:T(8,128)} fusion(bf16[1024,1152]{0,1:T(8,128)(2,1)} %bitcast.211, bf16[1,256,1152]{1,2,0:T(8,128)(2,1)S(1)} %all-gather), kind=kOutput, calls=%fused_computation.60 | convolution fusion | flops 603979776 | bytes 3997696 | tf_op jit(solution)/shard_map/dot_general | solution.py:62
  51.6 1.8 fusion.24
  53.4 1.8 fusion.23
  55.3 1.8 fusion.22
  57.1 1.8 fusion.15
  59.0 1.8 fusion.21
  60.8 1.8 fusion.20
  62.7 1.8 fusion.19
  64.5 1.8 fusion.18
  66.4 0.0 all-reduce.4.cloned.1.call-update
  66.4 0.0 slice-start
  66.4 0.7 pad_slice_fusion.9
  67.2 0.0 slice-start.1
  67.2 2.2 fusion.38
  69.4 0.8 fusion.44
  70.2 0.8 fusion.41
  71.1 0.8 fusion.55
  71.9 1.1 convolution_add_fusion.3
  73.0 0.9 convolution_add_fusion.2
  73.9 0.9 convolution_add_fusion.1
  74.8 1.0 fusion.1
  75.8 0.8 fusion.3
  76.6 2.4 copy.15
  79.1 1.1 convert_bitcast_fusion
  80.2 0.9 copy.14
  81.1 172.0 %all-reduce.4.cloned.1.call-done = f32[1024,9,256]{2,0,1:T(8,128)} async-done(((f32[1024,9,256]{2,0,1:T(8,128)}), f32[1024,9,256]{2,0,1:T(8,128)}) %all-reduce.4.cloned.1.call-update) | async-done | bytes 9437200 | tf_op jit(solution)/shard_map/psum | solution.py:72
  253.1 8.2 %broadcast_multiply_fusion = f32[1024,9,256]{2,0,1:T(8,128)} fusion(f32[1024,9,256]{2,0,1:T(8,128)} %all-reduce.4.cloned.1.call-done), kind=kLoop, calls=%fused_computation.25 | loop fusion | flops 2359296 | bytes 18874368 | tf_op jit(solution)/shard_map/div | solution.py:73
  (31 shorter events, 0.1 us)
Async XLA Ops:
  8.0 71.1 %reduce-scatter.2.cloned.1.call-start = ((), (), s32[]{:S(2)}) async-start(), calls=%async_computation.1 | async-start | bytes 1769472 | tf_op jit(solution)/shard_map/reduce_scatter | solution.py:45
  12.3 8.5 %copy-start.4 = (bf16[1024,9,256]{2,0,1:T(8,128)(2,1)S(1)}, bf16[1024,9,256]{2,0,1:T(8,128)(2,1)}, u32[]{:S(2)}) copy-start(bf16[1024,9,256]{2,0,1:T(8,128)(2,1)} %param.4) | copy-start | bytes 14155780
  20.8 5.1 %copy-start.9 = (bf16[1024,16,72]{0,2,1:T(8,128)(2,1)}, bf16[1024,16,72]{0,2,1:T(8,128)(2,1)S(1)}, u32[]{:S(2)}) copy-start(bf16[1024,16,72]{0,2,1:T(8,128)(2,1)S(1)} %get-tuple-element.14) | copy-start | bytes 7077892
  20.8 5.8 %copy-start.11 = (bf16[1024,16,72]{0,2,1:T(8,128)(2,1)}, bf16[1024,16,72]{0,2,1:T(8,128)(2,1)S(1)}, u32[]{:S(2)}) copy-start(bf16[1024,16,72]{0,2,1:T(8,128)(2,1)S(1)} %get-tuple-element.13) | copy-start | bytes 7077892
  20.8 5.8 %copy-start.7 = (bf16[1024,16,72]{0,2,1:T(8,128)(2,1)}, bf16[1024,16,72]{0,2,1:T(8,128)(2,1)S(1)}, u32[]{:S(2)}) copy-start(bf16[1024,16,72]{0,2,1:T(8,128)(2,1)S(1)} %get-tuple-element.15) | copy-start | bytes 7077892
  20.8 8.3 %copy-start.2 = (bf16[1024,16,72]{0,2,1:T(8,128)(2,1)}, bf16[1024,16,72]{0,2,1:T(8,128)(2,1)S(1)}, u32[]{:S(2)}) copy-start(bf16[1024,16,72]{0,2,1:T(8,128)(2,1)S(1)} %get-tuple-element.10) | copy-start | bytes 7077892
  20.8 9.1 %copy-start = (bf16[1024,16,72]{0,2,1:T(8,128)(2,1)}, bf16[1024,16,72]{0,2,1:T(8,128)(2,1)S(1)}, u32[]{:S(2)}) copy-start(bf16[1024,16,72]{0,2,1:T(8,128)(2,1)S(1)} %get-tuple-element.11) | copy-start | bytes 7077892
  26.6 1.7 copy-start.14
  30.7 1.7 copy-start.5
  32.3 2.4 copy-start.15
  34.7 218.4 %all-reduce.4.cloned.1.call-start = ((), (), s32[]{:S(2)}) async-start(), calls=%async_computation.2 | async-start | bytes 18874368 | tf_op jit(solution)/shard_map/psum | solution.py:72
  47.9 3.7 %copy-start.3 = (bf16[1024,16,72]{0,2,1:T(8,128)(2,1)S(1)}, bf16[1024,16,72]{0,2,1:T(8,128)(2,1)}, u32[]{:S(2)}) copy-start(bf16[1024,16,72]{0,2,1:T(8,128)(2,1)} %copy-done.2) | copy-start | bytes 7077892
  51.6 1.9 copy-start.1
  55.3 1.9 copy-start.6
  57.1 1.8 copy-start.13
  59.0 1.9 copy-start.12
  60.8 1.9 copy-start.10
  62.7 1.9 copy-start.8
  66.4 3.0 %slice-start = ((s8[4718592]{0:T(1024)(128)(4,1)}), s8[4194304]{0:T(1024)(128)(4,1)S(1)}, s32[]{:S(2)}) async-start(s8[4718592]{0:T(1024)(128)(4,1)} %bitcast.191), calls=%async_computation.3 | async-start | bytes 8388608
  67.2 2.3 slice-start.1
Sparse Core Ops, SparseCore 0:
  34.8 24.7 reduce-scatter.1
Sparse Core Ops, SparseCore 1:
  66.5 186.5 all-reduce.3
where the time goes:
time: 269 us
  waiting for transfers between devices  172 us (64%)
  matrix products  39.8 us (15%)
  local copies, waits for them, and re-layouts  18.8 us (7%)
  between operations  15.8 us (6%)
  blocking collectives  12.9 us (5%)
  other arithmetic  9.34 us (3%)
    psum x1, waiting for transfers between devices, on_device(): summed_grad = lax.psum(local_grad, 'dp')  172 us
    dot_general x9, matrix products, on_device(): lax.dot_general(displaced_input[tap_index], flat_grads, contract_cols, pr...  18.4 us
    all_gather x1, blocking collectives, on_device(): flat_grads = lax.all_gather(cotangent[0], 'chan', axis=0, tiled=True)  12.9 us
    dot_general x9, matrix products, on_device(): lax.dot_general(columns, displaced_input[tap_index], contract_rows, prefe...  12 us
    unnamed x40, local copies, waits for them, and re-layouts  9.61 us
    dot_general x9, matrix products, on_device(): jnp.dot(weight[:, tap_index, :], displaced_gradient, preferred_element_ty...  9.38 us
    slice x2, local copies, waits for them, and re-layouts, translated_input(): bordered_input[:, reach + row_shift:reach + row_shift + height, reach + c...  9.19 us
    div x1, other arithmetic, on_device(): weight_grad = summed_grad / jnp.float32(lax.axis_size('dp'))  8.24 us
  transfers between devices with their start and end apart: 2, of which 1 were waited for; matrix products, arithmetic and copies ran while one was open for 12% of the time, Pallas kernels for 0%

commit v1 on v0

v1 whole, which is shorter than its diff:
```python
import jax
import jax.numpy as jnp
from jax import lax
from jax.experimental import pallas as pl
from jax.experimental.pallas import tpu as pltpu
from jax.sharding import PartitionSpec as P

DILATION_RATE = 12
MAP_HEIGHT = 16
MAP_WIDTH = 72
HW = MAP_HEIGHT * MAP_WIDTH
REACH = (MAP_HEIGHT - DILATION_RATE) * MAP_WIDTH
WINDOW = 384
PAD = WINDOW - REACH
COLUMN_SHIFTS = (-DILATION_RATE, 0, DILATION_RATE)
VMEM_LIMIT = 48 * 1024 * 1024


def column_mask(start, width, shift):
    position = lax.broadcasted_iota(jnp.int32, (1, width), 1) + start
    column = lax.rem(position, MAP_WIDTH) + shift
    return position, (column >= 0) & (column < MAP_WIDTH)


def moved(values, amount):
    amount = amount % values.shape[1]
    return values if amount == 0 else pltpu.roll(values, amount, 1)


def moved_cotangent(cot, group, shift):
    if group == 1:
        _, inside = column_mask(0, HW, -shift)
        values = moved(cot, shift)
    elif group == 0:
        position, inside = column_mask(0, WINDOW, -shift)
        inside = inside & (position < REACH)
        values = moved(cot[:, HW - WINDOW :], shift - PAD)
    else:
        position, inside = column_mask(HW - WINDOW, WINDOW, -shift)
        inside = inside & (position >= HW - REACH)
        values = moved(cot[:, :WINDOW], PAD + shift)
    return jnp.where(inside, values, 0.0).astype(jnp.bfloat16)


def window(group):
    return (slice(0, WINDOW), slice(0, HW), slice(HW - WINDOW, HW))[group]


def kernel_grad_kernel(half_ref, own_x, other_x, own_cot, other_cot, out_ref):
    step = pl.program_id(0)
    for group in range(3):

        @pl.when(step == group)
        def _(group=group):
            where = window(group)
            for column, shift in enumerate(COLUMN_SHIFTS):
                total = None
                for x_ref, cot_ref in ((own_x, own_cot), (other_x, other_cot)):
                    cot = moved_cotangent(cot_ref[...].astype(jnp.float32), group, shift)
                    term = lax.dot_general(
                        x_ref[:, where],
                        cot,
                        (((1,), (1,)), ((), ())),
                        preferred_element_type=jnp.float32,
                    )
                    total = term if total is None else total + term
                out_ref[column] = total


def kernel_grad(half, x, other_x, own_cot, other_cot):
    rows, positions = other_x.shape
    outs = own_cot.shape[0]
    whole = lambda g, h: (0, 0)
    return pl.pallas_call(
        kernel_grad_kernel,
        out_shape=jax.ShapeDtypeStruct((9, rows, outs), jnp.float32),
        grid_spec=pltpu.PrefetchScalarGridSpec(
            num_scalar_prefetch=1,
            grid=(3,),
            in_specs=[
                pl.BlockSpec((rows, positions), lambda g, h: (h[0], 0)),
                pl.BlockSpec((rows, positions), whole),
                pl.BlockSpec((outs, positions), whole),
                pl.BlockSpec((outs, positions), whole),
            ],
            out_specs=pl.BlockSpec((3, rows, outs), lambda g, h: (g, 0, 0)),
        ),
        compiler_params=pltpu.CompilerParams(vmem_limit_bytes=VMEM_LIMIT),
        cost_estimate=pl.CostEstimate(
            flops=4 * rows * outs * 3 * (HW + 2 * WINDOW),
            bytes_accessed=4 * rows * positions + 4 * outs * positions + 36 * rows * outs,
            transcendentals=0,
        ),
        name="kernel_grad",
    )(half, x, other_x, own_cot, other_cot)


def forward_kernel(x_ref, w_ref, out_ref):
    step = pl.program_id(0)
    for group in range(3):

        @pl.when(step == group)
        def _(group=group):
            where = window(group)
            total = None
            for column, shift in enumerate(COLUMN_SHIFTS):
                term = lax.dot_general(
                    w_ref[column],
                    x_ref[:, where],
                    (((0,), (0,)), ((), ())),
                    preferred_element_type=jnp.float32,
                )
                if group == 1:
                    _, inside = column_mask(0, HW, shift)
                    term = moved(term, -shift)
                elif group == 0:
                    position, inside = column_mask(HW - WINDOW, WINDOW, shift)
                    inside = inside & (position >= HW - REACH)
                    term = moved(term, PAD - shift)
                else:
                    position, inside = column_mask(0, WINDOW, shift)
                    inside = inside & (position < REACH)
                    term = moved(term, -PAD - shift)
                term = jnp.where(inside, term, 0.0)
                total = term if total is None else total + term
            if group == 0:
                out_ref[:, : HW - WINDOW] = jnp.zeros((out_ref.shape[0], HW - WINDOW), jnp.float32)
                out_ref[:, HW - WINDOW :] = total
            elif group == 1:
                out_ref[...] += total
            else:
                out_ref[:, :WINDOW] += total


def forward(x, w):
    rows, positions = x.shape
    outs = w.shape[2]
    return pl.pallas_call(
        forward_kernel,
        out_shape=jax.ShapeDtypeStruct((outs, positions), jnp.float32),
        grid=(3,),
        in_specs=[
            pl.BlockSpec((rows, positions), lambda g: (0, 0)),
            pl.BlockSpec((3, rows, outs), lambda g: (g, 0, 0)),
        ],
        out_specs=pl.BlockSpec((outs, positions), lambda g: (0, 0)),
        compiler_params=pltpu.CompilerParams(vmem_limit_bytes=VMEM_LIMIT),
        cost_estimate=pl.CostEstimate(
            flops=2 * rows * outs * 3 * (HW + 2 * WINDOW),
            bytes_accessed=2 * rows * positions + 18 * rows * outs + 4 * outs * positions,
            transcendentals=0,
        ),
        name="forward",
    )(x, w)


def input_grad_kernel(cot_ref, w_ref, out_ref, middle, upper, lower):
    @pl.when(pl.program_id(0) == 0)
    def _():
        cot = cot_ref[...].astype(jnp.float32)
        for group, held in enumerate((upper, middle, lower)):
            for column, shift in enumerate(COLUMN_SHIFTS):
                held[column] = moved_cotangent(cot, group, shift)

    def products(group, held):
        total = None
        for column in range(3):
            term = jnp.dot(
                w_ref[3 * group + column], held[column], preferred_element_type=jnp.float32
            )
            total = term if total is None else total + term
        return total

    edge = HW - WINDOW
    centre = products(1, middle)
    out_ref[:, :WINDOW] = (centre[:, :WINDOW] + products(0, upper)).astype(jnp.bfloat16)
    out_ref[:, WINDOW:edge] = centre[:, WINDOW:edge].astype(jnp.bfloat16)
    out_ref[:, edge:] = (centre[:, edge:] + products(2, lower)).astype(jnp.bfloat16)


def input_gradient(cot, w):
    outs, positions = cot.shape
    rows = w.shape[1]
    block = min(rows, 256)
    return pl.pallas_call(
        input_grad_kernel,
        out_shape=jax.ShapeDtypeStruct((rows, positions), jnp.bfloat16),
        grid=(rows // block,),
        in_specs=[
            pl.BlockSpec((outs, positions), lambda g: (0, 0)),
            pl.BlockSpec((9, block, outs), lambda g: (0, g, 0)),
        ],
        out_specs=pl.BlockSpec((block, positions), lambda g: (g, 0)),
        scratch_shapes=[
            pltpu.VMEM((3, outs, HW), jnp.bfloat16),
            pltpu.VMEM((3, outs, WINDOW), jnp.bfloat16),
            pltpu.VMEM((3, outs, WINDOW), jnp.bfloat16),
        ],
        compiler_params=pltpu.CompilerParams(vmem_limit_bytes=VMEM_LIMIT),
        cost_estimate=pl.CostEstimate(
            flops=2 * rows * outs * 3 * (HW + 2 * WINDOW),
            bytes_accessed=2 * outs * positions + 18 * rows * outs + 2 * rows * positions,
            transcendentals=0,
        ),
        name="input_gradient",
    )(cot, w)


def on_device(inputs, weight, cotangent):
    x = inputs[0]
    own_cot = cotangent[0]
    w = jnp.transpose(weight, (1, 0, 2))
    taps, rows, outs = w.shape
    own_outs, positions = own_cot.shape
    samples = lax.axis_size("dp")
    chans = lax.axis_size("chan")
    depth = samples // 4
    place = lax.axis_index("dp")
    chan = lax.axis_index("chan")
    core, column, level = place % 2, (place // 2) % 2, place // 4
    core_rows = rows // 2
    chip_rows = core_rows // 2
    shard_rows = chip_rows // depth

    def to(value, target):
        return lax.ppermute(value, "dp", [(i, target(i)) for i in range(samples)])

    def to_core(value):
        return to(value, lambda i: i ^ 1)

    def to_column(value):
        return to(value, lambda i: i ^ 2)

    def to_level(value, step):
        return to(value, lambda i: ((i // 4 + step) % depth) * 4 + i % 4)

    other_x = to_core(lax.dynamic_slice_in_dim(x, (1 - core) * core_rows, core_rows, 0))
    if chans == 2:
        their_cot = lax.ppermute(own_cot, "chan", [(0, 1), (1, 0)])
        cot = jnp.where(
            chan == 0,
            jnp.concatenate([own_cot, their_cot], 0),
            jnp.concatenate([their_cot, own_cot], 0),
        )
    else:
        cot = lax.all_gather(own_cot, "chan", axis=0, tiled=True)
    other_cot = to_core(cot)

    largest = lax.pmax(
        jnp.stack([jnp.max(jnp.abs(x)), jnp.max(jnp.abs(own_cot))]).astype(jnp.float32),
        ("dp", "chan"),
    )
    bound = jnp.maximum(largest[0] * largest[1] * (positions * samples), 1e-30)
    scale = 30000.0 / bound
    unscale = bound * (1.0 / (30000.0 * samples))

    half = jnp.reshape(core, (1,)).astype(jnp.int32)
    partial = kernel_grad(half, x, other_x, cot, other_cot)

    def piece(row):
        return lax.dynamic_slice_in_dim(partial, row, shard_rows, 1) * scale

    summed = [None] * depth
    for step in list(range(1, depth)) + [0]:
        owner = (level + step) % depth
        sent = piece((1 - column) * chip_rows + owner * shard_rows).astype(jnp.float16)
        came = to_column(sent)
        summed[step] = piece(column * chip_rows + owner * shard_rows) + came.astype(jnp.float32)
    own = summed[0]
    for step in range(1, depth):
        own = own + to_level(summed[step].astype(jnp.float16), step).astype(jnp.float32)
    shard = own.astype(jnp.float16)

    pieces = []
    for step in range(depth):
        near = shard if step == 0 else to_level(shard, step)
        far = to_column(near)
        owner = (level - step) % depth
        for which, value in ((column, near), (1 - column, far)):
            row = which * chip_rows + owner * shard_rows
            pieces.append((core * core_rows + row, value))
            pieces.append(((1 - core) * core_rows + row, to_core(value)))
    grad = jnp.zeros((taps, rows, outs), jnp.float32)
    for row, value in pieces:
        grad = lax.dynamic_update_slice_in_dim(grad, value.astype(jnp.float32) * unscale, row, 1)
    weight_grad = jnp.transpose(grad, (1, 0, 2))

    total = forward(x, w)
    if chans == 2:
        mine = lax.dynamic_slice_in_dim(total, chan * own_outs, own_outs, 0)
        theirs = lax.dynamic_slice_in_dim(total, (1 - chan) * own_outs, own_outs, 0)
        result = mine + lax.ppermute(theirs, "chan", [(0, 1), (1, 0)])
    else:
        result = lax.psum_scatter(total, "chan", scatter_dimension=0, tiled=True)
    result = result.astype(jnp.bfloat16)[None]
    input_grad = input_gradient(cot, w)[None]
    return (result, input_grad, weight_grad)


def solution(mesh):
    placed = (P("dp", "chan", None), P("chan", None, None), P("dp", "chan", None))
    return jax.shard_map(
        on_device,
        mesh=mesh,
        in_specs=placed,
        out_specs=(P("dp", "chan", None), P("dp", "chan", None), P("chan", None, None)),
        check_vma=False,
    )
```

time: 269 us -> 175 us (0.65)
  the two profiles are of different devices: /device:TPU:0 before, /device:TPU:13 now
where the time goes in v1:
time: 175 us; the launch traced here: 174 us
  waiting for transfers between devices  56.8 us (32%)
  blocking collectives  38.8 us (22%)
  starting transfers between devices  32.2 us (18%)
  Pallas kernels  18.3 us (10%)
  other arithmetic  15.6 us (9%)
  local copies, waits for them, and re-layouts  10.5 us (6%)
  between operations  2.25 us (1%)
    ppermute x24, waiting for transfers between devices, to(): return lax.ppermute(value, 'dp', [(i, target(i)) for i in range(samples)])  48.2 us
    pmax x1, blocking collectives, on_device(): lax.pmax(jnp.stack([jnp.max(jnp.abs(x)), jnp.max(jnp.abs(own_cot))]).asty...  38.8 us
    ppermute x24, starting transfers between devices, to(): return lax.ppermute(value, 'dp', [(i, target(i)) for i in range(samples)])  31.7 us
    ppermute x1, waiting for transfers between devices, on_device(): their_cot = lax.ppermute(own_cot, 'chan', [(0, 1), (1, 0)])  8.56 us
    unnamed x6, local copies, waits for them, and re-layouts  7.73 us
    pallas_call x1, Pallas kernels, input_gradient(): pl.pallas_call(input_grad_kernel, out_shape=jax.ShapeDtypeStruct((rows, p...  6.54 us
    pallas_call x1, Pallas kernels, forward(): pl.pallas_call(forward_kernel, out_shape=jax.ShapeDtypeStruct((outs, posi...  6.08 us
    pallas_call x1, Pallas kernels, kernel_grad(): pl.pallas_call(kernel_grad_kernel, out_shape=jax.ShapeDtypeStruct((9, row...  5.65 us
  transfers between devices with their start and end apart: 26, of which 10 were waited for; matrix products, arithmetic and copies ran while one was open for 8% of the time, Pallas kernels for 7%

profile of v1, /device:TPU:13, one launch (start us, length us, event | category | flops | bytes accessed | tf_op | source)
XLA Modules:
  0.0 174.4 jit_solution(12660823106351010781)
XLA Ops:
  0.7 1.4 dynamic-slice_bitcast_fusion
  2.0 0.7 collective-permute-start.2
  3.0 8.6 %collective-permute-done.1 = bf16[128,1152]{1,0:T(8,128)(2,1)S(1)} collective-permute-done((bf16[128,1152]{1,0:T(8,128)(2,1)}, bf16[128,1152]{1,0:T(8,128)(2,1)S(1)}, u32[]{:S(2)}, u32[]{:S(2)}) %collective-permute-start.1) | collective-permute-done | bytes 294944 | tf_op jit(solution)/shard_map/ppermute | solution.py:239
  11.6 1.2 maximum_select_fusion.cot_ref.own_cot
  12.8 0.9 collective-permute-start.3
  13.7 1.6 abs_reduce_fusion.1
  15.3 2.6 %abs_reduce_fusion = bf16[]{:T(256)} fusion(bf16[1,1024,1152]{2,1,0:T(8,128)(2,1)} %param.3), kind=kLoop, calls=%fused_computation | loop fusion | flops 2359295 | bytes 2359298 | tf_op jit(solution)/shard_map/reduce_max | solution.py:250
  17.8 1.4 maximum_convert_fusion
  19.2 38.8 %pmax.7 = f32[2]{0:T(128)S(1)} all-reduce(f32[2]{0:T(128)S(1)} %maximum_convert_fusion), channel_id=1, replica_groups=mesh['dp'=16,'chan'=2] {'dp','chan'}, use_global_device_ids=true, to_apply=%region_2.3 | all-reduce | flops 2 | bytes 16 | tf_op jit(solution)/shard_map/pmax | solution.py:249
  58.1 0.6 fusion.1
  60.0 1.7 copy-done
  61.7 5.7 %kernel_grad.1 = f32[9,512,256]{2,1,0:T(8,128)} custom-call(s32[1]{0:T(128)} %bitcast.5.half_ref, bf16[1024,1152]{1,0:T(8,128)(2,1)S(1)} %bitcast.16, bf16[512,1152]{1,0:T(8,128)(2,1)S(1)} %collective-permute-done.2.other_x, bf16[256,1152]{1,0:T(8,128)(2,1)S(1)} %maximum_select_fusion.cot_ref.own_cot, bf16[256,1152]{1,0:T(8,128)(2,1)S(1)} %collective-permute-done.3.other_cot), custom_call_target="tpu_custom_call" | custom-call | flops 3019898880 | bytes 8257536 | tf_op jit(solution)/shard_map/kernel_grad/pallas_call | solution.py:74
  67.3 2.7 %multiply_convert_fusion.3 = (f16[9,64,256]{2,1,0:T(8,128)(2,1)S(1)}, f16[9,64,256]{2,1,0:T(8,128)(2,1)}, f16[9,64,256]{2,1,0:T(8,128)(2,1)}, f16[9,64,256]{2,1,0:T(8,128)(2,1)}) fusion(f32[9,512,256]{2,1,0:T(8,128)} %kernel_grad.1, s32[]{:T(128)S(6)} %select_n.148, f32[]{:T(128)} %bitcast.9, s32[]{:T(128)S(6)} %select_n.157, s32[]{:T(128)S(6)} %select_n.154, ...), kind=kLoop, calls=%fused_computation.26 | loop fusion | flops 1179648 | bytes 3538964 | tf_op jit(solution)/shard_map/convert_element_type | solution.py:266
  70.0 1.2 collective-permute-start.5
  71.2 0.2 collective-permute-start.7
  71.5 1.2 collective-permute-start.9
  72.7 6.1 %forward.1 = f32[256,1152]{1,0:T(8,128)S(1)} custom-call(bf16[1024,1152]{1,0:T(8,128)(2,1)S(1)} %bitcast.17, bf16[9,1024,256]{2,1,0:T(8,128)(2,1)} %bitcast.18), custom_call_target="tpu_custom_call" | custom-call | flops 3019898880 | bytes 8257536 | tf_op jit(solution)/shard_map/forward/pallas_call | solution.py:138
  78.8 0.3 collective-permute-start
  79.1 0.4 collective-permute-start.4
  79.5 3.2 %collective-permute-done.7 = f16[9,64,256]{2,1,0:T(8,128)(2,1)} collective-permute-done((f16[9,64,256]{2,1,0:T(8,128)(2,1)}, f16[9,64,256]{2,1,0:T(8,128)(2,1)}, u32[]{:S(2)}, u32[]{:S(2)}) %collective-permute-start.7) | collective-permute-done | bytes 294944 | tf_op jit(solution)/shard_map/ppermute | solution.py:226
  82.7 6.3 %collective-permute-done.9 = f16[9,64,256]{2,1,0:T(8,128)(2,1)} collective-permute-done((f16[9,64,256]{2,1,0:T(8,128)(2,1)}, f16[9,64,256]{2,1,0:T(8,128)(2,1)}, u32[]{:S(2)}, u32[]{:S(2)}) %collective-permute-start.9) | collective-permute-done | bytes 294944 | tf_op jit(solution)/shard_map/ppermute | solution.py:226
  89.0 2.8 %add_convert_fusion.3 = (f16[9,64,256]{2,1,0:T(8,128)(2,1)}, f16[9,64,256]{2,1,0:T(8,128)(2,1)}, f16[9,64,256]{2,1,0:T(8,128)(2,1)}) fusion(f16[9,64,256]{2,1,0:T(8,128)(2,1)} %collective-permute-done.5, f32[9,512,256]{2,1,0:T(8,128)} %kernel_grad.1, s32[]{:T(128)S(6)} %select_n.150, f32[]{:T(128)} %bitcast.9, f16[9,64,256]{2,1,0:T(8,128)(2,1)} %collective-permute-done.9, ...), kind=kLoop, calls=%fused_computation.24 | loop fusion | flops 1769472 | bytes 3538960 | tf_op jit(solution)/shard_map/convert_element_type | solution.py:271
  91.8 0.2 collective-permute-start.10
  92.0 1.2 collective-permute-start.6
  93.3 2.8 %collective-permute-start.8 = (f16[9,64,256]{2,1,0:T(8,128)(2,1)}, f16[9,64,256]{2,1,0:T(8,128)(2,1)}, u32[]{:S(2)}, u32[]{:S(2)}) collective-permute-start(f16[9,64,256]{2,1,0:T(8,128)(2,1)} %get-tuple-element.11), channel_id=1, source_target_pairs={{0,16},{2,18},{4,20},{6,22},{8,24},{10,26},{12,28},{14,30},{16,0},... | collective-permute-start | bytes 884744 | tf_op jit(solution)/shard_map/ppermute | solution.py:226
  96.0 2.3 %copy-done.1 = bf16[1024,9,256]{2,0,1:T(8,128)(2,1)S(1)} copy-done((bf16[1024,9,256]{2,0,1:T(8,128)(2,1)S(1)}, bf16[1024,9,256]{2,0,1:T(8,128)(2,1)}, u32[]{:S(2)}) %copy-start.1) | copy-done | bytes 4718616
  98.4 6.5 %input_gradient.1 = bf16[1024,1152]{1,0:T(8,128)(2,1)} custom-call(bf16[256,1152]{1,0:T(8,128)(2,1)S(1)} %maximum_select_fusion.cot_ref.own_cot, bf16[9,1024,256]{2,1,0:T(8,128)(2,1)S(1)} %bitcast.19), custom_call_target="tpu_custom_call" | custom-call | flops 3019898880 | bytes 7667712 | tf_op jit(solution)/shard_map/input_gradient/pallas_call | solution.py:185
  104.9 10.6 %collective-permute-done.8 = f16[9,64,256]{2,1,0:T(8,128)(2,1)} collective-permute-done((f16[9,64,256]{2,1,0:T(8,128)(2,1)}, f16[9,64,256]{2,1,0:T(8,128)(2,1)}, u32[]{:S(2)}, u32[]{:S(2)}) %collective-permute-start.8) | collective-permute-done | bytes 294944 | tf_op jit(solution)/shard_map/ppermute | solution.py:226
  115.6 0.8 broadcast_in_dim.11
  116.4 1.6 multiply_dynamic-update-slice_fusion.15
  118.0 4.2 %collective-permute-start.11 = (f16[9,64,256]{2,1,0:T(8,128)(2,1)S(1)}, f16[9,64,256]{2,1,0:T(8,128)(2,1)S(1)}, u32[]{:S(2)}, u32[]{:S(2)}) collective-permute-start(f16[9,64,256]{2,1,0:T(8,128)(2,1)S(1)} %get-tuple-element.4), channel_id=1, source_target_pairs={{0,2},{2,0},{4,6},{6,4},{8,10},{10,8},{12,14},{14,12},{16,18},{18,... | collective-permute-start | bytes 884744 | tf_op jit(solution)/shard_map/ppermute | solution.py:226
  122.2 2.2 %collective-permute-start.12 = (f16[9,64,256]{2,1,0:T(8,128)(2,1)S(1)}, f16[9,64,256]{2,1,0:T(8,128)(2,1)S(1)}, u32[]{:S(2)}, u32[]{:S(2)}) collective-permute-start(f16[9,64,256]{2,1,0:T(8,128)(2,1)S(1)} %get-tuple-element.4), channel_id=1, source_target_pairs={{0,4},{2,6},{4,0},{6,2},{8,12},{10,14},{12,8},{14,10},{16,20},{18,... | collective-permute-start | bytes 884744 | tf_op jit(solution)/shard_map/ppermute | solution.py:226
  124.5 4.0 %collective-permute-start.18 = (f16[9,64,256]{2,1,0:T(8,128)(2,1)S(1)}, f16[9,64,256]{2,1,0:T(8,128)(2,1)S(1)}, u32[]{:S(2)}, u32[]{:S(2)}) collective-permute-start(f16[9,64,256]{2,1,0:T(8,128)(2,1)S(1)} %get-tuple-element.4), channel_id=1, source_target_pairs={{0,16},{2,18},{4,20},{6,22},{8,24},{10,26},{12,28},{14,30},{16,0},... | collective-permute-start | bytes 884744 | tf_op jit(solution)/shard_map/ppermute | solution.py:226
  128.5 0.8 fusion
  129.3 0.5 collective-permute-start.22
  129.8 3.7 %collective-permute-done.14 = f16[9,64,256]{2,1,0:T(8,128)(2,1)S(1)} collective-permute-done((f16[9,64,256]{2,1,0:T(8,128)(2,1)S(1)}, f16[9,64,256]{2,1,0:T(8,128)(2,1)S(1)}, u32[]{:S(2)}, u32[]{:S(2)}) %collective-permute-start.14) | collective-permute-done | bytes 294944 | tf_op jit(solution)/shard_map/ppermute | solution.py:226
  133.5 1.3 collective-permute-start.15
  135.0 14.5 %collective-permute-done.18 = f16[9,64,256]{2,1,0:T(8,128)(2,1)S(1)} collective-permute-done((f16[9,64,256]{2,1,0:T(8,128)(2,1)S(1)}, f16[9,64,256]{2,1,0:T(8,128)(2,1)S(1)}, u32[]{:S(2)}, u32[]{:S(2)}) %collective-permute-start.18) | collective-permute-done | bytes 294944 | tf_op jit(solution)/shard_map/ppermute | solution.py:226
  149.5 1.2 collective-permute-start.19
  150.8 2.9 %collective-permute-done.22 = f16[9,64,256]{2,1,0:T(8,128)(2,1)S(1)} collective-permute-done((f16[9,64,256]{2,1,0:T(8,128)(2,1)S(1)}, f16[9,64,256]{2,1,0:T(8,128)(2,1)S(1)}, u32[]{:S(2)}, u32[]{:S(2)}) %collective-permute-start.22) | collective-permute-done | bytes 294944 | tf_op jit(solution)/shard_map/ppermute | solution.py:226
  153.8 1.3 collective-permute-start.24
  155.3 1.8 %collective-permute-start.23 = (f16[9,64,256]{2,1,0:T(8,128)(2,1)S(1)}, f16[9,64,256]{2,1,0:T(8,128)(2,1)S(1)}, u32[]{:S(2)}, u32[]{:S(2)}) collective-permute-start(f16[9,64,256]{2,1,0:T(8,128)(2,1)S(1)} %collective-permute-done.22), channel_id=1, source_target_pairs={{0,2},{2,0},{4,6},{6,4},{8,10},{10,8},{12,14},{14,12},{16,18},{18,... | collective-permute-start | bytes 884744 | tf_op jit(solution)/shard_map/ppermute | solution.py:226
  157.1 3.9 %collective-permute-done.20 = f16[9,64,256]{2,1,0:T(8,128)(2,1)S(1)} collective-permute-done((f16[9,64,256]{2,1,0:T(8,128)(2,1)S(1)}, f16[9,64,256]{2,1,0:T(8,128)(2,1)S(1)}, u32[]{:S(2)}, u32[]{:S(2)}) %collective-permute-start.20) | collective-permute-done | bytes 294944 | tf_op jit(solution)/shard_map/ppermute | solution.py:226
  161.0 3.7 %collective-permute-start.21 = (f16[9,64,256]{2,1,0:T(8,128)(2,1)S(1)}, f16[9,64,256]{2,1,0:T(8,128)(2,1)S(1)}, u32[]{:S(2)}, u32[]{:S(2)}) collective-permute-start(f16[9,64,256]{2,1,0:T(8,128)(2,1)S(1)} %collective-permute-done.20), channel_id=1, source_target_pairs={{0,2},{2,0},{4,6},{6,4},{8,10},{10,8},{12,14},{14,12},{16,18},{18,... | collective-permute-start | bytes 884744 | tf_op jit(solution)/shard_map/ppermute | solution.py:226
  164.7 2.6 %collective-permute-done.24 = f16[9,64,256]{2,1,0:T(8,128)(2,1)S(1)} collective-permute-done((f16[9,64,256]{2,1,0:T(8,128)(2,1)S(1)}, f16[9,64,256]{2,1,0:T(8,128)(2,1)S(1)}, u32[]{:S(2)}, u32[]{:S(2)}) %collective-permute-start.24) | collective-permute-done | bytes 294944 | tf_op jit(solution)/shard_map/ppermute | solution.py:226
  167.4 2.0 %collective-permute-start.25 = (f16[9,64,256]{2,1,0:T(8,128)(2,1)S(1)}, f16[9,64,256]{2,1,0:T(8,128)(2,1)S(1)}, u32[]{:S(2)}, u32[]{:S(2)}) collective-permute-start(f16[9,64,256]{2,1,0:T(8,128)(2,1)S(1)} %collective-permute-done.24), channel_id=1, source_target_pairs={{0,2},{2,0},{4,6},{6,4},{8,10},{10,8},{12,14},{14,12},{16,18},{18,... | collective-permute-start | bytes 884744 | tf_op jit(solution)/shard_map/ppermute | solution.py:226
  170.2 0.4 collective-permute-done.25
  170.7 3.7 %copy-done.2 = f32[9,1024,256]{2,1,0:T(8,128)} copy-done((f32[9,1024,256]{2,1,0:T(8,128)}, f32[9,1024,256]{2,1,0:T(8,128)S(1)}, u32[]{:S(2)}) %copy-start.2) | copy-done | bytes 9437208
  (41 shorter events, 1.8 us)
Async XLA Ops:
  2.0 58.0 %collective-permute-start.2 = (bf16[512,1152]{1,0:T(8,128)(2,1)S(1)}, bf16[512,1152]{1,0:T(8,128)(2,1)S(1)}, u32[]{:S(2)}, u32[]{:S(2)}) collective-permute-start(bf16[512,1152]{1,0:T(8,128)(2,1)S(1)} %dynamic-slice_bitcast_fusion), channel_id=1, source_target_pairs={{0,2},{2,0},{4,6},{6,4},{8,10},{10,8},{12,14},{14,12},{16,18},{18,... | collective-permute-start | bytes 3538952 | tf_op jit(solution)/shard_map/ppermute | solution.py:226
  2.8 8.8 %collective-permute-start.1 = (bf16[128,1152]{1,0:T(8,128)(2,1)}, bf16[128,1152]{1,0:T(8,128)(2,1)S(1)}, u32[]{:S(2)}, u32[]{:S(2)}) collective-permute-start(bf16[128,1152]{1,0:T(8,128)(2,1)} %bitcast.21), channel_id=1, source_target_pairs={{0,1},{1,0},{2,3},{3,2},{4,5},{5,4},{6,7},{7,6},{8,9},{9,8},{10,11... | collective-permute-start | bytes 884744 | tf_op jit(solution)/shard_map/ppermute | solution.py:239
  12.8 47.2 %collective-permute-start.3 = (bf16[256,1152]{1,0:T(8,128)(2,1)S(1)}, bf16[256,1152]{1,0:T(8,128)(2,1)S(1)}, u32[]{:S(2)}, u32[]{:S(2)}) collective-permute-start(bf16[256,1152]{1,0:T(8,128)(2,1)S(1)} %maximum_select_fusion.cot_ref.own_cot), channel_id=1, source_target_pairs={{0,2},{2,0},{4,6},{6,4},{8,10},{10,8},{12,14},{14,12},{16,18},{18,... | collective-permute-start | bytes 1769480 | tf_op jit(solution)/shard_map/ppermute | solution.py:226
  60.0 1.7 copy-start
  70.0 9.5 %collective-permute-start.5 = (f16[9,64,256]{2,1,0:T(8,128)(2,1)}, f16[9,64,256]{2,1,0:T(8,128)(2,1)}, u32[]{:S(2)}, u32[]{:S(2)}) collective-permute-start(f16[9,64,256]{2,1,0:T(8,128)(2,1)} %get-tuple-element.8), channel_id=1, source_target_pairs={{0,4},{2,6},{4,0},{6,2},{8,12},{10,14},{12,8},{14,10},{16,20},{18,... | collective-permute-start | bytes 884744 | tf_op jit(solution)/shard_map/ppermute | solution.py:226
  71.2 11.5 %collective-permute-start.7 = (f16[9,64,256]{2,1,0:T(8,128)(2,1)}, f16[9,64,256]{2,1,0:T(8,128)(2,1)}, u32[]{:S(2)}, u32[]{:S(2)}) collective-permute-start(f16[9,64,256]{2,1,0:T(8,128)(2,1)} %get-tuple-element.7), channel_id=1, source_target_pairs={{0,4},{2,6},{4,0},{6,2},{8,12},{10,14},{12,8},{14,10},{16,20},{18,... | collective-permute-start | bytes 884744 | tf_op jit(solution)/shard_map/ppermute | solution.py:226
  71.5 17.6 %collective-permute-start.9 = (f16[9,64,256]{2,1,0:T(8,128)(2,1)}, f16[9,64,256]{2,1,0:T(8,128)(2,1)}, u32[]{:S(2)}, u32[]{:S(2)}) collective-permute-start(f16[9,64,256]{2,1,0:T(8,128)(2,1)} %get-tuple-element.6), channel_id=1, source_target_pairs={{0,4},{2,6},{4,0},{6,2},{8,12},{10,14},{12,8},{14,10},{16,20},{18,... | collective-permute-start | bytes 884744 | tf_op jit(solution)/shard_map/ppermute | solution.py:226
  78.8 49.7 %collective-permute-start = (f32[128,1152]{1,0:T(8,128)S(1)}, f32[128,1152]{1,0:T(8,128)S(1)}, u32[]{:S(2)}, u32[]{:S(2)}) collective-permute-start(f32[128,1152]{1,0:T(8,128)S(1)} %constant_dynamic-slice_fusion), channel_id=1, source_target_pairs={{0,1},{1,0},{2,3},{3,2},{4,5},{5,4},{6,7},{7,6},{8,9},{9,8},{10,11... | collective-permute-start | bytes 1769480 | tf_op jit(solution)/shard_map/ppermute | solution.py:292
  79.1 25.8 %collective-permute-start.4 = (f16[9,64,256]{2,1,0:T(8,128)(2,1)S(1)}, f16[9,64,256]{2,1,0:T(8,128)(2,1)S(1)}, u32[]{:S(2)}, u32[]{:S(2)}) collective-permute-start(f16[9,64,256]{2,1,0:T(8,128)(2,1)S(1)} %get-tuple-element.5), channel_id=1, source_target_pairs={{0,4},{2,6},{4,0},{6,2},{8,12},{10,14},{12,8},{14,10},{16,20},{18,... | collective-permute-start | bytes 884744 | tf_op jit(solution)/shard_map/ppermute | solution.py:226
  91.8 13.1 %collective-permute-start.10 = (f16[9,64,256]{2,1,0:T(8,128)(2,1)}, f16[9,64,256]{2,1,0:T(8,128)(2,1)}, u32[]{:S(2)}, u32[]{:S(2)}) collective-permute-start(f16[9,64,256]{2,1,0:T(8,128)(2,1)} %get-tuple-element.10), channel_id=1, source_target_pairs={{0,24},{2,26},{4,28},{6,30},{8,0},{10,2},{12,4},{14,6},{16,8},{18,... | collective-permute-start | bytes 884744 | tf_op jit(solution)/shard_map/ppermute | solution.py:226
  92.0 12.9 %collective-permute-start.6 = (f16[9,64,256]{2,1,0:T(8,128)(2,1)}, f16[9,64,256]{2,1,0:T(8,128)(2,1)}, u32[]{:S(2)}, u32[]{:S(2)}) collective-permute-start(f16[9,64,256]{2,1,0:T(8,128)(2,1)} %get-tuple-element.9), channel_id=1, source_target_pairs={{0,8},{2,10},{4,12},{6,14},{8,16},{10,18},{12,20},{14,22},{16,24},... | collective-permute-start | bytes 884744 | tf_op jit(solution)/shard_map/ppermute | solution.py:226
  93.3 22.3 %collective-permute-start.8 = (f16[9,64,256]{2,1,0:T(8,128)(2,1)}, f16[9,64,256]{2,1,0:T(8,128)(2,1)}, u32[]{:S(2)}, u32[]{:S(2)}) collective-permute-start(f16[9,64,256]{2,1,0:T(8,128)(2,1)} %get-tuple-element.11), channel_id=1, source_target_pairs={{0,16},{2,18},{4,20},{6,22},{8,24},{10,26},{12,28},{14,30},{16,0},... | collective-permute-start | bytes 884744 | tf_op jit(solution)/shard_map/ppermute | solution.py:226
  96.0 2.3 %copy-start.1 = (bf16[1024,9,256]{2,0,1:T(8,128)(2,1)S(1)}, bf16[1024,9,256]{2,0,1:T(8,128)(2,1)}, u32[]{:S(2)}) copy-start(bf16[1024,9,256]{2,0,1:T(8,128)(2,1)} %param.4) | copy-start | bytes 14155780
  118.0 16.8 %collective-permute-start.11 = (f16[9,64,256]{2,1,0:T(8,128)(2,1)S(1)}, f16[9,64,256]{2,1,0:T(8,128)(2,1)S(1)}, u32[]{:S(2)}, u32[]{:S(2)}) collective-permute-start(f16[9,64,256]{2,1,0:T(8,128)(2,1)S(1)} %get-tuple-element.4), channel_id=1, source_target_pairs={{0,2},{2,0},{4,6},{6,4},{8,10},{10,8},{12,14},{14,12},{16,18},{18,... | collective-permute-start | bytes 884744 | tf_op jit(solution)/shard_map/ppermute | solution.py:226
  122.2 12.6 %collective-permute-start.12 = (f16[9,64,256]{2,1,0:T(8,128)(2,1)S(1)}, f16[9,64,256]{2,1,0:T(8,128)(2,1)S(1)}, u32[]{:S(2)}, u32[]{:S(2)}) collective-permute-start(f16[9,64,256]{2,1,0:T(8,128)(2,1)S(1)} %get-tuple-element.4), channel_id=1, source_target_pairs={{0,4},{2,6},{4,0},{6,2},{8,12},{10,14},{12,8},{14,10},{16,20},{18,... | collective-permute-start | bytes 884744 | tf_op jit(solution)/shard_map/ppermute | solution.py:226
  124.4 9.1 %collective-permute-start.14 = (f16[9,64,256]{2,1,0:T(8,128)(2,1)S(1)}, f16[9,64,256]{2,1,0:T(8,128)(2,1)S(1)}, u32[]{:S(2)}, u32[]{:S(2)}) collective-permute-start(f16[9,64,256]{2,1,0:T(8,128)(2,1)S(1)} %get-tuple-element.4), channel_id=1, source_target_pairs={{0,8},{2,10},{4,12},{6,14},{8,16},{10,18},{12,20},{14,22},{16,24},... | collective-permute-start | bytes 884744 | tf_op jit(solution)/shard_map/ppermute | solution.py:226
  124.5 25.0 %collective-permute-start.18 = (f16[9,64,256]{2,1,0:T(8,128)(2,1)S(1)}, f16[9,64,256]{2,1,0:T(8,128)(2,1)S(1)}, u32[]{:S(2)}, u32[]{:S(2)}) collective-permute-start(f16[9,64,256]{2,1,0:T(8,128)(2,1)S(1)} %get-tuple-element.4), channel_id=1, source_target_pairs={{0,16},{2,18},{4,20},{6,22},{8,24},{10,26},{12,28},{14,30},{16,0},... | collective-permute-start | bytes 884744 | tf_op jit(solution)/shard_map/ppermute | solution.py:226
  129.3 24.4 %collective-permute-start.22 = (f16[9,64,256]{2,1,0:T(8,128)(2,1)S(1)}, f16[9,64,256]{2,1,0:T(8,128)(2,1)S(1)}, u32[]{:S(2)}, u32[]{:S(2)}) collective-permute-start(f16[9,64,256]{2,1,0:T(8,128)(2,1)S(1)} %get-tuple-element.4), channel_id=1, source_target_pairs={{0,24},{2,26},{4,28},{6,30},{8,0},{10,2},{12,4},{14,6},{16,8},{18,... | collective-permute-start | bytes 884744 | tf_op jit(solution)/shard_map/ppermute | solution.py:226
  133.5 21.8 %collective-permute-start.15 = (f16[9,64,256]{2,1,0:T(8,128)(2,1)S(1)}, f16[9,64,256]{2,1,0:T(8,128)(2,1)S(1)}, u32[]{:S(2)}, u32[]{:S(2)}) collective-permute-start(f16[9,64,256]{2,1,0:T(8,128)(2,1)S(1)} %collective-permute-done.14), channel_id=1, source_target_pairs={{0,2},{2,0},{4,6},{6,4},{8,10},{10,8},{12,14},{14,12},{16,18},{18,... | collective-permute-start | bytes 884744 | tf_op jit(solution)/shard_map/ppermute | solution.py:226
  134.8 22.2 %collective-permute-start.16 = (f16[9,64,256]{2,1,0:T(8,128)(2,1)S(1)}, f16[9,64,256]{2,1,0:T(8,128)(2,1)S(1)}, u32[]{:S(2)}, u32[]{:S(2)}) collective-permute-start(f16[9,64,256]{2,1,0:T(8,128)(2,1)S(1)} %collective-permute-done.14), channel_id=1, source_target_pairs={{0,4},{2,6},{4,0},{6,2},{8,12},{10,14},{12,8},{14,10},{16,20},{18,... | collective-permute-start | bytes 884744 | tf_op jit(solution)/shard_map/ppermute | solution.py:226
  134.8 19.0 %collective-permute-start.13 = (f16[9,64,256]{2,1,0:T(8,128)(2,1)S(1)}, f16[9,64,256]{2,1,0:T(8,128)(2,1)S(1)}, u32[]{:S(2)}, u32[]{:S(2)}) collective-permute-start(f16[9,64,256]{2,1,0:T(8,128)(2,1)S(1)} %collective-permute-done.12), channel_id=1, source_target_pairs={{0,2},{2,0},{4,6},{6,4},{8,10},{10,8},{12,14},{14,12},{16,18},{18,... | collective-permute-start | bytes 884744 | tf_op jit(solution)/shard_map/ppermute | solution.py:226
  149.5 20.2 %collective-permute-start.19 = (f16[9,64,256]{2,1,0:T(8,128)(2,1)S(1)}, f16[9,64,256]{2,1,0:T(8,128)(2,1)S(1)}, u32[]{:S(2)}, u32[]{:S(2)}) collective-permute-start(f16[9,64,256]{2,1,0:T(8,128)(2,1)S(1)} %collective-permute-done.18), channel_id=1, source_target_pairs={{0,2},{2,0},{4,6},{6,4},{8,10},{10,8},{12,14},{14,12},{16,18},{18,... | collective-permute-start | bytes 884744 | tf_op jit(solution)/shard_map/ppermute | solution.py:226
  153.7 7.4 %collective-permute-start.20 = (f16[9,64,256]{2,1,0:T(8,128)(2,1)S(1)}, f16[9,64,256]{2,1,0:T(8,128)(2,1)S(1)}, u32[]{:S(2)}, u32[]{:S(2)}) collective-permute-start(f16[9,64,256]{2,1,0:T(8,128)(2,1)S(1)} %collective-permute-done.18), channel_id=1, source_target_pairs={{0,4},{2,6},{4,0},{6,2},{8,12},{10,14},{12,8},{14,10},{16,20},{18,... | collective-permute-start | bytes 884744 | tf_op jit(solution)/shard_map/ppermute | solution.py:226
  153.8 13.5 %collective-permute-start.24 = (f16[9,64,256]{2,1,0:T(8,128)(2,1)S(1)}, f16[9,64,256]{2,1,0:T(8,128)(2,1)S(1)}, u32[]{:S(2)}, u32[]{:S(2)}) collective-permute-start(f16[9,64,256]{2,1,0:T(8,128)(2,1)S(1)} %collective-permute-done.22), channel_id=1, source_target_pairs={{0,4},{2,6},{4,0},{6,2},{8,12},{10,14},{12,8},{14,10},{16,20},{18,... | collective-permute-start | bytes 884744 | tf_op jit(solution)/shard_map/ppermute | solution.py:226
  155.3 14.7 %collective-permute-start.23 = (f16[9,64,256]{2,1,0:T(8,128)(2,1)S(1)}, f16[9,64,256]{2,1,0:T(8,128)(2,1)S(1)}, u32[]{:S(2)}, u32[]{:S(2)}) collective-permute-start(f16[9,64,256]{2,1,0:T(8,128)(2,1)S(1)} %collective-permute-done.22), channel_id=1, source_target_pairs={{0,2},{2,0},{4,6},{6,4},{8,10},{10,8},{12,14},{14,12},{16,18},{18,... | collective-permute-start | bytes 884744 | tf_op jit(solution)/shard_map/ppermute | solution.py:226
  157.0 12.5 %collective-permute-start.17 = (f16[9,64,256]{2,1,0:T(8,128)(2,1)S(1)}, f16[9,64,256]{2,1,0:T(8,128)(2,1)S(1)}, u32[]{:S(2)}, u32[]{:S(2)}) collective-permute-start(f16[9,64,256]{2,1,0:T(8,128)(2,1)S(1)} %collective-permute-done.16), channel_id=1, source_target_pairs={{0,2},{2,0},{4,6},{6,4},{8,10},{10,8},{12,14},{14,12},{16,18},{18,... | collective-permute-start | bytes 884744 | tf_op jit(solution)/shard_map/ppermute | solution.py:226
  161.0 8.8 %collective-permute-start.21 = (f16[9,64,256]{2,1,0:T(8,128)(2,1)S(1)}, f16[9,64,256]{2,1,0:T(8,128)(2,1)S(1)}, u32[]{:S(2)}, u32[]{:S(2)}) collective-permute-start(f16[9,64,256]{2,1,0:T(8,128)(2,1)S(1)} %collective-permute-done.20), channel_id=1, source_target_pairs={{0,2},{2,0},{4,6},{6,4},{8,10},{10,8},{12,14},{14,12},{16,18},{18,... | collective-permute-start | bytes 884744 | tf_op jit(solution)/shard_map/ppermute | solution.py:226
  167.4 3.3 %collective-permute-start.25 = (f16[9,64,256]{2,1,0:T(8,128)(2,1)S(1)}, f16[9,64,256]{2,1,0:T(8,128)(2,1)S(1)}, u32[]{:S(2)}, u32[]{:S(2)}) collective-permute-start(f16[9,64,256]{2,1,0:T(8,128)(2,1)S(1)} %collective-permute-done.24), channel_id=1, source_target_pairs={{0,2},{2,0},{4,6},{6,4},{8,10},{10,8},{12,14},{14,12},{16,18},{18,... | collective-permute-start | bytes 884744 | tf_op jit(solution)/shard_map/ppermute | solution.py:226
  170.7 3.7 %copy-start.2 = (f32[9,1024,256]{2,1,0:T(8,128)}, f32[9,1024,256]{2,1,0:T(8,128)S(1)}, u32[]{:S(2)}) copy-start(f32[9,1024,256]{2,1,0:T(8,128)S(1)} %multiply_dynamic-update-slice_fusion) | copy-start | bytes 28311556

commit v2 on v1

--- a/solution.py
+++ b/solution.py
@@ -1,3 +1,5 @@
+import functools
+
 import jax
 import jax.numpy as jnp
 from jax import lax
@@ -46,8 +48,22 @@
     return (slice(0, WINDOW), slice(0, HW), slice(HW - WINDOW, HW))[group]
 
 
-def kernel_grad_kernel(half_ref, own_x, other_x, own_cot, other_cot, out_ref):
+TILE = 8
+LANES = 128
+TOP = 30000.0
+
+
+def kernel_grad_kernel(shards, place_ref, own_x, other_x, own_cot, other_cot, _, *refs):
+    outs, sums, peak_ref = refs[:shards], refs[shards], refs[shards + 1]
     step = pl.program_id(0)
+    rows, width = own_x.shape[0], own_cot.shape[0]
+    shard_rows = rows // shards
+    tiles = shard_rows // TILE
+
+    @pl.when(step == 0)
+    def _():
+        peak_ref[...] = jnp.zeros(peak_ref.shape, jnp.float32)
+
     for group in range(3):
 
         @pl.when(step == group)
@@ -64,16 +80,39 @@
                         preferred_element_type=jnp.float32,
                     )
                     total = term if total is None else total + term
-                out_ref[column] = total
-
-
-def kernel_grad(half, x, other_x, own_cot, other_cot):
+                peak_ref[...] = jnp.maximum(
+                    peak_ref[...], jnp.max(jnp.abs(total), axis=0, keepdims=True)
+                )
+                lanes = width // LANES
+                for shard in range(shards):
+                    for tile in range(tiles):
+                        for lane in range(lanes):
+                            row = shard * shard_rows + tile * TILE
+                            slot = ((3 * group + column) * tiles + tile) * lanes + lane
+                            sums[shard, slot] = total[
+                                row : row + TILE, lane * LANES : (lane + 1) * LANES
+                            ]
+
+    @pl.when(step == 2)
+    def _():
+        peak = jnp.max(peak_ref[...], axis=1, keepdims=True)
+        exponent = jnp.floor(jnp.log2(TOP / jnp.maximum(peak, 1e-30)))
+        exponent = jnp.broadcast_to(exponent, (TILE, LANES))
+        scale = jnp.exp2(exponent)
+        for distance, out in enumerate(outs):
+            count = sums.shape[1]
+            out[:count] = sums[place_ref[1] ^ distance] * scale
+            out[count] = exponent
+
+
+def kernel_grad(place, shards, x, other_x, own_cot, other_cot, after):
     rows, positions = other_x.shape
     outs = own_cot.shape[0]
+    tiles = 9 * rows * outs // (shards * TILE * LANES)
     whole = lambda g, h: (0, 0)
     return pl.pallas_call(
-        kernel_grad_kernel,
-        out_shape=jax.ShapeDtypeStruct((9, rows, outs), jnp.float32),
+        functools.partial(kernel_grad_kernel, shards),
+        out_shape=[jax.ShapeDtypeStruct((tiles + 1, TILE, LANES), jnp.float32)] * shards,
         grid_spec=pltpu.PrefetchScalarGridSpec(
             num_scalar_prefetch=1,
             grid=(3,),
@@ -82,8 +121,13 @@
                 pl.BlockSpec((rows, positions), whole),
                 pl.BlockSpec((outs, positions), whole),
                 pl.BlockSpec((outs, positions), whole),
+                pl.BlockSpec(memory_space=pl.ANY),
             ],
-            out_specs=pl.BlockSpec((3, rows, outs), lambda g, h: (g, 0, 0)),
+            out_specs=[pl.BlockSpec((tiles + 1, TILE, LANES), lambda g, h: (0, 0, 0))] * shards,
+            scratch_shapes=[
+                pltpu.VMEM((shards, tiles, TILE, LANES), jnp.float32),
+                pltpu.VMEM((1, outs), jnp.float32),
+            ],
         ),
         compiler_params=pltpu.CompilerParams(vmem_limit_bytes=VMEM_LIMIT),
         cost_estimate=pl.CostEstimate(
@@ -92,10 +136,10 @@
             transcendentals=0,
         ),
         name="kernel_grad",
-    )(half, x, other_x, own_cot, other_cot)
-
-
-def forward_kernel(x_ref, w_ref, out_ref):
+    )(place, x, other_x, own_cot, other_cot, after)
+
+
+def forward_kernel(x_ref, w_ref, _, out_ref):
     step = pl.program_id(0)
     for group in range(3):
 
@@ -132,7 +176,7 @@
                 out_ref[:, :WINDOW] += total
 
 
-def forward(x, w):
+def forward(x, w, after):
     rows, positions = x.shape
     outs = w.shape[2]
     return pl.pallas_call(
@@ -142,6 +186,7 @@
         in_specs=[
             pl.BlockSpec((rows, positions), lambda g: (0, 0)),
             pl.BlockSpec((3, rows, outs), lambda g: (g, 0, 0)),
+            pl.BlockSpec(memory_space=pl.ANY),
         ],
         out_specs=pl.BlockSpec((outs, positions), lambda g: (0, 0)),
         compiler_params=pltpu.CompilerParams(vmem_limit_bytes=VMEM_LIMIT),
@@ -151,10 +196,10 @@
             transcendentals=0,
         ),
         name="forward",
-    )(x, w)
-
-
-def input_grad_kernel(cot_ref, w_ref, out_ref, middle, upper, lower):
+    )(x, w, after)
+
+
+def input_grad_kernel(cot_ref, w_ref, _, out_ref, middle, upper, lower):
     @pl.when(pl.program_id(0) == 0)
     def _():
         cot = cot_ref[...].astype(jnp.float32)
@@ -178,7 +223,7 @@
     out_ref[:, edge:] = (centre[:, edge:] + products(2, lower)).astype(jnp.bfloat16)
 
 
-def input_gradient(cot, w):
+def input_gradient(cot, w, after):
     outs, positions = cot.shape
     rows = w.shape[1]
     block = min(rows, 256)
@@ -189,6 +234,7 @@
         in_specs=[
             pl.BlockSpec((outs, positions), lambda g: (0, 0)),
             pl.BlockSpec((9, block, outs), lambda g: (0, g, 0)),
+            pl.BlockSpec(memory_space=pl.ANY),
         ],
         out_specs=pl.BlockSpec((block, positions), lambda g: (g, 0)),
         scratch_shapes=[
@@ -203,7 +249,22 @@
             transcendentals=0,
         ),
         name="input_gradient",
-    )(cot, w)
+    )(cot, w, after)
+
+
+def summed(values):
+    exponents = [value[-1:].astype(jnp.float32) for value in values]
+    lowest = functools.reduce(jnp.minimum, exponents) - float((len(values) - 1).bit_length())
+    total = sum(
+        value.astype(jnp.float32) * jnp.exp2(lowest - exponent)
+        for value, exponent in zip(values, exponents)
+    )
+    last = lax.broadcasted_iota(jnp.int32, total.shape, 0) == total.shape[0] - 1
+    return jnp.where(last, jnp.broadcast_to(lowest, total.shape), total).astype(jnp.float16)
+
+
+def token(value):
+    return value[0].astype(jnp.float32)
 
 
 def on_device(inputs, weight, cotangent):
@@ -219,22 +280,22 @@
     chan = lax.axis_index("chan")
     core, column, level = place % 2, (place // 2) % 2, place // 4
     core_rows = rows // 2
-    chip_rows = core_rows // 2
-    shard_rows = chip_rows // depth
-
-    def to(value, target):
-        return lax.ppermute(value, "dp", [(i, target(i)) for i in range(samples)])
+    core_tiles = core_rows // TILE
+    chip_tiles = core_tiles // 2
+    shard_tiles = chip_tiles // depth
+
+    def to(value, distance):
+        return lax.ppermute(value, "dp", [(i, i ^ distance) for i in range(samples)])
 
     def to_core(value):
-        return to(value, lambda i: i ^ 1)
+        return to(value, 1)
 
     def to_column(value):
-        return to(value, lambda i: i ^ 2)
+        return to(value, 2)
 
     def to_level(value, step):
-        return to(value, lambda i: ((i // 4 + step) % depth) * 4 + i % 4)
-
-    other_x = to_core(lax.dynamic_slice_in_dim(x, (1 - core) * core_rows, core_rows, 0))
+        return to(value, 4 * step)
+
     if chans == 2:
         their_cot = lax.ppermute(own_cot, "chan", [(0, 1), (1, 0)])
         cot = jnp.where(
@@ -244,48 +305,42 @@
         )
     else:
         cot = lax.all_gather(own_cot, "chan", axis=0, tiled=True)
+    other_x = to_core(lax.dynamic_slice_in_dim(x, (1 - core) * core_rows, core_rows, 0))
     other_cot = to_core(cot)
-
-    largest = lax.pmax(
-        jnp.stack([jnp.max(jnp.abs(x)), jnp.max(jnp.abs(own_cot))]).astype(jnp.float32),
-        ("dp", "chan"),
-    )
-    bound = jnp.maximum(largest[0] * largest[1] * (positions * samples), 1e-30)
-    scale = 30000.0 / bound
-    unscale = bound * (1.0 / (30000.0 * samples))
-
-    half = jnp.reshape(core, (1,)).astype(jnp.int32)
-    partial = kernel_grad(half, x, other_x, cot, other_cot)
-
-    def piece(row):
-        return lax.dynamic_slice_in_dim(partial, row, shard_rows, 1) * scale
-
-    summed = [None] * depth
-    for step in list(range(1, depth)) + [0]:
-        owner = (level + step) % depth
-        sent = piece((1 - column) * chip_rows + owner * shard_rows).astype(jnp.float16)
-        came = to_column(sent)
-        summed[step] = piece(column * chip_rows + owner * shard_rows) + came.astype(jnp.float32)
-    own = summed[0]
-    for step in range(1, depth):
-        own = own + to_level(summed[step].astype(jnp.float16), step).astype(jnp.float32)
-    shard = own.astype(jnp.float16)
-
-    pieces = []
+    where = jnp.stack([core, column * depth + level]).astype(jnp.int32)
+
+    shards = kernel_grad(where, 2 * depth, x, other_x, cot, other_cot, own_cot)
+    near, far = shards[:depth], shards[depth:]
+
+    total = forward(x, w, token(near[0]))
+
+    order = list(range(depth - 1, -1, -1))
+    kept = None
+    line = []
+    for step in order:
+        came = to_column(far[step].astype(jnp.float16))
+        pair = [near[step], came]
+        if step:
+            line.append(to_level(summed(pair), step))
+        else:
+            kept = summed(pair)
+    shard = summed([kept] + line[::-1])
+    input_grad = input_gradient(cot, w, token(line[0]))[None]
+
+    grad = jnp.zeros((taps, rows // TILE, outs // LANES, TILE, LANES), jnp.float32)
     for step in range(depth):
-        near = shard if step == 0 else to_level(shard, step)
-        far = to_column(near)
-        owner = (level - step) % depth
-        for which, value in ((column, near), (1 - column, far)):
-            row = which * chip_rows + owner * shard_rows
-            pieces.append((core * core_rows + row, value))
-            pieces.append(((1 - core) * core_rows + row, to_core(value)))
-    grad = jnp.zeros((taps, rows, outs), jnp.float32)
-    for row, value in pieces:
-        grad = lax.dynamic_update_slice_in_dim(grad, value.astype(jnp.float32) * unscale, row, 1)
-    weight_grad = jnp.transpose(grad, (1, 0, 2))
-
-    total = forward(x, w)
+        here = shard if step == 0 else to_level(shard, step)
+        there = to_column(here)
+        owner = level ^ step
+        for chip, value in ((column, here), (1 - column, there)):
+            row = chip * chip_tiles + owner * shard_tiles
+            for base, part in ((core, value), (1 - core, to_core(value))):
+                factor = jnp.exp2(-part[-1].astype(jnp.float32)) * (1.0 / samples)
+                part = part[:-1].reshape(taps, shard_tiles, outs // LANES, TILE, LANES)
+                part = part.astype(jnp.float32) * factor
+                grad = lax.dynamic_update_slice_in_dim(grad, part, base * core_tiles + row, 1)
+    weight_grad = jnp.transpose(grad, (1, 3, 0, 2, 4)).reshape(rows, taps, outs)
+
     if chans == 2:
         mine = lax.dynamic_slice_in_dim(total, chan * own_outs, own_outs, 0)
         theirs = lax.dynamic_slice_in_dim(total, (1 - chan) * own_outs, own_outs, 0)
@@ -293,7 +348,6 @@
     else:
         result = lax.psum_scatter(total, "chan", scatter_dimension=0, tiled=True)
     result = result.astype(jnp.bfloat16)[None]
-    input_grad = input_gradient(cot, w)[None]
     return (result, input_grad, weight_grad)
 
 

time: 175 us -> 137 us (0.78)
  the two profiles are of different devices: /device:TPU:13 before, /device:TPU:17 now
where the time goes in v2:
time: 137 us
  waiting for transfers between devices  63.8 us (47%)
  Pallas kernels  20.9 us (15%)
  local copies, waits for them, and re-layouts  20 us (15%)
  starting transfers between devices  20 us (15%)
  other arithmetic  10.9 us (8%)
    ppermute x24, waiting for transfers between devices, to(): lax.ppermute(value, 'dp', [(i, i ^ distance) for i in range(samples)])  56.3 us
    ppermute x24, starting transfers between devices, to(): lax.ppermute(value, 'dp', [(i, i ^ distance) for i in range(samples)])  17.4 us
    unnamed x24, local copies, waits for them, and re-layouts  12.1 us
    pallas_call x1, Pallas kernels, kernel_grad(): pl.pallas_call(functools.partial(kernel_grad_kernel, shards), out_shape=[...  8.07 us
    ppermute x1, waiting for transfers between devices, on_device(): their_cot = lax.ppermute(own_cot, 'chan', [(0, 1), (1, 0)])  7.54 us
    pallas_call x1, Pallas kernels, input_gradient(): pl.pallas_call(input_grad_kernel, out_shape=jax.ShapeDtypeStruct((rows, p...  6.54 us
    pallas_call x1, Pallas kernels, forward(): pl.pallas_call(forward_kernel, out_shape=jax.ShapeDtypeStruct((outs, posi...  6.31 us
    slice x16, local copies, waits for them, and re-layouts, on_device(): part = part[:-1].reshape(taps, shard_tiles, outs // LANES, TILE, LANES)  4.83 us
  transfers between devices with their start and end apart: 26, of which 12 were waited for; matrix products, arithmetic and copies ran while one was open for 12% of the time, Pallas kernels for 9%

profile of v2, /device:TPU:17, one launch (start us, length us, event | category | flops | bytes accessed | tf_op | source)
XLA Modules:
  0.0 136.6 jit_solution(11282885130325125252)
XLA Ops:
  0.7 1.4 %dynamic-slice_bitcast_fusion = bf16[512,1152]{1,0:T(8,128)(2,1)S(1)} fusion(bf16[1,1024,1152]{2,1,0:T(8,128)(2,1)} %param.3, s32[]{:T(128)S(6)} %select_n.103), kind=kLoop, calls=%fused_computation | loop fusion | bytes 2359300 | tf_op jit(solution)/shard_map/dynamic_slice | solution.py:308
  2.0 0.7 collective-permute-start
  2.8 1.3 collective-permute-start.1
  4.0 7.5 %collective-permute-done.1 = bf16[128,1152]{1,0:T(8,128)(2,1)S(1)} collective-permute-done((bf16[128,1152]{1,0:T(8,128)(2,1)}, bf16[128,1152]{1,0:T(8,128)(2,1)S(1)}, u32[]{:S(2)}, u32[]{:S(2)}) %collective-permute-start.1) | collective-permute-done | bytes 294944 | tf_op jit(solution)/shard_map/ppermute | solution.py:300
  11.6 1.2 maximum_select_fusion.own_cot.cot_ref
  12.8 0.9 collective-permute-start.2
  13.7 0.8 copy-done.2
  14.6 0.7 collective-permute-done.2.other_cot
  15.3 0.8 copy-done.6
  16.1 1.0 copy-done.9
  17.1 1.1 copy-done.3
  18.2 1.0 copy-done.5
  19.2 1.1 copy-done.7
  20.2 8.1 %kernel_grad.1 = (f32[145,8,128]{2,1,0:T(8,128)S(1)}, f32[145,8,128]{2,1,0:T(8,128)S(1)}, f32[145,8,128]{2,1,0:T(8,128)S(1)}, f32[145,8,128]{2,1,0:T(8,128)S(1)}...) custom-call(s32[2]{0:T(128)S(1)} %pad_add_fusion.place_ref, ...), custom_call_target="tpu_custom_call" | custom-call | flops 3019898880 | bytes 8257536 | tf_op jit(solution)/shard_map/kernel_grad/pallas_call | solution.py:113
  28.3 0.8 copy-done
  29.1 0.8 convert_element_type.319
  29.9 1.2 collective-permute-start.7
  31.1 1.1 convert_element_type.324
  32.6 1.3 collective-permute-start.6
  33.8 1.1 convert_element_type.308
  35.3 3.1 %collective-permute-done.7 = f16[145,8,128]{2,1,0:T(8,128)(2,1)S(1)} collective-permute-done((f16[145,8,128]{2,1,0:T(8,128)(2,1)}, f16[145,8,128]{2,1,0:T(8,128)(2,1)S(1)}, u32[]{:S(2)}, u32[]{:S(2)}) %collective-permute-start.7) | collective-permute-done | bytes 296992 | tf_op jit(solution)/shard_map/ppermute | solution.py:288
  38.4 6.4 %collective-permute-done.9 = f16[145,8,128]{2,1,0:T(8,128)(2,1)S(1)} collective-permute-done((f16[145,8,128]{2,1,0:T(8,128)(2,1)S(1)}, f16[145,8,128]{2,1,0:T(8,128)(2,1)S(1)}, u32[]{:S(2)}, u32[]{:S(2)}) %collective-permute-start.9) | collective-permute-done | bytes 296992 | tf_op jit(solution)/shard_map/ppermute | solution.py:288
  44.7 6.4 %collective-permute-done.6 = f16[145,8,128]{2,1,0:T(8,128)(2,1)S(1)} collective-permute-done((f16[145,8,128]{2,1,0:T(8,128)(2,1)S(1)}, f16[145,8,128]{2,1,0:T(8,128)(2,1)S(1)}, u32[]{:S(2)}, u32[]{:S(2)}) %collective-permute-start.6) | collective-permute-done | bytes 296992 | tf_op jit(solution)/shard_map/ppermute | solution.py:288
  51.6 1.4 collective-permute-start.8
  53.0 4.4 %collective-permute-done.4 = f16[145,8,128]{2,1,0:T(8,128)(2,1)S(1)} collective-permute-done((f16[145,8,128]{2,1,0:T(8,128)(2,1)S(1)}, f16[145,8,128]{2,1,0:T(8,128)(2,1)S(1)}, u32[]{:S(2)}, u32[]{:S(2)}) %collective-permute-start.4) | collective-permute-done | bytes 296992 | tf_op jit(solution)/shard_map/ppermute | solution.py:288
  57.9 1.7 %copy-done.1 = bf16[1,1024,1152]{2,1,0:T(8,128)(2,1)S(1)} copy-done((bf16[1,1024,1152]{2,1,0:T(8,128)(2,1)S(1)}, bf16[1,1024,1152]{2,1,0:T(8,128)(2,1)}, u32[]{:S(2)}) %copy-start.1) | copy-done | bytes 2359320
  59.6 6.3 %forward.1 = f32[256,1152]{1,0:T(8,128)S(1)} custom-call(bf16[1024,1152]{1,0:T(8,128)(2,1)S(1)} %bitcast.118, bf16[9,1024,256]{2,1,0:T(8,128)(2,1)} %bitcast.122, f32[8,128]{1,0:T(8,128)S(1)} %get-tuple-element.33._), custom_call_target="tpu_custom_call" | custom-call | flops 3019898880 | bytes 8257536 | tf_op jit(solution)/shard_map/forward/pallas_call | solution.py:182
  65.9 0.9 constant_dynamic-slice_fusion
  66.8 1.3 collective-permute-start.3
  68.0 12.6 %collective-permute-done.5 = f16[145,8,128]{2,1,0:T(8,128)(2,1)S(1)} collective-permute-done((f16[145,8,128]{2,1,0:T(8,128)(2,1)S(1)}, f16[145,8,128]{2,1,0:T(8,128)(2,1)S(1)}, u32[]{:S(2)}, u32[]{:S(2)}) %collective-permute-start.5) | collective-permute-done | bytes 296992 | tf_op jit(solution)/shard_map/ppermute | solution.py:288
  81.5 1.2 collective-permute-start.12
  83.2 0.8 broadcast_in_dim.30
  84.3 6.5 %input_gradient.1 = bf16[1024,1152]{1,0:T(8,128)(2,1)} custom-call(bf16[256,1152]{1,0:T(8,128)(2,1)S(1)} %copy-done.4, bf16[9,1024,256]{2,1,0:T(8,128)(2,1)S(1)} %bitcast.125, f32[8,128]{1,0:T(8,128)S(1)} %fusion.66._), custom_call_target="tpu_custom_call" | custom-call | flops 3019898880 | bytes 7667712 | tf_op jit(solution)/shard_map/input_gradient/pallas_call | solution.py:230
  90.8 2.2 %collective-permute-start.22 = (f16[145,8,128]{2,1,0:T(8,128)(2,1)S(1)}, f16[145,8,128]{2,1,0:T(8,128)(2,1)S(1)}, u32[]{:S(2)}, u32[]{:S(2)}) collective-permute-start(f16[145,8,128]{2,1,0:T(8,128)(2,1)S(1)} %select_convert_fusion), channel_id=1, source_target_pairs={{0,24},{2,26},{4,28},{6,30},{8,16},{10,18},{12,20},{14,22},{16,8},... | collective-permute-start | bytes 890888 | tf_op jit(solution)/shard_map/ppermute | solution.py:288
  93.0 1.9 %fusion.16 = bf16[1,128,1152]{2,1,0:T(8,128)(2,1)} fusion(f32[128,1152]{1,0:T(8,128)} %collective-permute-done.3, f32[256,1152]{1,0:T(8,128)S(1)} %forward.1, s32[]{:T(128)S(6)} %select_n.106), kind=kLoop, calls=%fused_computation.40 | loop fusion | flops 294912 | bytes 1474564 | tf_op jit(solution)/shard_map/broadcast_in_dim | solution.py:350
  94.9 0.7 multiply_bitcast_fusion.14
  95.6 1.0 slice.195
  97.4 1.0 slice.197
  98.4 1.3 collective-permute-start.13
  101.4 9.5 %collective-permute-done.22 = f16[145,8,128]{2,1,0:T(8,128)(2,1)S(1)} collective-permute-done((f16[145,8,128]{2,1,0:T(8,128)(2,1)S(1)}, f16[145,8,128]{2,1,0:T(8,128)(2,1)S(1)}, u32[]{:S(2)}, u32[]{:S(2)}) %collective-permute-start.22) | collective-permute-done | bytes 296992 | tf_op jit(solution)/shard_map/ppermute | solution.py:288
  111.0 1.0 slice.201
  112.0 1.0 slice.209
  113.0 1.6 %collective-permute-start.19 = (f16[145,8,128]{2,1,0:T(8,128)(2,1)}, f16[145,8,128]{2,1,0:T(8,128)(2,1)S(1)}, u32[]{:S(2)}, u32[]{:S(2)}) collective-permute-start(f16[145,8,128]{2,1,0:T(8,128)(2,1)} %collective-permute-done.18), channel_id=1, source_target_pairs={{0,2},{2,0},{4,6},{6,4},{8,10},{10,8},{12,14},{14,12},{16,18},{18,... | collective-permute-start | bytes 890888 | tf_op jit(solution)/shard_map/ppermute | solution.py:288
  115.4 1.3 collective-permute-start.24
  117.3 6.1 %collective-permute-done.20 = f16[145,8,128]{2,1,0:T(8,128)(2,1)S(1)} collective-permute-done((f16[145,8,128]{2,1,0:T(8,128)(2,1)}, f16[145,8,128]{2,1,0:T(8,128)(2,1)S(1)}, u32[]{:S(2)}, u32[]{:S(2)}) %collective-permute-start.20) | collective-permute-done | bytes 296992 | tf_op jit(solution)/shard_map/ppermute | solution.py:288
  123.7 6.1 %collective-permute-done.24 = f16[145,8,128]{2,1,0:T(8,128)(2,1)S(1)} collective-permute-done((f16[145,8,128]{2,1,0:T(8,128)(2,1)S(1)}, f16[145,8,128]{2,1,0:T(8,128)(2,1)S(1)}, u32[]{:S(2)}, u32[]{:S(2)}) %collective-permute-start.24) | collective-permute-done | bytes 296992 | tf_op jit(solution)/shard_map/ppermute | solution.py:288
  130.0 0.9 collective-permute-start.21
  132.9 3.7 %copy-done.8 = f32[9,128,2,8,128]{4,3,2,1,0:T(8,128)} copy-done((f32[9,128,2,8,128]{4,3,2,1,0:T(8,128)}, f32[9,128,2,8,128]{4,3,2,1,0:T(8,128)S(1)}, u32[]{:S(2)}) %copy-start.8) | copy-done | bytes 9437208
  (101 shorter events, 9.4 us)
Async XLA Ops:
  2.0 14.1 %collective-permute-start = (bf16[512,1152]{1,0:T(8,128)(2,1)S(1)}, bf16[512,1152]{1,0:T(8,128)(2,1)S(1)}, u32[]{:S(2)}, u32[]{:S(2)}) collective-permute-start(bf16[512,1152]{1,0:T(8,128)(2,1)S(1)} %dynamic-slice_bitcast_fusion), channel_id=1, source_target_pairs={{0,2},{2,0},{4,6},{6,4},{8,10},{10,8},{12,14},{14,12},{16,18},{18,... | collective-permute-start | bytes 3538952 | tf_op jit(solution)/shard_map/ppermute | solution.py:288
  2.8 8.8 %collective-permute-start.1 = (bf16[128,1152]{1,0:T(8,128)(2,1)}, bf16[128,1152]{1,0:T(8,128)(2,1)S(1)}, u32[]{:S(2)}, u32[]{:S(2)}) collective-permute-start(bf16[128,1152]{1,0:T(8,128)(2,1)} %bitcast.119), channel_id=1, source_target_pairs={{0,1},{1,0},{2,3},{3,2},{4,5},{5,4},{6,7},{7,6},{8,9},{9,8},{10,11... | collective-permute-start | bytes 884744 | tf_op jit(solution)/shard_map/ppermute | solution.py:300
  12.8 2.5 %collective-permute-start.2 = (bf16[256,1152]{1,0:T(8,128)(2,1)S(1)}, bf16[256,1152]{1,0:T(8,128)(2,1)S(1)}, u32[]{:S(2)}, u32[]{:S(2)}) collective-permute-start(bf16[256,1152]{1,0:T(8,128)(2,1)S(1)} %maximum_select_fusion.own_cot.cot_ref), channel_id=1, source_target_pairs={{0,2},{2,0},{4,6},{6,4},{8,10},{10,8},{12,14},{14,12},{16,18},{18,... | collective-permute-start | bytes 1769480 | tf_op jit(solution)/shard_map/ppermute | solution.py:288
  13.7 0.8 copy-start.2
  15.3 0.8 copy-start.6
  16.1 1.0 copy-start.9
  17.1 1.1 copy-start.3
  18.2 1.0 copy-start.5
  19.2 1.1 copy-start.7
  28.3 0.8 copy-start
  29.9 8.5 %collective-permute-start.7 = (f16[145,8,128]{2,1,0:T(8,128)(2,1)}, f16[145,8,128]{2,1,0:T(8,128)(2,1)S(1)}, u32[]{:S(2)}, u32[]{:S(2)}) collective-permute-start(f16[145,8,128]{2,1,0:T(8,128)(2,1)} %convert_element_type.319), channel_id=1, source_target_pairs={{0,4},{2,6},{4,0},{6,2},{8,12},{10,14},{12,8},{14,10},{16,20},{18,... | collective-permute-start | bytes 890888 | tf_op jit(solution)/shard_map/ppermute | solution.py:288
  32.2 12.5 %collective-permute-start.9 = (f16[145,8,128]{2,1,0:T(8,128)(2,1)S(1)}, f16[145,8,128]{2,1,0:T(8,128)(2,1)S(1)}, u32[]{:S(2)}, u32[]{:S(2)}) collective-permute-start(f16[145,8,128]{2,1,0:T(8,128)(2,1)S(1)} %convert_element_type.324), channel_id=1, source_target_pairs={{0,4},{2,6},{4,0},{6,2},{8,12},{10,14},{12,8},{14,10},{16,20},{18,... | collective-permute-start | bytes 890888 | tf_op jit(solution)/shard_map/ppermute | solution.py:288
  32.6 18.5 %collective-permute-start.6 = (f16[145,8,128]{2,1,0:T(8,128)(2,1)S(1)}, f16[145,8,128]{2,1,0:T(8,128)(2,1)S(1)}, u32[]{:S(2)}, u32[]{:S(2)}) collective-permute-start(f16[145,8,128]{2,1,0:T(8,128)(2,1)S(1)} %convert_element_type.314), channel_id=1, source_target_pairs={{0,4},{2,6},{4,0},{6,2},{8,12},{10,14},{12,8},{14,10},{16,20},{18,... | collective-permute-start | bytes 890888 | tf_op jit(solution)/shard_map/ppermute | solution.py:288
  34.9 22.5 %collective-permute-start.4 = (f16[145,8,128]{2,1,0:T(8,128)(2,1)S(1)}, f16[145,8,128]{2,1,0:T(8,128)(2,1)S(1)}, u32[]{:S(2)}, u32[]{:S(2)}) collective-permute-start(f16[145,8,128]{2,1,0:T(8,128)(2,1)S(1)} %convert_element_type.308), channel_id=1, source_target_pairs={{0,4},{2,6},{4,0},{6,2},{8,12},{10,14},{12,8},{14,10},{16,20},{18,... | collective-permute-start | bytes 890888 | tf_op jit(solution)/shard_map/ppermute | solution.py:288
  51.6 16.5 %collective-permute-start.10 = (f16[145,8,128]{2,1,0:T(8,128)(2,1)S(1)}, f16[145,8,128]{2,1,0:T(8,128)(2,1)S(1)}, u32[]{:S(2)}, u32[]{:S(2)}) collective-permute-start(f16[145,8,128]{2,1,0:T(8,128)(2,1)S(1)} %get-tuple-element.39), channel_id=1, source_target_pairs={{0,16},{2,18},{4,20},{6,22},{8,24},{10,26},{12,28},{14,30},{16,0},... | collective-permute-start | bytes 890888 | tf_op jit(solution)/shard_map/ppermute | solution.py:288
  51.6 16.4 %collective-permute-start.8 = (f16[145,8,128]{2,1,0:T(8,128)(2,1)S(1)}, f16[145,8,128]{2,1,0:T(8,128)(2,1)S(1)}, u32[]{:S(2)}, u32[]{:S(2)}) collective-permute-start(f16[145,8,128]{2,1,0:T(8,128)(2,1)S(1)} %get-tuple-element.38), channel_id=1, source_target_pairs={{0,8},{2,10},{4,12},{6,14},{8,0},{10,2},{12,4},{14,6},{16,24},{18,... | collective-permute-start | bytes 890888 | tf_op jit(solution)/shard_map/ppermute | solution.py:288
  57.7 23.0 %collective-permute-start.5 = (f16[145,8,128]{2,1,0:T(8,128)(2,1)S(1)}, f16[145,8,128]{2,1,0:T(8,128)(2,1)S(1)}, u32[]{:S(2)}, u32[]{:S(2)}) collective-permute-start(f16[145,8,128]{2,1,0:T(8,128)(2,1)S(1)} %select_convert_fusion.4), channel_id=1, source_target_pairs={{0,24},{2,26},{4,28},{6,30},{8,16},{10,18},{12,20},{14,22},{16,8},... | collective-permute-start | bytes 890888 | tf_op jit(solution)/shard_map/ppermute | solution.py:288
  57.9 1.7 %copy-start.1 = (bf16[1,1024,1152]{2,1,0:T(8,128)(2,1)S(1)}, bf16[1,1024,1152]{2,1,0:T(8,128)(2,1)}, u32[]{:S(2)}) copy-start(bf16[1,1024,1152]{2,1,0:T(8,128)(2,1)} %param.3) | copy-start | bytes 7077892
  65.9 18.2 %copy-start.4 = (bf16[256,1152]{1,0:T(8,128)(2,1)S(1)}, bf16[256,1152]{1,0:T(8,128)(2,1)}, u32[]{:S(2)}) copy-start(bf16[256,1152]{1,0:T(8,128)(2,1)} %copy-done.2) | copy-start | bytes 1769476
  65.9 18.2 %slice-start = ((s8[4718592]{0:T(1024)(128)(4,1)}), s8[4194304]{0:T(1024)(128)(4,1)S(1)}, s32[]{:S(2)}) async-start(s8[4718592]{0:T(1024)(128)(4,1)} %bitcast.123), calls=%async_computation | async-start | bytes 8388608
  66.8 24.0 %collective-permute-start.3 = (f32[128,1152]{1,0:T(8,128)}, f32[128,1152]{1,0:T(8,128)}, u32[]{:S(2)}, u32[]{:S(2)}) collective-permute-start(f32[128,1152]{1,0:T(8,128)} %constant_dynamic-slice_fusion), channel_id=1, source_target_pairs={{0,1},{1,0},{2,3},{3,2},{4,5},{5,4},{6,7},{7,6},{8,9},{9,8},{10,11... | collective-permute-start | bytes 1769480 | tf_op jit(solution)/shard_map/ppermute | solution.py:347
  81.0 13.8 %collective-permute-start.11 = (f16[145,8,128]{2,1,0:T(8,128)(2,1)S(1)}, f16[145,8,128]{2,1,0:T(8,128)(2,1)}, u32[]{:S(2)}, u32[]{:S(2)}) collective-permute-start(f16[145,8,128]{2,1,0:T(8,128)(2,1)S(1)} %select_convert_fusion), channel_id=1, source_target_pairs={{0,2},{2,0},{4,6},{6,4},{8,10},{10,8},{12,14},{14,12},{16,18},{18,... | collective-permute-start | bytes 890888 | tf_op jit(solution)/shard_map/ppermute | solution.py:288
  81.5 15.2 %collective-permute-start.12 = (f16[145,8,128]{2,1,0:T(8,128)(2,1)S(1)}, f16[145,8,128]{2,1,0:T(8,128)(2,1)}, u32[]{:S(2)}, u32[]{:S(2)}) collective-permute-start(f16[145,8,128]{2,1,0:T(8,128)(2,1)S(1)} %select_convert_fusion), channel_id=1, source_target_pairs={{0,4},{2,6},{4,0},{6,2},{8,12},{10,14},{12,8},{14,10},{16,20},{18,... | collective-permute-start | bytes 890888 | tf_op jit(solution)/shard_map/ppermute | solution.py:288
  82.7 17.1 %collective-permute-start.14 = (f16[145,8,128]{2,1,0:T(8,128)(2,1)S(1)}, f16[145,8,128]{2,1,0:T(8,128)(2,1)}, u32[]{:S(2)}, u32[]{:S(2)}) collective-permute-start(f16[145,8,128]{2,1,0:T(8,128)(2,1)S(1)} %select_convert_fusion), channel_id=1, source_target_pairs={{0,8},{2,10},{4,12},{6,14},{8,0},{10,2},{12,4},{14,6},{16,24},{18,... | collective-permute-start | bytes 890888 | tf_op jit(solution)/shard_map/ppermute | solution.py:288
  82.7 18.0 %collective-permute-start.18 = (f16[145,8,128]{2,1,0:T(8,128)(2,1)S(1)}, f16[145,8,128]{2,1,0:T(8,128)(2,1)}, u32[]{:S(2)}, u32[]{:S(2)}) collective-permute-start(f16[145,8,128]{2,1,0:T(8,128)(2,1)S(1)} %select_convert_fusion), channel_id=1, source_target_pairs={{0,16},{2,18},{4,20},{6,22},{8,24},{10,26},{12,28},{14,30},{16,0},... | collective-permute-start | bytes 890888 | tf_op jit(solution)/shard_map/ppermute | solution.py:288
  83.2 1.0 slice-start.1
  90.8 20.1 %collective-permute-start.22 = (f16[145,8,128]{2,1,0:T(8,128)(2,1)S(1)}, f16[145,8,128]{2,1,0:T(8,128)(2,1)S(1)}, u32[]{:S(2)}, u32[]{:S(2)}) collective-permute-start(f16[145,8,128]{2,1,0:T(8,128)(2,1)S(1)} %select_convert_fusion), channel_id=1, source_target_pairs={{0,24},{2,26},{4,28},{6,30},{8,16},{10,18},{12,20},{14,22},{16,8},... | collective-permute-start | bytes 890888 | tf_op jit(solution)/shard_map/ppermute | solution.py:288
  98.4 16.5 %collective-permute-start.13 = (f16[145,8,128]{2,1,0:T(8,128)(2,1)}, f16[145,8,128]{2,1,0:T(8,128)(2,1)S(1)}, u32[]{:S(2)}, u32[]{:S(2)}) collective-permute-start(f16[145,8,128]{2,1,0:T(8,128)(2,1)} %collective-permute-done.12), channel_id=1, source_target_pairs={{0,2},{2,0},{4,6},{6,4},{8,10},{10,8},{12,14},{14,12},{16,18},{18,... | collective-permute-start | bytes 890888 | tf_op jit(solution)/shard_map/ppermute | solution.py:288
  100.4 16.2 %collective-permute-start.15 = (f16[145,8,128]{2,1,0:T(8,128)(2,1)}, f16[145,8,128]{2,1,0:T(8,128)(2,1)S(1)}, u32[]{:S(2)}, u32[]{:S(2)}) collective-permute-start(f16[145,8,128]{2,1,0:T(8,128)(2,1)} %collective-permute-done.14), channel_id=1, source_target_pairs={{0,2},{2,0},{4,6},{6,4},{8,10},{10,8},{12,14},{14,12},{16,18},{18,... | collective-permute-start | bytes 890888 | tf_op jit(solution)/shard_map/ppermute | solution.py:288
  100.5 14.9 %collective-permute-start.16 = (f16[145,8,128]{2,1,0:T(8,128)(2,1)}, f16[145,8,128]{2,1,0:T(8,128)(2,1)S(1)}, u32[]{:S(2)}, u32[]{:S(2)}) collective-permute-start(f16[145,8,128]{2,1,0:T(8,128)(2,1)} %collective-permute-done.14), channel_id=1, source_target_pairs={{0,4},{2,6},{4,0},{6,2},{8,12},{10,14},{12,8},{14,10},{16,20},{18,... | collective-permute-start | bytes 890888 | tf_op jit(solution)/shard_map/ppermute | solution.py:288
  113.0 4.2 %collective-permute-start.19 = (f16[145,8,128]{2,1,0:T(8,128)(2,1)}, f16[145,8,128]{2,1,0:T(8,128)(2,1)S(1)}, u32[]{:S(2)}, u32[]{:S(2)}) collective-permute-start(f16[145,8,128]{2,1,0:T(8,128)(2,1)} %collective-permute-done.18), channel_id=1, source_target_pairs={{0,2},{2,0},{4,6},{6,4},{8,10},{10,8},{12,14},{14,12},{16,18},{18,... | collective-permute-start | bytes 890888 | tf_op jit(solution)/shard_map/ppermute | solution.py:288
  114.6 8.8 %collective-permute-start.20 = (f16[145,8,128]{2,1,0:T(8,128)(2,1)}, f16[145,8,128]{2,1,0:T(8,128)(2,1)S(1)}, u32[]{:S(2)}, u32[]{:S(2)}) collective-permute-start(f16[145,8,128]{2,1,0:T(8,128)(2,1)} %collective-permute-done.18), channel_id=1, source_target_pairs={{0,4},{2,6},{4,0},{6,2},{8,12},{10,14},{12,8},{14,10},{16,20},{18,... | collective-permute-start | bytes 890888 | tf_op jit(solution)/shard_map/ppermute | solution.py:288
  115.0 8.6 %collective-permute-start.23 = (f16[145,8,128]{2,1,0:T(8,128)(2,1)S(1)}, f16[145,8,128]{2,1,0:T(8,128)(2,1)S(1)}, u32[]{:S(2)}, u32[]{:S(2)}) collective-permute-start(f16[145,8,128]{2,1,0:T(8,128)(2,1)S(1)} %collective-permute-done.22), channel_id=1, source_target_pairs={{0,2},{2,0},{4,6},{6,4},{8,10},{10,8},{12,14},{14,12},{16,18},{18,... | collective-permute-start | bytes 890888 | tf_op jit(solution)/shard_map/ppermute | solution.py:288
  115.4 14.4 %collective-permute-start.24 = (f16[145,8,128]{2,1,0:T(8,128)(2,1)S(1)}, f16[145,8,128]{2,1,0:T(8,128)(2,1)S(1)}, u32[]{:S(2)}, u32[]{:S(2)}) collective-permute-start(f16[145,8,128]{2,1,0:T(8,128)(2,1)S(1)} %collective-permute-done.22), channel_id=1, source_target_pairs={{0,4},{2,6},{4,0},{6,2},{8,12},{10,14},{12,8},{14,10},{16,20},{18,... | collective-permute-start | bytes 890888 | tf_op jit(solution)/shard_map/ppermute | solution.py:288
  116.7 14.6 %collective-permute-start.17 = (f16[145,8,128]{2,1,0:T(8,128)(2,1)S(1)}, f16[145,8,128]{2,1,0:T(8,128)(2,1)S(1)}, u32[]{:S(2)}, u32[]{:S(2)}) collective-permute-start(f16[145,8,128]{2,1,0:T(8,128)(2,1)S(1)} %collective-permute-done.16), channel_id=1, source_target_pairs={{0,2},{2,0},{4,6},{6,4},{8,10},{10,8},{12,14},{14,12},{16,18},{18,... | collective-permute-start | bytes 890888 | tf_op jit(solution)/shard_map/ppermute | solution.py:288
  130.0 2.1 %collective-permute-start.21 = (f16[145,8,128]{2,1,0:T(8,128)(2,1)S(1)}, f16[145,8,128]{2,1,0:T(8,128)(2,1)S(1)}, u32[]{:S(2)}, u32[]{:S(2)}) collective-permute-start(f16[145,8,128]{2,1,0:T(8,128)(2,1)S(1)} %collective-permute-done.20), channel_id=1, source_target_pairs={{0,2},{2,0},{4,6},{6,4},{8,10},{10,8},{12,14},{14,12},{16,18},{18,... | collective-permute-start | bytes 890888 | tf_op jit(solution)/shard_map/ppermute | solution.py:288
  131.1 1.7 %collective-permute-start.25 = (f16[145,8,128]{2,1,0:T(8,128)(2,1)S(1)}, f16[145,8,128]{2,1,0:T(8,128)(2,1)S(1)}, u32[]{:S(2)}, u32[]{:S(2)}) collective-permute-start(f16[145,8,128]{2,1,0:T(8,128)(2,1)S(1)} %collective-permute-done.24), channel_id=1, source_target_pairs={{0,2},{2,0},{4,6},{6,4},{8,10},{10,8},{12,14},{14,12},{16,18},{18,... | collective-permute-start | bytes 890888 | tf_op jit(solution)/shard_map/ppermute | solution.py:288
  132.9 3.7 %copy-start.8 = (f32[9,128,2,8,128]{4,3,2,1,0:T(8,128)}, f32[9,128,2,8,128]{4,3,2,1,0:T(8,128)S(1)}, u32[]{:S(2)}) copy-start(f32[9,128,2,8,128]{4,3,2,1,0:T(8,128)S(1)} %fusion) | copy-start | bytes 28311556

commit v3 on v2

--- a/solution.py
+++ b/solution.py
@@ -15,7 +15,7 @@
 WINDOW = 384
 PAD = WINDOW - REACH
 COLUMN_SHIFTS = (-DILATION_RATE, 0, DILATION_RATE)
-VMEM_LIMIT = 48 * 1024 * 1024
+VMEM_LIMIT = 24 * 1024 * 1024
 
 
 def column_mask(start, width, shift):
@@ -252,15 +252,26 @@
     )(cot, w, after)
 
 
-def summed(values):
-    exponents = [value[-1:].astype(jnp.float32) for value in values]
-    lowest = functools.reduce(jnp.minimum, exponents) - float((len(values) - 1).bit_length())
-    total = sum(
-        value.astype(jnp.float32) * jnp.exp2(lowest - exponent)
-        for value, exponent in zip(values, exponents)
+def common_exponent(values, bits):
+    lowest = functools.reduce(
+        jnp.minimum, [value[-1:].astype(jnp.float32) + bit for value, bit in values]
     )
-    last = lax.broadcasted_iota(jnp.int32, total.shape, 0) == total.shape[0] - 1
-    return jnp.where(last, jnp.broadcast_to(lowest, total.shape), total).astype(jnp.float16)
+    return lowest - bits
+
+
+def scaled_sum(values, lowest):
+    return sum(
+        value.astype(jnp.float32) * jnp.exp2(lowest - value[-1:].astype(jnp.float32))
+        for value, _ in values
+    )
+
+
+def summed(values, bits, key):
+    lowest = common_exponent(values, bits)
+    total = scaled_sum(values, lowest)
+    tile = lax.broadcasted_iota(jnp.int32, total.shape, 0)
+    marked = tile * key >= (total.shape[0] - 1) * key
+    return jnp.where(marked, jnp.broadcast_to(lowest, total.shape), total).astype(jnp.float16)
 
 
 def token(value):
@@ -298,56 +309,73 @@
 
     if chans == 2:
         their_cot = lax.ppermute(own_cot, "chan", [(0, 1), (1, 0)])
+        parts = (own_cot, their_cot)
+        first = chan
+    else:
+        cot = lax.all_gather(own_cot, "chan", axis=0, tiled=True)
+        parts = (cot[:LANES], cot[LANES:])
+        first = 0
+    other_cots = [to_core(part) for part in parts]
+    other_x = to_core(lax.dynamic_slice_in_dim(x, (1 - core) * core_rows, core_rows, 0))
+    where = jnp.stack([core, column * depth + level]).astype(jnp.int32)
+    halves, exponents = [], []
+    after = own_cot
+    for side, (part, other) in enumerate(zip(parts, other_cots)):
+        shards = kernel_grad(where, 2 * depth, x, other_x, part, other, after)
+        held = [None] * depth
+        for step in range(depth - 1, -1, -1):
+            sent = shards[depth + step].astype(jnp.float16)
+            held[step] = [(shards[step], 0.0), (to_column(sent), 0.0)]
+        bits = 1.0
+        for bit in [1 << shift for shift in range(depth.bit_length() - 1)]:
+            for step in range(depth - bit, 0, -2 * bit):
+                pair = summed(held[step], bits, 2 * step + side)
+                held[step ^ bit].append((to_level(pair, bit), bits))
+                after = token(pair) if step == depth - 1 else after
+            bits += 1.0
+        lowest = common_exponent(held[0], bits)
+        halves.append(scaled_sum([(v, b) for v, b in held[0]], lowest)[:-1].astype(jnp.float16))
+        exponents.append(lowest)
+    halves = [jnp.where(first == side, halves[0], halves[1]) for side in range(2)]
+    exponents = [jnp.where(first == side, exponents[0], exponents[1]) for side in range(2)]
+    halves = [half.reshape(taps, shard_tiles, TILE, LANES) for half in halves]
+    shard = jnp.stack(halves, 2)
+    exponent = jnp.concatenate(exponents, 0)
+
+    grad = jnp.zeros((taps, rows // TILE, 2, TILE, LANES), jnp.float16)
+    near = [shard]
+    for step in range(1, depth):
+        low = step & -step
+        near.append(to_level(near[step ^ low], low))
+    far = [to_column(value) for value in near]
+    for chip, values, group in ((column, near, depth), (1 - column, far, 2)):
+        for start in range(0, depth, group):
+            across = to_core(jnp.stack(values[start : start + group]))
+            for step in range(start, start + group):
+                row = chip * chip_tiles + (level ^ step) * shard_tiles
+                for base, part in ((core, values[step]), (1 - core, across[step - start])):
+                    grad = lax.dynamic_update_slice_in_dim(grad, part, base * core_tiles + row, 1)
+    other = to_core(exponent + 0.0 * token(near[-1][0, 0])[0])
+    by_core = [jnp.where(core == side, exponent, other) for side in range(2)]
+    factor = jnp.exp2(-jnp.stack(by_core)) * (1.0 / samples)
+    grad = grad.reshape(taps, 2, core_tiles, 2, TILE, LANES).astype(jnp.float32)
+    grad = (grad * factor[None, :, None]).reshape(taps, rows // TILE, 2, TILE, LANES)
+    weight_grad = jnp.transpose(grad, (1, 3, 0, 2, 4)).reshape(rows, taps, outs)
+
+    total = forward(x, w, token(shard[0, 0]))
+    if chans == 2:
+        mine = lax.dynamic_slice_in_dim(total, chan * own_outs, own_outs, 0)
+        theirs = lax.dynamic_slice_in_dim(total, (1 - chan) * own_outs, own_outs, 0)
+        result = mine + lax.ppermute(theirs, "chan", [(0, 1), (1, 0)])
         cot = jnp.where(
             chan == 0,
             jnp.concatenate([own_cot, their_cot], 0),
             jnp.concatenate([their_cot, own_cot], 0),
         )
     else:
-        cot = lax.all_gather(own_cot, "chan", axis=0, tiled=True)
-    other_x = to_core(lax.dynamic_slice_in_dim(x, (1 - core) * core_rows, core_rows, 0))
-    other_cot = to_core(cot)
-    where = jnp.stack([core, column * depth + level]).astype(jnp.int32)
-
-    shards = kernel_grad(where, 2 * depth, x, other_x, cot, other_cot, own_cot)
-    near, far = shards[:depth], shards[depth:]
-
-    total = forward(x, w, token(near[0]))
-
-    order = list(range(depth - 1, -1, -1))
-    kept = None
-    line = []
-    for step in order:
-        came = to_column(far[step].astype(jnp.float16))
-        pair = [near[step], came]
-        if step:
-            line.append(to_level(summed(pair), step))
-        else:
-            kept = summed(pair)
-    shard = summed([kept] + line[::-1])
-    input_grad = input_gradient(cot, w, token(line[0]))[None]
-
-    grad = jnp.zeros((taps, rows // TILE, outs // LANES, TILE, LANES), jnp.float32)
-    for step in range(depth):
-        here = shard if step == 0 else to_level(shard, step)
-        there = to_column(here)
-        owner = level ^ step
-        for chip, value in ((column, here), (1 - column, there)):
-            row = chip * chip_tiles + owner * shard_tiles
-            for base, part in ((core, value), (1 - core, to_core(value))):
-                factor = jnp.exp2(-part[-1].astype(jnp.float32)) * (1.0 / samples)
-                part = part[:-1].reshape(taps, shard_tiles, outs // LANES, TILE, LANES)
-                part = part.astype(jnp.float32) * factor
-                grad = lax.dynamic_update_slice_in_dim(grad, part, base * core_tiles + row, 1)
-    weight_grad = jnp.transpose(grad, (1, 3, 0, 2, 4)).reshape(rows, taps, outs)
-
-    if chans == 2:
-        mine = lax.dynamic_slice_in_dim(total, chan * own_outs, own_outs, 0)
-        theirs = lax.dynamic_slice_in_dim(total, (1 - chan) * own_outs, own_outs, 0)
-        result = mine + lax.ppermute(theirs, "chan", [(0, 1), (1, 0)])
-    else:
         result = lax.psum_scatter(total, "chan", scatter_dimension=0, tiled=True)
     result = result.astype(jnp.bfloat16)[None]
+    input_grad = input_gradient(cot, w, token(near[depth // 2][0, 0]))[None]
     return (result, input_grad, weight_grad)
 
 

time: 137 us -> 115 us (0.84)
  the two profiles are of different devices: /device:TPU:17 before, /device:TPU:0 now
where the time goes in v3:
time: 115 us; the launch traced here: 114 us
  waiting for transfers between devices  31.2 us (27%)
  starting transfers between devices  28.5 us (25%)
  Pallas kernels  23.6 us (21%)
  other arithmetic  17.3 us (15%)
  local copies, waits for them, and re-layouts  12.5 us (11%)
  between operations  1.19 us (1%)
    ppermute x28, waiting for transfers between devices, to(): lax.ppermute(value, 'dp', [(i, i ^ distance) for i in range(samples)])  31.1 us
    ppermute x28, starting transfers between devices, to(): lax.ppermute(value, 'dp', [(i, i ^ distance) for i in range(samples)])  25 us
    pallas_call x2, Pallas kernels, kernel_grad(): pl.pallas_call(functools.partial(kernel_grad_kernel, shards), out_shape=[...  12.1 us
    unnamed x34, local copies, waits for them, and re-layouts  7.77 us
    pallas_call x1, Pallas kernels, input_gradient(): pl.pallas_call(input_grad_kernel, out_shape=jax.ShapeDtypeStruct((rows, p...  6.54 us
    pallas_call x1, Pallas kernels, forward(): pl.pallas_call(forward_kernel, out_shape=jax.ShapeDtypeStruct((outs, posi...  4.97 us
    reshape x1, other arithmetic, on_device(): weight_grad = jnp.transpose(grad, (1, 3, 0, 2, 4)).reshape(rows, taps, outs)  4.65 us
    convert_element_type x8, other arithmetic, on_device(): sent = shards[depth + step].astype(jnp.float16)  3.73 us
  transfers between devices with their start and end apart: 30, of which 10 were waited for; matrix products, arithmetic and copies ran while one was open for 12% of the time, Pallas kernels for 21%

profile of v3, /device:TPU:0, one launch (start us, length us, event | category | flops | bytes accessed | tf_op | source)
XLA Modules:
  0.0 114.3 jit_solution(17653524747138498841)
XLA Ops:
  0.7 2.5 %dynamic-slice_bitcast_fusion = bf16[512,1152]{1,0:T(8,128)(2,1)} fusion(bf16[1,1024,1152]{2,1,0:T(8,128)(2,1)} %param.3, s32[]{:T(128)S(6)} %select_n.149), kind=kLoop, calls=%fused_computation.2 | loop fusion | bytes 2359300 | tf_op jit(solution)/shard_map/dynamic_slice | solution.py:319
  3.7 3.0 %collective-permute-start.9 = (bf16[128,1152]{1,0:T(8,128)(2,1)}, bf16[128,1152]{1,0:T(8,128)(2,1)}, u32[]{:S(2)}, u32[]{:S(2)}) collective-permute-start(bf16[128,1152]{1,0:T(8,128)(2,1)} %bitcast.137), channel_id=1, source_target_pairs={{0,1},{1,0},{2,3},{3,2},{4,5},{5,4},{6,7},{7,6},{8,9},{9,8},{10,11... | collective-permute-start | bytes 884744 | tf_op jit(solution)/shard_map/ppermute | solution.py:311
  9.0 0.7 copy-done.7
  9.7 1.7 %copy-done = bf16[1,1024,1152]{2,1,0:T(8,128)(2,1)S(1)} copy-done((bf16[1,1024,1152]{2,1,0:T(8,128)(2,1)S(1)}, bf16[1,1024,1152]{2,1,0:T(8,128)(2,1)}, u32[]{:S(2)}) %copy-start) | copy-done | bytes 2359320
  11.4 1.0 copy-done.5
  12.3 1.0 copy-done.8
  13.3 6.1 %kernel_grad.2 = (f32[73,8,128]{2,1,0:T(8,128)S(1)}, f32[73,8,128]{2,1,0:T(8,128)S(1)}, f32[73,8,128]{2,1,0:T(8,128)S(1)}, f32[73,8,128]{2,1,0:T(8,128)S(1)}, f3...) custom-call(s32[2]{0:T(128)S(1)} %pad_add_fusion.place_ref, ...), custom_call_target="tpu_custom_call" | custom-call | flops 1509949440 | bytes 5308416 | tf_op jit(solution)/shard_map/kernel_grad/pallas_call | solution.py:113
  19.4 0.7 copy-done.2
  20.1 0.7 copy-done.3
  20.8 0.7 copy-done.4
  22.1 0.7 convert_element_type.175
  22.8 1.5 %collective-permute-start.6 = (f16[73,8,128]{2,1,0:T(8,128)(2,1)}, f16[73,8,128]{2,1,0:T(8,128)(2,1)}, u32[]{:S(2)}, u32[]{:S(2)}) collective-permute-start(f16[73,8,128]{2,1,0:T(8,128)(2,1)} %convert_element_type.175), channel_id=1, source_target_pairs={{0,4},{2,6},{4,0},{6,2},{8,12},{10,14},{12,8},{14,10},{16,20},{18,... | collective-permute-start | bytes 448520 | tf_op jit(solution)/shard_map/ppermute | solution.py:299
  24.9 1.0 convert_element_type.168
  25.9 0.6 collective-permute-start.3
  26.5 1.0 convert_element_type.173
  27.5 1.6 %collective-permute-start.5 = (f16[73,8,128]{2,1,0:T(8,128)(2,1)S(1)}, f16[73,8,128]{2,1,0:T(8,128)(2,1)S(1)}, u32[]{:S(2)}, u32[]{:S(2)}) collective-permute-start(f16[73,8,128]{2,1,0:T(8,128)(2,1)S(1)} %convert_element_type.173), channel_id=1, source_target_pairs={{0,4},{2,6},{4,0},{6,2},{8,12},{10,14},{12,8},{14,10},{16,20},{18,... | collective-permute-start | bytes 448520 | tf_op jit(solution)/shard_map/ppermute | solution.py:299
  29.0 1.0 convert_element_type.166
  30.6 0.7 fusion.46
  31.3 1.1 select_convert_fusion.4
  32.4 1.6 %collective-permute-start.7 = (f16[73,8,128]{2,1,0:T(8,128)(2,1)S(1)}, f16[73,8,128]{2,1,0:T(8,128)(2,1)S(1)}, u32[]{:S(2)}, u32[]{:S(2)}) collective-permute-start(f16[73,8,128]{2,1,0:T(8,128)(2,1)S(1)} %select_convert_fusion.4), channel_id=1, source_target_pairs={{0,8},{2,10},{4,12},{6,14},{8,0},{10,2},{12,4},{14,6},{16,24},{18,... | collective-permute-start | bytes 448520 | tf_op jit(solution)/shard_map/ppermute | solution.py:299
  34.0 0.7 copy-done.10
  34.7 6.0 %kernel_grad.3 = (f32[73,8,128]{2,1,0:T(8,128)S(1)}, f32[73,8,128]{2,1,0:T(8,128)S(1)}, f32[73,8,128]{2,1,0:T(8,128)S(1)}, f32[73,8,128]{2,1,0:T(8,128)S(1)}, f3...) custom-call(s32[2]{0:T(128)S(1)} %copy-done.10, ...), custom_call_target="tpu_custom_call" | custom-call | flops 1509949440 | bytes 5308416 | tf_op jit(solution)/shard_map/kernel_grad/pallas_call | solution.py:113
  40.8 1.6 %collective-permute-start.15 = (f16[73,8,128]{2,1,0:T(8,128)(2,1)S(1)}, f16[73,8,128]{2,1,0:T(8,128)(2,1)S(1)}, u32[]{:S(2)}, u32[]{:S(2)}) collective-permute-start(f16[73,8,128]{2,1,0:T(8,128)(2,1)S(1)} %convert_element_type.198), channel_id=1, source_target_pairs={{0,4},{2,6},{4,0},{6,2},{8,12},{10,14},{12,8},{14,10},{16,20},{18,... | collective-permute-start | bytes 448520 | tf_op jit(solution)/shard_map/ppermute | solution.py:299
  43.2 2.9 %collective-permute-done.15 = f16[73,8,128]{2,1,0:T(8,128)(2,1)S(1)} collective-permute-done((f16[73,8,128]{2,1,0:T(8,128)(2,1)S(1)}, f16[73,8,128]{2,1,0:T(8,128)(2,1)S(1)}, u32[]{:S(2)}, u32[]{:S(2)}) %collective-permute-start.15) | collective-permute-done | bytes 149536 | tf_op jit(solution)/shard_map/ppermute | solution.py:299
  46.1 1.5 %collective-permute-start.12 = (f16[73,8,128]{2,1,0:T(8,128)(2,1)S(1)}, f16[73,8,128]{2,1,0:T(8,128)(2,1)S(1)}, u32[]{:S(2)}, u32[]{:S(2)}) collective-permute-start(f16[73,8,128]{2,1,0:T(8,128)(2,1)S(1)} %convert_element_type.191), channel_id=1, source_target_pairs={{0,4},{2,6},{4,0},{6,2},{8,12},{10,14},{12,8},{14,10},{16,20},{18,... | collective-permute-start | bytes 448520 | tf_op jit(solution)/shard_map/ppermute | solution.py:299
  47.6 0.6 collective-permute-start.14
  48.2 1.5 %collective-permute-start.11 = (f16[73,8,128]{2,1,0:T(8,128)(2,1)S(1)}, f16[73,8,128]{2,1,0:T(8,128)(2,1)S(1)}, u32[]{:S(2)}, u32[]{:S(2)}) collective-permute-start(f16[73,8,128]{2,1,0:T(8,128)(2,1)S(1)} %convert_element_type.189), channel_id=1, source_target_pairs={{0,4},{2,6},{4,0},{6,2},{8,12},{10,14},{12,8},{14,10},{16,20},{18,... | collective-permute-start | bytes 448520 | tf_op jit(solution)/shard_map/ppermute | solution.py:299
  49.9 3.0 %collective-permute-done.12 = f16[73,8,128]{2,1,0:T(8,128)(2,1)S(1)} collective-permute-done((f16[73,8,128]{2,1,0:T(8,128)(2,1)S(1)}, f16[73,8,128]{2,1,0:T(8,128)(2,1)S(1)}, u32[]{:S(2)}, u32[]{:S(2)}) %collective-permute-start.12) | collective-permute-done | bytes 149536 | tf_op jit(solution)/shard_map/ppermute | solution.py:299
  53.7 1.2 %collective-permute-done.14 = f16[73,8,128]{2,1,0:T(8,128)(2,1)S(1)} collective-permute-done((f16[73,8,128]{2,1,0:T(8,128)(2,1)S(1)}, f16[73,8,128]{2,1,0:T(8,128)(2,1)S(1)}, u32[]{:S(2)}, u32[]{:S(2)}) %collective-permute-start.14) | collective-permute-done | bytes 149536 | tf_op jit(solution)/shard_map/ppermute | solution.py:299
  54.9 2.6 %collective-permute-start.8 = (f16[73,8,128]{2,1,0:T(8,128)(2,1)S(1)}, f16[73,8,128]{2,1,0:T(8,128)(2,1)S(1)}, u32[]{:S(2)}, u32[]{:S(2)}) collective-permute-start(f16[73,8,128]{2,1,0:T(8,128)(2,1)S(1)} %select_convert_fusion.3), channel_id=1, source_target_pairs={{0,16},{2,18},{4,20},{6,22},{8,24},{10,26},{12,28},{14,30},{16,0},... | collective-permute-start | bytes 448520 | tf_op jit(solution)/shard_map/ppermute | solution.py:299
  57.5 5.2 %collective-permute-done.16 = f16[73,8,128]{2,1,0:T(8,128)(2,1)S(1)} collective-permute-done((f16[73,8,128]{2,1,0:T(8,128)(2,1)S(1)}, f16[73,8,128]{2,1,0:T(8,128)(2,1)S(1)}, u32[]{:S(2)}, u32[]{:S(2)}) %collective-permute-start.16) | collective-permute-done | bytes 149536 | tf_op jit(solution)/shard_map/ppermute | solution.py:299
  62.8 1.6 %collective-permute-start.17 = (f16[73,8,128]{2,1,0:T(8,128)(2,1)S(1)}, f16[73,8,128]{2,1,0:T(8,128)(2,1)S(1)}, u32[]{:S(2)}, u32[]{:S(2)}) collective-permute-start(f16[73,8,128]{2,1,0:T(8,128)(2,1)S(1)} %select_convert_fusion), channel_id=1, source_target_pairs={{0,16},{2,18},{4,20},{6,22},{8,24},{10,26},{12,28},{14,30},{16,0},... | collective-permute-start | bytes 448520 | tf_op jit(solution)/shard_map/ppermute | solution.py:299
  64.5 1.2 %maximum_select_fusion.cot_ref = bf16[256,1152]{1,0:T(8,128)(2,1)S(1)} fusion(bf16[128,1152]{1,0:T(8,128)(2,1)} %collective-permute-done.9.own_cot, bf16[128,1152]{1,0:T(8,128)(2,1)S(1)} %bitcast.140, pred[]{:T(512)S(6)} %eq.18), kind=kLoop, calls=%fused_computation.3 | loop fusion | flops 2654208 | bytes 1179649 | tf_op jit(solution)/shard_map/jit(_where)/select_n | solution.py:370
  65.8 3.2 %collective-permute-done.13 = f16[73,8,128]{2,1,0:T(8,128)(2,1)S(1)} collective-permute-done((f16[73,8,128]{2,1,0:T(8,128)(2,1)S(1)}, f16[73,8,128]{2,1,0:T(8,128)(2,1)S(1)}, u32[]{:S(2)}, u32[]{:S(2)}) %collective-permute-start.13) | collective-permute-done | bytes 149536 | tf_op jit(solution)/shard_map/ppermute | solution.py:299
  68.9 6.4 %collective-permute-done.17 = f16[73,8,128]{2,1,0:T(8,128)(2,1)S(1)} collective-permute-done((f16[73,8,128]{2,1,0:T(8,128)(2,1)S(1)}, f16[73,8,128]{2,1,0:T(8,128)(2,1)S(1)}, u32[]{:S(2)}, u32[]{:S(2)}) %collective-permute-start.17) | collective-permute-done | bytes 149536 | tf_op jit(solution)/shard_map/ppermute | solution.py:299
  75.7 0.7 broadcast_in_dim.67
  76.8 2.1 %collective-permute-start.20 = (f16[9,8,2,8,128]{4,3,2,1,0:T(8,128)(2,1)S(1)}, f16[9,8,2,8,128]{4,3,2,1,0:T(8,128)(2,1)S(1)}, u32[]{:S(2)}, u32[]{:S(2)}) collective-permute-start(f16[9,8,2,8,128]{4,3,2,1,0:T(8,128)(2,1)S(1)} %get-tuple-element.59), channel_id=1, source_target_pairs={{0,8},{2,10},{4,12},{6,14},{8,0},{10,2},{12,4},{14,6},{16,24},{18,... | collective-permute-start | bytes 884744 | tf_op jit(solution)/shard_map/ppermute | solution.py:299
  78.9 1.5 %collective-permute-start.23 = (f16[9,8,2,8,128]{4,3,2,1,0:T(8,128)(2,1)S(1)}, f16[9,8,2,8,128]{4,3,2,1,0:T(8,128)(2,1)S(1)}, u32[]{:S(2)}, u32[]{:S(2)}) collective-permute-start(f16[9,8,2,8,128]{4,3,2,1,0:T(8,128)(2,1)S(1)} %get-tuple-element.59), channel_id=1, source_target_pairs={{0,4},{2,6},{4,0},{6,2},{8,12},{10,14},{12,8},{14,10},{16,20},{18,... | collective-permute-start | bytes 884744 | tf_op jit(solution)/shard_map/ppermute | solution.py:299
  80.4 5.0 %forward.1 = f32[256,1152]{1,0:T(8,128)S(1)} custom-call(bf16[1024,1152]{1,0:T(8,128)(2,1)S(1)} %bitcast.135, bf16[9,1024,256]{2,1,0:T(8,128)(2,1)S(1)} %bitcast.143, f32[8,128]{1,0:T(8,128)S(1)} %fusion.98._), custom_call_target="tpu_custom_call" | custom-call | flops 3019898880 | bytes 8257536 | tf_op jit(solution)/shard_map/forward/pallas_call | solution.py:182
  86.0 1.0 collective-permute-done.19
  87.0 1.5 %collective-permute-start.26 = (f16[9,8,2,8,128]{4,3,2,1,0:T(8,128)(2,1)S(1)}, f16[9,8,2,8,128]{4,3,2,1,0:T(8,128)(2,1)S(1)}, u32[]{:S(2)}, u32[]{:S(2)}) collective-permute-start(f16[9,8,2,8,128]{4,3,2,1,0:T(8,128)(2,1)S(1)} %collective-permute-done.19), channel_id=1, source_target_pairs={{0,4},{2,6},{4,0},{6,2},{8,12},{10,14},{12,8},{14,10},{16,20},{18,... | collective-permute-start | bytes 884744 | tf_op jit(solution)/shard_map/ppermute | solution.py:299
  88.5 1.2 %collective-permute-start.24 = (f16[9,8,2,8,128]{4,3,2,1,0:T(8,128)(2,1)S(1)}, f16[9,8,2,8,128]{4,3,2,1,0:T(8,128)(2,1)S(1)}, u32[]{:S(2)}, u32[]{:S(2)}) collective-permute-start(f16[9,8,2,8,128]{4,3,2,1,0:T(8,128)(2,1)S(1)} %collective-permute-done.20), channel_id=1, source_target_pairs={{0,4},{2,6},{4,0},{6,2},{8,12},{10,14},{12,8},{14,10},{16,20},{18,... | collective-permute-start | bytes 884744 | tf_op jit(solution)/shard_map/ppermute | solution.py:299
  89.7 6.5 %input_gradient.1 = bf16[1024,1152]{1,0:T(8,128)(2,1)} custom-call(bf16[256,1152]{1,0:T(8,128)(2,1)S(1)} %maximum_select_fusion.cot_ref, bf16[9,1024,256]{2,1,0:T(8,128)(2,1)S(1)} %bitcast.144, f32[8,128]{1,0:T(8,128)S(1)} %fusion.97._), custom_call_target="tpu_custom_call" | custom-call | flops 3019898880 | bytes 7667712 | tf_op jit(solution)/shard_map/input_gradient/pallas_call | solution.py:230
  97.6 1.1 collective-permute-start.27
  98.7 0.8 fusion
  99.6 7.4 %collective-permute-done.27 = f16[9,8,2,8,128]{4,3,2,1,0:T(8,128)(2,1)S(1)} collective-permute-done((f16[9,8,2,8,128]{4,3,2,1,0:T(8,128)(2,1)S(1)}, f16[9,8,2,8,128]{4,3,2,1,0:T(8,128)(2,1)S(1)}, u32[]{:S(2)}, u32[]{:S(2)}) %collective-permute-start.27) | collective-permute-done | bytes 294944 | tf_op jit(solution)/shard_map/ppermute | solution.py:299
  108.5 0.8 collective-permute-done.28
  109.7 4.6 %multiply_bitcast_fusion = f32[1024,9,256]{2,0,1:T(8,128)} fusion(f16[9,128,2,8,128]{4,3,2,1,0:T(8,128)(2,1)S(1)} %fusion.1, f32[128,2,8,128]{3,2,1,0:T(8,128)S(1)} %bitcast.145), kind=kLoop, calls=%fused_computation | loop fusion | flops 4718592 | bytes 15204352 | tf_op jit(solution)/shard_map/reshape | solution.py:363
  (117 shorter events, 11.1 us)
Async XLA Ops:
  0.7 33.4 %copy-start.1 = (bf16[1,1024,1152]{2,1,0:T(8,128)(2,1)S(1)}, bf16[1,1024,1152]{2,1,0:T(8,128)(2,1)}, u32[]{:S(2)}) copy-start(bf16[1,1024,1152]{2,1,0:T(8,128)(2,1)} %param.3) | copy-start | bytes 7077892
  3.2 6.5 %collective-permute-start = (bf16[512,1152]{1,0:T(8,128)(2,1)}, bf16[512,1152]{1,0:T(8,128)(2,1)}, u32[]{:S(2)}, u32[]{:S(2)}) collective-permute-start(bf16[512,1152]{1,0:T(8,128)(2,1)} %dynamic-slice_bitcast_fusion), channel_id=1, source_target_pairs={{0,2},{2,0},{4,6},{6,4},{8,10},{10,8},{12,14},{14,12},{16,18},{18,... | collective-permute-start | bytes 3538952 | tf_op jit(solution)/shard_map/ppermute | solution.py:299
  3.6 5.3 %collective-permute-start.1 = (bf16[128,1152]{1,0:T(8,128)(2,1)}, bf16[128,1152]{1,0:T(8,128)(2,1)S(1)}, u32[]{:S(2)}, u32[]{:S(2)}) collective-permute-start(bf16[128,1152]{1,0:T(8,128)(2,1)} %bitcast.136), channel_id=1, source_target_pairs={{0,2},{2,0},{4,6},{6,4},{8,10},{10,8},{12,14},{14,12},{16,18},{18,... | collective-permute-start | bytes 884744 | tf_op jit(solution)/shard_map/ppermute | solution.py:299
  3.7 21.1 %collective-permute-start.9 = (bf16[128,1152]{1,0:T(8,128)(2,1)}, bf16[128,1152]{1,0:T(8,128)(2,1)}, u32[]{:S(2)}, u32[]{:S(2)}) collective-permute-start(bf16[128,1152]{1,0:T(8,128)(2,1)} %bitcast.137), channel_id=1, source_target_pairs={{0,1},{1,0},{2,3},{3,2},{4,5},{5,4},{6,7},{7,6},{8,9},{9,8},{10,11... | collective-permute-start | bytes 884744 | tf_op jit(solution)/shard_map/ppermute | solution.py:311
  9.0 0.7 copy-start.7
  9.7 1.7 %copy-start = (bf16[1,1024,1152]{2,1,0:T(8,128)(2,1)S(1)}, bf16[1,1024,1152]{2,1,0:T(8,128)(2,1)}, u32[]{:S(2)}) copy-start(bf16[1,1024,1152]{2,1,0:T(8,128)(2,1)} %param.3) | copy-start | bytes 7077892
  11.4 1.0 copy-start.5
  12.3 1.0 copy-start.8
  19.4 0.7 copy-start.2
  20.1 0.7 copy-start.3
  20.8 0.7 copy-start.4
  21.5 0.6 copy-start.9
  22.8 7.8 %collective-permute-start.6 = (f16[73,8,128]{2,1,0:T(8,128)(2,1)}, f16[73,8,128]{2,1,0:T(8,128)(2,1)}, u32[]{:S(2)}, u32[]{:S(2)}) collective-permute-start(f16[73,8,128]{2,1,0:T(8,128)(2,1)} %convert_element_type.175), channel_id=1, source_target_pairs={{0,4},{2,6},{4,0},{6,2},{8,12},{10,14},{12,8},{14,10},{16,20},{18,... | collective-permute-start | bytes 448520 | tf_op jit(solution)/shard_map/ppermute | solution.py:299
  24.8 17.6 %copy-start.14 = (pred[73]{0:T(512)(128)(4,1)S(1)}, pred[73]{0:T(512)(128)(4,1)}, u32[]{:S(2)}) copy-start(pred[73]{0:T(512)(128)(4,1)} %multiply_compare_fusion.5) | copy-start | bytes 223
  24.8 9.2 %collective-permute-start.10 = (bf16[128,1152]{1,0:T(8,128)(2,1)}, bf16[128,1152]{1,0:T(8,128)(2,1)S(1)}, u32[]{:S(2)}, u32[]{:S(2)}) collective-permute-start(bf16[128,1152]{1,0:T(8,128)(2,1)} %collective-permute-done.9.own_cot), channel_id=1, source_target_pairs={{0,2},{2,0},{4,6},{6,4},{8,10},{10,8},{12,14},{14,12},{16,18},{18,... | collective-permute-start | bytes 884744 | tf_op jit(solution)/shard_map/ppermute | solution.py:299
  25.9 16.5 %collective-permute-start.3 = (f16[73,8,128]{2,1,0:T(8,128)(2,1)S(1)}, f16[73,8,128]{2,1,0:T(8,128)(2,1)S(1)}, u32[]{:S(2)}, u32[]{:S(2)}) collective-permute-start(f16[73,8,128]{2,1,0:T(8,128)(2,1)S(1)} %convert_element_type.168), channel_id=1, source_target_pairs={{0,4},{2,6},{4,0},{6,2},{8,12},{10,14},{12,8},{14,10},{16,20},{18,... | collective-permute-start | bytes 448520 | tf_op jit(solution)/shard_map/ppermute | solution.py:299
  26.5 23.2 %copy-start.13 = (pred[73]{0:T(512)(128)(4,1)S(1)}, pred[73]{0:T(512)(128)(4,1)}, u32[]{:S(2)}) copy-start(pred[73]{0:T(512)(128)(4,1)} %multiply_compare_fusion) | copy-start | bytes 223
  27.5 20.1 %collective-permute-start.5 = (f16[73,8,128]{2,1,0:T(8,128)(2,1)S(1)}, f16[73,8,128]{2,1,0:T(8,128)(2,1)S(1)}, u32[]{:S(2)}, u32[]{:S(2)}) collective-permute-start(f16[73,8,128]{2,1,0:T(8,128)(2,1)S(1)} %convert_element_type.173), channel_id=1, source_target_pairs={{0,4},{2,6},{4,0},{6,2},{8,12},{10,14},{12,8},{14,10},{16,20},{18,... | collective-permute-start | bytes 448520 | tf_op jit(solution)/shard_map/ppermute | solution.py:299
  30.0 23.4 %copy-start.12 = (pred[73]{0:T(512)(128)(4,1)S(1)}, pred[73]{0:T(512)(128)(4,1)}, u32[]{:S(2)}) copy-start(pred[73]{0:T(512)(128)(4,1)} %multiply_compare_fusion.4) | copy-start | bytes 223
  30.0 32.8 %collective-permute-start.2 = (f16[73,8,128]{2,1,0:T(8,128)(2,1)S(1)}, f16[73,8,128]{2,1,0:T(8,128)(2,1)S(1)}, u32[]{:S(2)}, u32[]{:S(2)}) collective-permute-start(f16[73,8,128]{2,1,0:T(8,128)(2,1)S(1)} %convert_element_type.166), channel_id=1, source_target_pairs={{0,4},{2,6},{4,0},{6,2},{8,12},{10,14},{12,8},{14,10},{16,20},{18,... | collective-permute-start | bytes 448520 | tf_op jit(solution)/shard_map/ppermute | solution.py:299
  32.4 15.8 %collective-permute-start.7 = (f16[73,8,128]{2,1,0:T(8,128)(2,1)S(1)}, f16[73,8,128]{2,1,0:T(8,128)(2,1)S(1)}, u32[]{:S(2)}, u32[]{:S(2)}) collective-permute-start(f16[73,8,128]{2,1,0:T(8,128)(2,1)S(1)} %select_convert_fusion.4), channel_id=1, source_target_pairs={{0,8},{2,10},{4,12},{6,14},{8,0},{10,2},{12,4},{14,6},{16,24},{18,... | collective-permute-start | bytes 448520 | tf_op jit(solution)/shard_map/ppermute | solution.py:299
  34.0 30.5 %copy-start.6 = (bf16[1,128,1152]{2,1,0:T(8,128)(2,1)S(1)}, bf16[1,128,1152]{2,1,0:T(8,128)(2,1)}, u32[]{:S(2)}) copy-start(bf16[1,128,1152]{2,1,0:T(8,128)(2,1)} %param.5) | copy-start | bytes 884740
  34.0 0.7 copy-start.10
  34.7 18.8 %copy-start.11 = (pred[73]{0:T(512)(128)(4,1)S(1)}, pred[73]{0:T(512)(128)(4,1)}, u32[]{:S(2)}) copy-start(pred[73]{0:T(512)(128)(4,1)} %multiply_compare_fusion.2) | copy-start | bytes 223
  40.8 5.2 %collective-permute-start.15 = (f16[73,8,128]{2,1,0:T(8,128)(2,1)S(1)}, f16[73,8,128]{2,1,0:T(8,128)(2,1)S(1)}, u32[]{:S(2)}, u32[]{:S(2)}) collective-permute-start(f16[73,8,128]{2,1,0:T(8,128)(2,1)S(1)} %convert_element_type.198), channel_id=1, source_target_pairs={{0,4},{2,6},{4,0},{6,2},{8,12},{10,14},{12,8},{14,10},{16,20},{18,... | collective-permute-start | bytes 448520 | tf_op jit(solution)/shard_map/ppermute | solution.py:299
  42.6 23.2 %collective-permute-start.4 = (f16[73,8,128]{2,1,0:T(8,128)(2,1)S(1)}, f16[73,8,128]{2,1,0:T(8,128)(2,1)S(1)}, u32[]{:S(2)}, u32[]{:S(2)}) collective-permute-start(f16[73,8,128]{2,1,0:T(8,128)(2,1)S(1)} %select_convert_fusion.5), channel_id=1, source_target_pairs={{0,8},{2,10},{4,12},{6,14},{8,0},{10,2},{12,4},{14,6},{16,24},{18,... | collective-permute-start | bytes 448520 | tf_op jit(solution)/shard_map/ppermute | solution.py:299
  43.1 37.2 %slice-start = ((s8[4718592]{0:T(1024)(128)(4,1)}), s8[4194304]{0:T(1024)(128)(4,1)S(1)}, s32[]{:S(2)}) async-start(s8[4718592]{0:T(1024)(128)(4,1)} %bitcast.141), calls=%async_computation | async-start | bytes 8388608
  46.1 6.8 %collective-permute-start.12 = (f16[73,8,128]{2,1,0:T(8,128)(2,1)S(1)}, f16[73,8,128]{2,1,0:T(8,128)(2,1)S(1)}, u32[]{:S(2)}, u32[]{:S(2)}) collective-permute-start(f16[73,8,128]{2,1,0:T(8,128)(2,1)S(1)} %convert_element_type.191), channel_id=1, source_target_pairs={{0,4},{2,6},{4,0},{6,2},{8,12},{10,14},{12,8},{14,10},{16,20},{18,... | collective-permute-start | bytes 448520 | tf_op jit(solution)/shard_map/ppermute | solution.py:299
  47.6 7.3 %collective-permute-start.14 = (f16[73,8,128]{2,1,0:T(8,128)(2,1)S(1)}, f16[73,8,128]{2,1,0:T(8,128)(2,1)S(1)}, u32[]{:S(2)}, u32[]{:S(2)}) collective-permute-start(f16[73,8,128]{2,1,0:T(8,128)(2,1)S(1)} %convert_element_type.196), channel_id=1, source_target_pairs={{0,4},{2,6},{4,0},{6,2},{8,12},{10,14},{12,8},{14,10},{16,20},{18,... | collective-permute-start | bytes 448520 | tf_op jit(solution)/shard_map/ppermute | solution.py:299
  48.2 17.6 %collective-permute-start.11 = (f16[73,8,128]{2,1,0:T(8,128)(2,1)S(1)}, f16[73,8,128]{2,1,0:T(8,128)(2,1)S(1)}, u32[]{:S(2)}, u32[]{:S(2)}) collective-permute-start(f16[73,8,128]{2,1,0:T(8,128)(2,1)S(1)} %convert_element_type.189), channel_id=1, source_target_pairs={{0,4},{2,6},{4,0},{6,2},{8,12},{10,14},{12,8},{14,10},{16,20},{18,... | collective-permute-start | bytes 448520 | tf_op jit(solution)/shard_map/ppermute | solution.py:299
  52.9 9.7 %collective-permute-start.16 = (f16[73,8,128]{2,1,0:T(8,128)(2,1)S(1)}, f16[73,8,128]{2,1,0:T(8,128)(2,1)S(1)}, u32[]{:S(2)}, u32[]{:S(2)}) collective-permute-start(f16[73,8,128]{2,1,0:T(8,128)(2,1)S(1)} %select_convert_fusion.1), channel_id=1, source_target_pairs={{0,8},{2,10},{4,12},{6,14},{8,0},{10,2},{12,4},{14,6},{16,24},{18,... | collective-permute-start | bytes 448520 | tf_op jit(solution)/shard_map/ppermute | solution.py:299
  54.9 10.9 %collective-permute-start.8 = (f16[73,8,128]{2,1,0:T(8,128)(2,1)S(1)}, f16[73,8,128]{2,1,0:T(8,128)(2,1)S(1)}, u32[]{:S(2)}, u32[]{:S(2)}) collective-permute-start(f16[73,8,128]{2,1,0:T(8,128)(2,1)S(1)} %select_convert_fusion.3), channel_id=1, source_target_pairs={{0,16},{2,18},{4,20},{6,22},{8,24},{10,26},{12,28},{14,30},{16,0},... | collective-permute-start | bytes 448520 | tf_op jit(solution)/shard_map/ppermute | solution.py:299
  62.6 6.3 %collective-permute-start.13 = (f16[73,8,128]{2,1,0:T(8,128)(2,1)S(1)}, f16[73,8,128]{2,1,0:T(8,128)(2,1)S(1)}, u32[]{:S(2)}, u32[]{:S(2)}) collective-permute-start(f16[73,8,128]{2,1,0:T(8,128)(2,1)S(1)} %select_convert_fusion.2), channel_id=1, source_target_pairs={{0,8},{2,10},{4,12},{6,14},{8,0},{10,2},{12,4},{14,6},{16,24},{18,... | collective-permute-start | bytes 448520 | tf_op jit(solution)/shard_map/ppermute | solution.py:299
  62.8 12.4 %collective-permute-start.17 = (f16[73,8,128]{2,1,0:T(8,128)(2,1)S(1)}, f16[73,8,128]{2,1,0:T(8,128)(2,1)S(1)}, u32[]{:S(2)}, u32[]{:S(2)}) collective-permute-start(f16[73,8,128]{2,1,0:T(8,128)(2,1)S(1)} %select_convert_fusion), channel_id=1, source_target_pairs={{0,16},{2,18},{4,20},{6,22},{8,24},{10,26},{12,28},{14,30},{16,0},... | collective-permute-start | bytes 448520 | tf_op jit(solution)/shard_map/ppermute | solution.py:299
  75.3 5.0 %slice-start.1 = ((s8[4718592]{0:T(1024)(128)(4,1)}), s8[524288]{0:T(1024)(128)(4,1)S(1)}, s32[]{:S(2)}) async-start(s8[4718592]{0:T(1024)(128)(4,1)} %bitcast.141), calls=%async_computation.1 | async-start | bytes 1048576
  76.7 10.3 %collective-permute-start.19 = (f16[9,8,2,8,128]{4,3,2,1,0:T(8,128)(2,1)S(1)}, f16[9,8,2,8,128]{4,3,2,1,0:T(8,128)(2,1)S(1)}, u32[]{:S(2)}, u32[]{:S(2)}) collective-permute-start(f16[9,8,2,8,128]{4,3,2,1,0:T(8,128)(2,1)S(1)} %get-tuple-element.59), channel_id=1, source_target_pairs={{0,16},{2,18},{4,20},{6,22},{8,24},{10,26},{12,28},{14,30},{16,0},... | collective-permute-start | bytes 884744 | tf_op jit(solution)/shard_map/ppermute | solution.py:299
  76.8 11.7 %collective-permute-start.20 = (f16[9,8,2,8,128]{4,3,2,1,0:T(8,128)(2,1)S(1)}, f16[9,8,2,8,128]{4,3,2,1,0:T(8,128)(2,1)S(1)}, u32[]{:S(2)}, u32[]{:S(2)}) collective-permute-start(f16[9,8,2,8,128]{4,3,2,1,0:T(8,128)(2,1)S(1)} %get-tuple-element.59), channel_id=1, source_target_pairs={{0,8},{2,10},{4,12},{6,14},{8,0},{10,2},{12,4},{14,6},{16,24},{18,... | collective-permute-start | bytes 884744 | tf_op jit(solution)/shard_map/ppermute | solution.py:299
  78.9 17.9 %collective-permute-start.23 = (f16[9,8,2,8,128]{4,3,2,1,0:T(8,128)(2,1)S(1)}, f16[9,8,2,8,128]{4,3,2,1,0:T(8,128)(2,1)S(1)}, u32[]{:S(2)}, u32[]{:S(2)}) collective-permute-start(f16[9,8,2,8,128]{4,3,2,1,0:T(8,128)(2,1)S(1)} %get-tuple-element.59), channel_id=1, source_target_pairs={{0,4},{2,6},{4,0},{6,2},{8,12},{10,14},{12,8},{14,10},{16,20},{18,... | collective-permute-start | bytes 884744 | tf_op jit(solution)/shard_map/ppermute | solution.py:299
  85.4 12.2 %collective-permute-start.18 = (f32[128,1152]{1,0:T(8,128)S(1)}, f32[128,1152]{1,0:T(8,128)S(1)}, u32[]{:S(2)}, u32[]{:S(2)}) collective-permute-start(f32[128,1152]{1,0:T(8,128)S(1)} %constant_dynamic-slice_fusion), channel_id=1, source_target_pairs={{0,1},{1,0},{2,3},{3,2},{4,5},{5,4},{6,7},{7,6},{8,9},{9,8},{10,11... | collective-permute-start | bytes 1769480 | tf_op jit(solution)/shard_map/ppermute | solution.py:369
  87.0 9.2 %collective-permute-start.21 = (f16[9,8,2,8,128]{4,3,2,1,0:T(8,128)(2,1)S(1)}, f16[9,8,2,8,128]{4,3,2,1,0:T(8,128)(2,1)S(1)}, u32[]{:S(2)}, u32[]{:S(2)}) collective-permute-start(f16[9,8,2,8,128]{4,3,2,1,0:T(8,128)(2,1)S(1)} %collective-permute-done.19), channel_id=1, source_target_pairs={{0,8},{2,10},{4,12},{6,14},{8,0},{10,2},{12,4},{14,6},{16,24},{18,... | collective-permute-start | bytes 884744 | tf_op jit(solution)/shard_map/ppermute | solution.py:299
  87.0 12.6 %collective-permute-start.26 = (f16[9,8,2,8,128]{4,3,2,1,0:T(8,128)(2,1)S(1)}, f16[9,8,2,8,128]{4,3,2,1,0:T(8,128)(2,1)S(1)}, u32[]{:S(2)}, u32[]{:S(2)}) collective-permute-start(f16[9,8,2,8,128]{4,3,2,1,0:T(8,128)(2,1)S(1)} %collective-permute-done.19), channel_id=1, source_target_pairs={{0,4},{2,6},{4,0},{6,2},{8,12},{10,14},{12,8},{14,10},{16,20},{18,... | collective-permute-start | bytes 884744 | tf_op jit(solution)/shard_map/ppermute | solution.py:299
  88.5 8.8 %collective-permute-start.24 = (f16[9,8,2,8,128]{4,3,2,1,0:T(8,128)(2,1)S(1)}, f16[9,8,2,8,128]{4,3,2,1,0:T(8,128)(2,1)S(1)}, u32[]{:S(2)}, u32[]{:S(2)}) collective-permute-start(f16[9,8,2,8,128]{4,3,2,1,0:T(8,128)(2,1)S(1)} %collective-permute-done.20), channel_id=1, source_target_pairs={{0,4},{2,6},{4,0},{6,2},{8,12},{10,14},{12,8},{14,10},{16,20},{18,... | collective-permute-start | bytes 884744 | tf_op jit(solution)/shard_map/ppermute | solution.py:299
  96.7 10.6 %collective-permute-start.22 = (f16[4,9,8,2,8,128]{5,4,3,2,1,0:T(8,128)(2,1)S(1)}, f16[4,9,8,2,8,128]{5,4,3,2,1,0:T(8,128)(2,1)S(1)}, u32[]{:S(2)}, u32[]{:S(2)}) collective-permute-start(f16[4,9,8,2,8,128]{5,4,3,2,1,0:T(8,128)(2,1)S(1)} %pad_maximum_fusion), channel_id=1, source_target_pairs={{0,2},{2,0},{4,6},{6,4},{8,10},{10,8},{12,14},{14,12},{16,18},{18,... | collective-permute-start | bytes 3538952 | tf_op jit(solution)/shard_map/ppermute | solution.py:299
  96.8 2.8 %collective-permute-start.29 = (f32[2,8,128]{2,1,0:T(8,128)S(1)}, f32[2,8,128]{2,1,0:T(8,128)S(1)}, u32[]{:S(2)}, u32[]{:S(2)}) collective-permute-start(f32[2,8,128]{2,1,0:T(8,128)S(1)} %fusion.20), channel_id=1, source_target_pairs={{0,2},{2,0},{4,6},{6,4},{8,10},{10,8},{12,14},{14,12},{16,18},{18,... | collective-permute-start | bytes 24584 | tf_op jit(solution)/shard_map/ppermute | solution.py:299
  97.5 10.6 %collective-permute-start.25 = (f16[2,9,8,2,8,128]{5,4,3,2,1,0:T(8,128)(2,1)S(1)}, f16[2,9,8,2,8,128]{5,4,3,2,1,0:T(8,128)(2,1)S(1)}, u32[]{:S(2)}, u32[]{:S(2)}) collective-permute-start(f16[2,9,8,2,8,128]{5,4,3,2,1,0:T(8,128)(2,1)S(1)} %pad_maximum_fusion.1), channel_id=1, source_target_pairs={{0,2},{2,0},{4,6},{6,4},{8,10},{10,8},{12,14},{14,12},{16,18},{18,... | collective-permute-start | bytes 1769480 | tf_op jit(solution)/shard_map/ppermute | solution.py:299
  97.6 9.4 %collective-permute-start.27 = (f16[9,8,2,8,128]{4,3,2,1,0:T(8,128)(2,1)S(1)}, f16[9,8,2,8,128]{4,3,2,1,0:T(8,128)(2,1)S(1)}, u32[]{:S(2)}, u32[]{:S(2)}) collective-permute-start(f16[9,8,2,8,128]{4,3,2,1,0:T(8,128)(2,1)S(1)} %collective-permute-done.21), channel_id=1, source_target_pairs={{0,4},{2,6},{4,0},{6,2},{8,12},{10,14},{12,8},{14,10},{16,20},{18,... | collective-permute-start | bytes 884744 | tf_op jit(solution)/shard_map/ppermute | solution.py:299
  107.2 2.1 %collective-permute-start.28 = (f16[2,9,8,2,8,128]{5,4,3,2,1,0:T(8,128)(2,1)S(1)}, f16[2,9,8,2,8,128]{5,4,3,2,1,0:T(8,128)(2,1)S(1)}, u32[]{:S(2)}, u32[]{:S(2)}) collective-permute-start(f16[2,9,8,2,8,128]{5,4,3,2,1,0:T(8,128)(2,1)S(1)} %pad_maximum_fusion.2), channel_id=1, source_target_pairs={{0,2},{2,0},{4,6},{6,4},{8,10},{10,8},{12,14},{14,12},{16,18},{18,... | collective-permute-start | bytes 1769480 | tf_op jit(solution)/shard_map/ppermute | solution.py:299

commit v4 on v3

--- a/solution.py
+++ b/solution.py
@@ -15,7 +15,7 @@
 WINDOW = 384
 PAD = WINDOW - REACH
 COLUMN_SHIFTS = (-DILATION_RATE, 0, DILATION_RATE)
-VMEM_LIMIT = 24 * 1024 * 1024
+VMEM_LIMIT = 16 * 1024 * 1024
 
 
 def column_mask(start, width, shift):
@@ -53,12 +53,15 @@
 TOP = 30000.0
 
 
-def kernel_grad_kernel(shards, place_ref, own_x, other_x, own_cot, other_cot, _, *refs):
-    outs, sums, peak_ref = refs[:shards], refs[shards], refs[shards + 1]
+def kernel_grad_kernel(depth, place_ref, own_x, other_x, own_cot, other_cot, _, *refs):
+    near, far = refs[:depth], refs[depth : depth + 2]
+    sums, peak_ref = refs[depth + 2 :]
     step = pl.program_id(0)
     rows, width = own_x.shape[0], own_cot.shape[0]
+    shards = 2 * depth
     shard_rows = rows // shards
     tiles = shard_rows // TILE
+    lanes = width // LANES
 
     @pl.when(step == 0)
     def _():
@@ -69,29 +72,28 @@
         @pl.when(step == group)
         def _(group=group):
             where = window(group)
-            for column, shift in enumerate(COLUMN_SHIFTS):
-                total = None
-                for x_ref, cot_ref in ((own_x, own_cot), (other_x, other_cot)):
-                    cot = moved_cotangent(cot_ref[...].astype(jnp.float32), group, shift)
-                    term = lax.dot_general(
-                        x_ref[:, where],
-                        cot,
-                        (((1,), (1,)), ((), ())),
-                        preferred_element_type=jnp.float32,
-                    )
-                    total = term if total is None else total + term
-                peak_ref[...] = jnp.maximum(
-                    peak_ref[...], jnp.max(jnp.abs(total), axis=0, keepdims=True)
+            total = None
+            for x_ref, cot_ref in ((own_x, own_cot), (other_x, other_cot)):
+                cot = cot_ref[...].astype(jnp.float32)
+                cots = [moved_cotangent(cot, group, shift) for shift in COLUMN_SHIFTS]
+                term = lax.dot_general(
+                    x_ref[:, where],
+                    jnp.concatenate(cots, 0),
+                    (((1,), (1,)), ((), ())),
+                    preferred_element_type=jnp.float32,
                 )
-                lanes = width // LANES
+                total = term if total is None else total + term
+            peak_ref[...] = jnp.maximum(
+                peak_ref[...], jnp.max(jnp.abs(total), axis=0, keepdims=True)
+            )
+            for column in range(3):
                 for shard in range(shards):
                     for tile in range(tiles):
                         for lane in range(lanes):
                             row = shard * shard_rows + tile * TILE
+                            first = column * width + lane * LANES
                             slot = ((3 * group + column) * tiles + tile) * lanes + lane
-                            sums[shard, slot] = total[
-                                row : row + TILE, lane * LANES : (lane + 1) * LANES
-                            ]
+                            sums[shard, slot] = total[row : row + TILE, first : first + LANES]
 
     @pl.when(step == 2)
     def _():
@@ -99,34 +101,44 @@
         exponent = jnp.floor(jnp.log2(TOP / jnp.maximum(peak, 1e-30)))
         exponent = jnp.broadcast_to(exponent, (TILE, LANES))
         scale = jnp.exp2(exponent)
-        for distance, out in enumerate(outs):
-            count = sums.shape[1]
+        count = sums.shape[1]
+        for distance in range(shards):
+            if distance < depth:
+                out = near[distance]
+            else:
+                message, slot = divmod(distance - depth, depth // 2)
+                out = far[message].at[slot]
             out[:count] = sums[place_ref[1] ^ distance] * scale
             out[count] = exponent
 
 
-def kernel_grad(place, shards, x, other_x, own_cot, other_cot, after):
+def kernel_grad(place, depth, x, other_x, own_cot, other_cot, after):
     rows, positions = other_x.shape
     outs = own_cot.shape[0]
-    tiles = 9 * rows * outs // (shards * TILE * LANES)
+    tiles = 9 * rows * outs // (2 * depth * TILE * LANES)
     whole = lambda g, h: (0, 0)
+    once = pl.Buffered(1)
+    shapes = [(tiles + 1, TILE, LANES)] * depth + [(depth // 2, tiles + 1, TILE, LANES)] * 2
     return pl.pallas_call(
-        functools.partial(kernel_grad_kernel, shards),
-        out_shape=[jax.ShapeDtypeStruct((tiles + 1, TILE, LANES), jnp.float32)] * shards,
+        functools.partial(kernel_grad_kernel, depth),
+        out_shape=[jax.ShapeDtypeStruct(shape, jnp.float32) for shape in shapes],
         grid_spec=pltpu.PrefetchScalarGridSpec(
             num_scalar_prefetch=1,
             grid=(3,),
             in_specs=[
-                pl.BlockSpec((rows, positions), lambda g, h: (h[0], 0)),
-                pl.BlockSpec((rows, positions), whole),
-                pl.BlockSpec((outs, positions), whole),
-                pl.BlockSpec((outs, positions), whole),
+                pl.BlockSpec((rows, positions), lambda g, h: (h[0], 0), pipeline_mode=once),
+                pl.BlockSpec((rows, positions), whole, pipeline_mode=once),
+                pl.BlockSpec((outs, positions), whole, pipeline_mode=once),
+                pl.BlockSpec((outs, positions), whole, pipeline_mode=once),
                 pl.BlockSpec(memory_space=pl.ANY),
             ],
-            out_specs=[pl.BlockSpec((tiles + 1, TILE, LANES), lambda g, h: (0, 0, 0))] * shards,
+            out_specs=[
+                pl.BlockSpec(shape, functools.partial(lambda n, g, h: (0,) * n, len(shape)))
+                for shape in shapes
+            ],
             scratch_shapes=[
-                pltpu.VMEM((shards, tiles, TILE, LANES), jnp.float32),
-                pltpu.VMEM((1, outs), jnp.float32),
+                pltpu.VMEM((2 * depth, tiles, TILE, LANES), jnp.float32),
+                pltpu.VMEM((1, 3 * outs), jnp.float32),
             ],
         ),
         compiler_params=pltpu.CompilerParams(vmem_limit_bytes=VMEM_LIMIT),
@@ -184,7 +196,7 @@
         out_shape=jax.ShapeDtypeStruct((outs, positions), jnp.float32),
         grid=(3,),
         in_specs=[
-            pl.BlockSpec((rows, positions), lambda g: (0, 0)),
+            pl.BlockSpec((rows, positions), lambda g: (0, 0), pipeline_mode=pl.Buffered(1)),
             pl.BlockSpec((3, rows, outs), lambda g: (g, 0, 0)),
             pl.BlockSpec(memory_space=pl.ANY),
         ],
@@ -266,12 +278,12 @@
     )
 
 
-def summed(values, bits, key):
+def summed(values, bits):
     lowest = common_exponent(values, bits)
-    total = scaled_sum(values, lowest)
-    tile = lax.broadcasted_iota(jnp.int32, total.shape, 0)
-    marked = tile * key >= (total.shape[0] - 1) * key
-    return jnp.where(marked, jnp.broadcast_to(lowest, total.shape), total).astype(jnp.float16)
+    total = scaled_sum(values, lowest).astype(jnp.float16)
+    return lax.dynamic_update_slice(
+        total, lowest.astype(jnp.float16), (total.shape[0] - 1, 0, 0)
+    )
 
 
 def token(value):
@@ -315,26 +327,31 @@
         cot = lax.all_gather(own_cot, "chan", axis=0, tiled=True)
         parts = (cot[:LANES], cot[LANES:])
         first = 0
-    other_cots = [to_core(part) for part in parts]
     other_x = to_core(lax.dynamic_slice_in_dim(x, (1 - core) * core_rows, core_rows, 0))
     where = jnp.stack([core, column * depth + level]).astype(jnp.int32)
     halves, exponents = [], []
     after = own_cot
-    for side, (part, other) in enumerate(zip(parts, other_cots)):
-        shards = kernel_grad(where, 2 * depth, x, other_x, part, other, after)
+    for side in range(2):
+        part = parts[side]
+        if side == 1:
+            part = jnp.where(shards[0][-1, 0, 0] > -1e30, part, jnp.zeros_like(part))
+            their_cot = part
+        shards = kernel_grad(where, depth, x, other_x, part, to_core(part), after)
         held = [None] * depth
-        for step in range(depth - 1, -1, -1):
-            sent = shards[depth + step].astype(jnp.float16)
-            held[step] = [(shards[step], 0.0), (to_column(sent), 0.0)]
+        for message in (1, 0):
+            sent = shards[depth + message].astype(jnp.float16)
+            came = to_column(sent)
+            for slot in range(depth // 2 - 1, -1, -1):
+                step = message * (depth // 2) + slot
+                held[step] = [(shards[step], 0.0), (came[slot], 0.0)]
+        after = sent[0, 0].astype(jnp.float32)
         bits = 1.0
         for bit in [1 << shift for shift in range(depth.bit_length() - 1)]:
             for step in range(depth - bit, 0, -2 * bit):
-                pair = summed(held[step], bits, 2 * step + side)
-                held[step ^ bit].append((to_level(pair, bit), bits))
-                after = token(pair) if step == depth - 1 else after
+                held[step ^ bit].append((to_level(summed(held[step], bits), bit), bits))
             bits += 1.0
         lowest = common_exponent(held[0], bits)
-        halves.append(scaled_sum([(v, b) for v, b in held[0]], lowest)[:-1].astype(jnp.float16))
+        halves.append(scaled_sum(held[0], lowest)[:-1].astype(jnp.float16))
         exponents.append(lowest)
     halves = [jnp.where(first == side, halves[0], halves[1]) for side in range(2)]
     exponents = [jnp.where(first == side, exponents[0], exponents[1]) for side in range(2)]

time: 115 us -> 100 us (0.87)
  other arithmetic: 17.3 us -> 7.91 us
  local copies, waits for them, and re-layouts: 12.5 us -> 6.86 us
  Pallas kernels: 23.6 us -> 19.4 us
  starting transfers between devices: 28.5 us -> 32.5 us
    unnamed x34 -> x12, local copies, waits for them, and re-layouts: 7.77 us -> 2.71 us
    convert_element_type x14 -> x11, other arithmetic: 5.57 us -> 0.65 us  [the longest x6 0.48 us: summed(): total = scaled_sum(values, lowest).astype(jnp.float16)]
    pallas_call x2, Pallas kernels: 12.1 us -> 7.95 us  [kernel_grad(): pl.pallas_call(functools.partial(kernel_grad_kernel, depth), out_shape=[j...]
    ppermute x28 -> x24, starting transfers between devices: 25 us -> 28 us  [to(): lax.ppermute(value, 'dp', [(i, i ^ distance) for i in range(samples)])]
    ge x6 -> x0, other arithmetic: 2.75 us -> none  [summed(): marked = tile * key >= (total.shape[0] - 1) * key]
    dynamic_slice x1, local copies, waits for them, and re-layouts: 2.53 us -> 1.37 us  [on_device(): lax.dynamic_slice_in_dim(x, (1 - core) * core_rows, core_rows, 0)]
    ppermute x28 -> x24, waiting for transfers between devices: 31.1 us -> 31.8 us  [to(): lax.ppermute(value, 'dp', [(i, i ^ distance) for i in range(samples)])]
  transfers between devices with their start and end apart: 30 -> 26, of which waited for: 10 -> 10; matrix products, arithmetic and copies ran while one was open for 12% -> 4% of each run, Pallas kernels for 21% -> 19%
where the time goes in v4:
time: 100 us
  starting transfers between devices  32.5 us (32%)
  waiting for transfers between devices  31.8 us (32%)
  Pallas kernels  19.4 us (19%)
  other arithmetic  7.91 us (8%)
  local copies, waits for them, and re-layouts  6.86 us (7%)
  between operations  1.79 us (2%)
    ppermute x24, waiting for transfers between devices, to(): lax.ppermute(value, 'dp', [(i, i ^ distance) for i in range(samples)])  31.8 us
    ppermute x24, starting transfers between devices, to(): lax.ppermute(value, 'dp', [(i, i ^ distance) for i in range(samples)])  28 us
    pallas_call x2, Pallas kernels, kernel_grad(): pl.pallas_call(functools.partial(kernel_grad_kernel, depth), out_shape=[j...  7.95 us
    pallas_call x1, Pallas kernels, input_gradient(): pl.pallas_call(input_grad_kernel, out_shape=jax.ShapeDtypeStruct((rows, p...  6.54 us
    pallas_call x1, Pallas kernels, forward(): pl.pallas_call(forward_kernel, out_shape=jax.ShapeDtypeStruct((outs, posi...  4.9 us
    reshape x1, other arithmetic, on_device(): weight_grad = jnp.transpose(grad, (1, 3, 0, 2, 4)).reshape(rows, taps, outs)  4.64 us
    ppermute x1, starting transfers between devices, on_device(): their_cot = lax.ppermute(own_cot, 'chan', [(0, 1), (1, 0)])  2.95 us
    unnamed x12, local copies, waits for them, and re-layouts  2.71 us
  transfers between devices with their start and end apart: 26, of which 10 were waited for; matrix products, arithmetic and copies ran while one was open for 4% of the time, Pallas kernels for 19%

profile of v4, /device:TPU:0, one launch (start us, length us, event | category | flops | bytes accessed | tf_op | source)
XLA Modules:
  0.0 100.3 jit_solution(7716168992264707665)
XLA Ops:
  0.7 1.4 %dynamic-slice_bitcast_fusion = bf16[512,1152]{1,0:T(8,128)(2,1)S(1)} fusion(bf16[1,1024,1152]{2,1,0:T(8,128)(2,1)} %param.3, s32[]{:T(128)S(6)} %select_n.138), kind=kLoop, calls=%fused_computation.2 | loop fusion | bytes 2359300 | tf_op jit(solution)/shard_map/dynamic_slice | solution.py:330
  2.0 0.5 collective-permute-start
  2.6 2.9 %collective-permute-start.7 = (bf16[128,1152]{1,0:T(8,128)(2,1)}, bf16[128,1152]{1,0:T(8,128)(2,1)S(1)}, u32[]{:S(2)}, u32[]{:S(2)}) collective-permute-start(bf16[128,1152]{1,0:T(8,128)(2,1)} %bitcast.232), channel_id=1, source_target_pairs={{0,1},{1,0},{2,3},{3,2},{4,5},{5,4},{6,7},{7,6},{8,9},{9,8},{10,11... | collective-permute-start | bytes 884744 | tf_op jit(solution)/shard_map/ppermute | solution.py:323
  5.6 1.7 %copy-done = bf16[1,1024,1152]{2,1,0:T(8,128)(2,1)S(1)} copy-done((bf16[1,1024,1152]{2,1,0:T(8,128)(2,1)S(1)}, bf16[1,1024,1152]{2,1,0:T(8,128)(2,1)}, u32[]{:S(2)}) %copy-start) | copy-done | bytes 2359320
  7.3 1.0 copy-done.2
  8.3 4.0 %kernel_grad.2 = (f32[73,8,128]{2,1,0:T(8,128)S(1)}, f32[73,8,128]{2,1,0:T(8,128)S(1)}, f32[73,8,128]{2,1,0:T(8,128)S(1)}, f32[73,8,128]{2,1,0:T(8,128)S(1)}, f3...) custom-call(s32[2]{0:T(128)S(1)} %pad_add_fusion.place_ref, bf16[1024,1152]{1,0:T(8,128)(2,1)S(1)} %bitcast.228, ...), custom_call_target="tpu_custom_call" | custom-call | flops 1509949440 | bytes 5308416 | tf_op jit(solution)/shard_map/kernel_grad/pallas_call | solution.py:122
  12.3 2.7 %collective-permute-start.2 = (f16[2,73,8,128]{3,2,1,0:T(8,128)(2,1)S(1)}, f16[2,73,8,128]{3,2,1,0:T(8,128)(2,1)S(1)}, u32[]{:S(2)}, u32[]{:S(2)}) collective-permute-start(f16[2,73,8,128]{3,2,1,0:T(8,128)(2,1)S(1)} %convert_element_type.284), channel_id=1, source_target_pairs={{0,4},{2,6},{4,0},{6,2},{8,12},{10,14},{12,8},{14,10},{16,20},{18,... | collective-permute-start | bytes 897032 | tf_op jit(solution)/shard_map/ppermute | solution.py:311
  15.2 0.5 slice.207
  16.4 0.1 maximum_select_fusion.cot_ref
  16.6 1.4 %collective-permute-done.8.other_cot = bf16[128,1152]{1,0:T(8,128)(2,1)S(1)} collective-permute-done((bf16[128,1152]{1,0:T(8,128)(2,1)S(1)}, bf16[128,1152]{1,0:T(8,128)(2,1)S(1)}, u32[]{:S(2)}, u32[]{:S(2)}) %collective-permute-start.8) | collective-permute-done | bytes 294944 | tf_op jit(solution)/shard_map/ppermute | solution.py:311
  18.0 4.0 %kernel_grad.3 = (f32[73,8,128]{2,1,0:T(8,128)S(1)}, f32[73,8,128]{2,1,0:T(8,128)S(1)}, f32[73,8,128]{2,1,0:T(8,128)S(1)}, f32[73,8,128]{2,1,0:T(8,128)S(1)}, f3...) custom-call(s32[2]{0:T(128)S(1)} %pad_add_fusion.place_ref, bf16[1024,1152]{1,0:T(8,128)(2,1)S(1)} %bitcast.229, ...), custom_call_target="tpu_custom_call" | custom-call | flops 1509949440 | bytes 5308416 | tf_op jit(solution)/shard_map/kernel_grad/pallas_call | solution.py:122
  22.1 2.1 %collective-permute-start.9 = (f16[2,73,8,128]{3,2,1,0:T(8,128)(2,1)S(1)}, f16[2,73,8,128]{3,2,1,0:T(8,128)(2,1)S(1)}, u32[]{:S(2)}, u32[]{:S(2)}) collective-permute-start(f16[2,73,8,128]{3,2,1,0:T(8,128)(2,1)S(1)} %convert_element_type.316), channel_id=1, source_target_pairs={{0,4},{2,6},{4,0},{6,2},{8,12},{10,14},{12,8},{14,10},{16,20},{18,... | collective-permute-start | bytes 897032 | tf_op jit(solution)/shard_map/ppermute | solution.py:311
  24.4 2.2 %collective-permute-start.3 = (f16[73,8,128]{2,1,0:T(8,128)(2,1)S(1)}, f16[73,8,128]{2,1,0:T(8,128)(2,1)S(1)}, u32[]{:S(2)}, u32[]{:S(2)}) collective-permute-start(f16[73,8,128]{2,1,0:T(8,128)(2,1)S(1)} %constant_dynamic-update-slice_fusion.13), channel_id=1, source_target_pairs={{0,8},{2,10},{4,12},{6,14},{8,0},{10,2},{12,4},{14,6},{16,24},{18,... | collective-permute-start | bytes 448520 | tf_op jit(solution)/shard_map/ppermute | solution.py:311
  26.5 2.8 %collective-permute-done.4 = f16[2,73,8,128]{3,2,1,0:T(8,128)(2,1)S(1)} collective-permute-done((f16[2,73,8,128]{3,2,1,0:T(8,128)(2,1)S(1)}, f16[2,73,8,128]{3,2,1,0:T(8,128)(2,1)S(1)}, u32[]{:S(2)}, u32[]{:S(2)}) %collective-permute-start.4) | collective-permute-done | bytes 299040 | tf_op jit(solution)/shard_map/ppermute | solution.py:311
  29.4 2.2 %collective-permute-start.5 = (f16[73,8,128]{2,1,0:T(8,128)(2,1)S(1)}, f16[73,8,128]{2,1,0:T(8,128)(2,1)S(1)}, u32[]{:S(2)}, u32[]{:S(2)}) collective-permute-start(f16[73,8,128]{2,1,0:T(8,128)(2,1)S(1)} %constant_dynamic-update-slice_fusion.12), channel_id=1, source_target_pairs={{0,8},{2,10},{4,12},{6,14},{8,0},{10,2},{12,4},{14,6},{16,24},{18,... | collective-permute-start | bytes 448520 | tf_op jit(solution)/shard_map/ppermute | solution.py:311
  31.7 3.1 %collective-permute-done.5 = f16[73,8,128]{2,1,0:T(8,128)(2,1)S(1)} collective-permute-done((f16[73,8,128]{2,1,0:T(8,128)(2,1)S(1)}, f16[73,8,128]{2,1,0:T(8,128)(2,1)S(1)}, u32[]{:S(2)}, u32[]{:S(2)}) %collective-permute-start.5) | collective-permute-done | bytes 149536 | tf_op jit(solution)/shard_map/ppermute | solution.py:311
  34.8 0.1 fusion.9
  34.9 3.1 %collective-permute-start.6 = (f16[73,8,128]{2,1,0:T(8,128)(2,1)S(1)}, f16[73,8,128]{2,1,0:T(8,128)(2,1)S(1)}, u32[]{:S(2)}, u32[]{:S(2)}) collective-permute-start(f16[73,8,128]{2,1,0:T(8,128)(2,1)S(1)} %constant_dynamic-update-slice_fusion.11), channel_id=1, source_target_pairs={{0,16},{2,18},{4,20},{6,22},{8,24},{10,26},{12,28},{14,30},{16,0},... | collective-permute-start | bytes 448520 | tf_op jit(solution)/shard_map/ppermute | solution.py:311
  38.0 3.7 %collective-permute-done.11 = f16[2,73,8,128]{3,2,1,0:T(8,128)(2,1)S(1)} collective-permute-done((f16[2,73,8,128]{3,2,1,0:T(8,128)(2,1)S(1)}, f16[2,73,8,128]{3,2,1,0:T(8,128)(2,1)S(1)}, u32[]{:S(2)}, u32[]{:S(2)}) %collective-permute-start.11) | collective-permute-done | bytes 299040 | tf_op jit(solution)/shard_map/ppermute | solution.py:311
  41.8 1.9 %collective-permute-start.12 = (f16[73,8,128]{2,1,0:T(8,128)(2,1)S(1)}, f16[73,8,128]{2,1,0:T(8,128)(2,1)S(1)}, u32[]{:S(2)}, u32[]{:S(2)}) collective-permute-start(f16[73,8,128]{2,1,0:T(8,128)(2,1)S(1)} %constant_dynamic-update-slice_fusion.9), channel_id=1, source_target_pairs={{0,8},{2,10},{4,12},{6,14},{8,0},{10,2},{12,4},{14,6},{16,24},{18,... | collective-permute-start | bytes 448520 | tf_op jit(solution)/shard_map/ppermute | solution.py:311
  43.8 0.3 collective-permute-start.10
  44.1 4.6 %collective-permute-done.12 = f16[73,8,128]{2,1,0:T(8,128)(2,1)S(1)} collective-permute-done((f16[73,8,128]{2,1,0:T(8,128)(2,1)S(1)}, f16[73,8,128]{2,1,0:T(8,128)(2,1)S(1)}, u32[]{:S(2)}, u32[]{:S(2)}) %collective-permute-start.12) | collective-permute-done | bytes 149536 | tf_op jit(solution)/shard_map/ppermute | solution.py:311
  48.7 0.1 fusion.2
  48.9 2.9 %collective-permute-start.13 = (f16[73,8,128]{2,1,0:T(8,128)(2,1)S(1)}, f16[73,8,128]{2,1,0:T(8,128)(2,1)S(1)}, u32[]{:S(2)}, u32[]{:S(2)}) collective-permute-start(f16[73,8,128]{2,1,0:T(8,128)(2,1)S(1)} %constant_dynamic-update-slice_fusion.8), channel_id=1, source_target_pairs={{0,16},{2,18},{4,20},{6,22},{8,24},{10,26},{12,28},{14,30},{16,0},... | collective-permute-start | bytes 448520 | tf_op jit(solution)/shard_map/ppermute | solution.py:311
  51.9 0.4 collective-permute-done.10
  52.2 4.8 %collective-permute-done.13 = f16[73,8,128]{2,1,0:T(8,128)(2,1)S(1)} collective-permute-done((f16[73,8,128]{2,1,0:T(8,128)(2,1)S(1)}, f16[73,8,128]{2,1,0:T(8,128)(2,1)S(1)}, u32[]{:S(2)}, u32[]{:S(2)}) %collective-permute-start.13) | collective-permute-done | bytes 149536 | tf_op jit(solution)/shard_map/ppermute | solution.py:311
  57.0 0.3 broadcast_select_fusion.1
  57.4 0.7 broadcast_in_dim.17
  58.1 0.2 fusion.116
  58.3 1.0 %collective-permute-start.15 = (f16[9,8,2,8,128]{4,3,2,1,0:T(8,128)(2,1)S(1)}, f16[9,8,2,8,128]{4,3,2,1,0:T(8,128)(2,1)S(1)}, u32[]{:S(2)}, u32[]{:S(2)}) collective-permute-start(f16[9,8,2,8,128]{4,3,2,1,0:T(8,128)(2,1)S(1)} %get-tuple-element.47), channel_id=1, source_target_pairs={{0,16},{2,18},{4,20},{6,22},{8,24},{10,26},{12,28},{14,30},{16,0},... | collective-permute-start | bytes 884744 | tf_op jit(solution)/shard_map/ppermute | solution.py:311
  59.4 3.0 %collective-permute-start.16 = (f16[9,8,2,8,128]{4,3,2,1,0:T(8,128)(2,1)S(1)}, f16[9,8,2,8,128]{4,3,2,1,0:T(8,128)(2,1)S(1)}, u32[]{:S(2)}, u32[]{:S(2)}) collective-permute-start(f16[9,8,2,8,128]{4,3,2,1,0:T(8,128)(2,1)S(1)} %get-tuple-element.47), channel_id=1, source_target_pairs={{0,8},{2,10},{4,12},{6,14},{8,0},{10,2},{12,4},{14,6},{16,24},{18,... | collective-permute-start | bytes 884744 | tf_op jit(solution)/shard_map/ppermute | solution.py:311
  62.3 1.5 %collective-permute-start.19 = (f16[9,8,2,8,128]{4,3,2,1,0:T(8,128)(2,1)S(1)}, f16[9,8,2,8,128]{4,3,2,1,0:T(8,128)(2,1)S(1)}, u32[]{:S(2)}, u32[]{:S(2)}) collective-permute-start(f16[9,8,2,8,128]{4,3,2,1,0:T(8,128)(2,1)S(1)} %get-tuple-element.47), channel_id=1, source_target_pairs={{0,4},{2,6},{4,0},{6,2},{8,12},{10,14},{12,8},{14,10},{16,20},{18,... | collective-permute-start | bytes 884744 | tf_op jit(solution)/shard_map/ppermute | solution.py:311
  63.8 4.9 %forward.1 = f32[256,1152]{1,0:T(8,128)S(1)} custom-call(bf16[1024,1152]{1,0:T(8,128)(2,1)S(1)} %bitcast.230, bf16[9,1024,256]{2,1,0:T(8,128)(2,1)S(1)} %bitcast.238, f32[8,128]{1,0:T(8,128)S(1)} %fusion.112._), custom_call_target="tpu_custom_call" | custom-call | flops 3019898880 | bytes 8257536 | tf_op jit(solution)/shard_map/forward/pallas_call | solution.py:194
  68.8 1.6 %collective-permute-start.14 = (f32[128,1152]{1,0:T(8,128)S(1)}, f32[128,1152]{1,0:T(8,128)S(1)}, u32[]{:S(2)}, u32[]{:S(2)}) collective-permute-start(f32[128,1152]{1,0:T(8,128)S(1)} %constant_dynamic-slice_fusion), channel_id=1, source_target_pairs={{0,1},{1,0},{2,3},{3,2},{4,5},{5,4},{6,7},{7,6},{8,9},{9,8},{10,11... | collective-permute-start | bytes 1769480 | tf_op jit(solution)/shard_map/ppermute | solution.py:386
  70.4 1.4 %collective-permute-start.22 = (f16[9,8,2,8,128]{4,3,2,1,0:T(8,128)(2,1)S(1)}, f16[9,8,2,8,128]{4,3,2,1,0:T(8,128)(2,1)S(1)}, u32[]{:S(2)}, u32[]{:S(2)}) collective-permute-start(f16[9,8,2,8,128]{4,3,2,1,0:T(8,128)(2,1)S(1)} %collective-permute-done.15), channel_id=1, source_target_pairs={{0,4},{2,6},{4,0},{6,2},{8,12},{10,14},{12,8},{14,10},{16,20},{18,... | collective-permute-start | bytes 884744 | tf_op jit(solution)/shard_map/ppermute | solution.py:311
  71.8 0.7 collective-permute-start.20
  72.4 6.5 %input_gradient.1 = bf16[1024,1152]{1,0:T(8,128)(2,1)} custom-call(bf16[256,1152]{1,0:T(8,128)(2,1)S(1)} %maximum_select_fusion.cot_ref, bf16[9,1024,256]{2,1,0:T(8,128)(2,1)S(1)} %bitcast.239, f32[8,128]{1,0:T(8,128)S(1)} %fusion.111._), custom_call_target="tpu_custom_call" | custom-call | flops 3019898880 | bytes 7667712 | tf_op jit(solution)/shard_map/input_gradient/pallas_call | solution.py:242
  79.0 0.5 pad_maximum_fusion
  79.6 0.5 collective-permute-start.25
  80.1 3.2 %collective-permute-done.20 = f16[9,8,2,8,128]{4,3,2,1,0:T(8,128)(2,1)S(1)} collective-permute-done((f16[9,8,2,8,128]{4,3,2,1,0:T(8,128)(2,1)S(1)}, f16[9,8,2,8,128]{4,3,2,1,0:T(8,128)(2,1)S(1)}, u32[]{:S(2)}, u32[]{:S(2)}) %collective-permute-start.20) | collective-permute-done | bytes 294944 | tf_op jit(solution)/shard_map/ppermute | solution.py:311
  83.3 0.2 pad_maximum_fusion.1
  83.6 1.6 %collective-permute-start.23 = (f16[9,8,2,8,128]{4,3,2,1,0:T(8,128)(2,1)S(1)}, f16[9,8,2,8,128]{4,3,2,1,0:T(8,128)(2,1)S(1)}, u32[]{:S(2)}, u32[]{:S(2)}) collective-permute-start(f16[9,8,2,8,128]{4,3,2,1,0:T(8,128)(2,1)S(1)} %collective-permute-done.17), channel_id=1, source_target_pairs={{0,4},{2,6},{4,0},{6,2},{8,12},{10,14},{12,8},{14,10},{16,20},{18,... | collective-permute-start | bytes 884744 | tf_op jit(solution)/shard_map/ppermute | solution.py:311
  85.1 0.8 fusion.14
  86.0 7.0 %collective-permute-done.23 = f16[9,8,2,8,128]{4,3,2,1,0:T(8,128)(2,1)S(1)} collective-permute-done((f16[9,8,2,8,128]{4,3,2,1,0:T(8,128)(2,1)S(1)}, f16[9,8,2,8,128]{4,3,2,1,0:T(8,128)(2,1)S(1)}, u32[]{:S(2)}, u32[]{:S(2)}) %collective-permute-start.23) | collective-permute-done | bytes 294944 | tf_op jit(solution)/shard_map/ppermute | solution.py:311
  93.0 0.2 pad_maximum_fusion.2
  93.4 0.1 constant_dynamic-update-slice_fusion.6
  94.5 0.7 collective-permute-done.24
  95.6 4.6 %multiply_bitcast_fusion = f32[1024,9,256]{2,0,1:T(8,128)} fusion(f16[9,128,2,8,128]{4,3,2,1,0:T(8,128)(2,1)S(1)} %fusion.15, f32[128,2,8,128]{3,2,1,0:T(8,128)S(1)} %bitcast.240), kind=kLoop, calls=%fused_computation | loop fusion | flops 4718592 | bytes 15204352 | tf_op jit(solution)/shard_map/reshape | solution.py:380
  (85 shorter events, 2.9 us)
Async XLA Ops:
  2.0 3.6 %collective-permute-start = (bf16[512,1152]{1,0:T(8,128)(2,1)S(1)}, bf16[512,1152]{1,0:T(8,128)(2,1)S(1)}, u32[]{:S(2)}, u32[]{:S(2)}) collective-permute-start(bf16[512,1152]{1,0:T(8,128)(2,1)S(1)} %dynamic-slice_bitcast_fusion), channel_id=1, source_target_pairs={{0,2},{2,0},{4,6},{6,4},{8,10},{10,8},{12,14},{14,12},{16,18},{18,... | collective-permute-start | bytes 3538952 | tf_op jit(solution)/shard_map/ppermute | solution.py:311
  2.5 3.1 %collective-permute-start.1 = (bf16[128,1152]{1,0:T(8,128)(2,1)}, bf16[128,1152]{1,0:T(8,128)(2,1)S(1)}, u32[]{:S(2)}, u32[]{:S(2)}) collective-permute-start(bf16[128,1152]{1,0:T(8,128)(2,1)} %bitcast.231), channel_id=1, source_target_pairs={{0,2},{2,0},{4,6},{6,4},{8,10},{10,8},{12,14},{14,12},{16,18},{18,... | collective-permute-start | bytes 884744 | tf_op jit(solution)/shard_map/ppermute | solution.py:311
  2.6 13.7 %collective-permute-start.7 = (bf16[128,1152]{1,0:T(8,128)(2,1)}, bf16[128,1152]{1,0:T(8,128)(2,1)S(1)}, u32[]{:S(2)}, u32[]{:S(2)}) collective-permute-start(bf16[128,1152]{1,0:T(8,128)(2,1)} %bitcast.232), channel_id=1, source_target_pairs={{0,1},{1,0},{2,3},{3,2},{4,5},{5,4},{6,7},{7,6},{8,9},{9,8},{10,11... | collective-permute-start | bytes 884744 | tf_op jit(solution)/shard_map/ppermute | solution.py:323
  5.6 1.7 %copy-start = (bf16[1,1024,1152]{2,1,0:T(8,128)(2,1)S(1)}, bf16[1,1024,1152]{2,1,0:T(8,128)(2,1)}, u32[]{:S(2)}) copy-start(bf16[1,1024,1152]{2,1,0:T(8,128)(2,1)} %param.3) | copy-start | bytes 7077892
  7.3 1.0 copy-start.2
  12.3 12.0 %collective-permute-start.2 = (f16[2,73,8,128]{3,2,1,0:T(8,128)(2,1)S(1)}, f16[2,73,8,128]{3,2,1,0:T(8,128)(2,1)S(1)}, u32[]{:S(2)}, u32[]{:S(2)}) collective-permute-start(f16[2,73,8,128]{3,2,1,0:T(8,128)(2,1)S(1)} %convert_element_type.284), channel_id=1, source_target_pairs={{0,4},{2,6},{4,0},{6,2},{8,12},{10,14},{12,8},{14,10},{16,20},{18,... | collective-permute-start | bytes 897032 | tf_op jit(solution)/shard_map/ppermute | solution.py:311
  15.1 14.2 %collective-permute-start.4 = (f16[2,73,8,128]{3,2,1,0:T(8,128)(2,1)S(1)}, f16[2,73,8,128]{3,2,1,0:T(8,128)(2,1)S(1)}, u32[]{:S(2)}, u32[]{:S(2)}) collective-permute-start(f16[2,73,8,128]{3,2,1,0:T(8,128)(2,1)S(1)} %convert_element_type.294), channel_id=1, source_target_pairs={{0,4},{2,6},{4,0},{6,2},{8,12},{10,14},{12,8},{14,10},{16,20},{18,... | collective-permute-start | bytes 897032 | tf_op jit(solution)/shard_map/ppermute | solution.py:311
  16.4 1.6 %collective-permute-start.8 = (bf16[128,1152]{1,0:T(8,128)(2,1)S(1)}, bf16[128,1152]{1,0:T(8,128)(2,1)S(1)}, u32[]{:S(2)}, u32[]{:S(2)}) collective-permute-start(bf16[128,1152]{1,0:T(8,128)(2,1)S(1)} %broadcast_select_fusion.own_cot), channel_id=1, source_target_pairs={{0,2},{2,0},{4,6},{6,4},{8,10},{10,8},{12,14},{14,12},{16,18},{18,... | collective-permute-start | bytes 884744 | tf_op jit(solution)/shard_map/ppermute | solution.py:311
  18.0 45.8 %slice-start = ((s8[4718592]{0:T(1024)(128)(4,1)}), s8[4194304]{0:T(1024)(128)(4,1)S(1)}, s32[]{:S(2)}) async-start(s8[4718592]{0:T(1024)(128)(4,1)} %bitcast.236), calls=%async_computation | async-start | bytes 8388608
  22.1 21.7 %collective-permute-start.9 = (f16[2,73,8,128]{3,2,1,0:T(8,128)(2,1)S(1)}, f16[2,73,8,128]{3,2,1,0:T(8,128)(2,1)S(1)}, u32[]{:S(2)}, u32[]{:S(2)}) collective-permute-start(f16[2,73,8,128]{3,2,1,0:T(8,128)(2,1)S(1)} %convert_element_type.316), channel_id=1, source_target_pairs={{0,4},{2,6},{4,0},{6,2},{8,12},{10,14},{12,8},{14,10},{16,20},{18,... | collective-permute-start | bytes 897032 | tf_op jit(solution)/shard_map/ppermute | solution.py:311
  24.2 17.6 %collective-permute-start.11 = (f16[2,73,8,128]{3,2,1,0:T(8,128)(2,1)S(1)}, f16[2,73,8,128]{3,2,1,0:T(8,128)(2,1)S(1)}, u32[]{:S(2)}, u32[]{:S(2)}) collective-permute-start(f16[2,73,8,128]{3,2,1,0:T(8,128)(2,1)S(1)} %convert_element_type.326), channel_id=1, source_target_pairs={{0,4},{2,6},{4,0},{6,2},{8,12},{10,14},{12,8},{14,10},{16,20},{18,... | collective-permute-start | bytes 897032 | tf_op jit(solution)/shard_map/ppermute | solution.py:311
  24.4 27.5 %collective-permute-start.3 = (f16[73,8,128]{2,1,0:T(8,128)(2,1)S(1)}, f16[73,8,128]{2,1,0:T(8,128)(2,1)S(1)}, u32[]{:S(2)}, u32[]{:S(2)}) collective-permute-start(f16[73,8,128]{2,1,0:T(8,128)(2,1)S(1)} %constant_dynamic-update-slice_fusion.13), channel_id=1, source_target_pairs={{0,8},{2,10},{4,12},{6,14},{8,0},{10,2},{12,4},{14,6},{16,24},{18,... | collective-permute-start | bytes 448520 | tf_op jit(solution)/shard_map/ppermute | solution.py:311
  29.4 5.4 %collective-permute-start.5 = (f16[73,8,128]{2,1,0:T(8,128)(2,1)S(1)}, f16[73,8,128]{2,1,0:T(8,128)(2,1)S(1)}, u32[]{:S(2)}, u32[]{:S(2)}) collective-permute-start(f16[73,8,128]{2,1,0:T(8,128)(2,1)S(1)} %constant_dynamic-update-slice_fusion.12), channel_id=1, source_target_pairs={{0,8},{2,10},{4,12},{6,14},{8,0},{10,2},{12,4},{14,6},{16,24},{18,... | collective-permute-start | bytes 448520 | tf_op jit(solution)/shard_map/ppermute | solution.py:311
  34.9 16.9 %collective-permute-start.6 = (f16[73,8,128]{2,1,0:T(8,128)(2,1)S(1)}, f16[73,8,128]{2,1,0:T(8,128)(2,1)S(1)}, u32[]{:S(2)}, u32[]{:S(2)}) collective-permute-start(f16[73,8,128]{2,1,0:T(8,128)(2,1)S(1)} %constant_dynamic-update-slice_fusion.11), channel_id=1, source_target_pairs={{0,16},{2,18},{4,20},{6,22},{8,24},{10,26},{12,28},{14,30},{16,0},... | collective-permute-start | bytes 448520 | tf_op jit(solution)/shard_map/ppermute | solution.py:311
  41.7 22.1 %slice-start.1 = ((s8[4718592]{0:T(1024)(128)(4,1)}), s8[524288]{0:T(1024)(128)(4,1)S(1)}, s32[]{:S(2)}) async-start(s8[4718592]{0:T(1024)(128)(4,1)} %bitcast.236), calls=%async_computation.1 | async-start | bytes 1048576
  41.8 6.9 %collective-permute-start.12 = (f16[73,8,128]{2,1,0:T(8,128)(2,1)S(1)}, f16[73,8,128]{2,1,0:T(8,128)(2,1)S(1)}, u32[]{:S(2)}, u32[]{:S(2)}) collective-permute-start(f16[73,8,128]{2,1,0:T(8,128)(2,1)S(1)} %constant_dynamic-update-slice_fusion.9), channel_id=1, source_target_pairs={{0,8},{2,10},{4,12},{6,14},{8,0},{10,2},{12,4},{14,6},{16,24},{18,... | collective-permute-start | bytes 448520 | tf_op jit(solution)/shard_map/ppermute | solution.py:311
  43.8 8.4 %collective-permute-start.10 = (f16[73,8,128]{2,1,0:T(8,128)(2,1)S(1)}, f16[73,8,128]{2,1,0:T(8,128)(2,1)S(1)}, u32[]{:S(2)}, u32[]{:S(2)}) collective-permute-start(f16[73,8,128]{2,1,0:T(8,128)(2,1)S(1)} %constant_dynamic-update-slice_fusion.10), channel_id=1, source_target_pairs={{0,8},{2,10},{4,12},{6,14},{8,0},{10,2},{12,4},{14,6},{16,24},{18,... | collective-permute-start | bytes 448520 | tf_op jit(solution)/shard_map/ppermute | solution.py:311
  48.7 15.1 %copy-start.1 = (bf16[1,1024,1152]{2,1,0:T(8,128)(2,1)S(1)}, bf16[1,1024,1152]{2,1,0:T(8,128)(2,1)}, u32[]{:S(2)}) copy-start(bf16[1,1024,1152]{2,1,0:T(8,128)(2,1)} %param.3) | copy-start | bytes 7077892
  48.9 8.1 %collective-permute-start.13 = (f16[73,8,128]{2,1,0:T(8,128)(2,1)S(1)}, f16[73,8,128]{2,1,0:T(8,128)(2,1)S(1)}, u32[]{:S(2)}, u32[]{:S(2)}) collective-permute-start(f16[73,8,128]{2,1,0:T(8,128)(2,1)S(1)} %constant_dynamic-update-slice_fusion.8), channel_id=1, source_target_pairs={{0,16},{2,18},{4,20},{6,22},{8,24},{10,26},{12,28},{14,30},{16,0},... | collective-permute-start | bytes 448520 | tf_op jit(solution)/shard_map/ppermute | solution.py:311
  58.3 12.1 %collective-permute-start.15 = (f16[9,8,2,8,128]{4,3,2,1,0:T(8,128)(2,1)S(1)}, f16[9,8,2,8,128]{4,3,2,1,0:T(8,128)(2,1)S(1)}, u32[]{:S(2)}, u32[]{:S(2)}) collective-permute-start(f16[9,8,2,8,128]{4,3,2,1,0:T(8,128)(2,1)S(1)} %get-tuple-element.47), channel_id=1, source_target_pairs={{0,16},{2,18},{4,20},{6,22},{8,24},{10,26},{12,28},{14,30},{16,0},... | collective-permute-start | bytes 884744 | tf_op jit(solution)/shard_map/ppermute | solution.py:311
  59.4 12.4 %collective-permute-start.16 = (f16[9,8,2,8,128]{4,3,2,1,0:T(8,128)(2,1)S(1)}, f16[9,8,2,8,128]{4,3,2,1,0:T(8,128)(2,1)S(1)}, u32[]{:S(2)}, u32[]{:S(2)}) collective-permute-start(f16[9,8,2,8,128]{4,3,2,1,0:T(8,128)(2,1)S(1)} %get-tuple-element.47), channel_id=1, source_target_pairs={{0,8},{2,10},{4,12},{6,14},{8,0},{10,2},{12,4},{14,6},{16,24},{18,... | collective-permute-start | bytes 884744 | tf_op jit(solution)/shard_map/ppermute | solution.py:311
  62.3 17.2 %collective-permute-start.19 = (f16[9,8,2,8,128]{4,3,2,1,0:T(8,128)(2,1)S(1)}, f16[9,8,2,8,128]{4,3,2,1,0:T(8,128)(2,1)S(1)}, u32[]{:S(2)}, u32[]{:S(2)}) collective-permute-start(f16[9,8,2,8,128]{4,3,2,1,0:T(8,128)(2,1)S(1)} %get-tuple-element.47), channel_id=1, source_target_pairs={{0,4},{2,6},{4,0},{6,2},{8,12},{10,14},{12,8},{14,10},{16,20},{18,... | collective-permute-start | bytes 884744 | tf_op jit(solution)/shard_map/ppermute | solution.py:311
  68.8 14.7 %collective-permute-start.14 = (f32[128,1152]{1,0:T(8,128)S(1)}, f32[128,1152]{1,0:T(8,128)S(1)}, u32[]{:S(2)}, u32[]{:S(2)}) collective-permute-start(f32[128,1152]{1,0:T(8,128)S(1)} %constant_dynamic-slice_fusion), channel_id=1, source_target_pairs={{0,1},{1,0},{2,3},{3,2},{4,5},{5,4},{6,7},{7,6},{8,9},{9,8},{10,11... | collective-permute-start | bytes 1769480 | tf_op jit(solution)/shard_map/ppermute | solution.py:386
  70.4 8.6 %collective-permute-start.17 = (f16[9,8,2,8,128]{4,3,2,1,0:T(8,128)(2,1)S(1)}, f16[9,8,2,8,128]{4,3,2,1,0:T(8,128)(2,1)S(1)}, u32[]{:S(2)}, u32[]{:S(2)}) collective-permute-start(f16[9,8,2,8,128]{4,3,2,1,0:T(8,128)(2,1)S(1)} %collective-permute-done.15), channel_id=1, source_target_pairs={{0,8},{2,10},{4,12},{6,14},{8,0},{10,2},{12,4},{14,6},{16,24},{18,... | collective-permute-start | bytes 884744 | tf_op jit(solution)/shard_map/ppermute | solution.py:311
  70.4 15.6 %collective-permute-start.22 = (f16[9,8,2,8,128]{4,3,2,1,0:T(8,128)(2,1)S(1)}, f16[9,8,2,8,128]{4,3,2,1,0:T(8,128)(2,1)S(1)}, u32[]{:S(2)}, u32[]{:S(2)}) collective-permute-start(f16[9,8,2,8,128]{4,3,2,1,0:T(8,128)(2,1)S(1)} %collective-permute-done.15), channel_id=1, source_target_pairs={{0,4},{2,6},{4,0},{6,2},{8,12},{10,14},{12,8},{14,10},{16,20},{18,... | collective-permute-start | bytes 884744 | tf_op jit(solution)/shard_map/ppermute | solution.py:311
  71.8 11.5 %collective-permute-start.20 = (f16[9,8,2,8,128]{4,3,2,1,0:T(8,128)(2,1)S(1)}, f16[9,8,2,8,128]{4,3,2,1,0:T(8,128)(2,1)S(1)}, u32[]{:S(2)}, u32[]{:S(2)}) collective-permute-start(f16[9,8,2,8,128]{4,3,2,1,0:T(8,128)(2,1)S(1)} %collective-permute-done.16), channel_id=1, source_target_pairs={{0,4},{2,6},{4,0},{6,2},{8,12},{10,14},{12,8},{14,10},{16,20},{18,... | collective-permute-start | bytes 884744 | tf_op jit(solution)/shard_map/ppermute | solution.py:311
  79.4 13.8 %collective-permute-start.18 = (f16[4,9,8,2,8,128]{5,4,3,2,1,0:T(8,128)(2,1)S(1)}, f16[4,9,8,2,8,128]{5,4,3,2,1,0:T(8,128)(2,1)S(1)}, u32[]{:S(2)}, u32[]{:S(2)}) collective-permute-start(f16[4,9,8,2,8,128]{5,4,3,2,1,0:T(8,128)(2,1)S(1)} %pad_maximum_fusion), channel_id=1, source_target_pairs={{0,2},{2,0},{4,6},{6,4},{8,10},{10,8},{12,14},{14,12},{16,18},{18,... | collective-permute-start | bytes 3538952 | tf_op jit(solution)/shard_map/ppermute | solution.py:311
  79.6 6.4 %collective-permute-start.25 = (f32[2,8,128]{2,1,0:T(8,128)S(1)}, f32[2,8,128]{2,1,0:T(8,128)S(1)}, u32[]{:S(2)}, u32[]{:S(2)}) collective-permute-start(f32[2,8,128]{2,1,0:T(8,128)S(1)} %fusion.34), channel_id=1, source_target_pairs={{0,2},{2,0},{4,6},{6,4},{8,10},{10,8},{12,14},{14,12},{16,18},{18,... | collective-permute-start | bytes 24584 | tf_op jit(solution)/shard_map/ppermute | solution.py:311
  83.5 10.6 %collective-permute-start.21 = (f16[2,9,8,2,8,128]{5,4,3,2,1,0:T(8,128)(2,1)S(1)}, f16[2,9,8,2,8,128]{5,4,3,2,1,0:T(8,128)(2,1)S(1)}, u32[]{:S(2)}, u32[]{:S(2)}) collective-permute-start(f16[2,9,8,2,8,128]{5,4,3,2,1,0:T(8,128)(2,1)S(1)} %pad_maximum_fusion.1), channel_id=1, source_target_pairs={{0,2},{2,0},{4,6},{6,4},{8,10},{10,8},{12,14},{14,12},{16,18},{18,... | collective-permute-start | bytes 1769480 | tf_op jit(solution)/shard_map/ppermute | solution.py:311
  83.6 9.4 %collective-permute-start.23 = (f16[9,8,2,8,128]{4,3,2,1,0:T(8,128)(2,1)S(1)}, f16[9,8,2,8,128]{4,3,2,1,0:T(8,128)(2,1)S(1)}, u32[]{:S(2)}, u32[]{:S(2)}) collective-permute-start(f16[9,8,2,8,128]{4,3,2,1,0:T(8,128)(2,1)S(1)} %collective-permute-done.17), channel_id=1, source_target_pairs={{0,4},{2,6},{4,0},{6,2},{8,12},{10,14},{12,8},{14,10},{16,20},{18,... | collective-permute-start | bytes 884744 | tf_op jit(solution)/shard_map/ppermute | solution.py:311
  93.2 2.1 %collective-permute-start.24 = (f16[2,9,8,2,8,128]{5,4,3,2,1,0:T(8,128)(2,1)S(1)}, f16[2,9,8,2,8,128]{5,4,3,2,1,0:T(8,128)(2,1)S(1)}, u32[]{:S(2)}, u32[]{:S(2)}) collective-permute-start(f16[2,9,8,2,8,128]{5,4,3,2,1,0:T(8,128)(2,1)S(1)} %pad_maximum_fusion.2), channel_id=1, source_target_pairs={{0,2},{2,0},{4,6},{6,4},{8,10},{10,8},{12,14},{14,12},{16,18},{18,... | collective-permute-start | bytes 1769480 | tf_op jit(solution)/shard_map/ppermute | solution.py:311

commit v5 on v4

--- a/solution.py
+++ b/solution.py
@@ -278,9 +278,16 @@
     )
 
 
-def summed(values, bits):
+def later(value, *gates):
+    for gate in gates:
+        gate = gate[(0,) * (gate.ndim - 2)]
+        value = jnp.where(gate.astype(jnp.float32) > -1e30, value, jnp.zeros_like(value))
+    return value
+
+
+def summed(values, bits, *gates):
     lowest = common_exponent(values, bits)
-    total = scaled_sum(values, lowest).astype(jnp.float16)
+    total = later(scaled_sum(values, lowest), *gates).astype(jnp.float16)
     return lax.dynamic_update_slice(
         total, lowest.astype(jnp.float16), (total.shape[0] - 1, 0, 0)
     )
@@ -292,6 +299,7 @@
 
 def on_device(inputs, weight, cotangent):
     x = inputs[0]
+    x_held = pltpu.with_memory_space_constraint(x, pltpu.HBM)
     own_cot = cotangent[0]
     w = jnp.transpose(weight, (1, 0, 2))
     taps, rows, outs = w.shape
@@ -329,49 +337,68 @@
         first = 0
     other_x = to_core(lax.dynamic_slice_in_dim(x, (1 - core) * core_rows, core_rows, 0))
     where = jnp.stack([core, column * depth + level]).astype(jnp.int32)
-    halves, exponents = [], []
+    halves, exponents, arrived, sends = [], [], [], []
+    grad = jnp.zeros((taps, rows // TILE, 2, TILE, LANES), jnp.float16)
     after = own_cot
     for side in range(2):
         part = parts[side]
         if side == 1:
-            part = jnp.where(shards[0][-1, 0, 0] > -1e30, part, jnp.zeros_like(part))
+            part = later(part, shards[0][-1:, :1, :1])
             their_cot = part
-        shards = kernel_grad(where, depth, x, other_x, part, to_core(part), after)
+        shards = kernel_grad(where, depth, x_held, other_x, part, to_core(part), after)
         held = [None] * depth
+        gates = ()
         for message in (1, 0):
-            sent = shards[depth + message].astype(jnp.float16)
+            sent = later(shards[depth + message], *gates).astype(jnp.float16)
             came = to_column(sent)
+            gates = (sent,)
             for slot in range(depth // 2 - 1, -1, -1):
                 step = message * (depth // 2) + slot
                 held[step] = [(shards[step], 0.0), (came[slot], 0.0)]
         after = sent[0, 0].astype(jnp.float32)
         bits = 1.0
+        gates = (sends[-1],) if side else ()
         for bit in [1 << shift for shift in range(depth.bit_length() - 1)]:
             for step in range(depth - bit, 0, -2 * bit):
-                held[step ^ bit].append((to_level(summed(held[step], bits), bit), bits))
+                pair = summed(held[step], bits, *gates)
+                held[step ^ bit].append((to_level(pair, bit), bits))
+                gates = (pair, halves[0]) if side else (pair,)
+                sends.append(pair)
             bits += 1.0
         lowest = common_exponent(held[0], bits)
-        halves.append(scaled_sum(held[0], lowest)[:-1].astype(jnp.float16))
+        total = later(scaled_sum(held[0], lowest)[:-1], *arrived).astype(jnp.float16)
+        shard = total.reshape(taps, shard_tiles, 1, TILE, LANES)
+        halves.append(shard)
         exponents.append(lowest)
-    halves = [jnp.where(first == side, halves[0], halves[1]) for side in range(2)]
+
+        near = [shard]
+        for step in range(1, depth):
+            low = step & -step
+            source = near[step ^ low]
+            if side == 1 and step == depth - 1:
+                source = later(source, rest)
+            near.append(to_level(source, low))
+        if side == 0:
+            rest = to_column(jnp.stack(near[1:]))
+            far = [to_column(shard)] + [rest[step] for step in range(depth - 1)]
+            arrived = [near[depth // 2], far[0]]
+            groups = ((column, near), (1 - column, far))
+        else:
+            far = [to_column(value) for value in near]
+            groups = ((column, near), (1 - column, far[:-1]), (1 - column, far[-1:]))
+        lane = first if side == 0 else 1 - first
+        step = 0
+        for chip, values in groups:
+            across = to_core(jnp.stack(values))
+            for slot, value in enumerate(values):
+                row = chip * chip_tiles + (level ^ (step % depth)) * shard_tiles
+                step += 1
+                for base, piece in ((core, value), (1 - core, across[slot])):
+                    grad = lax.dynamic_update_slice(
+                        grad, piece, (0, base * core_tiles + row, lane, 0, 0)
+                    )
     exponents = [jnp.where(first == side, exponents[0], exponents[1]) for side in range(2)]
-    halves = [half.reshape(taps, shard_tiles, TILE, LANES) for half in halves]
-    shard = jnp.stack(halves, 2)
     exponent = jnp.concatenate(exponents, 0)
-
-    grad = jnp.zeros((taps, rows // TILE, 2, TILE, LANES), jnp.float16)
-    near = [shard]
-    for step in range(1, depth):
-        low = step & -step
-        near.append(to_level(near[step ^ low], low))
-    far = [to_column(value) for value in near]
-    for chip, values, group in ((column, near, depth), (1 - column, far, 2)):
-        for start in range(0, depth, group):
-            across = to_core(jnp.stack(values[start : start + group]))
-            for step in range(start, start + group):
-                row = chip * chip_tiles + (level ^ step) * shard_tiles
-                for base, part in ((core, values[step]), (1 - core, across[step - start])):
-                    grad = lax.dynamic_update_slice_in_dim(grad, part, base * core_tiles + row, 1)
     other = to_core(exponent + 0.0 * token(near[-1][0, 0])[0])
     by_core = [jnp.where(core == side, exponent, other) for side in range(2)]
     factor = jnp.exp2(-jnp.stack(by_core)) * (1.0 / samples)
@@ -379,7 +406,7 @@
     grad = (grad * factor[None, :, None]).reshape(taps, rows // TILE, 2, TILE, LANES)
     weight_grad = jnp.transpose(grad, (1, 3, 0, 2, 4)).reshape(rows, taps, outs)
 
-    total = forward(x, w, token(shard[0, 0]))
+    total = forward(x, w, token(sends[depth - 2]))
     if chans == 2:
         mine = lax.dynamic_slice_in_dim(total, chan * own_outs, own_outs, 0)
         theirs = lax.dynamic_slice_in_dim(total, (1 - chan) * own_outs, own_outs, 0)
@@ -392,7 +419,7 @@
     else:
         result = lax.psum_scatter(total, "chan", scatter_dimension=0, tiled=True)
     result = result.astype(jnp.bfloat16)[None]
-    input_grad = input_gradient(cot, w, token(near[depth // 2][0, 0]))[None]
+    input_grad = input_gradient(cot, w, token(halves[1][0, 0]))[None]
     return (result, input_grad, weight_grad)
 
 

time: 100 us -> 98.6 us (0.986)
  waiting for transfers between devices: 31.8 us -> 24.4 us
  starting transfers between devices: 32.5 us -> 36.1 us
  Pallas kernels: 19.4 us -> 22 us
  local copies, waits for them, and re-layouts: 6.86 us -> 5.86 us
    ppermute x24 -> x31, waiting for transfers between devices: 31.8 us -> 24.4 us  [to(): lax.ppermute(value, 'dp', [(i, i ^ distance) for i in range(samples)])]
    ppermute x24 -> x31, starting transfers between devices: 28 us -> 31.5 us  [to(): lax.ppermute(value, 'dp', [(i, i ^ distance) for i in range(samples)])]
    pallas_call x2, Pallas kernels: 7.95 us -> 10.5 us  [kernel_grad(): pl.pallas_call(functools.partial(kernel_grad_kernel, depth), out_shape=[j...]
    unnamed x12 -> x10, local copies, waits for them, and re-layouts: 2.71 us -> 1.05 us
    dynamic_update_slice x15 -> x32, local copies, waits for them, and re-layouts: 1.41 us -> 2.01 us  [on_device(): lax.dynamic_update_slice(grad, piece, (0, base * core_tiles + row, lane,...]
  transfers between devices with their start and end apart: 26 -> 33, of which waited for: 10 -> 10; matrix products, arithmetic and copies ran while one was open for 4% -> 7% of each run, Pallas kernels for 19% -> 22%
where the time goes in v5:
time: 98.6 us; the launch traced here: 98.2 us
  starting transfers between devices  36.1 us (37%)
  waiting for transfers between devices  24.4 us (25%)
  Pallas kernels  22 us (22%)
  other arithmetic  7.95 us (8%)
  local copies, waits for them, and re-layouts  5.86 us (6%)
  between operations  1.88 us (2%)
    ppermute x31, starting transfers between devices, to(): lax.ppermute(value, 'dp', [(i, i ^ distance) for i in range(samples)])  31.5 us
    ppermute x31, waiting for transfers between devices, to(): lax.ppermute(value, 'dp', [(i, i ^ distance) for i in range(samples)])  24.4 us
    pallas_call x2, Pallas kernels, kernel_grad(): pl.pallas_call(functools.partial(kernel_grad_kernel, depth), out_shape=[j...  10.5 us
    pallas_call x1, Pallas kernels, input_gradient(): pl.pallas_call(input_grad_kernel, out_shape=jax.ShapeDtypeStruct((rows, p...  6.56 us
    pallas_call x1, Pallas kernels, forward(): pl.pallas_call(forward_kernel, out_shape=jax.ShapeDtypeStruct((outs, posi...  4.98 us
    reshape x1, other arithmetic, on_device(): weight_grad = jnp.transpose(grad, (1, 3, 0, 2, 4)).reshape(rows, taps, outs)  4.64 us
    ppermute x1, starting transfers between devices, on_device(): their_cot = lax.ppermute(own_cot, 'chan', [(0, 1), (1, 0)])  2.95 us
    dynamic_update_slice x32, local copies, waits for them, and re-layouts, on_device(): lax.dynamic_update_slice(grad, piece, (0, base * core_tiles + row, lane,...  2.01 us
  transfers between devices with their start and end apart: 33, of which 10 were waited for; matrix products, arithmetic and copies ran while one was open for 7% of the time, Pallas kernels for 22%

profile of v5, /device:TPU:0, one launch (start us, length us, event | category | flops | bytes accessed | tf_op | source)
XLA Modules:
  0.0 98.2 jit_solution(12442811566473375098)
XLA Ops:
  0.7 1.4 %dynamic-slice_bitcast_fusion = bf16[512,1152]{1,0:T(8,128)(2,1)S(1)} fusion(bf16[1,1024,1152]{2,1,0:T(8,128)(2,1)} %param.3, s32[]{:T(128)S(6)} %select_n.211), kind=kLoop, calls=%fused_computation.1 | loop fusion | bytes 2359300 | tf_op jit(solution)/shard_map/dynamic_slice | solution.py:338
  2.1 0.5 collective-permute-start
  2.7 2.9 %collective-permute-start.6 = (bf16[128,1152]{1,0:T(8,128)(2,1)}, bf16[128,1152]{1,0:T(8,128)(2,1)S(1)}, u32[]{:S(2)}, u32[]{:S(2)}) collective-permute-start(bf16[128,1152]{1,0:T(8,128)(2,1)} %bitcast.360), channel_id=1, source_target_pairs={{0,1},{1,0},{2,3},{3,2},{4,5},{5,4},{6,7},{7,6},{8,9},{9,8},{10,11... | collective-permute-start | bytes 884744 | tf_op jit(solution)/shard_map/ppermute | solution.py:331
  5.7 1.0 copy-done.1
  6.7 5.2 %kernel_grad.2 = (f32[73,8,128]{2,1,0:T(8,128)S(1)}, f32[73,8,128]{2,1,0:T(8,128)S(1)}, f32[73,8,128]{2,1,0:T(8,128)S(1)}, f32[73,8,128]{2,1,0:T(8,128)S(1)}, f3...) custom-call(s32[2]{0:T(128)S(1)} %pad_add_fusion.place_ref, bf16[1024,1152]{1,0:T(8,128)(2,1)} %bitcast.356, ...), custom_call_target="tpu_custom_call" | custom-call | flops 1509949440 | bytes 5308416 | tf_op jit(solution)/shard_map/kernel_grad/pallas_call | solution.py:122
  12.0 2.7 %collective-permute-start.2 = (f16[2,73,8,128]{3,2,1,0:T(8,128)(2,1)S(1)}, f16[2,73,8,128]{3,2,1,0:T(8,128)(2,1)S(1)}, u32[]{:S(2)}, u32[]{:S(2)}) collective-permute-start(f16[2,73,8,128]{3,2,1,0:T(8,128)(2,1)S(1)} %convert_element_type.328), channel_id=1, source_target_pairs={{0,4},{2,6},{4,0},{6,2},{8,12},{10,14},{12,8},{14,10},{16,20},{18,... | collective-permute-start | bytes 897032 | tf_op jit(solution)/shard_map/ppermute | solution.py:319
  14.9 0.5 slice.257
  16.3 1.4 %collective-permute-done.11.other_cot = bf16[128,1152]{1,0:T(8,128)(2,1)S(1)} collective-permute-done((bf16[128,1152]{1,0:T(8,128)(2,1)S(1)}, bf16[128,1152]{1,0:T(8,128)(2,1)S(1)}, u32[]{:S(2)}, u32[]{:S(2)}) %collective-permute-start.11) | collective-permute-done | bytes 294944 | tf_op jit(solution)/shard_map/ppermute | solution.py:319
  17.7 5.2 %kernel_grad.3 = (f32[73,8,128]{2,1,0:T(8,128)S(1)}, f32[73,8,128]{2,1,0:T(8,128)S(1)}, f32[73,8,128]{2,1,0:T(8,128)S(1)}, f32[73,8,128]{2,1,0:T(8,128)S(1)}, f3...) custom-call(s32[2]{0:T(128)S(1)} %pad_add_fusion.place_ref, bf16[1024,1152]{1,0:T(8,128)(2,1)} %bitcast.357, ...), custom_call_target="tpu_custom_call" | custom-call | flops 1509949440 | bytes 5308416 | tf_op jit(solution)/shard_map/kernel_grad/pallas_call | solution.py:122
  23.0 2.1 %collective-permute-start.13 = (f16[2,73,8,128]{3,2,1,0:T(8,128)(2,1)S(1)}, f16[2,73,8,128]{3,2,1,0:T(8,128)(2,1)S(1)}, u32[]{:S(2)}, u32[]{:S(2)}) collective-permute-start(f16[2,73,8,128]{3,2,1,0:T(8,128)(2,1)S(1)} %convert_element_type.368), channel_id=1, source_target_pairs={{0,4},{2,6},{4,0},{6,2},{8,12},{10,14},{12,8},{14,10},{16,20},{18,... | collective-permute-start | bytes 897032 | tf_op jit(solution)/shard_map/ppermute | solution.py:319
  25.4 2.1 %collective-permute-start.4 = (f16[73,8,128]{2,1,0:T(8,128)(2,1)S(1)}, f16[73,8,128]{2,1,0:T(8,128)(2,1)S(1)}, u32[]{:S(2)}, u32[]{:S(2)}) collective-permute-start(f16[73,8,128]{2,1,0:T(8,128)(2,1)S(1)} %constant_dynamic-update-slice_fusion.8), channel_id=1, source_target_pairs={{0,8},{2,10},{4,12},{6,14},{8,0},{10,2},{12,4},{14,6},{16,24},{18,... | collective-permute-start | bytes 448520 | tf_op jit(solution)/shard_map/ppermute | solution.py:319
  27.5 1.5 %collective-permute-done.3 = f16[2,73,8,128]{3,2,1,0:T(8,128)(2,1)S(1)} collective-permute-done((f16[2,73,8,128]{3,2,1,0:T(8,128)(2,1)S(1)}, f16[2,73,8,128]{3,2,1,0:T(8,128)(2,1)S(1)}, u32[]{:S(2)}, u32[]{:S(2)}) %collective-permute-start.3) | collective-permute-done | bytes 299040 | tf_op jit(solution)/shard_map/ppermute | solution.py:319
  29.1 2.2 %collective-permute-start.7 = (f16[73,8,128]{2,1,0:T(8,128)(2,1)S(1)}, f16[73,8,128]{2,1,0:T(8,128)(2,1)S(1)}, u32[]{:S(2)}, u32[]{:S(2)}) collective-permute-start(f16[73,8,128]{2,1,0:T(8,128)(2,1)S(1)} %constant_dynamic-update-slice_fusion.7), channel_id=1, source_target_pairs={{0,8},{2,10},{4,12},{6,14},{8,0},{10,2},{12,4},{14,6},{16,24},{18,... | collective-permute-start | bytes 448520 | tf_op jit(solution)/shard_map/ppermute | solution.py:319
  31.6 3.0 %collective-permute-start.8 = (f16[73,8,128]{2,1,0:T(8,128)(2,1)S(1)}, f16[73,8,128]{2,1,0:T(8,128)(2,1)S(1)}, u32[]{:S(2)}, u32[]{:S(2)}) collective-permute-start(f16[73,8,128]{2,1,0:T(8,128)(2,1)S(1)} %constant_dynamic-update-slice_fusion.6), channel_id=1, source_target_pairs={{0,16},{2,18},{4,20},{6,22},{8,24},{10,26},{12,28},{14,30},{16,0},... | collective-permute-start | bytes 448520 | tf_op jit(solution)/shard_map/ppermute | solution.py:319
  34.7 5.0 %forward.1 = f32[256,1152]{1,0:T(8,128)S(1)} custom-call(bf16[1024,1152]{1,0:T(8,128)(2,1)S(1)} %bitcast.358, bf16[9,1024,256]{2,1,0:T(8,128)(2,1)S(1)} %bitcast.366, f32[8,128]{1,0:T(8,128)S(1)} %fusion.142._), custom_call_target="tpu_custom_call" | custom-call | flops 3019898880 | bytes 8257536 | tf_op jit(solution)/shard_map/forward/pallas_call | solution.py:194
  39.7 1.6 %collective-permute-start.5 = (f32[128,1152]{1,0:T(8,128)S(1)}, f32[128,1152]{1,0:T(8,128)S(1)}, u32[]{:S(2)}, u32[]{:S(2)}) collective-permute-start(f32[128,1152]{1,0:T(8,128)S(1)} %constant_dynamic-slice_fusion), channel_id=1, source_target_pairs={{0,1},{1,0},{2,3},{3,2},{4,5},{5,4},{6,7},{7,6},{8,9},{9,8},{10,11... | collective-permute-start | bytes 1769480 | tf_op jit(solution)/shard_map/ppermute | solution.py:413
  41.4 1.6 %collective-permute-start.15 = (f16[73,8,128]{2,1,0:T(8,128)(2,1)S(1)}, f16[73,8,128]{2,1,0:T(8,128)(2,1)S(1)}, u32[]{:S(2)}, u32[]{:S(2)}) collective-permute-start(f16[73,8,128]{2,1,0:T(8,128)(2,1)S(1)} %constant_dynamic-update-slice_fusion.5), channel_id=1, source_target_pairs={{0,8},{2,10},{4,12},{6,14},{8,0},{10,2},{12,4},{14,6},{16,24},{18,... | collective-permute-start | bytes 448520 | tf_op jit(solution)/shard_map/ppermute | solution.py:319
  43.4 1.2 %collective-permute-start.10 = (f16[9,8,1,8,128]{4,3,1,0,2:T(8,128)(2,1)S(1)}, f16[9,8,1,8,128]{4,3,1,0,2:T(8,128)(2,1)S(1)}, u32[]{:S(2)}, u32[]{:S(2)}) collective-permute-start(f16[9,8,1,8,128]{4,3,1,0,2:T(8,128)(2,1)S(1)} %bitcast.377), channel_id=1, source_target_pairs={{0,16},{2,18},{4,20},{6,22},{8,24},{10,26},{12,28},{14,30},{16,0},... | collective-permute-start | bytes 442376 | tf_op jit(solution)/shard_map/ppermute | solution.py:319
  44.6 1.6 %collective-permute-start.17 = (f16[9,8,1,8,128]{4,3,1,0,2:T(8,128)(2,1)S(1)}, f16[9,8,1,8,128]{4,3,1,0,2:T(8,128)(2,1)S(1)}, u32[]{:S(2)}, u32[]{:S(2)}) collective-permute-start(f16[9,8,1,8,128]{4,3,1,0,2:T(8,128)(2,1)S(1)} %bitcast.378), channel_id=1, source_target_pairs={{0,8},{2,10},{4,12},{6,14},{8,0},{10,2},{12,4},{14,6},{16,24},{18,... | collective-permute-start | bytes 442376 | tf_op jit(solution)/shard_map/ppermute | solution.py:319
  46.3 0.5 collective-permute-start.14
  46.8 0.7 broadcast_in_dim.80
  47.6 3.1 %collective-permute-done.15 = f16[73,8,128]{2,1,0:T(8,128)(2,1)S(1)} collective-permute-done((f16[73,8,128]{2,1,0:T(8,128)(2,1)S(1)}, f16[73,8,128]{2,1,0:T(8,128)(2,1)S(1)}, u32[]{:S(2)}, u32[]{:S(2)}) %collective-permute-start.15) | collective-permute-done | bytes 149536 | tf_op jit(solution)/shard_map/ppermute | solution.py:319
  50.7 1.4 %collective-permute-start.9 = (f16[9,8,1,8,128]{4,3,1,0,2:T(8,128)(2,1)S(1)}, f16[9,8,1,8,128]{4,3,1,0,2:T(8,128)(2,1)S(1)}, u32[]{:S(2)}, u32[]{:S(2)}) collective-permute-start(f16[9,8,1,8,128]{4,3,1,0,2:T(8,128)(2,1)S(1)} %bitcast.381), channel_id=1, source_target_pairs={{0,4},{2,6},{4,0},{6,2},{8,12},{10,14},{12,8},{14,10},{16,20},{18,... | collective-permute-start | bytes 442376 | tf_op jit(solution)/shard_map/ppermute | solution.py:319
  52.3 1.6 %collective-permute-start.16 = (f16[73,8,128]{2,1,0:T(8,128)(2,1)S(1)}, f16[73,8,128]{2,1,0:T(8,128)(2,1)S(1)}, u32[]{:S(2)}, u32[]{:S(2)}) collective-permute-start(f16[73,8,128]{2,1,0:T(8,128)(2,1)S(1)} %constant_dynamic-update-slice_fusion.3), channel_id=1, source_target_pairs={{0,16},{2,18},{4,20},{6,22},{8,24},{10,26},{12,28},{14,30},{16,0},... | collective-permute-start | bytes 448520 | tf_op jit(solution)/shard_map/ppermute | solution.py:319
  53.9 1.9 %collective-permute-done.9 = f16[9,8,1,8,128]{4,3,1,0,2:T(8,128)(2,1)S(1)} collective-permute-done((f16[9,8,1,8,128]{4,3,1,0,2:T(8,128)(2,1)S(1)}, f16[9,8,1,8,128]{4,3,1,0,2:T(8,128)(2,1)S(1)}, u32[]{:S(2)}, u32[]{:S(2)}) %collective-permute-start.9) | collective-permute-done | bytes 147488 | tf_op jit(solution)/shard_map/ppermute | solution.py:319
  55.8 4.8 %collective-permute-done.14 = f16[73,8,128]{2,1,0:T(8,128)(2,1)S(1)} collective-permute-done((f16[73,8,128]{2,1,0:T(8,128)(2,1)S(1)}, f16[73,8,128]{2,1,0:T(8,128)(2,1)S(1)}, u32[]{:S(2)}, u32[]{:S(2)}) %collective-permute-start.14) | collective-permute-done | bytes 149536 | tf_op jit(solution)/shard_map/ppermute | solution.py:319
  60.7 0.1 fusion.27
  60.9 2.9 %collective-permute-start.23 = (f16[9,8,1,8,128]{4,3,1,0,2:T(8,128)(2,1)S(1)}, f16[9,8,1,8,128]{4,3,1,0,2:T(8,128)(2,1)S(1)}, u32[]{:S(2)}, u32[]{:S(2)}) collective-permute-start(f16[9,8,1,8,128]{4,3,1,0,2:T(8,128)(2,1)S(1)} %bitcast.371), channel_id=1, source_target_pairs={{0,16},{2,18},{4,20},{6,22},{8,24},{10,26},{12,28},{14,30},{16,0},... | collective-permute-start | bytes 442376 | tf_op jit(solution)/shard_map/ppermute | solution.py:319
  63.7 1.2 %collective-permute-done.18 = f16[9,8,1,8,128]{4,3,1,0,2:T(8,128)(2,1)S(1)} collective-permute-done((f16[9,8,1,8,128]{4,3,1,0,2:T(8,128)(2,1)S(1)}, f16[9,8,1,8,128]{4,3,1,0,2:T(8,128)(2,1)S(1)}, u32[]{:S(2)}, u32[]{:S(2)}) %collective-permute-start.18) | collective-permute-done | bytes 147488 | tf_op jit(solution)/shard_map/ppermute | solution.py:319
  65.0 0.1 pad_maximum_fusion.3
  65.1 1.5 %collective-permute-start.20 = (f16[3,9,8,1,8,128]{5,4,2,1,3,0:T(8,128)(2,1)S(1)}, f16[3,9,8,1,8,128]{5,4,2,1,3,0:T(8,128)(2,1)S(1)}, u32[]{:S(2)}, u32[]{:S(2)}) collective-permute-start(f16[3,9,8,1,8,128]{5,4,2,1,3,0:T(8,128)(2,1)S(1)} %pad_maximum_fusion.3), channel_id=1, source_target_pairs={{0,4},{2,6},{4,0},{6,2},{8,12},{10,14},{12,8},{14,10},{16,20},{18,... | collective-permute-start | bytes 1327112 | tf_op jit(solution)/shard_map/ppermute | solution.py:319
  66.6 0.6 collective-permute-start.26
  67.2 0.2 pad_maximum_fusion
  67.4 6.6 %input_gradient.1 = bf16[1024,1152]{1,0:T(8,128)(2,1)} custom-call(bf16[256,1152]{1,0:T(8,128)(2,1)S(1)} %maximum_select_fusion.cot_ref, bf16[9,1024,256]{2,1,0:T(8,128)(2,1)S(1)} %bitcast.367, f32[8,128]{1,0:T(8,128)S(1)} %fusion.140._), custom_call_target="tpu_custom_call" | custom-call | flops 3019898880 | bytes 7667712 | tf_op jit(solution)/shard_map/input_gradient/pallas_call | solution.py:242
  74.0 0.8 fusion.21
  74.8 1.4 %collective-permute-start.27 = (f16[9,8,1,8,128]{4,3,1,0,2:T(8,128)(2,1)S(1)}, f16[9,8,1,8,128]{4,3,1,0,2:T(8,128)(2,1)S(1)}, u32[]{:S(2)}, u32[]{:S(2)}) collective-permute-start(f16[9,8,1,8,128]{4,3,1,0,2:T(8,128)(2,1)S(1)} %collective-permute-done.22), channel_id=1, source_target_pairs={{0,4},{2,6},{4,0},{6,2},{8,12},{10,14},{12,8},{14,10},{16,20},{18,... | collective-permute-start | bytes 442376 | tf_op jit(solution)/shard_map/ppermute | solution.py:319
  76.2 0.6 collective-permute-start.28
  76.8 0.9 collective-permute-start.24
  77.7 3.7 %collective-permute-done.27 = f16[9,8,1,8,128]{4,3,1,0,2:T(8,128)(2,1)S(1)} collective-permute-done((f16[9,8,1,8,128]{4,3,1,0,2:T(8,128)(2,1)S(1)}, f16[9,8,1,8,128]{4,3,1,0,2:T(8,128)(2,1)S(1)}, u32[]{:S(2)}, u32[]{:S(2)}) %collective-permute-start.27) | collective-permute-done | bytes 147488 | tf_op jit(solution)/shard_map/ppermute | solution.py:319
  81.4 2.8 %collective-permute-done.28 = f16[9,8,1,8,128]{4,3,1,0,2:T(8,128)(2,1)S(1)} collective-permute-done((f16[9,8,1,8,128]{4,3,1,0,2:T(8,128)(2,1)S(1)}, f16[9,8,1,8,128]{4,3,1,0,2:T(8,128)(2,1)S(1)}, u32[]{:S(2)}, u32[]{:S(2)}) %collective-permute-start.28) | collective-permute-done | bytes 147488 | tf_op jit(solution)/shard_map/ppermute | solution.py:319
  84.2 0.1 pad_maximum_fusion.4
  84.4 0.2 pad_maximum_fusion.1
  84.6 0.6 collective-permute-start.21
  85.3 0.2 pad_maximum_fusion.2
  85.5 0.5 collective-permute-start.25
  86.0 1.4 %collective-permute-start.30 = (f16[9,8,1,8,128]{4,3,1,0,2:T(8,128)(2,1)S(1)}, f16[9,8,1,8,128]{4,3,1,0,2:T(8,128)(2,1)S(1)}, u32[]{:S(2)}, u32[]{:S(2)}) collective-permute-start(f16[9,8,1,8,128]{4,3,1,0,2:T(8,128)(2,1)S(1)} %collective-permute-done.24), channel_id=1, source_target_pairs={{0,4},{2,6},{4,0},{6,2},{8,12},{10,14},{12,8},{14,10},{16,20},{18,... | collective-permute-start | bytes 442376 | tf_op jit(solution)/shard_map/ppermute | solution.py:319
  88.0 3.9 %collective-permute-done.30 = f16[9,8,1,8,128]{4,3,1,0,2:T(8,128)(2,1)S(1)} collective-permute-done((f16[9,8,1,8,128]{4,3,1,0,2:T(8,128)(2,1)S(1)}, f16[9,8,1,8,128]{4,3,1,0,2:T(8,128)(2,1)S(1)}, u32[]{:S(2)}, u32[]{:S(2)}) %collective-permute-start.30) | collective-permute-done | bytes 147488 | tf_op jit(solution)/shard_map/ppermute | solution.py:319
  93.5 4.6 %multiply_bitcast_fusion = f32[1024,9,256]{2,0,1:T(8,128)} fusion(f16[9,128,2,8,128]{4,3,2,1,0:T(8,128)(2,1)S(1)} %bitcast_dynamic-update-slice_fusion, f32[128,2,8,128]{3,2,1,0:T(8,128)S(1)} %bitcast.368), kind=kLoop, calls=%fused_computation | loop fusion | flops 4718592 | bytes 15204352 | tf_op jit(solution)/shard_map/reshape | solution.py:407
  (129 shorter events, 4.4 us)
Async XLA Ops:
  0.7 34.0 %slice-start = ((s8[4718592]{0:T(1024)(128)(4,1)}), s8[524288]{0:T(1024)(128)(4,1)S(1)}, s32[]{:S(2)}) async-start(s8[4718592]{0:T(1024)(128)(4,1)} %bitcast.364), calls=%async_computation | async-start | bytes 1048576
  2.1 3.6 %collective-permute-start = (bf16[512,1152]{1,0:T(8,128)(2,1)S(1)}, bf16[512,1152]{1,0:T(8,128)(2,1)S(1)}, u32[]{:S(2)}, u32[]{:S(2)}) collective-permute-start(bf16[512,1152]{1,0:T(8,128)(2,1)S(1)} %dynamic-slice_bitcast_fusion), channel_id=1, source_target_pairs={{0,2},{2,0},{4,6},{6,4},{8,10},{10,8},{12,14},{14,12},{16,18},{18,... | collective-permute-start | bytes 3538952 | tf_op jit(solution)/shard_map/ppermute | solution.py:319
  2.6 3.1 %collective-permute-start.1 = (bf16[128,1152]{1,0:T(8,128)(2,1)}, bf16[128,1152]{1,0:T(8,128)(2,1)S(1)}, u32[]{:S(2)}, u32[]{:S(2)}) collective-permute-start(bf16[128,1152]{1,0:T(8,128)(2,1)} %bitcast.359), channel_id=1, source_target_pairs={{0,2},{2,0},{4,6},{6,4},{8,10},{10,8},{12,14},{14,12},{16,18},{18,... | collective-permute-start | bytes 884744 | tf_op jit(solution)/shard_map/ppermute | solution.py:319
  2.7 13.3 %collective-permute-start.6 = (bf16[128,1152]{1,0:T(8,128)(2,1)}, bf16[128,1152]{1,0:T(8,128)(2,1)S(1)}, u32[]{:S(2)}, u32[]{:S(2)}) collective-permute-start(bf16[128,1152]{1,0:T(8,128)(2,1)} %bitcast.360), channel_id=1, source_target_pairs={{0,1},{1,0},{2,3},{3,2},{4,5},{5,4},{6,7},{7,6},{8,9},{9,8},{10,11... | collective-permute-start | bytes 884744 | tf_op jit(solution)/shard_map/ppermute | solution.py:331
  5.7 1.0 copy-start.1
  12.0 13.3 %collective-permute-start.2 = (f16[2,73,8,128]{3,2,1,0:T(8,128)(2,1)S(1)}, f16[2,73,8,128]{3,2,1,0:T(8,128)(2,1)S(1)}, u32[]{:S(2)}, u32[]{:S(2)}) collective-permute-start(f16[2,73,8,128]{3,2,1,0:T(8,128)(2,1)S(1)} %convert_element_type.328), channel_id=1, source_target_pairs={{0,4},{2,6},{4,0},{6,2},{8,12},{10,14},{12,8},{14,10},{16,20},{18,... | collective-permute-start | bytes 897032 | tf_op jit(solution)/shard_map/ppermute | solution.py:319
  14.8 14.2 %collective-permute-start.3 = (f16[2,73,8,128]{3,2,1,0:T(8,128)(2,1)S(1)}, f16[2,73,8,128]{3,2,1,0:T(8,128)(2,1)S(1)}, u32[]{:S(2)}, u32[]{:S(2)}) collective-permute-start(f16[2,73,8,128]{3,2,1,0:T(8,128)(2,1)S(1)} %select_convert_fusion.1), channel_id=1, source_target_pairs={{0,4},{2,6},{4,0},{6,2},{8,12},{10,14},{12,8},{14,10},{16,20},{18,... | collective-permute-start | bytes 897032 | tf_op jit(solution)/shard_map/ppermute | solution.py:319
  16.1 1.6 %collective-permute-start.11 = (bf16[128,1152]{1,0:T(8,128)(2,1)S(1)}, bf16[128,1152]{1,0:T(8,128)(2,1)S(1)}, u32[]{:S(2)}, u32[]{:S(2)}) collective-permute-start(bf16[128,1152]{1,0:T(8,128)(2,1)S(1)} %broadcast_select_fusion.own_cot), channel_id=1, source_target_pairs={{0,2},{2,0},{4,6},{6,4},{8,10},{10,8},{12,14},{14,12},{16,18},{18,... | collective-permute-start | bytes 884744 | tf_op jit(solution)/shard_map/ppermute | solution.py:319
  16.2 18.5 %slice-start.1 = ((s8[4718592]{0:T(1024)(128)(4,1)}), s8[4194304]{0:T(1024)(128)(4,1)S(1)}, s32[]{:S(2)}) async-start(s8[4718592]{0:T(1024)(128)(4,1)} %bitcast.364), calls=%async_computation.1 | async-start | bytes 8388608
  16.3 18.3 %copy-start = (bf16[1,1024,1152]{2,1,0:T(8,128)(2,1)S(1)}, bf16[1,1024,1152]{2,1,0:T(8,128)(2,1)}, u32[]{:S(2)}) copy-start(bf16[1,1024,1152]{2,1,0:T(8,128)(2,1)} %param.3) | copy-start | bytes 7077892
  23.0 18.3 %collective-permute-start.13 = (f16[2,73,8,128]{3,2,1,0:T(8,128)(2,1)S(1)}, f16[2,73,8,128]{3,2,1,0:T(8,128)(2,1)S(1)}, u32[]{:S(2)}, u32[]{:S(2)}) collective-permute-start(f16[2,73,8,128]{3,2,1,0:T(8,128)(2,1)S(1)} %convert_element_type.368), channel_id=1, source_target_pairs={{0,4},{2,6},{4,0},{6,2},{8,12},{10,14},{12,8},{14,10},{16,20},{18,... | collective-permute-start | bytes 897032 | tf_op jit(solution)/shard_map/ppermute | solution.py:319
  25.2 17.9 %collective-permute-start.12 = (f16[2,73,8,128]{3,2,1,0:T(8,128)(2,1)S(1)}, f16[2,73,8,128]{3,2,1,0:T(8,128)(2,1)S(1)}, u32[]{:S(2)}, u32[]{:S(2)}) collective-permute-start(f16[2,73,8,128]{3,2,1,0:T(8,128)(2,1)S(1)} %select_convert_fusion), channel_id=1, source_target_pairs={{0,4},{2,6},{4,0},{6,2},{8,12},{10,14},{12,8},{14,10},{16,20},{18,... | collective-permute-start | bytes 897032 | tf_op jit(solution)/shard_map/ppermute | solution.py:319
  25.4 6.1 %collective-permute-start.4 = (f16[73,8,128]{2,1,0:T(8,128)(2,1)S(1)}, f16[73,8,128]{2,1,0:T(8,128)(2,1)S(1)}, u32[]{:S(2)}, u32[]{:S(2)}) collective-permute-start(f16[73,8,128]{2,1,0:T(8,128)(2,1)S(1)} %constant_dynamic-update-slice_fusion.8), channel_id=1, source_target_pairs={{0,8},{2,10},{4,12},{6,14},{8,0},{10,2},{12,4},{14,6},{16,24},{18,... | collective-permute-start | bytes 448520 | tf_op jit(solution)/shard_map/ppermute | solution.py:319
  29.1 14.1 %collective-permute-start.7 = (f16[73,8,128]{2,1,0:T(8,128)(2,1)S(1)}, f16[73,8,128]{2,1,0:T(8,128)(2,1)S(1)}, u32[]{:S(2)}, u32[]{:S(2)}) collective-permute-start(f16[73,8,128]{2,1,0:T(8,128)(2,1)S(1)} %constant_dynamic-update-slice_fusion.7), channel_id=1, source_target_pairs={{0,8},{2,10},{4,12},{6,14},{8,0},{10,2},{12,4},{14,6},{16,24},{18,... | collective-permute-start | bytes 448520 | tf_op jit(solution)/shard_map/ppermute | solution.py:319
  31.6 11.5 %collective-permute-start.8 = (f16[73,8,128]{2,1,0:T(8,128)(2,1)S(1)}, f16[73,8,128]{2,1,0:T(8,128)(2,1)S(1)}, u32[]{:S(2)}, u32[]{:S(2)}) collective-permute-start(f16[73,8,128]{2,1,0:T(8,128)(2,1)S(1)} %constant_dynamic-update-slice_fusion.6), channel_id=1, source_target_pairs={{0,16},{2,18},{4,20},{6,22},{8,24},{10,26},{12,28},{14,30},{16,0},... | collective-permute-start | bytes 448520 | tf_op jit(solution)/shard_map/ppermute | solution.py:319
  39.7 34.2 %collective-permute-start.5 = (f32[128,1152]{1,0:T(8,128)S(1)}, f32[128,1152]{1,0:T(8,128)S(1)}, u32[]{:S(2)}, u32[]{:S(2)}) collective-permute-start(f32[128,1152]{1,0:T(8,128)S(1)} %constant_dynamic-slice_fusion), channel_id=1, source_target_pairs={{0,1},{1,0},{2,3},{3,2},{4,5},{5,4},{6,7},{7,6},{8,9},{9,8},{10,11... | collective-permute-start | bytes 1769480 | tf_op jit(solution)/shard_map/ppermute | solution.py:413
  41.4 9.2 %collective-permute-start.15 = (f16[73,8,128]{2,1,0:T(8,128)(2,1)S(1)}, f16[73,8,128]{2,1,0:T(8,128)(2,1)S(1)}, u32[]{:S(2)}, u32[]{:S(2)}) collective-permute-start(f16[73,8,128]{2,1,0:T(8,128)(2,1)S(1)} %constant_dynamic-update-slice_fusion.5), channel_id=1, source_target_pairs={{0,8},{2,10},{4,12},{6,14},{8,0},{10,2},{12,4},{14,6},{16,24},{18,... | collective-permute-start | bytes 448520 | tf_op jit(solution)/shard_map/ppermute | solution.py:319
  43.4 8.9 %collective-permute-start.10 = (f16[9,8,1,8,128]{4,3,1,0,2:T(8,128)(2,1)S(1)}, f16[9,8,1,8,128]{4,3,1,0,2:T(8,128)(2,1)S(1)}, u32[]{:S(2)}, u32[]{:S(2)}) collective-permute-start(f16[9,8,1,8,128]{4,3,1,0,2:T(8,128)(2,1)S(1)} %bitcast.377), channel_id=1, source_target_pairs={{0,16},{2,18},{4,20},{6,22},{8,24},{10,26},{12,28},{14,30},{16,0},... | collective-permute-start | bytes 442376 | tf_op jit(solution)/shard_map/ppermute | solution.py:319
  44.6 19.2 %collective-permute-start.17 = (f16[9,8,1,8,128]{4,3,1,0,2:T(8,128)(2,1)S(1)}, f16[9,8,1,8,128]{4,3,1,0,2:T(8,128)(2,1)S(1)}, u32[]{:S(2)}, u32[]{:S(2)}) collective-permute-start(f16[9,8,1,8,128]{4,3,1,0,2:T(8,128)(2,1)S(1)} %bitcast.378), channel_id=1, source_target_pairs={{0,8},{2,10},{4,12},{6,14},{8,0},{10,2},{12,4},{14,6},{16,24},{18,... | collective-permute-start | bytes 442376 | tf_op jit(solution)/shard_map/ppermute | solution.py:319
  46.3 14.4 %collective-permute-start.14 = (f16[73,8,128]{2,1,0:T(8,128)(2,1)S(1)}, f16[73,8,128]{2,1,0:T(8,128)(2,1)S(1)}, u32[]{:S(2)}, u32[]{:S(2)}) collective-permute-start(f16[73,8,128]{2,1,0:T(8,128)(2,1)S(1)} %constant_dynamic-update-slice_fusion.4), channel_id=1, source_target_pairs={{0,8},{2,10},{4,12},{6,14},{8,0},{10,2},{12,4},{14,6},{16,24},{18,... | collective-permute-start | bytes 448520 | tf_op jit(solution)/shard_map/ppermute | solution.py:319
  50.7 5.1 %collective-permute-start.9 = (f16[9,8,1,8,128]{4,3,1,0,2:T(8,128)(2,1)S(1)}, f16[9,8,1,8,128]{4,3,1,0,2:T(8,128)(2,1)S(1)}, u32[]{:S(2)}, u32[]{:S(2)}) collective-permute-start(f16[9,8,1,8,128]{4,3,1,0,2:T(8,128)(2,1)S(1)} %bitcast.381), channel_id=1, source_target_pairs={{0,4},{2,6},{4,0},{6,2},{8,12},{10,14},{12,8},{14,10},{16,20},{18,... | collective-permute-start | bytes 442376 | tf_op jit(solution)/shard_map/ppermute | solution.py:319
  52.3 8.4 %collective-permute-start.16 = (f16[73,8,128]{2,1,0:T(8,128)(2,1)S(1)}, f16[73,8,128]{2,1,0:T(8,128)(2,1)S(1)}, u32[]{:S(2)}, u32[]{:S(2)}) collective-permute-start(f16[73,8,128]{2,1,0:T(8,128)(2,1)S(1)} %constant_dynamic-update-slice_fusion.3), channel_id=1, source_target_pairs={{0,16},{2,18},{4,20},{6,22},{8,24},{10,26},{12,28},{14,30},{16,0},... | collective-permute-start | bytes 448520 | tf_op jit(solution)/shard_map/ppermute | solution.py:319
  55.8 9.1 %collective-permute-start.18 = (f16[9,8,1,8,128]{4,3,1,0,2:T(8,128)(2,1)S(1)}, f16[9,8,1,8,128]{4,3,1,0,2:T(8,128)(2,1)S(1)}, u32[]{:S(2)}, u32[]{:S(2)}) collective-permute-start(f16[9,8,1,8,128]{4,3,1,0,2:T(8,128)(2,1)S(1)} %collective-permute-done.10), channel_id=1, source_target_pairs={{0,8},{2,10},{4,12},{6,14},{8,0},{10,2},{12,4},{14,6},{16,24},{18,... | collective-permute-start | bytes 442376 | tf_op jit(solution)/shard_map/ppermute | solution.py:319
  60.9 15.3 %collective-permute-start.23 = (f16[9,8,1,8,128]{4,3,1,0,2:T(8,128)(2,1)S(1)}, f16[9,8,1,8,128]{4,3,1,0,2:T(8,128)(2,1)S(1)}, u32[]{:S(2)}, u32[]{:S(2)}) collective-permute-start(f16[9,8,1,8,128]{4,3,1,0,2:T(8,128)(2,1)S(1)} %bitcast.371), channel_id=1, source_target_pairs={{0,16},{2,18},{4,20},{6,22},{8,24},{10,26},{12,28},{14,30},{16,0},... | collective-permute-start | bytes 442376 | tf_op jit(solution)/shard_map/ppermute | solution.py:319
  63.7 11.0 %collective-permute-start.22 = (f16[9,8,1,8,128]{4,3,1,0,2:T(8,128)(2,1)S(1)}, f16[9,8,1,8,128]{4,3,1,0,2:T(8,128)(2,1)S(1)}, u32[]{:S(2)}, u32[]{:S(2)}) collective-permute-start(f16[9,8,1,8,128]{4,3,1,0,2:T(8,128)(2,1)S(1)} %bitcast.372), channel_id=1, source_target_pairs={{0,8},{2,10},{4,12},{6,14},{8,0},{10,2},{12,4},{14,6},{16,24},{18,... | collective-permute-start | bytes 442376 | tf_op jit(solution)/shard_map/ppermute | solution.py:319
  65.1 11.7 %collective-permute-start.20 = (f16[3,9,8,1,8,128]{5,4,2,1,3,0:T(8,128)(2,1)S(1)}, f16[3,9,8,1,8,128]{5,4,2,1,3,0:T(8,128)(2,1)S(1)}, u32[]{:S(2)}, u32[]{:S(2)}) collective-permute-start(f16[3,9,8,1,8,128]{5,4,2,1,3,0:T(8,128)(2,1)S(1)} %pad_maximum_fusion.3), channel_id=1, source_target_pairs={{0,4},{2,6},{4,0},{6,2},{8,12},{10,14},{12,8},{14,10},{16,20},{18,... | collective-permute-start | bytes 1327112 | tf_op jit(solution)/shard_map/ppermute | solution.py:319
  66.6 11.2 %collective-permute-start.26 = (f16[9,8,1,8,128]{4,3,2,1,0:T(8,128)(2,1)S(1)}, f16[9,8,1,8,128]{4,3,2,1,0:T(8,128)(2,1)S(1)}, u32[]{:S(2)}, u32[]{:S(2)}) collective-permute-start(f16[9,8,1,8,128]{4,3,2,1,0:T(8,128)(2,1)S(1)} %bitcast.373), channel_id=1, source_target_pairs={{0,4},{2,6},{4,0},{6,2},{8,12},{10,14},{12,8},{14,10},{16,20},{18,... | collective-permute-start | bytes 442376 | tf_op jit(solution)/shard_map/ppermute | solution.py:319
  74.0 12.1 %collective-permute-start.19 = (f16[4,9,8,1,8,128]{5,4,2,1,3,0:T(8,128)(2,1)S(1)}, f16[4,9,8,1,8,128]{5,4,2,1,3,0:T(8,128)(2,1)S(1)}, u32[]{:S(2)}, u32[]{:S(2)}) collective-permute-start(f16[4,9,8,1,8,128]{5,4,2,1,3,0:T(8,128)(2,1)S(1)} %pad_maximum_fusion), channel_id=1, source_target_pairs={{0,2},{2,0},{4,6},{6,4},{8,10},{10,8},{12,14},{14,12},{16,18},{18,... | collective-permute-start | bytes 1769480 | tf_op jit(solution)/shard_map/ppermute | solution.py:319
  74.8 6.6 %collective-permute-start.27 = (f16[9,8,1,8,128]{4,3,1,0,2:T(8,128)(2,1)S(1)}, f16[9,8,1,8,128]{4,3,1,0,2:T(8,128)(2,1)S(1)}, u32[]{:S(2)}, u32[]{:S(2)}) collective-permute-start(f16[9,8,1,8,128]{4,3,1,0,2:T(8,128)(2,1)S(1)} %collective-permute-done.22), channel_id=1, source_target_pairs={{0,4},{2,6},{4,0},{6,2},{8,12},{10,14},{12,8},{14,10},{16,20},{18,... | collective-permute-start | bytes 442376 | tf_op jit(solution)/shard_map/ppermute | solution.py:319
  76.2 8.0 %collective-permute-start.28 = (f16[9,8,1,8,128]{4,3,1,0,2:T(8,128)(2,1)S(1)}, f16[9,8,1,8,128]{4,3,1,0,2:T(8,128)(2,1)S(1)}, u32[]{:S(2)}, u32[]{:S(2)}) collective-permute-start(f16[9,8,1,8,128]{4,3,1,0,2:T(8,128)(2,1)S(1)} %collective-permute-done.23), channel_id=1, source_target_pairs={{0,4},{2,6},{4,0},{6,2},{8,12},{10,14},{12,8},{14,10},{16,20},{18,... | collective-permute-start | bytes 442376 | tf_op jit(solution)/shard_map/ppermute | solution.py:319
  76.8 8.3 %collective-permute-start.24 = (f16[9,8,1,8,128]{4,3,1,0,2:T(8,128)(2,1)S(1)}, f16[9,8,1,8,128]{4,3,1,0,2:T(8,128)(2,1)S(1)}, u32[]{:S(2)}, u32[]{:S(2)}) collective-permute-start(f16[9,8,1,8,128]{4,3,1,0,2:T(8,128)(2,1)S(1)} %broadcast_select_fusion.1), channel_id=1, source_target_pairs={{0,8},{2,10},{4,12},{6,14},{8,0},{10,2},{12,4},{14,6},{16,24},{18,... | collective-permute-start | bytes 442376 | tf_op jit(solution)/shard_map/ppermute | solution.py:319
  84.3 8.6 %collective-permute-start.29 = (f16[3,9,8,1,8,128]{5,4,2,1,3,0:T(8,128)(2,1)S(1)}, f16[3,9,8,1,8,128]{5,4,2,1,3,0:T(8,128)(2,1)S(1)}, u32[]{:S(2)}, u32[]{:S(2)}) collective-permute-start(f16[3,9,8,1,8,128]{5,4,2,1,3,0:T(8,128)(2,1)S(1)} %pad_maximum_fusion.4), channel_id=1, source_target_pairs={{0,2},{2,0},{4,6},{6,4},{8,10},{10,8},{12,14},{14,12},{16,18},{18,... | collective-permute-start | bytes 1327112 | tf_op jit(solution)/shard_map/ppermute | solution.py:319
  84.6 7.3 %collective-permute-start.21 = (f16[4,9,8,1,8,128]{5,4,2,1,3,0:T(8,128)(2,1)S(1)}, f16[4,9,8,1,8,128]{5,4,2,1,3,0:T(8,128)(2,1)S(1)}, u32[]{:S(2)}, u32[]{:S(2)}) collective-permute-start(f16[4,9,8,1,8,128]{5,4,2,1,3,0:T(8,128)(2,1)S(1)} %pad_maximum_fusion.1), channel_id=1, source_target_pairs={{0,2},{2,0},{4,6},{6,4},{8,10},{10,8},{12,14},{14,12},{16,18},{18,... | collective-permute-start | bytes 1769480 | tf_op jit(solution)/shard_map/ppermute | solution.py:319
  85.2 2.8 %collective-permute-start.32 = (f32[2,8,128]{2,1,0:T(8,128)S(1)}, f32[2,8,128]{2,1,0:T(8,128)S(1)}, u32[]{:S(2)}, u32[]{:S(2)}) collective-permute-start(f32[2,8,128]{2,1,0:T(8,128)S(1)} %fusion.53), channel_id=1, source_target_pairs={{0,2},{2,0},{4,6},{6,4},{8,10},{10,8},{12,14},{14,12},{16,18},{18,... | collective-permute-start | bytes 24584 | tf_op jit(solution)/shard_map/ppermute | solution.py:319
  85.5 6.9 %collective-permute-start.25 = (f16[4,9,8,1,8,128]{5,4,2,1,3,0:T(8,128)(2,1)S(1)}, f16[4,9,8,1,8,128]{5,4,2,1,3,0:T(8,128)(2,1)S(1)}, u32[]{:S(2)}, u32[]{:S(2)}) collective-permute-start(f16[4,9,8,1,8,128]{5,4,2,1,3,0:T(8,128)(2,1)S(1)} %pad_maximum_fusion.2), channel_id=1, source_target_pairs={{0,2},{2,0},{4,6},{6,4},{8,10},{10,8},{12,14},{14,12},{16,18},{18,... | collective-permute-start | bytes 1769480 | tf_op jit(solution)/shard_map/ppermute | solution.py:319
  86.0 5.8 %collective-permute-start.30 = (f16[9,8,1,8,128]{4,3,1,0,2:T(8,128)(2,1)S(1)}, f16[9,8,1,8,128]{4,3,1,0,2:T(8,128)(2,1)S(1)}, u32[]{:S(2)}, u32[]{:S(2)}) collective-permute-start(f16[9,8,1,8,128]{4,3,1,0,2:T(8,128)(2,1)S(1)} %collective-permute-done.24), channel_id=1, source_target_pairs={{0,4},{2,6},{4,0},{6,2},{8,12},{10,14},{12,8},{14,10},{16,20},{18,... | collective-permute-start | bytes 442376 | tf_op jit(solution)/shard_map/ppermute | solution.py:319
  91.9 1.5 %collective-permute-start.31 = (f16[1,9,8,1,8,128]{5,4,2,1,3,0:T(8,128)(2,1)S(1)}, f16[1,9,8,1,8,128]{5,4,2,1,3,0:T(8,128)(2,1)S(1)}, u32[]{:S(2)}, u32[]{:S(2)}) collective-permute-start(f16[1,9,8,1,8,128]{5,4,2,1,3,0:T(8,128)(2,1)S(1)} %bitcast.394), channel_id=1, source_target_pairs={{0,2},{2,0},{4,6},{6,4},{8,10},{10,8},{12,14},{14,12},{16,18},{18,... | collective-permute-start | bytes 442376 | tf_op jit(solution)/shard_map/ppermute | solution.py:319

commit v6 on v5

--- a/solution.py
+++ b/solution.py
@@ -337,7 +337,8 @@
         first = 0
     other_x = to_core(lax.dynamic_slice_in_dim(x, (1 - core) * core_rows, core_rows, 0))
     where = jnp.stack([core, column * depth + level]).astype(jnp.int32)
-    halves, exponents, arrived, sends = [], [], [], []
+    halves, exponents, arrived, sends, gathers = [], [], [], [], []
+    bits_of_depth = [1 << shift for shift in range(depth.bit_length() - 1)]
     grad = jnp.zeros((taps, rows // TILE, 2, TILE, LANES), jnp.float16)
     after = own_cot
     for side in range(2):
@@ -358,11 +359,11 @@
         after = sent[0, 0].astype(jnp.float32)
         bits = 1.0
         gates = (sends[-1],) if side else ()
-        for bit in [1 << shift for shift in range(depth.bit_length() - 1)]:
+        for bit in bits_of_depth:
             for step in range(depth - bit, 0, -2 * bit):
                 pair = summed(held[step], bits, *gates)
                 held[step ^ bit].append((to_level(pair, bit), bits))
-                gates = (pair, halves[0]) if side else (pair,)
+                gates = (pair, halves[0]) if side and step == 1 else (pair,)
                 sends.append(pair)
             bits += 1.0
         lowest = common_exponent(held[0], bits)
@@ -371,42 +372,62 @@
         halves.append(shard)
         exponents.append(lowest)
 
-        near = [shard]
+        near = [shard] + [None] * (depth - 1)
+        for bit in bits_of_depth[::-1]:
+            near[bit] = to_level(shard, bit)
+        own = to_column(shard)
+        arrived = [own]
+        gathers.append((near, own))
+
+    for side, (near, own) in enumerate(gathers):
         for step in range(1, depth):
-            low = step & -step
-            source = near[step ^ low]
-            if side == 1 and step == depth - 1:
-                source = later(source, rest)
-            near.append(to_level(source, low))
+            if near[step] is None:
+                low = step & -step
+                source = near[step ^ low] if side else later(near[step ^ low], gathers[1][0][1])
+                near[step] = to_level(source, low)
+        steps = list(range(depth))
+        cuts = [steps[1:2], steps[2:]] if side == 0 else [steps[1:]]
+        here = [jnp.stack([near[step] for step in cut]) for cut in cuts]
+        if side == 1:
+            here = [later(values, returned) for values in here]
+        there = [to_column(values) for values in here]
         if side == 0:
-            rest = to_column(jnp.stack(near[1:]))
-            far = [to_column(shard)] + [rest[step] for step in range(depth - 1)]
-            arrived = [near[depth // 2], far[0]]
-            groups = ((column, near), (1 - column, far))
+            returned = there[1]
+        here, there = [near[0][None]] + here, [own[None]] + there
+        pieces = [(column, step, near[step]) for step in steps]
+        arrivals = [(steps[0], own)] + [
+            (step, values[slot])
+            for cut, values in zip(cuts, there[1:])
+            for slot, step in enumerate(cut)
+        ]
+        pieces += [(1 - column, step, value) for step, value in arrivals]
+        if side == 0:
+            messages = [(pieces, jnp.concatenate(here + there))]
         else:
-            far = [to_column(value) for value in near]
-            groups = ((column, near), (1 - column, far[:-1]), (1 - column, far[-1:]))
+            count = depth + 1
+            messages = [
+                (pieces[:count], jnp.concatenate(here + there[:1])),
+                (pieces[count:], there[1]),
+            ]
         lane = first if side == 0 else 1 - first
-        step = 0
-        for chip, values in groups:
-            across = to_core(jnp.stack(values))
-            for slot, value in enumerate(values):
-                row = chip * chip_tiles + (level ^ (step % depth)) * shard_tiles
-                step += 1
-                for base, piece in ((core, value), (1 - core, across[slot])):
+        for listed, message in messages:
+            across = to_core(message)
+            for slot, (chip, step, piece) in enumerate(listed):
+                row = chip * chip_tiles + (level ^ step) * shard_tiles
+                for base, value in ((core, piece), (1 - core, across[slot])):
                     grad = lax.dynamic_update_slice(
-                        grad, piece, (0, base * core_tiles + row, lane, 0, 0)
+                        grad, value, (0, base * core_tiles + row, lane, 0, 0)
                     )
     exponents = [jnp.where(first == side, exponents[0], exponents[1]) for side in range(2)]
     exponent = jnp.concatenate(exponents, 0)
-    other = to_core(exponent + 0.0 * token(near[-1][0, 0])[0])
+    other = to_core(later(exponent, returned))
     by_core = [jnp.where(core == side, exponent, other) for side in range(2)]
     factor = jnp.exp2(-jnp.stack(by_core)) * (1.0 / samples)
     grad = grad.reshape(taps, 2, core_tiles, 2, TILE, LANES).astype(jnp.float32)
     grad = (grad * factor[None, :, None]).reshape(taps, rows // TILE, 2, TILE, LANES)
     weight_grad = jnp.transpose(grad, (1, 3, 0, 2, 4)).reshape(rows, taps, outs)
 
-    total = forward(x, w, token(sends[depth - 2]))
+    total = forward(x, w, token(halves[1][0, 0]))
     if chans == 2:
         mine = lax.dynamic_slice_in_dim(total, chan * own_outs, own_outs, 0)
         theirs = lax.dynamic_slice_in_dim(total, (1 - chan) * own_outs, own_outs, 0)
@@ -419,7 +440,7 @@
     else:
         result = lax.psum_scatter(total, "chan", scatter_dimension=0, tiled=True)
     result = result.astype(jnp.bfloat16)[None]
-    input_grad = input_gradient(cot, w, token(halves[1][0, 0]))[None]
+    input_grad = input_gradient(cot, w, token(returned[0, 0, 0]))[None]
     return (result, input_grad, weight_grad)
 
 

time: 98.6 us -> 103 us (1.045)
  starting transfers between devices: 36.1 us -> 38 us
  waiting for transfers between devices: 24.4 us -> 26 us
  local copies, waits for them, and re-layouts: 5.86 us -> 7.27 us
    ppermute x31 -> x28, starting transfers between devices: 31.5 us -> 33.5 us  [to(): lax.ppermute(value, 'dp', [(i, i ^ distance) for i in range(samples)])]
    ppermute x31 -> x28, waiting for transfers between devices: 24.4 us -> 26 us  [to(): lax.ppermute(value, 'dp', [(i, i ^ distance) for i in range(samples)])]
    dynamic_update_slice x32 -> x33, local copies, waits for them, and re-layouts: 2.01 us -> 2.94 us  [on_device(): lax.dynamic_update_slice(grad, value, (0, base * core_tiles + row, lane,...]
  transfers between devices with their start and end apart: 33 -> 30, of which waited for: 10 -> 10; matrix products, arithmetic and copies ran while one was open for 7% -> 7% of each run, Pallas kernels for 22% -> 22%
where the time goes in v6:
time: 103 us
  starting transfers between devices  38 us (37%)
  waiting for transfers between devices  26 us (25%)
  Pallas kernels  22.3 us (22%)
  other arithmetic  7.55 us (7%)
  local copies, waits for them, and re-layouts  7.27 us (7%)
  between operations  1.96 us (2%)
    ppermute x28, starting transfers between devices, to(): lax.ppermute(value, 'dp', [(i, i ^ distance) for i in range(samples)])  33.5 us
    ppermute x28, waiting for transfers between devices, to(): lax.ppermute(value, 'dp', [(i, i ^ distance) for i in range(samples)])  26 us
    pallas_call x2, Pallas kernels, kernel_grad(): pl.pallas_call(functools.partial(kernel_grad_kernel, depth), out_shape=[j...  10.7 us
    pallas_call x1, Pallas kernels, input_gradient(): pl.pallas_call(input_grad_kernel, out_shape=jax.ShapeDtypeStruct((rows, p...  6.54 us
    pallas_call x1, Pallas kernels, forward(): pl.pallas_call(forward_kernel, out_shape=jax.ShapeDtypeStruct((outs, posi...  5.03 us
    reshape x1, other arithmetic, on_device(): weight_grad = jnp.transpose(grad, (1, 3, 0, 2, 4)).reshape(rows, taps, outs)  4.63 us
    ppermute x1, starting transfers between devices, on_device(): their_cot = lax.ppermute(own_cot, 'chan', [(0, 1), (1, 0)])  2.95 us
    dynamic_update_slice x33, local copies, waits for them, and re-layouts, on_device(): lax.dynamic_update_slice(grad, value, (0, base * core_tiles + row, lane,...  2.94 us
  transfers between devices with their start and end apart: 30, of which 10 were waited for; matrix products, arithmetic and copies ran while one was open for 7% of the time, Pallas kernels for 22%

profile of v6, /device:TPU:0, one launch (start us, length us, event | category | flops | bytes accessed | tf_op | source)
XLA Modules:
  0.0 103.1 jit_solution(5774384722236849413)
XLA Ops:
  0.7 1.4 %dynamic-slice_bitcast_fusion = bf16[512,1152]{1,0:T(8,128)(2,1)S(1)} fusion(bf16[1,1024,1152]{2,1,0:T(8,128)(2,1)} %param.3, s32[]{:T(128)S(6)} %select_n.221), kind=kLoop, calls=%fused_computation.1 | loop fusion | bytes 2359300 | tf_op jit(solution)/shard_map/dynamic_slice | solution.py:338
  2.0 0.5 collective-permute-start
  2.6 2.9 %collective-permute-start.8 = (bf16[128,1152]{1,0:T(8,128)(2,1)}, bf16[128,1152]{1,0:T(8,128)(2,1)S(1)}, u32[]{:S(2)}, u32[]{:S(2)}) collective-permute-start(bf16[128,1152]{1,0:T(8,128)(2,1)} %bitcast.355), channel_id=1, source_target_pairs={{0,1},{1,0},{2,3},{3,2},{4,5},{5,4},{6,7},{7,6},{8,9},{9,8},{10,11... | collective-permute-start | bytes 884744 | tf_op jit(solution)/shard_map/ppermute | solution.py:331
  5.6 1.0 copy-done.1
  6.6 5.2 %kernel_grad.2 = (f32[73,8,128]{2,1,0:T(8,128)S(1)}, f32[73,8,128]{2,1,0:T(8,128)S(1)}, f32[73,8,128]{2,1,0:T(8,128)S(1)}, f32[73,8,128]{2,1,0:T(8,128)S(1)}, f3...) custom-call(s32[2]{0:T(128)S(1)} %pad_add_fusion.place_ref, bf16[1024,1152]{1,0:T(8,128)(2,1)} %bitcast.351, ...), custom_call_target="tpu_custom_call" | custom-call | flops 1509949440 | bytes 5308416 | tf_op jit(solution)/shard_map/kernel_grad/pallas_call | solution.py:122
  11.9 2.7 %collective-permute-start.3 = (f16[2,73,8,128]{3,2,1,0:T(8,128)(2,1)S(1)}, f16[2,73,8,128]{3,2,1,0:T(8,128)(2,1)S(1)}, u32[]{:S(2)}, u32[]{:S(2)}) collective-permute-start(f16[2,73,8,128]{3,2,1,0:T(8,128)(2,1)S(1)} %convert_element_type.326), channel_id=1, source_target_pairs={{0,4},{2,6},{4,0},{6,2},{8,12},{10,14},{12,8},{14,10},{16,20},{18,... | collective-permute-start | bytes 897032 | tf_op jit(solution)/shard_map/ppermute | solution.py:319
  14.8 0.5 slice.262
  16.2 1.4 %collective-permute-done.9.other_cot = bf16[128,1152]{1,0:T(8,128)(2,1)S(1)} collective-permute-done((bf16[128,1152]{1,0:T(8,128)(2,1)S(1)}, bf16[128,1152]{1,0:T(8,128)(2,1)S(1)}, u32[]{:S(2)}, u32[]{:S(2)}) %collective-permute-start.9) | collective-permute-done | bytes 294944 | tf_op jit(solution)/shard_map/ppermute | solution.py:319
  17.7 5.5 %kernel_grad.3 = (f32[73,8,128]{2,1,0:T(8,128)S(1)}, f32[73,8,128]{2,1,0:T(8,128)S(1)}, f32[73,8,128]{2,1,0:T(8,128)S(1)}, f32[73,8,128]{2,1,0:T(8,128)S(1)}, f3...) custom-call(s32[2]{0:T(128)S(1)} %pad_add_fusion.place_ref, bf16[1024,1152]{1,0:T(8,128)(2,1)} %bitcast.352, ...), custom_call_target="tpu_custom_call" | custom-call | flops 1509949440 | bytes 5308416 | tf_op jit(solution)/shard_map/kernel_grad/pallas_call | solution.py:122
  23.2 2.1 %collective-permute-start.11 = (f16[2,73,8,128]{3,2,1,0:T(8,128)(2,1)S(1)}, f16[2,73,8,128]{3,2,1,0:T(8,128)(2,1)S(1)}, u32[]{:S(2)}, u32[]{:S(2)}) collective-permute-start(f16[2,73,8,128]{3,2,1,0:T(8,128)(2,1)S(1)} %convert_element_type.362), channel_id=1, source_target_pairs={{0,4},{2,6},{4,0},{6,2},{8,12},{10,14},{12,8},{14,10},{16,20},{18,... | collective-permute-start | bytes 897032 | tf_op jit(solution)/shard_map/ppermute | solution.py:319
  25.6 2.1 %collective-permute-start.5 = (f16[73,8,128]{2,1,0:T(8,128)(2,1)S(1)}, f16[73,8,128]{2,1,0:T(8,128)(2,1)S(1)}, u32[]{:S(2)}, u32[]{:S(2)}) collective-permute-start(f16[73,8,128]{2,1,0:T(8,128)(2,1)S(1)} %constant_dynamic-update-slice_fusion.15), channel_id=1, source_target_pairs={{0,8},{2,10},{4,12},{6,14},{8,0},{10,2},{12,4},{14,6},{16,24},{18,... | collective-permute-start | bytes 448520 | tf_op jit(solution)/shard_map/ppermute | solution.py:319
  27.7 1.2 %collective-permute-done.2 = f16[2,73,8,128]{3,2,1,0:T(8,128)(2,1)S(1)} collective-permute-done((f16[2,73,8,128]{3,2,1,0:T(8,128)(2,1)S(1)}, f16[2,73,8,128]{3,2,1,0:T(8,128)(2,1)S(1)}, u32[]{:S(2)}, u32[]{:S(2)}) %collective-permute-start.2) | collective-permute-done | bytes 299040 | tf_op jit(solution)/shard_map/ppermute | solution.py:319
  29.0 2.2 %collective-permute-start.4 = (f16[73,8,128]{2,1,0:T(8,128)(2,1)S(1)}, f16[73,8,128]{2,1,0:T(8,128)(2,1)S(1)}, u32[]{:S(2)}, u32[]{:S(2)}) collective-permute-start(f16[73,8,128]{2,1,0:T(8,128)(2,1)S(1)} %constant_dynamic-update-slice_fusion.14), channel_id=1, source_target_pairs={{0,8},{2,10},{4,12},{6,14},{8,0},{10,2},{12,4},{14,6},{16,24},{18,... | collective-permute-start | bytes 448520 | tf_op jit(solution)/shard_map/ppermute | solution.py:319
  31.3 0.3 collective-permute-done.5
  31.8 3.1 %collective-permute-start.6 = (f16[73,8,128]{2,1,0:T(8,128)(2,1)S(1)}, f16[73,8,128]{2,1,0:T(8,128)(2,1)S(1)}, u32[]{:S(2)}, u32[]{:S(2)}) collective-permute-start(f16[73,8,128]{2,1,0:T(8,128)(2,1)S(1)} %constant_dynamic-update-slice_fusion.13), channel_id=1, source_target_pairs={{0,16},{2,18},{4,20},{6,22},{8,24},{10,26},{12,28},{14,30},{16,0},... | collective-permute-start | bytes 448520 | tf_op jit(solution)/shard_map/ppermute | solution.py:319
  34.9 0.4 collective-permute-done.11
  35.4 2.2 %collective-permute-start.13 = (f16[73,8,128]{2,1,0:T(8,128)(2,1)S(1)}, f16[73,8,128]{2,1,0:T(8,128)(2,1)S(1)}, u32[]{:S(2)}, u32[]{:S(2)}) collective-permute-start(f16[73,8,128]{2,1,0:T(8,128)(2,1)S(1)} %constant_dynamic-update-slice_fusion.12), channel_id=1, source_target_pairs={{0,8},{2,10},{4,12},{6,14},{8,0},{10,2},{12,4},{14,6},{16,24},{18,... | collective-permute-start | bytes 448520 | tf_op jit(solution)/shard_map/ppermute | solution.py:319
  37.7 3.7 %collective-permute-done.10 = f16[2,73,8,128]{3,2,1,0:T(8,128)(2,1)S(1)} collective-permute-done((f16[2,73,8,128]{3,2,1,0:T(8,128)(2,1)S(1)}, f16[2,73,8,128]{3,2,1,0:T(8,128)(2,1)S(1)}, u32[]{:S(2)}, u32[]{:S(2)}) %collective-permute-start.10) | collective-permute-done | bytes 299040 | tf_op jit(solution)/shard_map/ppermute | solution.py:319
  41.5 1.9 %collective-permute-start.12 = (f16[73,8,128]{2,1,0:T(8,128)(2,1)S(1)}, f16[73,8,128]{2,1,0:T(8,128)(2,1)S(1)}, u32[]{:S(2)}, u32[]{:S(2)}) collective-permute-start(f16[73,8,128]{2,1,0:T(8,128)(2,1)S(1)} %constant_dynamic-update-slice_fusion.11), channel_id=1, source_target_pairs={{0,8},{2,10},{4,12},{6,14},{8,0},{10,2},{12,4},{14,6},{16,24},{18,... | collective-permute-start | bytes 448520 | tf_op jit(solution)/shard_map/ppermute | solution.py:319
  43.5 0.1 fusion.29
  43.6 0.3 collective-permute-start.20
  43.9 2.8 %collective-permute-start.16 = (f16[9,8,1,8,128]{4,3,1,0,2:T(8,128)(2,1)S(1)}, f16[9,8,1,8,128]{4,3,1,0,2:T(8,128)(2,1)S(1)}, u32[]{:S(2)}, u32[]{:S(2)}) collective-permute-start(f16[9,8,1,8,128]{4,3,1,0,2:T(8,128)(2,1)S(1)} %bitcast.372), channel_id=1, source_target_pairs={{0,16},{2,18},{4,20},{6,22},{8,24},{10,26},{12,28},{14,30},{16,0},... | collective-permute-start | bytes 442376 | tf_op jit(solution)/shard_map/ppermute | solution.py:319
  46.7 1.5 %collective-permute-start.7 = (f16[9,8,1,8,128]{4,3,1,0,2:T(8,128)(2,1)S(1)}, f16[9,8,1,8,128]{4,3,1,0,2:T(8,128)(2,1)S(1)}, u32[]{:S(2)}, u32[]{:S(2)}) collective-permute-start(f16[9,8,1,8,128]{4,3,1,0,2:T(8,128)(2,1)S(1)} %bitcast.374), channel_id=1, source_target_pairs={{0,4},{2,6},{4,0},{6,2},{8,12},{10,14},{12,8},{14,10},{16,20},{18,... | collective-permute-start | bytes 442376 | tf_op jit(solution)/shard_map/ppermute | solution.py:319
  48.2 0.9 broadcast_in_dim.100
  49.4 0.4 collective-permute-start.14
  49.8 4.9 %collective-permute-done.20 = f16[9,8,1,8,128]{4,3,1,0,2:T(8,128)(2,1)S(1)} collective-permute-done((f16[9,8,1,8,128]{4,3,1,0,2:T(8,128)(2,1)S(1)}, f16[9,8,1,8,128]{4,3,1,0,2:T(8,128)(2,1)S(1)}, u32[]{:S(2)}, u32[]{:S(2)}) %collective-permute-start.20) | collective-permute-done | bytes 147488 | tf_op jit(solution)/shard_map/ppermute | solution.py:319
  54.7 2.0 %collective-permute-start.21 = (f16[1,9,8,1,8,128]{5,4,3,2,1,0:T(8,128)(2,1)S(1)}, f16[1,9,8,1,8,128]{5,4,3,2,1,0:T(8,128)(2,1)S(1)}, u32[]{:S(2)}, u32[]{:S(2)}) collective-permute-start(f16[1,9,8,1,8,128]{5,4,3,2,1,0:T(8,128)(2,1)S(1)} %bitcast.380), channel_id=1, source_target_pairs={{0,4},{2,6},{4,0},{6,2},{8,12},{10,14},{12,8},{14,10},{16,20},{18,... | collective-permute-start | bytes 442376 | tf_op jit(solution)/shard_map/ppermute | solution.py:319
  56.9 3.6 %collective-permute-done.14 = f16[73,8,128]{2,1,0:T(8,128)(2,1)S(1)} collective-permute-done((f16[73,8,128]{2,1,0:T(8,128)(2,1)S(1)}, f16[73,8,128]{2,1,0:T(8,128)(2,1)S(1)}, u32[]{:S(2)}, u32[]{:S(2)}) %collective-permute-start.14) | collective-permute-done | bytes 149536 | tf_op jit(solution)/shard_map/ppermute | solution.py:319
  60.5 0.1 fusion.25
  60.7 3.2 %collective-permute-start.23 = (f16[9,8,1,8,128]{4,3,1,0,2:T(8,128)(2,1)S(1)}, f16[9,8,1,8,128]{4,3,1,0,2:T(8,128)(2,1)S(1)}, u32[]{:S(2)}, u32[]{:S(2)}) collective-permute-start(f16[9,8,1,8,128]{4,3,1,0,2:T(8,128)(2,1)S(1)} %bitcast.366), channel_id=1, source_target_pairs={{0,16},{2,18},{4,20},{6,22},{8,24},{10,26},{12,28},{14,30},{16,0},... | collective-permute-start | bytes 442376 | tf_op jit(solution)/shard_map/ppermute | solution.py:319
  64.0 1.1 %collective-permute-start.25 = (f16[9,8,1,8,128]{4,3,1,0,2:T(8,128)(2,1)S(1)}, f16[9,8,1,8,128]{4,3,1,0,2:T(8,128)(2,1)S(1)}, u32[]{:S(2)}, u32[]{:S(2)}) collective-permute-start(f16[9,8,1,8,128]{4,3,1,0,2:T(8,128)(2,1)S(1)} %bitcast.367), channel_id=1, source_target_pairs={{0,4},{2,6},{4,0},{6,2},{8,12},{10,14},{12,8},{14,10},{16,20},{18,... | collective-permute-start | bytes 442376 | tf_op jit(solution)/shard_map/ppermute | solution.py:319
  65.1 5.0 %forward.1 = f32[256,1152]{1,0:T(8,128)S(1)} custom-call(bf16[1024,1152]{1,0:T(8,128)(2,1)S(1)} %bitcast.353, bf16[9,1024,256]{2,1,0:T(8,128)(2,1)S(1)} %bitcast.361, f32[8,128]{1,0:T(8,128)S(1)} %fusion.142._), custom_call_target="tpu_custom_call" | custom-call | flops 3019898880 | bytes 8257536 | tf_op jit(solution)/shard_map/forward/pallas_call | solution.py:194
  70.2 0.1 collective-permute-start.18
  70.4 1.6 %collective-permute-start.15 = (f32[128,1152]{1,0:T(8,128)S(1)}, f32[128,1152]{1,0:T(8,128)S(1)}, u32[]{:S(2)}, u32[]{:S(2)}) collective-permute-start(f32[128,1152]{1,0:T(8,128)S(1)} %constant_dynamic-slice_fusion), channel_id=1, source_target_pairs={{0,1},{1,0},{2,3},{3,2},{4,5},{5,4},{6,7},{7,6},{8,9},{9,8},{10,11... | collective-permute-start | bytes 1769480 | tf_op jit(solution)/shard_map/ppermute | solution.py:434
  72.0 1.9 %collective-permute-start.24 = (f16[9,8,1,8,128]{4,3,1,0,2:T(8,128)(2,1)S(1)}, f16[9,8,1,8,128]{4,3,1,0,2:T(8,128)(2,1)S(1)}, u32[]{:S(2)}, u32[]{:S(2)}) collective-permute-start(f16[9,8,1,8,128]{4,3,1,0,2:T(8,128)(2,1)S(1)} %collective-permute-done.23), channel_id=1, source_target_pairs={{0,8},{2,10},{4,12},{6,14},{8,0},{10,2},{12,4},{14,6},{16,24},{18,... | collective-permute-start | bytes 442376 | tf_op jit(solution)/shard_map/ppermute | solution.py:319
  74.0 1.5 %collective-permute-done.18 = f16[9,8,1,8,128]{4,3,1,0,2:T(8,128)(2,1)S(1)} collective-permute-done((f16[9,8,1,8,128]{4,3,1,0,2:T(8,128)(2,1)S(1)}, f16[9,8,1,8,128]{4,3,1,0,2:T(8,128)(2,1)S(1)}, u32[]{:S(2)}, u32[]{:S(2)}) %collective-permute-start.18) | collective-permute-done | bytes 147488 | tf_op jit(solution)/shard_map/ppermute | solution.py:319
  75.5 1.1 %collective-permute-start.19 = (f16[2,9,8,1,8,128]{5,4,3,2,1,0:T(8,128)(2,1)S(1)}, f16[2,9,8,1,8,128]{5,4,3,2,1,0:T(8,128)(2,1)S(1)}, u32[]{:S(2)}, u32[]{:S(2)}) collective-permute-start(f16[2,9,8,1,8,128]{5,4,3,2,1,0:T(8,128)(2,1)S(1)} %maximum_bitcast_fusion), channel_id=1, source_target_pairs={{0,4},{2,6},{4,0},{6,2},{8,12},{10,14},{12,8},{14,10},{16,20},{18,... | collective-permute-start | bytes 884744 | tf_op jit(solution)/shard_map/ppermute | solution.py:319
  76.8 5.6 %collective-permute-done.19 = f16[2,9,8,1,8,128]{5,4,3,2,1,0:T(8,128)(2,1)S(1)} collective-permute-done((f16[2,9,8,1,8,128]{5,4,3,2,1,0:T(8,128)(2,1)S(1)}, f16[2,9,8,1,8,128]{5,4,3,2,1,0:T(8,128)(2,1)S(1)}, u32[]{:S(2)}, u32[]{:S(2)}) %collective-permute-start.19) | collective-permute-done | bytes 294944 | tf_op jit(solution)/shard_map/ppermute | solution.py:319
  82.5 0.2 maximum_select_fusion.1
  82.7 1.1 %collective-permute-start.27 = (f16[3,9,8,1,8,128]{5,4,2,1,3,0:T(8,128)(2,1)S(1)}, f16[3,9,8,1,8,128]{5,4,2,1,3,0:T(8,128)(2,1)S(1)}, u32[]{:S(2)}, u32[]{:S(2)}) collective-permute-start(f16[3,9,8,1,8,128]{5,4,2,1,3,0:T(8,128)(2,1)S(1)} %maximum_select_fusion.1), channel_id=1, source_target_pairs={{0,4},{2,6},{4,0},{6,2},{8,12},{10,14},{12,8},{14,10},{16,20},{18,... | collective-permute-start | bytes 1327112 | tf_op jit(solution)/shard_map/ppermute | solution.py:319
  83.8 0.2 pad_maximum_fusion
  84.0 0.3 collective-permute-start.26
  84.3 0.3 collective-permute-start.29
  84.6 0.8 fusion.20
  85.4 6.5 %input_gradient.1 = bf16[1024,1152]{1,0:T(8,128)(2,1)} custom-call(bf16[256,1152]{1,0:T(8,128)(2,1)S(1)} %maximum_select_fusion.cot_ref, bf16[9,1024,256]{2,1,0:T(8,128)(2,1)S(1)} %bitcast.362, f32[8,128]{1,0:T(8,128)S(1)} %fusion.141._), custom_call_target="tpu_custom_call" | custom-call | flops 3019898880 | bytes 7667712 | tf_op jit(solution)/shard_map/input_gradient/pallas_call | solution.py:242
  92.0 3.3 %collective-permute-done.27 = f16[3,9,8,1,8,128]{5,4,2,1,3,0:T(8,128)(2,1)S(1)} collective-permute-done((f16[3,9,8,1,8,128]{5,4,2,1,3,0:T(8,128)(2,1)S(1)}, f16[3,9,8,1,8,128]{5,4,2,1,3,0:T(8,128)(2,1)S(1)}, u32[]{:S(2)}, u32[]{:S(2)}) %collective-permute-start.27) | collective-permute-done | bytes 442400 | tf_op jit(solution)/shard_map/ppermute | solution.py:319
  96.1 1.0 %copy.10 = f16[9,128,2,8,128]{4,3,2,1,0:T(8,128)(2,1)S(1)} copy(f16[9,128,2,8,128]{4,3,1,0,2:T(8,128)(2,1)S(1)} %fusion.43) | data formatting | bytes 9437184 | tf_op jit(solution)/shard_map/dynamic_update_slice | solution.py:418
  98.5 4.6 %multiply_bitcast_fusion = f32[1024,9,256]{2,0,1:T(8,128)} fusion(f16[9,128,2,8,128]{4,3,2,1,0:T(8,128)(2,1)S(1)} %fusion.30, f32[128,2,8,128]{3,2,1,0:T(8,128)S(1)} %bitcast.363), kind=kLoop, calls=%fused_computation | loop fusion | flops 4718592 | bytes 15204352 | tf_op jit(solution)/shard_map/reshape | solution.py:428
  (128 shorter events, 4.4 us)
Async XLA Ops:
  2.0 3.6 %collective-permute-start = (bf16[512,1152]{1,0:T(8,128)(2,1)S(1)}, bf16[512,1152]{1,0:T(8,128)(2,1)S(1)}, u32[]{:S(2)}, u32[]{:S(2)}) collective-permute-start(bf16[512,1152]{1,0:T(8,128)(2,1)S(1)} %dynamic-slice_bitcast_fusion), channel_id=1, source_target_pairs={{0,2},{2,0},{4,6},{6,4},{8,10},{10,8},{12,14},{14,12},{16,18},{18,... | collective-permute-start | bytes 3538952 | tf_op jit(solution)/shard_map/ppermute | solution.py:319
  2.5 3.1 %collective-permute-start.1 = (bf16[128,1152]{1,0:T(8,128)(2,1)}, bf16[128,1152]{1,0:T(8,128)(2,1)S(1)}, u32[]{:S(2)}, u32[]{:S(2)}) collective-permute-start(bf16[128,1152]{1,0:T(8,128)(2,1)} %bitcast.354), channel_id=1, source_target_pairs={{0,2},{2,0},{4,6},{6,4},{8,10},{10,8},{12,14},{14,12},{16,18},{18,... | collective-permute-start | bytes 884744 | tf_op jit(solution)/shard_map/ppermute | solution.py:319
  2.6 13.3 %collective-permute-start.8 = (bf16[128,1152]{1,0:T(8,128)(2,1)}, bf16[128,1152]{1,0:T(8,128)(2,1)S(1)}, u32[]{:S(2)}, u32[]{:S(2)}) collective-permute-start(bf16[128,1152]{1,0:T(8,128)(2,1)} %bitcast.355), channel_id=1, source_target_pairs={{0,1},{1,0},{2,3},{3,2},{4,5},{5,4},{6,7},{7,6},{8,9},{9,8},{10,11... | collective-permute-start | bytes 884744 | tf_op jit(solution)/shard_map/ppermute | solution.py:331
  5.6 1.0 copy-start.1
  11.9 13.5 %collective-permute-start.3 = (f16[2,73,8,128]{3,2,1,0:T(8,128)(2,1)S(1)}, f16[2,73,8,128]{3,2,1,0:T(8,128)(2,1)S(1)}, u32[]{:S(2)}, u32[]{:S(2)}) collective-permute-start(f16[2,73,8,128]{3,2,1,0:T(8,128)(2,1)S(1)} %convert_element_type.326), channel_id=1, source_target_pairs={{0,4},{2,6},{4,0},{6,2},{8,12},{10,14},{12,8},{14,10},{16,20},{18,... | collective-permute-start | bytes 897032 | tf_op jit(solution)/shard_map/ppermute | solution.py:319
  14.7 14.2 %collective-permute-start.2 = (f16[2,73,8,128]{3,2,1,0:T(8,128)(2,1)S(1)}, f16[2,73,8,128]{3,2,1,0:T(8,128)(2,1)S(1)}, u32[]{:S(2)}, u32[]{:S(2)}) collective-permute-start(f16[2,73,8,128]{3,2,1,0:T(8,128)(2,1)S(1)} %select_convert_fusion.1), channel_id=1, source_target_pairs={{0,4},{2,6},{4,0},{6,2},{8,12},{10,14},{12,8},{14,10},{16,20},{18,... | collective-permute-start | bytes 897032 | tf_op jit(solution)/shard_map/ppermute | solution.py:319
  16.0 1.6 %collective-permute-start.9 = (bf16[128,1152]{1,0:T(8,128)(2,1)S(1)}, bf16[128,1152]{1,0:T(8,128)(2,1)S(1)}, u32[]{:S(2)}, u32[]{:S(2)}) collective-permute-start(bf16[128,1152]{1,0:T(8,128)(2,1)S(1)} %broadcast_select_fusion.own_cot), channel_id=1, source_target_pairs={{0,2},{2,0},{4,6},{6,4},{8,10},{10,8},{12,14},{14,12},{16,18},{18,... | collective-permute-start | bytes 884744 | tf_op jit(solution)/shard_map/ppermute | solution.py:319
  17.7 47.5 %slice-start = ((s8[4718592]{0:T(1024)(128)(4,1)}), s8[4194304]{0:T(1024)(128)(4,1)S(1)}, s32[]{:S(2)}) async-start(s8[4718592]{0:T(1024)(128)(4,1)} %bitcast.359), calls=%async_computation | async-start | bytes 8388608
  23.2 12.1 %collective-permute-start.11 = (f16[2,73,8,128]{3,2,1,0:T(8,128)(2,1)S(1)}, f16[2,73,8,128]{3,2,1,0:T(8,128)(2,1)S(1)}, u32[]{:S(2)}, u32[]{:S(2)}) collective-permute-start(f16[2,73,8,128]{3,2,1,0:T(8,128)(2,1)S(1)} %convert_element_type.362), channel_id=1, source_target_pairs={{0,4},{2,6},{4,0},{6,2},{8,12},{10,14},{12,8},{14,10},{16,20},{18,... | collective-permute-start | bytes 897032 | tf_op jit(solution)/shard_map/ppermute | solution.py:319
  25.4 16.0 %collective-permute-start.10 = (f16[2,73,8,128]{3,2,1,0:T(8,128)(2,1)S(1)}, f16[2,73,8,128]{3,2,1,0:T(8,128)(2,1)S(1)}, u32[]{:S(2)}, u32[]{:S(2)}) collective-permute-start(f16[2,73,8,128]{3,2,1,0:T(8,128)(2,1)S(1)} %select_convert_fusion), channel_id=1, source_target_pairs={{0,4},{2,6},{4,0},{6,2},{8,12},{10,14},{12,8},{14,10},{16,20},{18,... | collective-permute-start | bytes 897032 | tf_op jit(solution)/shard_map/ppermute | solution.py:319
  25.6 6.0 %collective-permute-start.5 = (f16[73,8,128]{2,1,0:T(8,128)(2,1)S(1)}, f16[73,8,128]{2,1,0:T(8,128)(2,1)S(1)}, u32[]{:S(2)}, u32[]{:S(2)}) collective-permute-start(f16[73,8,128]{2,1,0:T(8,128)(2,1)S(1)} %constant_dynamic-update-slice_fusion.15), channel_id=1, source_target_pairs={{0,8},{2,10},{4,12},{6,14},{8,0},{10,2},{12,4},{14,6},{16,24},{18,... | collective-permute-start | bytes 448520 | tf_op jit(solution)/shard_map/ppermute | solution.py:319
  29.0 14.4 %collective-permute-start.4 = (f16[73,8,128]{2,1,0:T(8,128)(2,1)S(1)}, f16[73,8,128]{2,1,0:T(8,128)(2,1)S(1)}, u32[]{:S(2)}, u32[]{:S(2)}) collective-permute-start(f16[73,8,128]{2,1,0:T(8,128)(2,1)S(1)} %constant_dynamic-update-slice_fusion.14), channel_id=1, source_target_pairs={{0,8},{2,10},{4,12},{6,14},{8,0},{10,2},{12,4},{14,6},{16,24},{18,... | collective-permute-start | bytes 448520 | tf_op jit(solution)/shard_map/ppermute | solution.py:319
  31.8 11.6 %collective-permute-start.6 = (f16[73,8,128]{2,1,0:T(8,128)(2,1)S(1)}, f16[73,8,128]{2,1,0:T(8,128)(2,1)S(1)}, u32[]{:S(2)}, u32[]{:S(2)}) collective-permute-start(f16[73,8,128]{2,1,0:T(8,128)(2,1)S(1)} %constant_dynamic-update-slice_fusion.13), channel_id=1, source_target_pairs={{0,16},{2,18},{4,20},{6,22},{8,24},{10,26},{12,28},{14,30},{16,0},... | collective-permute-start | bytes 448520 | tf_op jit(solution)/shard_map/ppermute | solution.py:319
  35.3 29.8 %slice-start.1 = ((s8[4718592]{0:T(1024)(128)(4,1)}), s8[524288]{0:T(1024)(128)(4,1)S(1)}, s32[]{:S(2)}) async-start(s8[4718592]{0:T(1024)(128)(4,1)} %bitcast.359), calls=%async_computation.1 | async-start | bytes 1048576
  35.4 13.8 %collective-permute-start.13 = (f16[73,8,128]{2,1,0:T(8,128)(2,1)S(1)}, f16[73,8,128]{2,1,0:T(8,128)(2,1)S(1)}, u32[]{:S(2)}, u32[]{:S(2)}) collective-permute-start(f16[73,8,128]{2,1,0:T(8,128)(2,1)S(1)} %constant_dynamic-update-slice_fusion.12), channel_id=1, source_target_pairs={{0,8},{2,10},{4,12},{6,14},{8,0},{10,2},{12,4},{14,6},{16,24},{18,... | collective-permute-start | bytes 448520 | tf_op jit(solution)/shard_map/ppermute | solution.py:319
  41.3 23.8 %copy-start = (bf16[1,1024,1152]{2,1,0:T(8,128)(2,1)S(1)}, bf16[1,1024,1152]{2,1,0:T(8,128)(2,1)}, u32[]{:S(2)}) copy-start(bf16[1,1024,1152]{2,1,0:T(8,128)(2,1)} %param.3) | copy-start | bytes 7077892
  41.5 15.4 %collective-permute-start.12 = (f16[73,8,128]{2,1,0:T(8,128)(2,1)S(1)}, f16[73,8,128]{2,1,0:T(8,128)(2,1)S(1)}, u32[]{:S(2)}, u32[]{:S(2)}) collective-permute-start(f16[73,8,128]{2,1,0:T(8,128)(2,1)S(1)} %constant_dynamic-update-slice_fusion.11), channel_id=1, source_target_pairs={{0,8},{2,10},{4,12},{6,14},{8,0},{10,2},{12,4},{14,6},{16,24},{18,... | collective-permute-start | bytes 448520 | tf_op jit(solution)/shard_map/ppermute | solution.py:319
  43.6 11.1 %collective-permute-start.20 = (f16[9,8,1,8,128]{4,3,1,0,2:T(8,128)(2,1)S(1)}, f16[9,8,1,8,128]{4,3,1,0,2:T(8,128)(2,1)S(1)}, u32[]{:S(2)}, u32[]{:S(2)}) collective-permute-start(f16[9,8,1,8,128]{4,3,1,0,2:T(8,128)(2,1)S(1)} %bitcast.371), channel_id=1, source_target_pairs={{0,8},{2,10},{4,12},{6,14},{8,0},{10,2},{12,4},{14,6},{16,24},{18,... | collective-permute-start | bytes 442376 | tf_op jit(solution)/shard_map/ppermute | solution.py:319
  43.9 12.9 %collective-permute-start.16 = (f16[9,8,1,8,128]{4,3,1,0,2:T(8,128)(2,1)S(1)}, f16[9,8,1,8,128]{4,3,1,0,2:T(8,128)(2,1)S(1)}, u32[]{:S(2)}, u32[]{:S(2)}) collective-permute-start(f16[9,8,1,8,128]{4,3,1,0,2:T(8,128)(2,1)S(1)} %bitcast.372), channel_id=1, source_target_pairs={{0,16},{2,18},{4,20},{6,22},{8,24},{10,26},{12,28},{14,30},{16,0},... | collective-permute-start | bytes 442376 | tf_op jit(solution)/shard_map/ppermute | solution.py:319
  46.7 10.1 %collective-permute-start.7 = (f16[9,8,1,8,128]{4,3,1,0,2:T(8,128)(2,1)S(1)}, f16[9,8,1,8,128]{4,3,1,0,2:T(8,128)(2,1)S(1)}, u32[]{:S(2)}, u32[]{:S(2)}) collective-permute-start(f16[9,8,1,8,128]{4,3,1,0,2:T(8,128)(2,1)S(1)} %bitcast.374), channel_id=1, source_target_pairs={{0,4},{2,6},{4,0},{6,2},{8,12},{10,14},{12,8},{14,10},{16,20},{18,... | collective-permute-start | bytes 442376 | tf_op jit(solution)/shard_map/ppermute | solution.py:319
  49.4 11.0 %collective-permute-start.14 = (f16[73,8,128]{2,1,0:T(8,128)(2,1)S(1)}, f16[73,8,128]{2,1,0:T(8,128)(2,1)S(1)}, u32[]{:S(2)}, u32[]{:S(2)}) collective-permute-start(f16[73,8,128]{2,1,0:T(8,128)(2,1)S(1)} %constant_dynamic-update-slice_fusion.10), channel_id=1, source_target_pairs={{0,16},{2,18},{4,20},{6,22},{8,24},{10,26},{12,28},{14,30},{16,0},... | collective-permute-start | bytes 448520 | tf_op jit(solution)/shard_map/ppermute | solution.py:319
  54.7 22.0 %collective-permute-start.21 = (f16[1,9,8,1,8,128]{5,4,3,2,1,0:T(8,128)(2,1)S(1)}, f16[1,9,8,1,8,128]{5,4,3,2,1,0:T(8,128)(2,1)S(1)}, u32[]{:S(2)}, u32[]{:S(2)}) collective-permute-start(f16[1,9,8,1,8,128]{5,4,3,2,1,0:T(8,128)(2,1)S(1)} %bitcast.380), channel_id=1, source_target_pairs={{0,4},{2,6},{4,0},{6,2},{8,12},{10,14},{12,8},{14,10},{16,20},{18,... | collective-permute-start | bytes 442376 | tf_op jit(solution)/shard_map/ppermute | solution.py:319
  60.6 9.5 %collective-permute-start.17 = (f16[9,8,1,8,128]{4,3,1,0,2:T(8,128)(2,1)S(1)}, f16[9,8,1,8,128]{4,3,1,0,2:T(8,128)(2,1)S(1)}, u32[]{:S(2)}, u32[]{:S(2)}) collective-permute-start(f16[9,8,1,8,128]{4,3,1,0,2:T(8,128)(2,1)S(1)} %bitcast.365), channel_id=1, source_target_pairs={{0,8},{2,10},{4,12},{6,14},{8,0},{10,2},{12,4},{14,6},{16,24},{18,... | collective-permute-start | bytes 442376 | tf_op jit(solution)/shard_map/ppermute | solution.py:319
  60.7 11.3 %collective-permute-start.23 = (f16[9,8,1,8,128]{4,3,1,0,2:T(8,128)(2,1)S(1)}, f16[9,8,1,8,128]{4,3,1,0,2:T(8,128)(2,1)S(1)}, u32[]{:S(2)}, u32[]{:S(2)}) collective-permute-start(f16[9,8,1,8,128]{4,3,1,0,2:T(8,128)(2,1)S(1)} %bitcast.366), channel_id=1, source_target_pairs={{0,16},{2,18},{4,20},{6,22},{8,24},{10,26},{12,28},{14,30},{16,0},... | collective-permute-start | bytes 442376 | tf_op jit(solution)/shard_map/ppermute | solution.py:319
  64.0 19.8 %collective-permute-start.25 = (f16[9,8,1,8,128]{4,3,1,0,2:T(8,128)(2,1)S(1)}, f16[9,8,1,8,128]{4,3,1,0,2:T(8,128)(2,1)S(1)}, u32[]{:S(2)}, u32[]{:S(2)}) collective-permute-start(f16[9,8,1,8,128]{4,3,1,0,2:T(8,128)(2,1)S(1)} %bitcast.367), channel_id=1, source_target_pairs={{0,4},{2,6},{4,0},{6,2},{8,12},{10,14},{12,8},{14,10},{16,20},{18,... | collective-permute-start | bytes 442376 | tf_op jit(solution)/shard_map/ppermute | solution.py:319
  70.2 5.2 %collective-permute-start.18 = (f16[9,8,1,8,128]{4,3,1,0,2:T(8,128)(2,1)S(1)}, f16[9,8,1,8,128]{4,3,1,0,2:T(8,128)(2,1)S(1)}, u32[]{:S(2)}, u32[]{:S(2)}) collective-permute-start(f16[9,8,1,8,128]{4,3,1,0,2:T(8,128)(2,1)S(1)} %broadcast_select_fusion.1), channel_id=1, source_target_pairs={{0,8},{2,10},{4,12},{6,14},{8,0},{10,2},{12,4},{14,6},{16,24},{18,... | collective-permute-start | bytes 442376 | tf_op jit(solution)/shard_map/ppermute | solution.py:319
  70.4 14.2 %collective-permute-start.15 = (f32[128,1152]{1,0:T(8,128)S(1)}, f32[128,1152]{1,0:T(8,128)S(1)}, u32[]{:S(2)}, u32[]{:S(2)}) collective-permute-start(f32[128,1152]{1,0:T(8,128)S(1)} %constant_dynamic-slice_fusion), channel_id=1, source_target_pairs={{0,1},{1,0},{2,3},{3,2},{4,5},{5,4},{6,7},{7,6},{8,9},{9,8},{10,11... | collective-permute-start | bytes 1769480 | tf_op jit(solution)/shard_map/ppermute | solution.py:434
  72.0 10.5 %collective-permute-start.24 = (f16[9,8,1,8,128]{4,3,1,0,2:T(8,128)(2,1)S(1)}, f16[9,8,1,8,128]{4,3,1,0,2:T(8,128)(2,1)S(1)}, u32[]{:S(2)}, u32[]{:S(2)}) collective-permute-start(f16[9,8,1,8,128]{4,3,1,0,2:T(8,128)(2,1)S(1)} %collective-permute-done.23), channel_id=1, source_target_pairs={{0,8},{2,10},{4,12},{6,14},{8,0},{10,2},{12,4},{14,6},{16,24},{18,... | collective-permute-start | bytes 442376 | tf_op jit(solution)/shard_map/ppermute | solution.py:319
  75.5 6.8 %collective-permute-start.19 = (f16[2,9,8,1,8,128]{5,4,3,2,1,0:T(8,128)(2,1)S(1)}, f16[2,9,8,1,8,128]{5,4,3,2,1,0:T(8,128)(2,1)S(1)}, u32[]{:S(2)}, u32[]{:S(2)}) collective-permute-start(f16[2,9,8,1,8,128]{5,4,3,2,1,0:T(8,128)(2,1)S(1)} %maximum_bitcast_fusion), channel_id=1, source_target_pairs={{0,4},{2,6},{4,0},{6,2},{8,12},{10,14},{12,8},{14,10},{16,20},{18,... | collective-permute-start | bytes 884744 | tf_op jit(solution)/shard_map/ppermute | solution.py:319
  82.4 12.9 %collective-permute-start.22 = (f16[8,9,8,1,8,128]{5,4,3,2,1,0:T(8,128)(2,1)S(1)}, f16[8,9,8,1,8,128]{5,4,3,2,1,0:T(8,128)(2,1)S(1)}, u32[]{:S(2)}, u32[]{:S(2)}) collective-permute-start(f16[8,9,8,1,8,128]{5,4,3,2,1,0:T(8,128)(2,1)S(1)} %constant_dynamic-update-slice_fusion), channel_id=1, source_target_pairs={{0,2},{2,0},{4,6},{6,4},{8,10},{10,8},{12,14},{14,12},{16,18},{18,... | collective-permute-start | bytes 3538952 | tf_op jit(solution)/shard_map/ppermute | solution.py:319
  82.7 12.6 %collective-permute-start.27 = (f16[3,9,8,1,8,128]{5,4,2,1,3,0:T(8,128)(2,1)S(1)}, f16[3,9,8,1,8,128]{5,4,2,1,3,0:T(8,128)(2,1)S(1)}, u32[]{:S(2)}, u32[]{:S(2)}) collective-permute-start(f16[3,9,8,1,8,128]{5,4,2,1,3,0:T(8,128)(2,1)S(1)} %maximum_select_fusion.1), channel_id=1, source_target_pairs={{0,4},{2,6},{4,0},{6,2},{8,12},{10,14},{12,8},{14,10},{16,20},{18,... | collective-permute-start | bytes 1327112 | tf_op jit(solution)/shard_map/ppermute | solution.py:319
  84.0 13.4 %collective-permute-start.26 = (f16[5,9,8,1,8,128]{5,4,2,1,3,0:T(8,128)(2,1)S(1)}, f16[5,9,8,1,8,128]{5,4,2,1,3,0:T(8,128)(2,1)S(1)}, u32[]{:S(2)}, u32[]{:S(2)}) collective-permute-start(f16[5,9,8,1,8,128]{5,4,2,1,3,0:T(8,128)(2,1)S(1)} %pad_maximum_fusion), channel_id=1, source_target_pairs={{0,2},{2,0},{4,6},{6,4},{8,10},{10,8},{12,14},{14,12},{16,18},{18,... | collective-permute-start | bytes 2211848 | tf_op jit(solution)/shard_map/ppermute | solution.py:319
  84.3 7.7 %collective-permute-start.29 = (f32[2,8,128]{2,1,0:T(8,128)S(1)}, f32[2,8,128]{2,1,0:T(8,128)S(1)}, u32[]{:S(2)}, u32[]{:S(2)}) collective-permute-start(f32[2,8,128]{2,1,0:T(8,128)S(1)} %fusion.54), channel_id=1, source_target_pairs={{0,2},{2,0},{4,6},{6,4},{8,10},{10,8},{12,14},{14,12},{16,18},{18,... | collective-permute-start | bytes 24584 | tf_op jit(solution)/shard_map/ppermute | solution.py:319
  95.3 2.7 %collective-permute-start.28 = (f16[3,9,8,1,8,128]{5,4,2,1,3,0:T(8,128)(2,1)S(1)}, f16[3,9,8,1,8,128]{5,4,2,1,3,0:T(8,128)(2,1)S(1)}, u32[]{:S(2)}, u32[]{:S(2)}) collective-permute-start(f16[3,9,8,1,8,128]{5,4,2,1,3,0:T(8,128)(2,1)S(1)} %collective-permute-done.27), channel_id=1, source_target_pairs={{0,2},{2,0},{4,6},{6,4},{8,10},{10,8},{12,14},{14,12},{16,18},{18,... | collective-permute-start | bytes 1327112 | tf_op jit(solution)/shard_map/ppermute | solution.py:319

commit v7 on v6

--- a/solution.py
+++ b/solution.py
@@ -337,16 +337,20 @@
         first = 0
     other_x = to_core(lax.dynamic_slice_in_dim(x, (1 - core) * core_rows, core_rows, 0))
     where = jnp.stack([core, column * depth + level]).astype(jnp.int32)
-    halves, exponents, arrived, sends, gathers = [], [], [], [], []
+    halves, exponents, sends, gathers = [], [], [], []
     bits_of_depth = [1 << shift for shift in range(depth.bit_length() - 1)]
     grad = jnp.zeros((taps, rows // TILE, 2, TILE, LANES), jnp.float16)
     after = own_cot
     for side in range(2):
         part = parts[side]
+        if side == 0:
+            held_part = pltpu.with_memory_space_constraint(part, pltpu.HBM)
         if side == 1:
             part = later(part, shards[0][-1:, :1, :1])
             their_cot = part
-        shards = kernel_grad(where, depth, x_held, other_x, part, to_core(part), after)
+        shards = kernel_grad(
+            where, depth, x_held, other_x, part if side else held_part, to_core(part), after
+        )
         held = [None] * depth
         gates = ()
         for message in (1, 0):
@@ -365,31 +369,29 @@
                 held[step ^ bit].append((to_level(pair, bit), bits))
                 gates = (pair, halves[0]) if side and step == 1 else (pair,)
                 sends.append(pair)
+                if side and step == depth - 1:
+                    total = forward(x, w, token(pair))
+                    gates += (total[:TILE, :LANES],)
             bits += 1.0
         lowest = common_exponent(held[0], bits)
-        total = later(scaled_sum(held[0], lowest)[:-1], *arrived).astype(jnp.float16)
-        shard = total.reshape(taps, shard_tiles, 1, TILE, LANES)
+        kept = scaled_sum(held[0], lowest)[:-1]
+        kept = later(kept, gathers[0][1]) if side else kept
+        shard = kept.astype(jnp.float16).reshape(taps, shard_tiles, 1, TILE, LANES)
         halves.append(shard)
         exponents.append(lowest)
-
         near = [shard] + [None] * (depth - 1)
         for bit in bits_of_depth[::-1]:
             near[bit] = to_level(shard, bit)
-        own = to_column(shard)
-        arrived = [own]
-        gathers.append((near, own))
+        gathers.append((near, to_column(shard)))
 
     for side, (near, own) in enumerate(gathers):
         for step in range(1, depth):
             if near[step] is None:
                 low = step & -step
-                source = near[step ^ low] if side else later(near[step ^ low], gathers[1][0][1])
-                near[step] = to_level(source, low)
+                near[step] = to_level(near[step ^ low], low)
         steps = list(range(depth))
-        cuts = [steps[1:2], steps[2:]] if side == 0 else [steps[1:]]
+        cuts = [steps[1:2], steps[2:]] if side == 0 else [steps[1:-1], steps[-1:]]
         here = [jnp.stack([near[step] for step in cut]) for cut in cuts]
-        if side == 1:
-            here = [later(values, returned) for values in here]
         there = [to_column(values) for values in here]
         if side == 0:
             returned = there[1]
@@ -404,10 +406,9 @@
         if side == 0:
             messages = [(pieces, jnp.concatenate(here + there))]
         else:
-            count = depth + 1
             messages = [
-                (pieces[:count], jnp.concatenate(here + there[:1])),
-                (pieces[count:], there[1]),
+                (pieces[:-1], jnp.concatenate(here + there[:-1])),
+                (pieces[-1:], there[-1]),
             ]
         lane = first if side == 0 else 1 - first
         for listed, message in messages:
@@ -427,10 +428,10 @@
     grad = (grad * factor[None, :, None]).reshape(taps, rows // TILE, 2, TILE, LANES)
     weight_grad = jnp.transpose(grad, (1, 3, 0, 2, 4)).reshape(rows, taps, outs)
 
-    total = forward(x, w, token(halves[1][0, 0]))
     if chans == 2:
         mine = lax.dynamic_slice_in_dim(total, chan * own_outs, own_outs, 0)
         theirs = lax.dynamic_slice_in_dim(total, (1 - chan) * own_outs, own_outs, 0)
+        theirs = jnp.where(token(halves[1][0, 0])[0, 0] > -1e30, theirs, 0.0)
         result = mine + lax.ppermute(theirs, "chan", [(0, 1), (1, 0)])
         cot = jnp.where(
             chan == 0,

time: 103 us -> 98.4 us (0.955)
  waiting for transfers between devices: 26 us -> 20 us
    ppermute x28 -> x29, waiting for transfers between devices: 26 us -> 20 us  [to(): lax.ppermute(value, 'dp', [(i, i ^ distance) for i in range(samples)])]
    ppermute x28 -> x29, starting transfers between devices: 33.5 us -> 34.5 us  [to(): lax.ppermute(value, 'dp', [(i, i ^ distance) for i in range(samples)])]
  transfers between devices with their start and end apart: 30 -> 31, of which waited for: 10 -> 9; matrix products, arithmetic and copies ran while one was open for 7% -> 8% of each run, Pallas kernels for 22% -> 23%
where the time goes in v7:
time: 98.4 us; the launch traced here: 98.1 us
  starting transfers between devices  38.9 us (40%)
  Pallas kernels  22.1 us (22%)
  waiting for transfers between devices  20 us (20%)
  other arithmetic  7.27 us (7%)
  local copies, waits for them, and re-layouts  7.15 us (7%)
  between operations  2.73 us (3%)
    ppermute x29, starting transfers between devices, to(): lax.ppermute(value, 'dp', [(i, i ^ distance) for i in range(samples)])  34.5 us
    ppermute x29, waiting for transfers between devices, to(): lax.ppermute(value, 'dp', [(i, i ^ distance) for i in range(samples)])  20 us
    pallas_call x2, Pallas kernels, kernel_grad(): pl.pallas_call(functools.partial(kernel_grad_kernel, depth), out_shape=[j...  10.5 us
    pallas_call x1, Pallas kernels, input_gradient(): pl.pallas_call(input_grad_kernel, out_shape=jax.ShapeDtypeStruct((rows, p...  6.55 us
    pallas_call x1, Pallas kernels, forward(): pl.pallas_call(forward_kernel, out_shape=jax.ShapeDtypeStruct((outs, posi...  5.01 us
    reshape x1, other arithmetic, on_device(): weight_grad = jnp.transpose(grad, (1, 3, 0, 2, 4)).reshape(rows, taps, outs)  4.63 us
    ppermute x1, starting transfers between devices, on_device(): their_cot = lax.ppermute(own_cot, 'chan', [(0, 1), (1, 0)])  2.95 us
    dynamic_update_slice x33, local copies, waits for them, and re-layouts, on_device(): lax.dynamic_update_slice(grad, value, (0, base * core_tiles + row, lane,...  2.93 us
  transfers between devices with their start and end apart: 31, of which 9 were waited for; matrix products, arithmetic and copies ran while one was open for 8% of the time, Pallas kernels for 23%

profile of v7, /device:TPU:0, one launch (start us, length us, event | category | flops | bytes accessed | tf_op | source)
XLA Modules:
  0.0 98.1 jit_solution(13507778956806000522)
XLA Ops:
  0.7 1.4 %dynamic-slice_bitcast_fusion = bf16[512,1152]{1,0:T(8,128)(2,1)S(1)} fusion(bf16[1,1024,1152]{2,1,0:T(8,128)(2,1)} %param.3, s32[]{:T(128)S(6)} %select_n.216), kind=kLoop, calls=%fused_computation.1 | loop fusion | bytes 2359300 | tf_op jit(solution)/shard_map/dynamic_slice | solution.py:338
  2.0 0.5 collective-permute-start
  2.6 2.9 %collective-permute-start.5 = (bf16[128,1152]{1,0:T(8,128)(2,1)}, bf16[128,1152]{1,0:T(8,128)(2,1)S(1)}, u32[]{:S(2)}, u32[]{:S(2)}) collective-permute-start(bf16[128,1152]{1,0:T(8,128)(2,1)} %bitcast.381), channel_id=1, source_target_pairs={{0,1},{1,0},{2,3},{3,2},{4,5},{5,4},{6,7},{7,6},{8,9},{9,8},{10,11... | collective-permute-start | bytes 884744 | tf_op jit(solution)/shard_map/ppermute | solution.py:331
  5.7 5.3 %kernel_grad.2 = (f32[73,8,128]{2,1,0:T(8,128)S(1)}, f32[73,8,128]{2,1,0:T(8,128)S(1)}, f32[73,8,128]{2,1,0:T(8,128)S(1)}, f32[73,8,128]{2,1,0:T(8,128)S(1)}, f3...) custom-call(s32[2]{0:T(128)S(1)} %pad_add_fusion.place_ref, bf16[1024,1152]{1,0:T(8,128)(2,1)} %bitcast.354, ...), custom_call_target="tpu_custom_call" | custom-call | flops 1509949440 | bytes 5308416 | tf_op jit(solution)/shard_map/kernel_grad/pallas_call | solution.py:122
  11.0 2.7 %collective-permute-start.2 = (f16[2,73,8,128]{3,2,1,0:T(8,128)(2,1)S(1)}, f16[2,73,8,128]{3,2,1,0:T(8,128)(2,1)S(1)}, u32[]{:S(2)}, u32[]{:S(2)}) collective-permute-start(f16[2,73,8,128]{3,2,1,0:T(8,128)(2,1)S(1)} %convert_element_type.322), channel_id=1, source_target_pairs={{0,4},{2,6},{4,0},{6,2},{8,12},{10,14},{12,8},{14,10},{16,20},{18,... | collective-permute-start | bytes 897032 | tf_op jit(solution)/shard_map/ppermute | solution.py:319
  13.9 0.5 slice.256
  15.2 0.1 maximum_select_fusion.cot_ref
  15.4 1.4 %collective-permute-done.6.other_cot = bf16[128,1152]{1,0:T(8,128)(2,1)S(1)} collective-permute-done((bf16[128,1152]{1,0:T(8,128)(2,1)S(1)}, bf16[128,1152]{1,0:T(8,128)(2,1)S(1)}, u32[]{:S(2)}, u32[]{:S(2)}) %collective-permute-start.6) | collective-permute-done | bytes 294944 | tf_op jit(solution)/shard_map/ppermute | solution.py:319
  16.7 5.2 %kernel_grad.3 = (f32[73,8,128]{2,1,0:T(8,128)S(1)}, f32[73,8,128]{2,1,0:T(8,128)S(1)}, f32[73,8,128]{2,1,0:T(8,128)S(1)}, f32[73,8,128]{2,1,0:T(8,128)S(1)}, f3...) custom-call(s32[2]{0:T(128)S(1)} %pad_add_fusion.place_ref, bf16[1024,1152]{1,0:T(8,128)(2,1)} %bitcast.355, ...), custom_call_target="tpu_custom_call" | custom-call | flops 1509949440 | bytes 5308416 | tf_op jit(solution)/shard_map/kernel_grad/pallas_call | solution.py:122
  22.1 2.1 %collective-permute-start.7 = (f16[2,73,8,128]{3,2,1,0:T(8,128)(2,1)S(1)}, f16[2,73,8,128]{3,2,1,0:T(8,128)(2,1)S(1)}, u32[]{:S(2)}, u32[]{:S(2)}) collective-permute-start(f16[2,73,8,128]{3,2,1,0:T(8,128)(2,1)S(1)} %convert_element_type.350), channel_id=1, source_target_pairs={{0,4},{2,6},{4,0},{6,2},{8,12},{10,14},{12,8},{14,10},{16,20},{18,... | collective-permute-start | bytes 897032 | tf_op jit(solution)/shard_map/ppermute | solution.py:319
  24.4 2.1 %collective-permute-start.4 = (f16[73,8,128]{2,1,0:T(8,128)(2,1)S(1)}, f16[73,8,128]{2,1,0:T(8,128)(2,1)S(1)}, u32[]{:S(2)}, u32[]{:S(2)}) collective-permute-start(f16[73,8,128]{2,1,0:T(8,128)(2,1)S(1)} %constant_dynamic-update-slice_fusion.20), channel_id=1, source_target_pairs={{0,8},{2,10},{4,12},{6,14},{8,0},{10,2},{12,4},{14,6},{16,24},{18,... | collective-permute-start | bytes 448520 | tf_op jit(solution)/shard_map/ppermute | solution.py:319
  26.6 1.4 %collective-permute-done.3 = f16[2,73,8,128]{3,2,1,0:T(8,128)(2,1)S(1)} collective-permute-done((f16[2,73,8,128]{3,2,1,0:T(8,128)(2,1)S(1)}, f16[2,73,8,128]{3,2,1,0:T(8,128)(2,1)S(1)}, u32[]{:S(2)}, u32[]{:S(2)}) %collective-permute-start.3) | collective-permute-done | bytes 299040 | tf_op jit(solution)/shard_map/ppermute | solution.py:319
  28.1 2.2 %collective-permute-start.8 = (f16[73,8,128]{2,1,0:T(8,128)(2,1)S(1)}, f16[73,8,128]{2,1,0:T(8,128)(2,1)S(1)}, u32[]{:S(2)}, u32[]{:S(2)}) collective-permute-start(f16[73,8,128]{2,1,0:T(8,128)(2,1)S(1)} %constant_dynamic-update-slice_fusion.19), channel_id=1, source_target_pairs={{0,8},{2,10},{4,12},{6,14},{8,0},{10,2},{12,4},{14,6},{16,24},{18,... | collective-permute-start | bytes 448520 | tf_op jit(solution)/shard_map/ppermute | solution.py:319
  30.4 0.4 collective-permute-done.4
  30.9 0.1 fusion.15
  31.0 3.0 %collective-permute-start.9 = (f16[73,8,128]{2,1,0:T(8,128)(2,1)S(1)}, f16[73,8,128]{2,1,0:T(8,128)(2,1)S(1)}, u32[]{:S(2)}, u32[]{:S(2)}) collective-permute-start(f16[73,8,128]{2,1,0:T(8,128)(2,1)S(1)} %constant_dynamic-update-slice_fusion.18), channel_id=1, source_target_pairs={{0,16},{2,18},{4,20},{6,22},{8,24},{10,26},{12,28},{14,30},{16,0},... | collective-permute-start | bytes 448520 | tf_op jit(solution)/shard_map/ppermute | solution.py:319
  34.0 0.4 collective-permute-done.7
  34.5 2.2 %collective-permute-start.13 = (f16[73,8,128]{2,1,0:T(8,128)(2,1)S(1)}, f16[73,8,128]{2,1,0:T(8,128)(2,1)S(1)}, u32[]{:S(2)}, u32[]{:S(2)}) collective-permute-start(f16[73,8,128]{2,1,0:T(8,128)(2,1)S(1)} %constant_dynamic-update-slice_fusion.17), channel_id=1, source_target_pairs={{0,8},{2,10},{4,12},{6,14},{8,0},{10,2},{12,4},{14,6},{16,24},{18,... | collective-permute-start | bytes 448520 | tf_op jit(solution)/shard_map/ppermute | solution.py:319
  36.8 5.0 %forward.1 = f32[256,1152]{1,0:T(8,128)S(1)} custom-call(bf16[1024,1152]{1,0:T(8,128)(2,1)S(1)} %bitcast.356, bf16[9,1024,256]{2,1,0:T(8,128)(2,1)S(1)} %bitcast.359, f32[8,128]{1,0:T(8,128)S(1)} %fusion.139._), custom_call_target="tpu_custom_call" | custom-call | flops 3019898880 | bytes 8257536 | tf_op jit(solution)/shard_map/forward/pallas_call | solution.py:194
  41.9 0.5 collective-permute-start.12
  42.6 0.1 fusion.30
  42.7 1.7 %collective-permute-start.19 = (f16[9,8,1,8,128]{4,3,1,0,2:T(8,128)(2,1)S(1)}, f16[9,8,1,8,128]{4,3,1,0,2:T(8,128)(2,1)S(1)}, u32[]{:S(2)}, u32[]{:S(2)}) collective-permute-start(f16[9,8,1,8,128]{4,3,1,0,2:T(8,128)(2,1)S(1)} %bitcast.362), channel_id=1, source_target_pairs={{0,8},{2,10},{4,12},{6,14},{8,0},{10,2},{12,4},{14,6},{16,24},{18,... | collective-permute-start | bytes 442376 | tf_op jit(solution)/shard_map/ppermute | solution.py:319
  44.4 2.6 %collective-permute-start.16 = (f16[9,8,1,8,128]{4,3,1,0,2:T(8,128)(2,1)S(1)}, f16[9,8,1,8,128]{4,3,1,0,2:T(8,128)(2,1)S(1)}, u32[]{:S(2)}, u32[]{:S(2)}) collective-permute-start(f16[9,8,1,8,128]{4,3,1,0,2:T(8,128)(2,1)S(1)} %bitcast.363), channel_id=1, source_target_pairs={{0,16},{2,18},{4,20},{6,22},{8,24},{10,26},{12,28},{14,30},{16,0},... | collective-permute-start | bytes 442376 | tf_op jit(solution)/shard_map/ppermute | solution.py:319
  46.9 1.5 %collective-permute-start.10 = (f16[9,8,1,8,128]{4,3,1,0,2:T(8,128)(2,1)S(1)}, f16[9,8,1,8,128]{4,3,1,0,2:T(8,128)(2,1)S(1)}, u32[]{:S(2)}, u32[]{:S(2)}) collective-permute-start(f16[9,8,1,8,128]{4,3,1,0,2:T(8,128)(2,1)S(1)} %bitcast.364), channel_id=1, source_target_pairs={{0,4},{2,6},{4,0},{6,2},{8,12},{10,14},{12,8},{14,10},{16,20},{18,... | collective-permute-start | bytes 442376 | tf_op jit(solution)/shard_map/ppermute | solution.py:319
  48.5 0.9 broadcast_in_dim.93
  49.5 0.1 fusion.4
  49.7 0.4 collective-permute-start.14
  50.1 3.0 %collective-permute-done.19 = f16[9,8,1,8,128]{4,3,1,0,2:T(8,128)(2,1)S(1)} collective-permute-done((f16[9,8,1,8,128]{4,3,1,0,2:T(8,128)(2,1)S(1)}, f16[9,8,1,8,128]{4,3,1,0,2:T(8,128)(2,1)S(1)}, u32[]{:S(2)}, u32[]{:S(2)}) %collective-permute-start.19) | collective-permute-done | bytes 147488 | tf_op jit(solution)/shard_map/ppermute | solution.py:319
  53.1 1.5 %collective-permute-start.20 = (f16[1,9,8,1,8,128]{5,4,3,2,1,0:T(8,128)(2,1)S(1)}, f16[1,9,8,1,8,128]{5,4,3,2,1,0:T(8,128)(2,1)S(1)}, u32[]{:S(2)}, u32[]{:S(2)}) collective-permute-start(f16[1,9,8,1,8,128]{5,4,3,2,1,0:T(8,128)(2,1)S(1)} %bitcast.378), channel_id=1, source_target_pairs={{0,4},{2,6},{4,0},{6,2},{8,12},{10,14},{12,8},{14,10},{16,20},{18,... | collective-permute-start | bytes 442376 | tf_op jit(solution)/shard_map/ppermute | solution.py:319
  54.7 2.2 %collective-permute-start.17 = (f16[9,8,1,8,128]{4,3,1,0,2:T(8,128)(2,1)S(1)}, f16[9,8,1,8,128]{4,3,1,0,2:T(8,128)(2,1)S(1)}, u32[]{:S(2)}, u32[]{:S(2)}) collective-permute-start(f16[9,8,1,8,128]{4,3,1,0,2:T(8,128)(2,1)S(1)} %collective-permute-done.16), channel_id=1, source_target_pairs={{0,8},{2,10},{4,12},{6,14},{8,0},{10,2},{12,4},{14,6},{16,24},{18,... | collective-permute-start | bytes 442376 | tf_op jit(solution)/shard_map/ppermute | solution.py:319
  57.0 3.1 %collective-permute-done.14 = f16[73,8,128]{2,1,0:T(8,128)(2,1)S(1)} collective-permute-done((f16[73,8,128]{2,1,0:T(8,128)(2,1)S(1)}, f16[73,8,128]{2,1,0:T(8,128)(2,1)S(1)}, u32[]{:S(2)}, u32[]{:S(2)}) %collective-permute-start.14) | collective-permute-done | bytes 149536 | tf_op jit(solution)/shard_map/ppermute | solution.py:319
  60.1 0.1 fusion.26
  60.3 2.9 %collective-permute-start.23 = (f16[9,8,1,8,128]{4,3,1,0,2:T(8,128)(2,1)S(1)}, f16[9,8,1,8,128]{4,3,1,0,2:T(8,128)(2,1)S(1)}, u32[]{:S(2)}, u32[]{:S(2)}) collective-permute-start(f16[9,8,1,8,128]{4,3,1,0,2:T(8,128)(2,1)S(1)} %bitcast.369), channel_id=1, source_target_pairs={{0,16},{2,18},{4,20},{6,22},{8,24},{10,26},{12,28},{14,30},{16,0},... | collective-permute-start | bytes 442376 | tf_op jit(solution)/shard_map/ppermute | solution.py:319
  63.2 1.1 %collective-permute-start.25 = (f16[9,8,1,8,128]{4,3,1,0,2:T(8,128)(2,1)S(1)}, f16[9,8,1,8,128]{4,3,1,0,2:T(8,128)(2,1)S(1)}, u32[]{:S(2)}, u32[]{:S(2)}) collective-permute-start(f16[9,8,1,8,128]{4,3,1,0,2:T(8,128)(2,1)S(1)} %bitcast.370), channel_id=1, source_target_pairs={{0,4},{2,6},{4,0},{6,2},{8,12},{10,14},{12,8},{14,10},{16,20},{18,... | collective-permute-start | bytes 442376 | tf_op jit(solution)/shard_map/ppermute | solution.py:319
  64.3 1.4 %collective-permute-start.18 = (f16[2,9,8,1,8,128]{5,4,3,2,1,0:T(8,128)(2,1)S(1)}, f16[2,9,8,1,8,128]{5,4,3,2,1,0:T(8,128)(2,1)S(1)}, u32[]{:S(2)}, u32[]{:S(2)}) collective-permute-start(f16[2,9,8,1,8,128]{5,4,3,2,1,0:T(8,128)(2,1)S(1)} %maximum_bitcast_fusion), channel_id=1, source_target_pairs={{0,4},{2,6},{4,0},{6,2},{8,12},{10,14},{12,8},{14,10},{16,20},{18,... | collective-permute-start | bytes 884744 | tf_op jit(solution)/shard_map/ppermute | solution.py:319
  65.7 0.5 slice.287
  67.1 1.5 %collective-permute-start.15 = (f32[128,1152]{1,0:T(8,128)S(1)}, f32[128,1152]{1,0:T(8,128)S(1)}, u32[]{:S(2)}, u32[]{:S(2)}) collective-permute-start(f32[128,1152]{1,0:T(8,128)S(1)} %dynamic-slice_select_fusion), channel_id=1, source_target_pairs={{0,1},{1,0},{2,3},{3,2},{4,5},{5,4},{6,7},{7,6},{8,9},{9,8},{10,11... | collective-permute-start | bytes 1769480 | tf_op jit(solution)/shard_map/ppermute | solution.py:435
  68.8 1.3 %collective-permute-start.26 = (f16[2,9,8,1,8,128]{5,4,2,1,3,0:T(8,128)(2,1)S(1)}, f16[2,9,8,1,8,128]{5,4,2,1,3,0:T(8,128)(2,1)S(1)}, u32[]{:S(2)}, u32[]{:S(2)}) collective-permute-start(f16[2,9,8,1,8,128]{5,4,2,1,3,0:T(8,128)(2,1)S(1)} %pad_maximum_fusion), channel_id=1, source_target_pairs={{0,4},{2,6},{4,0},{6,2},{8,12},{10,14},{12,8},{14,10},{16,20},{18,... | collective-permute-start | bytes 884744 | tf_op jit(solution)/shard_map/ppermute | solution.py:319
  70.1 0.5 collective-permute-start.24
  70.7 5.6 %collective-permute-done.18 = f16[2,9,8,1,8,128]{5,4,3,2,1,0:T(8,128)(2,1)S(1)} collective-permute-done((f16[2,9,8,1,8,128]{5,4,3,2,1,0:T(8,128)(2,1)S(1)}, f16[2,9,8,1,8,128]{5,4,3,2,1,0:T(8,128)(2,1)S(1)}, u32[]{:S(2)}, u32[]{:S(2)}) %collective-permute-start.18) | collective-permute-done | bytes 294944 | tf_op jit(solution)/shard_map/ppermute | solution.py:319
  76.5 6.6 %input_gradient.1 = bf16[1024,1152]{1,0:T(8,128)(2,1)} custom-call(bf16[256,1152]{1,0:T(8,128)(2,1)S(1)} %maximum_select_fusion.cot_ref, bf16[9,1024,256]{2,1,0:T(8,128)(2,1)S(1)} %bitcast.360, f32[8,128]{1,0:T(8,128)S(1)} %fusion.138._), custom_call_target="tpu_custom_call" | custom-call | flops 3019898880 | bytes 7667712 | tf_op jit(solution)/shard_map/input_gradient/pallas_call | solution.py:242
  83.1 0.5 collective-permute-start.30
  83.7 0.6 collective-permute-start.28
  84.6 0.4 collective-permute-start.27
  85.0 4.5 %collective-permute-done.28 = f16[1,9,8,1,8,128]{5,4,2,1,3,0:T(8,128)(2,1)S(1)} collective-permute-done((f16[1,9,8,1,8,128]{5,4,2,1,3,0:T(8,128)(2,1)S(1)}, f16[1,9,8,1,8,128]{5,4,2,1,3,0:T(8,128)(2,1)S(1)}, u32[]{:S(2)}, u32[]{:S(2)}) %collective-permute-start.28) | collective-permute-done | bytes 147488 | tf_op jit(solution)/shard_map/ppermute | solution.py:319
  89.5 0.8 fusion.21
  91.1 1.0 %copy.11 = f16[9,128,2,8,128]{4,3,2,1,0:T(8,128)(2,1)S(1)} copy(f16[9,128,2,8,128]{4,3,1,0,2:T(8,128)(2,1)S(1)} %fusion.42) | data formatting | bytes 9437184 | tf_op jit(solution)/shard_map/dynamic_update_slice | solution.py:419
  93.5 4.6 %multiply_bitcast_fusion = f32[1024,9,256]{2,0,1:T(8,128)} fusion(f16[9,128,2,8,128]{4,3,2,1,0:T(8,128)(2,1)S(1)} %bitcast_dynamic-update-slice_fusion, f32[128,2,8,128]{3,2,1,0:T(8,128)S(1)} %bitcast.361), kind=kLoop, calls=%fused_computation | loop fusion | flops 4718592 | bytes 15204352 | tf_op jit(solution)/shard_map/reshape | solution.py:429
  (136 shorter events, 4.6 us)
Async XLA Ops:
  2.0 13.2 %copy-start.1 = (bf16[1,128,1152]{2,1,0:T(8,128)(2,1)S(1)}, bf16[1,128,1152]{2,1,0:T(8,128)(2,1)}, u32[]{:S(2)}) copy-start(bf16[1,128,1152]{2,1,0:T(8,128)(2,1)} %param.5) | copy-start | bytes 884740
  2.0 3.6 %collective-permute-start = (bf16[512,1152]{1,0:T(8,128)(2,1)S(1)}, bf16[512,1152]{1,0:T(8,128)(2,1)S(1)}, u32[]{:S(2)}, u32[]{:S(2)}) collective-permute-start(bf16[512,1152]{1,0:T(8,128)(2,1)S(1)} %dynamic-slice_bitcast_fusion), channel_id=1, source_target_pairs={{0,2},{2,0},{4,6},{6,4},{8,10},{10,8},{12,14},{14,12},{16,18},{18,... | collective-permute-start | bytes 3538952 | tf_op jit(solution)/shard_map/ppermute | solution.py:319
  2.5 3.1 %collective-permute-start.1 = (bf16[128,1152]{1,0:T(8,128)(2,1)}, bf16[128,1152]{1,0:T(8,128)(2,1)S(1)}, u32[]{:S(2)}, u32[]{:S(2)}) collective-permute-start(bf16[128,1152]{1,0:T(8,128)(2,1)} %bitcast.380), channel_id=1, source_target_pairs={{0,2},{2,0},{4,6},{6,4},{8,10},{10,8},{12,14},{14,12},{16,18},{18,... | collective-permute-start | bytes 884744 | tf_op jit(solution)/shard_map/ppermute | solution.py:319
  2.6 12.4 %collective-permute-start.5 = (bf16[128,1152]{1,0:T(8,128)(2,1)}, bf16[128,1152]{1,0:T(8,128)(2,1)S(1)}, u32[]{:S(2)}, u32[]{:S(2)}) collective-permute-start(bf16[128,1152]{1,0:T(8,128)(2,1)} %bitcast.381), channel_id=1, source_target_pairs={{0,1},{1,0},{2,3},{3,2},{4,5},{5,4},{6,7},{7,6},{8,9},{9,8},{10,11... | collective-permute-start | bytes 884744 | tf_op jit(solution)/shard_map/ppermute | solution.py:331
  11.0 13.3 %collective-permute-start.2 = (f16[2,73,8,128]{3,2,1,0:T(8,128)(2,1)S(1)}, f16[2,73,8,128]{3,2,1,0:T(8,128)(2,1)S(1)}, u32[]{:S(2)}, u32[]{:S(2)}) collective-permute-start(f16[2,73,8,128]{3,2,1,0:T(8,128)(2,1)S(1)} %convert_element_type.322), channel_id=1, source_target_pairs={{0,4},{2,6},{4,0},{6,2},{8,12},{10,14},{12,8},{14,10},{16,20},{18,... | collective-permute-start | bytes 897032 | tf_op jit(solution)/shard_map/ppermute | solution.py:319
  13.8 14.2 %collective-permute-start.3 = (f16[2,73,8,128]{3,2,1,0:T(8,128)(2,1)S(1)}, f16[2,73,8,128]{3,2,1,0:T(8,128)(2,1)S(1)}, u32[]{:S(2)}, u32[]{:S(2)}) collective-permute-start(f16[2,73,8,128]{3,2,1,0:T(8,128)(2,1)S(1)} %select_convert_fusion.1), channel_id=1, source_target_pairs={{0,4},{2,6},{4,0},{6,2},{8,12},{10,14},{12,8},{14,10},{16,20},{18,... | collective-permute-start | bytes 897032 | tf_op jit(solution)/shard_map/ppermute | solution.py:319
  15.1 1.6 %collective-permute-start.6 = (bf16[128,1152]{1,0:T(8,128)(2,1)S(1)}, bf16[128,1152]{1,0:T(8,128)(2,1)S(1)}, u32[]{:S(2)}, u32[]{:S(2)}) collective-permute-start(bf16[128,1152]{1,0:T(8,128)(2,1)S(1)} %broadcast_select_fusion.own_cot), channel_id=1, source_target_pairs={{0,2},{2,0},{4,6},{6,4},{8,10},{10,8},{12,14},{14,12},{16,18},{18,... | collective-permute-start | bytes 884744 | tf_op jit(solution)/shard_map/ppermute | solution.py:319
  15.2 21.6 %slice-start = ((s8[4718592]{0:T(1024)(128)(4,1)}), s8[4194304]{0:T(1024)(128)(4,1)S(1)}, s32[]{:S(2)}) async-start(s8[4718592]{0:T(1024)(128)(4,1)} %bitcast.357), calls=%async_computation | async-start | bytes 8388608
  15.3 21.4 %copy-start = (bf16[1,1024,1152]{2,1,0:T(8,128)(2,1)S(1)}, bf16[1,1024,1152]{2,1,0:T(8,128)(2,1)}, u32[]{:S(2)}) copy-start(bf16[1,1024,1152]{2,1,0:T(8,128)(2,1)} %param.3) | copy-start | bytes 7077892
  15.4 21.4 %slice-start.1 = ((s8[4718592]{0:T(1024)(128)(4,1)}), s8[524288]{0:T(1024)(128)(4,1)S(1)}, s32[]{:S(2)}) async-start(s8[4718592]{0:T(1024)(128)(4,1)} %bitcast.357), calls=%async_computation.1 | async-start | bytes 1048576
  22.1 12.3 %collective-permute-start.7 = (f16[2,73,8,128]{3,2,1,0:T(8,128)(2,1)S(1)}, f16[2,73,8,128]{3,2,1,0:T(8,128)(2,1)S(1)}, u32[]{:S(2)}, u32[]{:S(2)}) collective-permute-start(f16[2,73,8,128]{3,2,1,0:T(8,128)(2,1)S(1)} %convert_element_type.350), channel_id=1, source_target_pairs={{0,4},{2,6},{4,0},{6,2},{8,12},{10,14},{12,8},{14,10},{16,20},{18,... | collective-permute-start | bytes 897032 | tf_op jit(solution)/shard_map/ppermute | solution.py:319
  24.2 17.6 %collective-permute-start.11 = (f16[2,73,8,128]{3,2,1,0:T(8,128)(2,1)S(1)}, f16[2,73,8,128]{3,2,1,0:T(8,128)(2,1)S(1)}, u32[]{:S(2)}, u32[]{:S(2)}) collective-permute-start(f16[2,73,8,128]{3,2,1,0:T(8,128)(2,1)S(1)} %select_convert_fusion), channel_id=1, source_target_pairs={{0,4},{2,6},{4,0},{6,2},{8,12},{10,14},{12,8},{14,10},{16,20},{18,... | collective-permute-start | bytes 897032 | tf_op jit(solution)/shard_map/ppermute | solution.py:319
  24.4 6.4 %collective-permute-start.4 = (f16[73,8,128]{2,1,0:T(8,128)(2,1)S(1)}, f16[73,8,128]{2,1,0:T(8,128)(2,1)S(1)}, u32[]{:S(2)}, u32[]{:S(2)}) collective-permute-start(f16[73,8,128]{2,1,0:T(8,128)(2,1)S(1)} %constant_dynamic-update-slice_fusion.20), channel_id=1, source_target_pairs={{0,8},{2,10},{4,12},{6,14},{8,0},{10,2},{12,4},{14,6},{16,24},{18,... | collective-permute-start | bytes 448520 | tf_op jit(solution)/shard_map/ppermute | solution.py:319
  28.1 14.4 %collective-permute-start.8 = (f16[73,8,128]{2,1,0:T(8,128)(2,1)S(1)}, f16[73,8,128]{2,1,0:T(8,128)(2,1)S(1)}, u32[]{:S(2)}, u32[]{:S(2)}) collective-permute-start(f16[73,8,128]{2,1,0:T(8,128)(2,1)S(1)} %constant_dynamic-update-slice_fusion.19), channel_id=1, source_target_pairs={{0,8},{2,10},{4,12},{6,14},{8,0},{10,2},{12,4},{14,6},{16,24},{18,... | collective-permute-start | bytes 448520 | tf_op jit(solution)/shard_map/ppermute | solution.py:319
  31.0 11.5 %collective-permute-start.9 = (f16[73,8,128]{2,1,0:T(8,128)(2,1)S(1)}, f16[73,8,128]{2,1,0:T(8,128)(2,1)S(1)}, u32[]{:S(2)}, u32[]{:S(2)}) collective-permute-start(f16[73,8,128]{2,1,0:T(8,128)(2,1)S(1)} %constant_dynamic-update-slice_fusion.18), channel_id=1, source_target_pairs={{0,16},{2,18},{4,20},{6,22},{8,24},{10,26},{12,28},{14,30},{16,0},... | collective-permute-start | bytes 448520 | tf_op jit(solution)/shard_map/ppermute | solution.py:319
  34.5 14.9 %collective-permute-start.13 = (f16[73,8,128]{2,1,0:T(8,128)(2,1)S(1)}, f16[73,8,128]{2,1,0:T(8,128)(2,1)S(1)}, u32[]{:S(2)}, u32[]{:S(2)}) collective-permute-start(f16[73,8,128]{2,1,0:T(8,128)(2,1)S(1)} %constant_dynamic-update-slice_fusion.17), channel_id=1, source_target_pairs={{0,8},{2,10},{4,12},{6,14},{8,0},{10,2},{12,4},{14,6},{16,24},{18,... | collective-permute-start | bytes 448520 | tf_op jit(solution)/shard_map/ppermute | solution.py:319
  41.9 15.0 %collective-permute-start.12 = (f16[73,8,128]{2,1,0:T(8,128)(2,1)S(1)}, f16[73,8,128]{2,1,0:T(8,128)(2,1)S(1)}, u32[]{:S(2)}, u32[]{:S(2)}) collective-permute-start(f16[73,8,128]{2,1,0:T(8,128)(2,1)S(1)} %constant_dynamic-update-slice_fusion.16), channel_id=1, source_target_pairs={{0,8},{2,10},{4,12},{6,14},{8,0},{10,2},{12,4},{14,6},{16,24},{18,... | collective-permute-start | bytes 448520 | tf_op jit(solution)/shard_map/ppermute | solution.py:319
  42.7 10.4 %collective-permute-start.19 = (f16[9,8,1,8,128]{4,3,1,0,2:T(8,128)(2,1)S(1)}, f16[9,8,1,8,128]{4,3,1,0,2:T(8,128)(2,1)S(1)}, u32[]{:S(2)}, u32[]{:S(2)}) collective-permute-start(f16[9,8,1,8,128]{4,3,1,0,2:T(8,128)(2,1)S(1)} %bitcast.362), channel_id=1, source_target_pairs={{0,8},{2,10},{4,12},{6,14},{8,0},{10,2},{12,4},{14,6},{16,24},{18,... | collective-permute-start | bytes 442376 | tf_op jit(solution)/shard_map/ppermute | solution.py:319
  44.4 10.3 %collective-permute-start.16 = (f16[9,8,1,8,128]{4,3,1,0,2:T(8,128)(2,1)S(1)}, f16[9,8,1,8,128]{4,3,1,0,2:T(8,128)(2,1)S(1)}, u32[]{:S(2)}, u32[]{:S(2)}) collective-permute-start(f16[9,8,1,8,128]{4,3,1,0,2:T(8,128)(2,1)S(1)} %bitcast.363), channel_id=1, source_target_pairs={{0,16},{2,18},{4,20},{6,22},{8,24},{10,26},{12,28},{14,30},{16,0},... | collective-permute-start | bytes 442376 | tf_op jit(solution)/shard_map/ppermute | solution.py:319
  46.9 10.0 %collective-permute-start.10 = (f16[9,8,1,8,128]{4,3,1,0,2:T(8,128)(2,1)S(1)}, f16[9,8,1,8,128]{4,3,1,0,2:T(8,128)(2,1)S(1)}, u32[]{:S(2)}, u32[]{:S(2)}) collective-permute-start(f16[9,8,1,8,128]{4,3,1,0,2:T(8,128)(2,1)S(1)} %bitcast.364), channel_id=1, source_target_pairs={{0,4},{2,6},{4,0},{6,2},{8,12},{10,14},{12,8},{14,10},{16,20},{18,... | collective-permute-start | bytes 442376 | tf_op jit(solution)/shard_map/ppermute | solution.py:319
  49.7 10.4 %collective-permute-start.14 = (f16[73,8,128]{2,1,0:T(8,128)(2,1)S(1)}, f16[73,8,128]{2,1,0:T(8,128)(2,1)S(1)}, u32[]{:S(2)}, u32[]{:S(2)}) collective-permute-start(f16[73,8,128]{2,1,0:T(8,128)(2,1)S(1)} %constant_dynamic-update-slice_fusion.15), channel_id=1, source_target_pairs={{0,16},{2,18},{4,20},{6,22},{8,24},{10,26},{12,28},{14,30},{16,0},... | collective-permute-start | bytes 448520 | tf_op jit(solution)/shard_map/ppermute | solution.py:319
  53.1 14.0 %collective-permute-start.20 = (f16[1,9,8,1,8,128]{5,4,3,2,1,0:T(8,128)(2,1)S(1)}, f16[1,9,8,1,8,128]{5,4,3,2,1,0:T(8,128)(2,1)S(1)}, u32[]{:S(2)}, u32[]{:S(2)}) collective-permute-start(f16[1,9,8,1,8,128]{5,4,3,2,1,0:T(8,128)(2,1)S(1)} %bitcast.378), channel_id=1, source_target_pairs={{0,4},{2,6},{4,0},{6,2},{8,12},{10,14},{12,8},{14,10},{16,20},{18,... | collective-permute-start | bytes 442376 | tf_op jit(solution)/shard_map/ppermute | solution.py:319
  54.7 9.6 %collective-permute-start.17 = (f16[9,8,1,8,128]{4,3,1,0,2:T(8,128)(2,1)S(1)}, f16[9,8,1,8,128]{4,3,1,0,2:T(8,128)(2,1)S(1)}, u32[]{:S(2)}, u32[]{:S(2)}) collective-permute-start(f16[9,8,1,8,128]{4,3,1,0,2:T(8,128)(2,1)S(1)} %collective-permute-done.16), channel_id=1, source_target_pairs={{0,8},{2,10},{4,12},{6,14},{8,0},{10,2},{12,4},{14,6},{16,24},{18,... | collective-permute-start | bytes 442376 | tf_op jit(solution)/shard_map/ppermute | solution.py:319
  60.2 8.5 %collective-permute-start.22 = (f16[9,8,1,8,128]{4,3,1,0,2:T(8,128)(2,1)S(1)}, f16[9,8,1,8,128]{4,3,1,0,2:T(8,128)(2,1)S(1)}, u32[]{:S(2)}, u32[]{:S(2)}) collective-permute-start(f16[9,8,1,8,128]{4,3,1,0,2:T(8,128)(2,1)S(1)} %bitcast.368), channel_id=1, source_target_pairs={{0,8},{2,10},{4,12},{6,14},{8,0},{10,2},{12,4},{14,6},{16,24},{18,... | collective-permute-start | bytes 442376 | tf_op jit(solution)/shard_map/ppermute | solution.py:319
  60.3 8.4 %collective-permute-start.23 = (f16[9,8,1,8,128]{4,3,1,0,2:T(8,128)(2,1)S(1)}, f16[9,8,1,8,128]{4,3,1,0,2:T(8,128)(2,1)S(1)}, u32[]{:S(2)}, u32[]{:S(2)}) collective-permute-start(f16[9,8,1,8,128]{4,3,1,0,2:T(8,128)(2,1)S(1)} %bitcast.369), channel_id=1, source_target_pairs={{0,16},{2,18},{4,20},{6,22},{8,24},{10,26},{12,28},{14,30},{16,0},... | collective-permute-start | bytes 442376 | tf_op jit(solution)/shard_map/ppermute | solution.py:319
  63.2 20.5 %collective-permute-start.25 = (f16[9,8,1,8,128]{4,3,1,0,2:T(8,128)(2,1)S(1)}, f16[9,8,1,8,128]{4,3,1,0,2:T(8,128)(2,1)S(1)}, u32[]{:S(2)}, u32[]{:S(2)}) collective-permute-start(f16[9,8,1,8,128]{4,3,1,0,2:T(8,128)(2,1)S(1)} %bitcast.370), channel_id=1, source_target_pairs={{0,4},{2,6},{4,0},{6,2},{8,12},{10,14},{12,8},{14,10},{16,20},{18,... | collective-permute-start | bytes 442376 | tf_op jit(solution)/shard_map/ppermute | solution.py:319
  64.3 12.0 %collective-permute-start.18 = (f16[2,9,8,1,8,128]{5,4,3,2,1,0:T(8,128)(2,1)S(1)}, f16[2,9,8,1,8,128]{5,4,3,2,1,0:T(8,128)(2,1)S(1)}, u32[]{:S(2)}, u32[]{:S(2)}) collective-permute-start(f16[2,9,8,1,8,128]{5,4,3,2,1,0:T(8,128)(2,1)S(1)} %maximum_bitcast_fusion), channel_id=1, source_target_pairs={{0,4},{2,6},{4,0},{6,2},{8,12},{10,14},{12,8},{14,10},{16,20},{18,... | collective-permute-start | bytes 884744 | tf_op jit(solution)/shard_map/ppermute | solution.py:319
  67.1 22.4 %collective-permute-start.15 = (f32[128,1152]{1,0:T(8,128)S(1)}, f32[128,1152]{1,0:T(8,128)S(1)}, u32[]{:S(2)}, u32[]{:S(2)}) collective-permute-start(f32[128,1152]{1,0:T(8,128)S(1)} %dynamic-slice_select_fusion), channel_id=1, source_target_pairs={{0,1},{1,0},{2,3},{3,2},{4,5},{5,4},{6,7},{7,6},{8,9},{9,8},{10,11... | collective-permute-start | bytes 1769480 | tf_op jit(solution)/shard_map/ppermute | solution.py:435
  68.8 15.7 %collective-permute-start.26 = (f16[2,9,8,1,8,128]{5,4,2,1,3,0:T(8,128)(2,1)S(1)}, f16[2,9,8,1,8,128]{5,4,2,1,3,0:T(8,128)(2,1)S(1)}, u32[]{:S(2)}, u32[]{:S(2)}) collective-permute-start(f16[2,9,8,1,8,128]{5,4,2,1,3,0:T(8,128)(2,1)S(1)} %pad_maximum_fusion), channel_id=1, source_target_pairs={{0,4},{2,6},{4,0},{6,2},{8,12},{10,14},{12,8},{14,10},{16,20},{18,... | collective-permute-start | bytes 884744 | tf_op jit(solution)/shard_map/ppermute | solution.py:319
  70.1 13.0 %collective-permute-start.24 = (f16[9,8,1,8,128]{4,3,1,0,2:T(8,128)(2,1)S(1)}, f16[9,8,1,8,128]{4,3,1,0,2:T(8,128)(2,1)S(1)}, u32[]{:S(2)}, u32[]{:S(2)}) collective-permute-start(f16[9,8,1,8,128]{4,3,1,0,2:T(8,128)(2,1)S(1)} %collective-permute-done.23), channel_id=1, source_target_pairs={{0,8},{2,10},{4,12},{6,14},{8,0},{10,2},{12,4},{14,6},{16,24},{18,... | collective-permute-start | bytes 442376 | tf_op jit(solution)/shard_map/ppermute | solution.py:319
  76.4 13.9 %collective-permute-start.21 = (f16[8,9,8,1,8,128]{5,4,3,2,1,0:T(8,128)(2,1)S(1)}, f16[8,9,8,1,8,128]{5,4,3,2,1,0:T(8,128)(2,1)S(1)}, u32[]{:S(2)}, u32[]{:S(2)}) collective-permute-start(f16[8,9,8,1,8,128]{5,4,3,2,1,0:T(8,128)(2,1)S(1)} %constant_dynamic-update-slice_fusion), channel_id=1, source_target_pairs={{0,2},{2,0},{4,6},{6,4},{8,10},{10,8},{12,14},{14,12},{16,18},{18,... | collective-permute-start | bytes 3538952 | tf_op jit(solution)/shard_map/ppermute | solution.py:319
  83.1 1.4 %collective-permute-start.30 = (f32[2,8,128]{2,1,0:T(8,128)S(1)}, f32[2,8,128]{2,1,0:T(8,128)S(1)}, u32[]{:S(2)}, u32[]{:S(2)}) collective-permute-start(f32[2,8,128]{2,1,0:T(8,128)S(1)} %fusion.53), channel_id=1, source_target_pairs={{0,2},{2,0},{4,6},{6,4},{8,10},{10,8},{12,14},{14,12},{16,18},{18,... | collective-permute-start | bytes 24584 | tf_op jit(solution)/shard_map/ppermute | solution.py:319
  83.7 5.9 %collective-permute-start.28 = (f16[1,9,8,1,8,128]{5,4,2,1,3,0:T(8,128)(2,1)S(1)}, f16[1,9,8,1,8,128]{5,4,2,1,3,0:T(8,128)(2,1)S(1)}, u32[]{:S(2)}, u32[]{:S(2)}) collective-permute-start(f16[1,9,8,1,8,128]{5,4,2,1,3,0:T(8,128)(2,1)S(1)} %bitcast.379), channel_id=1, source_target_pairs={{0,4},{2,6},{4,0},{6,2},{8,12},{10,14},{12,8},{14,10},{16,20},{18,... | collective-permute-start | bytes 442376 | tf_op jit(solution)/shard_map/ppermute | solution.py:319
  84.6 7.8 %collective-permute-start.27 = (f16[7,9,8,1,8,128]{5,4,2,1,3,0:T(8,128)(2,1)S(1)}, f16[7,9,8,1,8,128]{5,4,2,1,3,0:T(8,128)(2,1)S(1)}, u32[]{:S(2)}, u32[]{:S(2)}) collective-permute-start(f16[7,9,8,1,8,128]{5,4,2,1,3,0:T(8,128)(2,1)S(1)} %constant_dynamic-update-slice_fusion.4), channel_id=1, source_target_pairs={{0,2},{2,0},{4,6},{6,4},{8,10},{10,8},{12,14},{14,12},{16,18},{18,... | collective-permute-start | bytes 3096584 | tf_op jit(solution)/shard_map/ppermute | solution.py:319
  89.5 3.8 %collective-permute-start.29 = (f16[1,9,8,1,8,128]{5,4,2,1,3,0:T(8,128)(2,1)S(1)}, f16[1,9,8,1,8,128]{5,4,2,1,3,0:T(8,128)(2,1)S(1)}, u32[]{:S(2)}, u32[]{:S(2)}) collective-permute-start(f16[1,9,8,1,8,128]{5,4,2,1,3,0:T(8,128)(2,1)S(1)} %collective-permute-done.28), channel_id=1, source_target_pairs={{0,2},{2,0},{4,6},{6,4},{8,10},{10,8},{12,14},{14,12},{16,18},{18,... | collective-permute-start | bytes 442376 | tf_op jit(solution)/shard_map/ppermute | solution.py:319

commit v8 on v7

--- a/solution.py
+++ b/solution.py
@@ -337,7 +337,7 @@
         first = 0
     other_x = to_core(lax.dynamic_slice_in_dim(x, (1 - core) * core_rows, core_rows, 0))
     where = jnp.stack([core, column * depth + level]).astype(jnp.int32)
-    halves, exponents, sends, gathers = [], [], [], []
+    halves, exponents, sends, reduced, gathers = [], [], [], [], []
     bits_of_depth = [1 << shift for shift in range(depth.bit_length() - 1)]
     grad = jnp.zeros((taps, rows // TILE, 2, TILE, LANES), jnp.float16)
     after = own_cot
@@ -367,18 +367,21 @@
             for step in range(depth - bit, 0, -2 * bit):
                 pair = summed(held[step], bits, *gates)
                 held[step ^ bit].append((to_level(pair, bit), bits))
-                gates = (pair, halves[0]) if side and step == 1 else (pair,)
+                gates = (pair,)
                 sends.append(pair)
                 if side and step == depth - 1:
                     total = forward(x, w, token(pair))
                     gates += (total[:TILE, :LANES],)
             bits += 1.0
-        lowest = common_exponent(held[0], bits)
-        kept = scaled_sum(held[0], lowest)[:-1]
-        kept = later(kept, gathers[0][1]) if side else kept
+        reduced.append((held[0], bits))
+
+    for side, (values, bits) in enumerate(reduced):
+        lowest = common_exponent(values, bits)
+        gate = gathers[0][1] if side else sends[-1]
+        kept = later(scaled_sum(values, lowest)[:-1], gate)
         shard = kept.astype(jnp.float16).reshape(taps, shard_tiles, 1, TILE, LANES)
         halves.append(shard)
-        exponents.append(lowest)
+        exponents.append(later(lowest, shard))
         near = [shard] + [None] * (depth - 1)
         for bit in bits_of_depth[::-1]:
             near[bit] = to_level(shard, bit)
@@ -441,7 +444,7 @@
     else:
         result = lax.psum_scatter(total, "chan", scatter_dimension=0, tiled=True)
     result = result.astype(jnp.bfloat16)[None]
-    input_grad = input_gradient(cot, w, token(returned[0, 0, 0]))[None]
+    input_grad = input_gradient(cot, w, token(near[-1][0, 0]))[None]
     return (result, input_grad, weight_grad)
 
 

time: 98.4 us -> 95.4 us (0.970)
  waiting for transfers between devices: 20 us -> 17.7 us
  local copies, waits for them, and re-layouts: 7.15 us -> 6.01 us
    ppermute x29, waiting for transfers between devices: 20 us -> 17.6 us  [to(): lax.ppermute(value, 'dp', [(i, i ^ distance) for i in range(samples)])]
    dynamic_update_slice x33 -> x32, local copies, waits for them, and re-layouts: 2.93 us -> 2.02 us  [on_device(): lax.dynamic_update_slice(grad, value, (0, base * core_tiles + row, lane,...]
  transfers between devices with their start and end apart: 31 -> 31, of which waited for: 9 -> 10; matrix products, arithmetic and copies ran while one was open for 8% -> 7% of each run, Pallas kernels for 23% -> 23%
where the time goes in v8:
time: 95.4 us; the launch traced here: 95.2 us
  starting transfers between devices  39.6 us (42%)
  Pallas kernels  22 us (23%)
  waiting for transfers between devices  17.7 us (19%)
  other arithmetic  7.26 us (8%)
  local copies, waits for them, and re-layouts  6.01 us (6%)
  between operations  2.65 us (3%)
    ppermute x29, starting transfers between devices, to(): lax.ppermute(value, 'dp', [(i, i ^ distance) for i in range(samples)])  35.2 us
    ppermute x29, waiting for transfers between devices, to(): lax.ppermute(value, 'dp', [(i, i ^ distance) for i in range(samples)])  17.6 us
    pallas_call x2, Pallas kernels, kernel_grad(): pl.pallas_call(functools.partial(kernel_grad_kernel, depth), out_shape=[j...  10.5 us
    pallas_call x1, Pallas kernels, input_gradient(): pl.pallas_call(input_grad_kernel, out_shape=jax.ShapeDtypeStruct((rows, p...  6.56 us
    pallas_call x1, Pallas kernels, forward(): pl.pallas_call(forward_kernel, out_shape=jax.ShapeDtypeStruct((outs, posi...  4.92 us
    reshape x1, other arithmetic, on_device(): weight_grad = jnp.transpose(grad, (1, 3, 0, 2, 4)).reshape(rows, taps, outs)  4.64 us
    ppermute x1, starting transfers between devices, on_device(): their_cot = lax.ppermute(own_cot, 'chan', [(0, 1), (1, 0)])  2.95 us
    dynamic_update_slice x32, local copies, waits for them, and re-layouts, on_device(): lax.dynamic_update_slice(grad, value, (0, base * core_tiles + row, lane,...  2.02 us
  transfers between devices with their start and end apart: 31, of which 10 were waited for; matrix products, arithmetic and copies ran while one was open for 7% of the time, Pallas kernels for 23%

profile of v8, /device:TPU:0, one launch (start us, length us, event | category | flops | bytes accessed | tf_op | source)
XLA Modules:
  0.0 95.2 jit_solution(12904335778782110084)
XLA Ops:
  0.7 1.4 %dynamic-slice_bitcast_fusion = bf16[512,1152]{1,0:T(8,128)(2,1)S(1)} fusion(bf16[1,1024,1152]{2,1,0:T(8,128)(2,1)} %param.3, s32[]{:T(128)S(6)} %select_n.223), kind=kLoop, calls=%fused_computation.1 | loop fusion | bytes 2359300 | tf_op jit(solution)/shard_map/dynamic_slice | solution.py:338
  2.0 0.5 collective-permute-start
  2.6 2.9 %collective-permute-start.5 = (bf16[128,1152]{1,0:T(8,128)(2,1)}, bf16[128,1152]{1,0:T(8,128)(2,1)S(1)}, u32[]{:S(2)}, u32[]{:S(2)}) collective-permute-start(bf16[128,1152]{1,0:T(8,128)(2,1)} %bitcast.409), channel_id=1, source_target_pairs={{0,1},{1,0},{2,3},{3,2},{4,5},{5,4},{6,7},{7,6},{8,9},{9,8},{10,11... | collective-permute-start | bytes 884744 | tf_op jit(solution)/shard_map/ppermute | solution.py:331
  5.7 5.3 %kernel_grad.2 = (f32[73,8,128]{2,1,0:T(8,128)S(1)}, f32[73,8,128]{2,1,0:T(8,128)S(1)}, f32[73,8,128]{2,1,0:T(8,128)S(1)}, f32[73,8,128]{2,1,0:T(8,128)S(1)}, f3...) custom-call(s32[2]{0:T(128)S(1)} %pad_add_fusion.place_ref, bf16[1024,1152]{1,0:T(8,128)(2,1)} %bitcast.381, ...), custom_call_target="tpu_custom_call" | custom-call | flops 1509949440 | bytes 5308416 | tf_op jit(solution)/shard_map/kernel_grad/pallas_call | solution.py:122
  11.0 2.7 %collective-permute-start.2 = (f16[2,73,8,128]{3,2,1,0:T(8,128)(2,1)S(1)}, f16[2,73,8,128]{3,2,1,0:T(8,128)(2,1)S(1)}, u32[]{:S(2)}, u32[]{:S(2)}) collective-permute-start(f16[2,73,8,128]{3,2,1,0:T(8,128)(2,1)S(1)} %convert_element_type.349), channel_id=1, source_target_pairs={{0,4},{2,6},{4,0},{6,2},{8,12},{10,14},{12,8},{14,10},{16,20},{18,... | collective-permute-start | bytes 897032 | tf_op jit(solution)/shard_map/ppermute | solution.py:319
  13.9 0.5 slice.261
  15.2 0.1 maximum_select_fusion.cot_ref
  15.4 1.4 %collective-permute-done.6.other_cot = bf16[128,1152]{1,0:T(8,128)(2,1)S(1)} collective-permute-done((bf16[128,1152]{1,0:T(8,128)(2,1)S(1)}, bf16[128,1152]{1,0:T(8,128)(2,1)S(1)}, u32[]{:S(2)}, u32[]{:S(2)}) %collective-permute-start.6) | collective-permute-done | bytes 294944 | tf_op jit(solution)/shard_map/ppermute | solution.py:319
  16.7 5.2 %kernel_grad.3 = (f32[73,8,128]{2,1,0:T(8,128)S(1)}, f32[73,8,128]{2,1,0:T(8,128)S(1)}, f32[73,8,128]{2,1,0:T(8,128)S(1)}, f32[73,8,128]{2,1,0:T(8,128)S(1)}, f3...) custom-call(s32[2]{0:T(128)S(1)} %pad_add_fusion.place_ref, bf16[1024,1152]{1,0:T(8,128)(2,1)} %bitcast.382, ...), custom_call_target="tpu_custom_call" | custom-call | flops 1509949440 | bytes 5308416 | tf_op jit(solution)/shard_map/kernel_grad/pallas_call | solution.py:122
  22.1 2.1 %collective-permute-start.7 = (f16[2,73,8,128]{3,2,1,0:T(8,128)(2,1)S(1)}, f16[2,73,8,128]{3,2,1,0:T(8,128)(2,1)S(1)}, u32[]{:S(2)}, u32[]{:S(2)}) collective-permute-start(f16[2,73,8,128]{3,2,1,0:T(8,128)(2,1)S(1)} %convert_element_type.377), channel_id=1, source_target_pairs={{0,4},{2,6},{4,0},{6,2},{8,12},{10,14},{12,8},{14,10},{16,20},{18,... | collective-permute-start | bytes 897032 | tf_op jit(solution)/shard_map/ppermute | solution.py:319
  24.4 2.1 %collective-permute-start.4 = (f16[73,8,128]{2,1,0:T(8,128)(2,1)S(1)}, f16[73,8,128]{2,1,0:T(8,128)(2,1)S(1)}, u32[]{:S(2)}, u32[]{:S(2)}) collective-permute-start(f16[73,8,128]{2,1,0:T(8,128)(2,1)S(1)} %constant_dynamic-update-slice_fusion.21), channel_id=1, source_target_pairs={{0,8},{2,10},{4,12},{6,14},{8,0},{10,2},{12,4},{14,6},{16,24},{18,... | collective-permute-start | bytes 448520 | tf_op jit(solution)/shard_map/ppermute | solution.py:319
  26.5 1.4 %collective-permute-done.3 = f16[2,73,8,128]{3,2,1,0:T(8,128)(2,1)S(1)} collective-permute-done((f16[2,73,8,128]{3,2,1,0:T(8,128)(2,1)S(1)}, f16[2,73,8,128]{3,2,1,0:T(8,128)(2,1)S(1)}, u32[]{:S(2)}, u32[]{:S(2)}) %collective-permute-start.3) | collective-permute-done | bytes 299040 | tf_op jit(solution)/shard_map/ppermute | solution.py:319
  28.1 2.2 %collective-permute-start.10 = (f16[73,8,128]{2,1,0:T(8,128)(2,1)S(1)}, f16[73,8,128]{2,1,0:T(8,128)(2,1)S(1)}, u32[]{:S(2)}, u32[]{:S(2)}) collective-permute-start(f16[73,8,128]{2,1,0:T(8,128)(2,1)S(1)} %constant_dynamic-update-slice_fusion.20), channel_id=1, source_target_pairs={{0,8},{2,10},{4,12},{6,14},{8,0},{10,2},{12,4},{14,6},{16,24},{18,... | collective-permute-start | bytes 448520 | tf_op jit(solution)/shard_map/ppermute | solution.py:319
  30.4 0.4 collective-permute-done.4
  31.0 3.0 %collective-permute-start.11 = (f16[73,8,128]{2,1,0:T(8,128)(2,1)S(1)}, f16[73,8,128]{2,1,0:T(8,128)(2,1)S(1)}, u32[]{:S(2)}, u32[]{:S(2)}) collective-permute-start(f16[73,8,128]{2,1,0:T(8,128)(2,1)S(1)} %constant_dynamic-update-slice_fusion.19), channel_id=1, source_target_pairs={{0,16},{2,18},{4,20},{6,22},{8,24},{10,26},{12,28},{14,30},{16,0},... | collective-permute-start | bytes 448520 | tf_op jit(solution)/shard_map/ppermute | solution.py:319
  34.0 0.4 collective-permute-done.7
  34.5 2.2 %collective-permute-start.9 = (f16[73,8,128]{2,1,0:T(8,128)(2,1)S(1)}, f16[73,8,128]{2,1,0:T(8,128)(2,1)S(1)}, u32[]{:S(2)}, u32[]{:S(2)}) collective-permute-start(f16[73,8,128]{2,1,0:T(8,128)(2,1)S(1)} %constant_dynamic-update-slice_fusion.18), channel_id=1, source_target_pairs={{0,8},{2,10},{4,12},{6,14},{8,0},{10,2},{12,4},{14,6},{16,24},{18,... | collective-permute-start | bytes 448520 | tf_op jit(solution)/shard_map/ppermute | solution.py:319
  36.8 4.9 %forward.1 = f32[256,1152]{1,0:T(8,128)S(1)} custom-call(bf16[1024,1152]{1,0:T(8,128)(2,1)S(1)} %bitcast.383, bf16[9,1024,256]{2,1,0:T(8,128)(2,1)S(1)} %bitcast.386, f32[8,128]{1,0:T(8,128)S(1)} %fusion.146._), custom_call_target="tpu_custom_call" | custom-call | flops 3019898880 | bytes 8257536 | tf_op jit(solution)/shard_map/forward/pallas_call | solution.py:194
  41.9 0.6 collective-permute-start.13
  42.6 0.1 fusion.3
  42.7 2.6 %collective-permute-start.14 = (f16[73,8,128]{2,1,0:T(8,128)(2,1)S(1)}, f16[73,8,128]{2,1,0:T(8,128)(2,1)S(1)}, u32[]{:S(2)}, u32[]{:S(2)}) collective-permute-start(f16[73,8,128]{2,1,0:T(8,128)(2,1)S(1)} %constant_dynamic-update-slice_fusion.16), channel_id=1, source_target_pairs={{0,16},{2,18},{4,20},{6,22},{8,24},{10,26},{12,28},{14,30},{16,0},... | collective-permute-start | bytes 448520 | tf_op jit(solution)/shard_map/ppermute | solution.py:319
  45.4 0.1 fusion.30
  45.5 0.4 collective-permute-start.19
  45.9 1.5 %collective-permute-start.18 = (f16[9,8,1,8,128]{4,3,1,0,2:T(8,128)(2,1)S(1)}, f16[9,8,1,8,128]{4,3,1,0,2:T(8,128)(2,1)S(1)}, u32[]{:S(2)}, u32[]{:S(2)}) collective-permute-start(f16[9,8,1,8,128]{4,3,1,0,2:T(8,128)(2,1)S(1)} %bitcast.397), channel_id=1, source_target_pairs={{0,8},{2,10},{4,12},{6,14},{8,0},{10,2},{12,4},{14,6},{16,24},{18,... | collective-permute-start | bytes 442376 | tf_op jit(solution)/shard_map/ppermute | solution.py:319
  47.4 1.5 %collective-permute-start.12 = (f16[9,8,1,8,128]{4,3,2,1,0:T(8,128)(2,1)S(1)}, f16[9,8,1,8,128]{4,3,2,1,0:T(8,128)(2,1)S(1)}, u32[]{:S(2)}, u32[]{:S(2)}) collective-permute-start(f16[9,8,1,8,128]{4,3,2,1,0:T(8,128)(2,1)S(1)} %bitcast.398), channel_id=1, source_target_pairs={{0,4},{2,6},{4,0},{6,2},{8,12},{10,14},{12,8},{14,10},{16,20},{18,... | collective-permute-start | bytes 442376 | tf_op jit(solution)/shard_map/ppermute | solution.py:319
  49.0 0.7 broadcast_in_dim.92
  49.8 4.9 %collective-permute-done.18 = f16[9,8,1,8,128]{4,3,1,0,2:T(8,128)(2,1)S(1)} collective-permute-done((f16[9,8,1,8,128]{4,3,1,0,2:T(8,128)(2,1)S(1)}, f16[9,8,1,8,128]{4,3,1,0,2:T(8,128)(2,1)S(1)}, u32[]{:S(2)}, u32[]{:S(2)}) %collective-permute-start.18) | collective-permute-done | bytes 147488 | tf_op jit(solution)/shard_map/ppermute | solution.py:319
  54.7 1.5 %collective-permute-start.21 = (f16[1,9,8,1,8,128]{5,4,2,1,3,0:T(8,128)(2,1)S(1)}, f16[1,9,8,1,8,128]{5,4,2,1,3,0:T(8,128)(2,1)S(1)}, u32[]{:S(2)}, u32[]{:S(2)}) collective-permute-start(f16[1,9,8,1,8,128]{5,4,2,1,3,0:T(8,128)(2,1)S(1)} %bitcast.407), channel_id=1, source_target_pairs={{0,4},{2,6},{4,0},{6,2},{8,12},{10,14},{12,8},{14,10},{16,20},{18,... | collective-permute-start | bytes 442376 | tf_op jit(solution)/shard_map/ppermute | solution.py:319
  56.2 1.9 %collective-permute-done.19 = f16[9,8,1,8,128]{4,3,1,0,2:T(8,128)(2,1)S(1)} collective-permute-done((f16[9,8,1,8,128]{4,3,1,0,2:T(8,128)(2,1)S(1)}, f16[9,8,1,8,128]{4,3,1,0,2:T(8,128)(2,1)S(1)}, u32[]{:S(2)}, u32[]{:S(2)}) %collective-permute-start.19) | collective-permute-done | bytes 147488 | tf_op jit(solution)/shard_map/ppermute | solution.py:319
  58.2 0.6 collective-permute-start.20
  58.9 0.1 fusion.25
  59.0 1.5 %collective-permute-start.24 = (f16[9,8,1,8,128]{4,3,1,0,2:T(8,128)(2,1)S(1)}, f16[9,8,1,8,128]{4,3,1,0,2:T(8,128)(2,1)S(1)}, u32[]{:S(2)}, u32[]{:S(2)}) collective-permute-start(f16[9,8,1,8,128]{4,3,1,0,2:T(8,128)(2,1)S(1)} %bitcast.389), channel_id=1, source_target_pairs={{0,8},{2,10},{4,12},{6,14},{8,0},{10,2},{12,4},{14,6},{16,24},{18,... | collective-permute-start | bytes 442376 | tf_op jit(solution)/shard_map/ppermute | solution.py:319
  60.6 1.5 %collective-permute-start.25 = (f16[9,8,1,8,128]{4,3,1,0,2:T(8,128)(2,1)S(1)}, f16[9,8,1,8,128]{4,3,1,0,2:T(8,128)(2,1)S(1)}, u32[]{:S(2)}, u32[]{:S(2)}) collective-permute-start(f16[9,8,1,8,128]{4,3,1,0,2:T(8,128)(2,1)S(1)} %bitcast.390), channel_id=1, source_target_pairs={{0,4},{2,6},{4,0},{6,2},{8,12},{10,14},{12,8},{14,10},{16,20},{18,... | collective-permute-start | bytes 442376 | tf_op jit(solution)/shard_map/ppermute | solution.py:319
  62.1 1.4 %collective-permute-start.16 = (f16[9,8,1,8,128]{4,3,2,1,0:T(8,128)(2,1)S(1)}, f16[9,8,1,8,128]{4,3,2,1,0:T(8,128)(2,1)S(1)}, u32[]{:S(2)}, u32[]{:S(2)}) collective-permute-start(f16[9,8,1,8,128]{4,3,2,1,0:T(8,128)(2,1)S(1)} %bitcast.393), channel_id=1, source_target_pairs={{0,16},{2,18},{4,20},{6,22},{8,24},{10,26},{12,28},{14,30},{16,0},... | collective-permute-start | bytes 442376 | tf_op jit(solution)/shard_map/ppermute | solution.py:319
  63.5 0.5 slice.292
  64.8 1.1 %collective-permute-done.20 = f16[9,8,1,8,128]{4,3,1,0,2:T(8,128)(2,1)S(1)} collective-permute-done((f16[9,8,1,8,128]{4,3,1,0,2:T(8,128)(2,1)S(1)}, f16[9,8,1,8,128]{4,3,1,0,2:T(8,128)(2,1)S(1)}, u32[]{:S(2)}, u32[]{:S(2)}) %collective-permute-start.20) | collective-permute-done | bytes 147488 | tf_op jit(solution)/shard_map/ppermute | solution.py:319
  65.9 1.5 %collective-permute-start.15 = (f32[128,1152]{1,0:T(8,128)S(1)}, f32[128,1152]{1,0:T(8,128)S(1)}, u32[]{:S(2)}, u32[]{:S(2)}) collective-permute-start(f32[128,1152]{1,0:T(8,128)S(1)} %dynamic-slice_select_fusion), channel_id=1, source_target_pairs={{0,1},{1,0},{2,3},{3,2},{4,5},{5,4},{6,7},{7,6},{8,9},{9,8},{10,11... | collective-permute-start | bytes 1769480 | tf_op jit(solution)/shard_map/ppermute | solution.py:438
  67.6 1.8 %collective-permute-start.22 = (f16[2,9,8,1,8,128]{5,4,2,1,3,0:T(8,128)(2,1)S(1)}, f16[2,9,8,1,8,128]{5,4,2,1,3,0:T(8,128)(2,1)S(1)}, u32[]{:S(2)}, u32[]{:S(2)}) collective-permute-start(f16[2,9,8,1,8,128]{5,4,2,1,3,0:T(8,128)(2,1)S(1)} %pad_maximum_fusion), channel_id=1, source_target_pairs={{0,4},{2,6},{4,0},{6,2},{8,12},{10,14},{12,8},{14,10},{16,20},{18,... | collective-permute-start | bytes 884744 | tf_op jit(solution)/shard_map/ppermute | solution.py:319
  69.5 1.0 %collective-permute-done.16 = f16[9,8,1,8,128]{4,3,2,1,0:T(8,128)(2,1)S(1)} collective-permute-done((f16[9,8,1,8,128]{4,3,2,1,0:T(8,128)(2,1)S(1)}, f16[9,8,1,8,128]{4,3,2,1,0:T(8,128)(2,1)S(1)}, u32[]{:S(2)}, u32[]{:S(2)}) %collective-permute-start.16) | collective-permute-done | bytes 147488 | tf_op jit(solution)/shard_map/ppermute | solution.py:319
  70.7 1.8 %collective-permute-start.17 = (f16[9,8,1,8,128]{4,3,2,1,0:T(8,128)(2,1)S(1)}, f16[9,8,1,8,128]{4,3,2,1,0:T(8,128)(2,1)S(1)}, u32[]{:S(2)}, u32[]{:S(2)}) collective-permute-start(f16[9,8,1,8,128]{4,3,2,1,0:T(8,128)(2,1)S(1)} %collective-permute-done.16), channel_id=1, source_target_pairs={{0,8},{2,10},{4,12},{6,14},{8,0},{10,2},{12,4},{14,6},{16,24},{18,... | collective-permute-start | bytes 442376 | tf_op jit(solution)/shard_map/ppermute | solution.py:319
  72.5 3.4 %collective-permute-done.17 = f16[9,8,1,8,128]{4,3,2,1,0:T(8,128)(2,1)S(1)} collective-permute-done((f16[9,8,1,8,128]{4,3,2,1,0:T(8,128)(2,1)S(1)}, f16[9,8,1,8,128]{4,3,2,1,0:T(8,128)(2,1)S(1)}, u32[]{:S(2)}, u32[]{:S(2)}) %collective-permute-start.17) | collective-permute-done | bytes 147488 | tf_op jit(solution)/shard_map/ppermute | solution.py:319
  75.9 1.9 %collective-permute-start.28 = (f16[1,9,8,1,8,128]{5,4,2,1,3,0:T(8,128)(2,1)S(1)}, f16[1,9,8,1,8,128]{5,4,2,1,3,0:T(8,128)(2,1)S(1)}, u32[]{:S(2)}, u32[]{:S(2)}) collective-permute-start(f16[1,9,8,1,8,128]{5,4,2,1,3,0:T(8,128)(2,1)S(1)} %bitcast.406), channel_id=1, source_target_pairs={{0,4},{2,6},{4,0},{6,2},{8,12},{10,14},{12,8},{14,10},{16,20},{18,... | collective-permute-start | bytes 442376 | tf_op jit(solution)/shard_map/ppermute | solution.py:319
  78.0 6.6 %input_gradient.1 = bf16[1024,1152]{1,0:T(8,128)(2,1)} custom-call(bf16[256,1152]{1,0:T(8,128)(2,1)S(1)} %maximum_select_fusion.cot_ref, bf16[9,1024,256]{2,1,0:T(8,128)(2,1)S(1)} %bitcast.387, f32[8,128]{1,0:T(8,128)S(1)} %fusion.145._), custom_call_target="tpu_custom_call" | custom-call | flops 3019898880 | bytes 7667712 | tf_op jit(solution)/shard_map/input_gradient/pallas_call | solution.py:242
  84.7 0.5 collective-permute-start.30
  85.5 0.5 collective-permute-start.29
  86.0 1.6 %collective-permute-done.30 = f32[2,8,128]{2,1,0:T(8,128)S(1)} collective-permute-done((f32[2,8,128]{2,1,0:T(8,128)S(1)}, f32[2,8,128]{2,1,0:T(8,128)S(1)}, u32[]{:S(2)}, u32[]{:S(2)}) %collective-permute-start.30) | collective-permute-done | bytes 8224 | tf_op jit(solution)/shard_map/ppermute | solution.py:319
  87.6 0.8 fusion.20
  90.5 4.6 %multiply_bitcast_fusion = f32[1024,9,256]{2,0,1:T(8,128)} fusion(f16[9,128,2,8,128]{4,3,2,1,0:T(8,128)(2,1)S(1)} %bitcast_dynamic-update-slice_fusion, f32[128,2,8,128]{3,2,1,0:T(8,128)S(1)} %bitcast.388), kind=kLoop, calls=%fused_computation | loop fusion | flops 4718592 | bytes 15204352 | tf_op jit(solution)/shard_map/reshape | solution.py:432
  (136 shorter events, 4.8 us)
Async XLA Ops:
  2.0 13.2 %copy-start.1 = (bf16[1,128,1152]{2,1,0:T(8,128)(2,1)S(1)}, bf16[1,128,1152]{2,1,0:T(8,128)(2,1)}, u32[]{:S(2)}) copy-start(bf16[1,128,1152]{2,1,0:T(8,128)(2,1)} %param.5) | copy-start | bytes 884740
  2.0 3.6 %collective-permute-start = (bf16[512,1152]{1,0:T(8,128)(2,1)S(1)}, bf16[512,1152]{1,0:T(8,128)(2,1)S(1)}, u32[]{:S(2)}, u32[]{:S(2)}) collective-permute-start(bf16[512,1152]{1,0:T(8,128)(2,1)S(1)} %dynamic-slice_bitcast_fusion), channel_id=1, source_target_pairs={{0,2},{2,0},{4,6},{6,4},{8,10},{10,8},{12,14},{14,12},{16,18},{18,... | collective-permute-start | bytes 3538952 | tf_op jit(solution)/shard_map/ppermute | solution.py:319
  2.5 3.1 %collective-permute-start.1 = (bf16[128,1152]{1,0:T(8,128)(2,1)}, bf16[128,1152]{1,0:T(8,128)(2,1)S(1)}, u32[]{:S(2)}, u32[]{:S(2)}) collective-permute-start(bf16[128,1152]{1,0:T(8,128)(2,1)} %bitcast.408), channel_id=1, source_target_pairs={{0,2},{2,0},{4,6},{6,4},{8,10},{10,8},{12,14},{14,12},{16,18},{18,... | collective-permute-start | bytes 884744 | tf_op jit(solution)/shard_map/ppermute | solution.py:319
  2.6 12.4 %collective-permute-start.5 = (bf16[128,1152]{1,0:T(8,128)(2,1)}, bf16[128,1152]{1,0:T(8,128)(2,1)S(1)}, u32[]{:S(2)}, u32[]{:S(2)}) collective-permute-start(bf16[128,1152]{1,0:T(8,128)(2,1)} %bitcast.409), channel_id=1, source_target_pairs={{0,1},{1,0},{2,3},{3,2},{4,5},{5,4},{6,7},{7,6},{8,9},{9,8},{10,11... | collective-permute-start | bytes 884744 | tf_op jit(solution)/shard_map/ppermute | solution.py:331
  11.0 13.3 %collective-permute-start.2 = (f16[2,73,8,128]{3,2,1,0:T(8,128)(2,1)S(1)}, f16[2,73,8,128]{3,2,1,0:T(8,128)(2,1)S(1)}, u32[]{:S(2)}, u32[]{:S(2)}) collective-permute-start(f16[2,73,8,128]{3,2,1,0:T(8,128)(2,1)S(1)} %convert_element_type.349), channel_id=1, source_target_pairs={{0,4},{2,6},{4,0},{6,2},{8,12},{10,14},{12,8},{14,10},{16,20},{18,... | collective-permute-start | bytes 897032 | tf_op jit(solution)/shard_map/ppermute | solution.py:319
  13.8 14.2 %collective-permute-start.3 = (f16[2,73,8,128]{3,2,1,0:T(8,128)(2,1)S(1)}, f16[2,73,8,128]{3,2,1,0:T(8,128)(2,1)S(1)}, u32[]{:S(2)}, u32[]{:S(2)}) collective-permute-start(f16[2,73,8,128]{3,2,1,0:T(8,128)(2,1)S(1)} %select_convert_fusion.1), channel_id=1, source_target_pairs={{0,4},{2,6},{4,0},{6,2},{8,12},{10,14},{12,8},{14,10},{16,20},{18,... | collective-permute-start | bytes 897032 | tf_op jit(solution)/shard_map/ppermute | solution.py:319
  15.1 1.6 %collective-permute-start.6 = (bf16[128,1152]{1,0:T(8,128)(2,1)S(1)}, bf16[128,1152]{1,0:T(8,128)(2,1)S(1)}, u32[]{:S(2)}, u32[]{:S(2)}) collective-permute-start(bf16[128,1152]{1,0:T(8,128)(2,1)S(1)} %broadcast_select_fusion.own_cot), channel_id=1, source_target_pairs={{0,2},{2,0},{4,6},{6,4},{8,10},{10,8},{12,14},{14,12},{16,18},{18,... | collective-permute-start | bytes 884744 | tf_op jit(solution)/shard_map/ppermute | solution.py:319
  15.2 21.6 %slice-start = ((s8[4718592]{0:T(1024)(128)(4,1)}), s8[4194304]{0:T(1024)(128)(4,1)S(1)}, s32[]{:S(2)}) async-start(s8[4718592]{0:T(1024)(128)(4,1)} %bitcast.384), calls=%async_computation | async-start | bytes 8388608
  15.3 21.4 %copy-start = (bf16[1,1024,1152]{2,1,0:T(8,128)(2,1)S(1)}, bf16[1,1024,1152]{2,1,0:T(8,128)(2,1)}, u32[]{:S(2)}) copy-start(bf16[1,1024,1152]{2,1,0:T(8,128)(2,1)} %param.3) | copy-start | bytes 7077892
  15.4 21.4 %slice-start.1 = ((s8[4718592]{0:T(1024)(128)(4,1)}), s8[524288]{0:T(1024)(128)(4,1)S(1)}, s32[]{:S(2)}) async-start(s8[4718592]{0:T(1024)(128)(4,1)} %bitcast.384), calls=%async_computation.1 | async-start | bytes 1048576
  22.1 12.3 %collective-permute-start.7 = (f16[2,73,8,128]{3,2,1,0:T(8,128)(2,1)S(1)}, f16[2,73,8,128]{3,2,1,0:T(8,128)(2,1)S(1)}, u32[]{:S(2)}, u32[]{:S(2)}) collective-permute-start(f16[2,73,8,128]{3,2,1,0:T(8,128)(2,1)S(1)} %convert_element_type.377), channel_id=1, source_target_pairs={{0,4},{2,6},{4,0},{6,2},{8,12},{10,14},{12,8},{14,10},{16,20},{18,... | collective-permute-start | bytes 897032 | tf_op jit(solution)/shard_map/ppermute | solution.py:319
  24.2 17.5 %collective-permute-start.8 = (f16[2,73,8,128]{3,2,1,0:T(8,128)(2,1)S(1)}, f16[2,73,8,128]{3,2,1,0:T(8,128)(2,1)S(1)}, u32[]{:S(2)}, u32[]{:S(2)}) collective-permute-start(f16[2,73,8,128]{3,2,1,0:T(8,128)(2,1)S(1)} %select_convert_fusion), channel_id=1, source_target_pairs={{0,4},{2,6},{4,0},{6,2},{8,12},{10,14},{12,8},{14,10},{16,20},{18,... | collective-permute-start | bytes 897032 | tf_op jit(solution)/shard_map/ppermute | solution.py:319
  24.4 6.4 %collective-permute-start.4 = (f16[73,8,128]{2,1,0:T(8,128)(2,1)S(1)}, f16[73,8,128]{2,1,0:T(8,128)(2,1)S(1)}, u32[]{:S(2)}, u32[]{:S(2)}) collective-permute-start(f16[73,8,128]{2,1,0:T(8,128)(2,1)S(1)} %constant_dynamic-update-slice_fusion.21), channel_id=1, source_target_pairs={{0,8},{2,10},{4,12},{6,14},{8,0},{10,2},{12,4},{14,6},{16,24},{18,... | collective-permute-start | bytes 448520 | tf_op jit(solution)/shard_map/ppermute | solution.py:319
  28.1 14.4 %collective-permute-start.10 = (f16[73,8,128]{2,1,0:T(8,128)(2,1)S(1)}, f16[73,8,128]{2,1,0:T(8,128)(2,1)S(1)}, u32[]{:S(2)}, u32[]{:S(2)}) collective-permute-start(f16[73,8,128]{2,1,0:T(8,128)(2,1)S(1)} %constant_dynamic-update-slice_fusion.20), channel_id=1, source_target_pairs={{0,8},{2,10},{4,12},{6,14},{8,0},{10,2},{12,4},{14,6},{16,24},{18,... | collective-permute-start | bytes 448520 | tf_op jit(solution)/shard_map/ppermute | solution.py:319
  31.0 11.6 %collective-permute-start.11 = (f16[73,8,128]{2,1,0:T(8,128)(2,1)S(1)}, f16[73,8,128]{2,1,0:T(8,128)(2,1)S(1)}, u32[]{:S(2)}, u32[]{:S(2)}) collective-permute-start(f16[73,8,128]{2,1,0:T(8,128)(2,1)S(1)} %constant_dynamic-update-slice_fusion.19), channel_id=1, source_target_pairs={{0,16},{2,18},{4,20},{6,22},{8,24},{10,26},{12,28},{14,30},{16,0},... | collective-permute-start | bytes 448520 | tf_op jit(solution)/shard_map/ppermute | solution.py:319
  34.5 8.0 %collective-permute-start.9 = (f16[73,8,128]{2,1,0:T(8,128)(2,1)S(1)}, f16[73,8,128]{2,1,0:T(8,128)(2,1)S(1)}, u32[]{:S(2)}, u32[]{:S(2)}) collective-permute-start(f16[73,8,128]{2,1,0:T(8,128)(2,1)S(1)} %constant_dynamic-update-slice_fusion.18), channel_id=1, source_target_pairs={{0,8},{2,10},{4,12},{6,14},{8,0},{10,2},{12,4},{14,6},{16,24},{18,... | collective-permute-start | bytes 448520 | tf_op jit(solution)/shard_map/ppermute | solution.py:319
  41.9 17.0 %collective-permute-start.13 = (f16[73,8,128]{2,1,0:T(8,128)(2,1)S(1)}, f16[73,8,128]{2,1,0:T(8,128)(2,1)S(1)}, u32[]{:S(2)}, u32[]{:S(2)}) collective-permute-start(f16[73,8,128]{2,1,0:T(8,128)(2,1)S(1)} %constant_dynamic-update-slice_fusion.17), channel_id=1, source_target_pairs={{0,8},{2,10},{4,12},{6,14},{8,0},{10,2},{12,4},{14,6},{16,24},{18,... | collective-permute-start | bytes 448520 | tf_op jit(solution)/shard_map/ppermute | solution.py:319
  42.7 16.1 %collective-permute-start.14 = (f16[73,8,128]{2,1,0:T(8,128)(2,1)S(1)}, f16[73,8,128]{2,1,0:T(8,128)(2,1)S(1)}, u32[]{:S(2)}, u32[]{:S(2)}) collective-permute-start(f16[73,8,128]{2,1,0:T(8,128)(2,1)S(1)} %constant_dynamic-update-slice_fusion.16), channel_id=1, source_target_pairs={{0,16},{2,18},{4,20},{6,22},{8,24},{10,26},{12,28},{14,30},{16,0},... | collective-permute-start | bytes 448520 | tf_op jit(solution)/shard_map/ppermute | solution.py:319
  45.5 12.6 %collective-permute-start.19 = (f16[9,8,1,8,128]{4,3,1,0,2:T(8,128)(2,1)S(1)}, f16[9,8,1,8,128]{4,3,1,0,2:T(8,128)(2,1)S(1)}, u32[]{:S(2)}, u32[]{:S(2)}) collective-permute-start(f16[9,8,1,8,128]{4,3,1,0,2:T(8,128)(2,1)S(1)} %bitcast.396), channel_id=1, source_target_pairs={{0,16},{2,18},{4,20},{6,22},{8,24},{10,26},{12,28},{14,30},{16,0},... | collective-permute-start | bytes 442376 | tf_op jit(solution)/shard_map/ppermute | solution.py:319
  45.9 8.8 %collective-permute-start.18 = (f16[9,8,1,8,128]{4,3,1,0,2:T(8,128)(2,1)S(1)}, f16[9,8,1,8,128]{4,3,1,0,2:T(8,128)(2,1)S(1)}, u32[]{:S(2)}, u32[]{:S(2)}) collective-permute-start(f16[9,8,1,8,128]{4,3,1,0,2:T(8,128)(2,1)S(1)} %bitcast.397), channel_id=1, source_target_pairs={{0,8},{2,10},{4,12},{6,14},{8,0},{10,2},{12,4},{14,6},{16,24},{18,... | collective-permute-start | bytes 442376 | tf_op jit(solution)/shard_map/ppermute | solution.py:319
  47.4 11.4 %collective-permute-start.12 = (f16[9,8,1,8,128]{4,3,2,1,0:T(8,128)(2,1)S(1)}, f16[9,8,1,8,128]{4,3,2,1,0:T(8,128)(2,1)S(1)}, u32[]{:S(2)}, u32[]{:S(2)}) collective-permute-start(f16[9,8,1,8,128]{4,3,2,1,0:T(8,128)(2,1)S(1)} %bitcast.398), channel_id=1, source_target_pairs={{0,4},{2,6},{4,0},{6,2},{8,12},{10,14},{12,8},{14,10},{16,20},{18,... | collective-permute-start | bytes 442376 | tf_op jit(solution)/shard_map/ppermute | solution.py:319
  54.7 12.9 %collective-permute-start.21 = (f16[1,9,8,1,8,128]{5,4,2,1,3,0:T(8,128)(2,1)S(1)}, f16[1,9,8,1,8,128]{5,4,2,1,3,0:T(8,128)(2,1)S(1)}, u32[]{:S(2)}, u32[]{:S(2)}) collective-permute-start(f16[1,9,8,1,8,128]{5,4,2,1,3,0:T(8,128)(2,1)S(1)} %bitcast.407), channel_id=1, source_target_pairs={{0,4},{2,6},{4,0},{6,2},{8,12},{10,14},{12,8},{14,10},{16,20},{18,... | collective-permute-start | bytes 442376 | tf_op jit(solution)/shard_map/ppermute | solution.py:319
  58.2 7.7 %collective-permute-start.20 = (f16[9,8,1,8,128]{4,3,1,0,2:T(8,128)(2,1)S(1)}, f16[9,8,1,8,128]{4,3,1,0,2:T(8,128)(2,1)S(1)}, u32[]{:S(2)}, u32[]{:S(2)}) collective-permute-start(f16[9,8,1,8,128]{4,3,1,0,2:T(8,128)(2,1)S(1)} %collective-permute-done.19), channel_id=1, source_target_pairs={{0,8},{2,10},{4,12},{6,14},{8,0},{10,2},{12,4},{14,6},{16,24},{18,... | collective-permute-start | bytes 442376 | tf_op jit(solution)/shard_map/ppermute | solution.py:319
  59.0 10.4 %collective-permute-start.24 = (f16[9,8,1,8,128]{4,3,1,0,2:T(8,128)(2,1)S(1)}, f16[9,8,1,8,128]{4,3,1,0,2:T(8,128)(2,1)S(1)}, u32[]{:S(2)}, u32[]{:S(2)}) collective-permute-start(f16[9,8,1,8,128]{4,3,1,0,2:T(8,128)(2,1)S(1)} %bitcast.389), channel_id=1, source_target_pairs={{0,8},{2,10},{4,12},{6,14},{8,0},{10,2},{12,4},{14,6},{16,24},{18,... | collective-permute-start | bytes 442376 | tf_op jit(solution)/shard_map/ppermute | solution.py:319
  60.6 17.3 %collective-permute-start.25 = (f16[9,8,1,8,128]{4,3,1,0,2:T(8,128)(2,1)S(1)}, f16[9,8,1,8,128]{4,3,1,0,2:T(8,128)(2,1)S(1)}, u32[]{:S(2)}, u32[]{:S(2)}) collective-permute-start(f16[9,8,1,8,128]{4,3,1,0,2:T(8,128)(2,1)S(1)} %bitcast.390), channel_id=1, source_target_pairs={{0,4},{2,6},{4,0},{6,2},{8,12},{10,14},{12,8},{14,10},{16,20},{18,... | collective-permute-start | bytes 442376 | tf_op jit(solution)/shard_map/ppermute | solution.py:319
  62.1 8.4 %collective-permute-start.16 = (f16[9,8,1,8,128]{4,3,2,1,0:T(8,128)(2,1)S(1)}, f16[9,8,1,8,128]{4,3,2,1,0:T(8,128)(2,1)S(1)}, u32[]{:S(2)}, u32[]{:S(2)}) collective-permute-start(f16[9,8,1,8,128]{4,3,2,1,0:T(8,128)(2,1)S(1)} %bitcast.393), channel_id=1, source_target_pairs={{0,16},{2,18},{4,20},{6,22},{8,24},{10,26},{12,28},{14,30},{16,0},... | collective-permute-start | bytes 442376 | tf_op jit(solution)/shard_map/ppermute | solution.py:319
  65.9 21.7 %collective-permute-start.15 = (f32[128,1152]{1,0:T(8,128)S(1)}, f32[128,1152]{1,0:T(8,128)S(1)}, u32[]{:S(2)}, u32[]{:S(2)}) collective-permute-start(f32[128,1152]{1,0:T(8,128)S(1)} %dynamic-slice_select_fusion), channel_id=1, source_target_pairs={{0,1},{1,0},{2,3},{3,2},{4,5},{5,4},{6,7},{7,6},{8,9},{9,8},{10,11... | collective-permute-start | bytes 1769480 | tf_op jit(solution)/shard_map/ppermute | solution.py:438
  67.6 16.9 %collective-permute-start.22 = (f16[2,9,8,1,8,128]{5,4,2,1,3,0:T(8,128)(2,1)S(1)}, f16[2,9,8,1,8,128]{5,4,2,1,3,0:T(8,128)(2,1)S(1)}, u32[]{:S(2)}, u32[]{:S(2)}) collective-permute-start(f16[2,9,8,1,8,128]{5,4,2,1,3,0:T(8,128)(2,1)S(1)} %pad_maximum_fusion), channel_id=1, source_target_pairs={{0,4},{2,6},{4,0},{6,2},{8,12},{10,14},{12,8},{14,10},{16,20},{18,... | collective-permute-start | bytes 884744 | tf_op jit(solution)/shard_map/ppermute | solution.py:319
  70.6 14.7 %collective-permute-start.26 = (f16[2,9,8,1,8,128]{5,4,2,1,3,0:T(8,128)(2,1)S(1)}, f16[2,9,8,1,8,128]{5,4,2,1,3,0:T(8,128)(2,1)S(1)}, u32[]{:S(2)}, u32[]{:S(2)}) collective-permute-start(f16[2,9,8,1,8,128]{5,4,2,1,3,0:T(8,128)(2,1)S(1)} %pad_maximum_fusion.1), channel_id=1, source_target_pairs={{0,4},{2,6},{4,0},{6,2},{8,12},{10,14},{12,8},{14,10},{16,20},{18,... | collective-permute-start | bytes 884744 | tf_op jit(solution)/shard_map/ppermute | solution.py:319
  70.7 5.2 %collective-permute-start.17 = (f16[9,8,1,8,128]{4,3,2,1,0:T(8,128)(2,1)S(1)}, f16[9,8,1,8,128]{4,3,2,1,0:T(8,128)(2,1)S(1)}, u32[]{:S(2)}, u32[]{:S(2)}) collective-permute-start(f16[9,8,1,8,128]{4,3,2,1,0:T(8,128)(2,1)S(1)} %collective-permute-done.16), channel_id=1, source_target_pairs={{0,8},{2,10},{4,12},{6,14},{8,0},{10,2},{12,4},{14,6},{16,24},{18,... | collective-permute-start | bytes 442376 | tf_op jit(solution)/shard_map/ppermute | solution.py:319
  75.9 9.6 %collective-permute-start.28 = (f16[1,9,8,1,8,128]{5,4,2,1,3,0:T(8,128)(2,1)S(1)}, f16[1,9,8,1,8,128]{5,4,2,1,3,0:T(8,128)(2,1)S(1)}, u32[]{:S(2)}, u32[]{:S(2)}) collective-permute-start(f16[1,9,8,1,8,128]{5,4,2,1,3,0:T(8,128)(2,1)S(1)} %bitcast.406), channel_id=1, source_target_pairs={{0,4},{2,6},{4,0},{6,2},{8,12},{10,14},{12,8},{14,10},{16,20},{18,... | collective-permute-start | bytes 442376 | tf_op jit(solution)/shard_map/ppermute | solution.py:319
  84.6 3.7 %collective-permute-start.23 = (f16[8,9,8,1,8,128]{5,4,2,1,3,0:T(8,128)(2,1)S(1)}, f16[8,9,8,1,8,128]{5,4,2,1,3,0:T(8,128)(2,1)S(1)}, u32[]{:S(2)}, u32[]{:S(2)}) collective-permute-start(f16[8,9,8,1,8,128]{5,4,2,1,3,0:T(8,128)(2,1)S(1)} %constant_dynamic-update-slice_fusion), channel_id=1, source_target_pairs={{0,2},{2,0},{4,6},{6,4},{8,10},{10,8},{12,14},{14,12},{16,18},{18,... | collective-permute-start | bytes 3538952 | tf_op jit(solution)/shard_map/ppermute | solution.py:319
  84.7 2.8 %collective-permute-start.30 = (f32[2,8,128]{2,1,0:T(8,128)S(1)}, f32[2,8,128]{2,1,0:T(8,128)S(1)}, u32[]{:S(2)}, u32[]{:S(2)}) collective-permute-start(f32[2,8,128]{2,1,0:T(8,128)S(1)} %fusion.53), channel_id=1, source_target_pairs={{0,2},{2,0},{4,6},{6,4},{8,10},{10,8},{12,14},{14,12},{16,18},{18,... | collective-permute-start | bytes 24584 | tf_op jit(solution)/shard_map/ppermute | solution.py:319
  85.4 4.0 %collective-permute-start.27 = (f16[7,9,8,1,8,128]{5,4,2,1,3,0:T(8,128)(2,1)S(1)}, f16[7,9,8,1,8,128]{5,4,2,1,3,0:T(8,128)(2,1)S(1)}, u32[]{:S(2)}, u32[]{:S(2)}) collective-permute-start(f16[7,9,8,1,8,128]{5,4,2,1,3,0:T(8,128)(2,1)S(1)} %constant_dynamic-update-slice_fusion.6), channel_id=1, source_target_pairs={{0,2},{2,0},{4,6},{6,4},{8,10},{10,8},{12,14},{14,12},{16,18},{18,... | collective-permute-start | bytes 3096584 | tf_op jit(solution)/shard_map/ppermute | solution.py:319
  85.5 4.9 %collective-permute-start.29 = (f16[1,9,8,1,8,128]{5,4,2,1,3,0:T(8,128)(2,1)S(1)}, f16[1,9,8,1,8,128]{5,4,2,1,3,0:T(8,128)(2,1)S(1)}, u32[]{:S(2)}, u32[]{:S(2)}) collective-permute-start(f16[1,9,8,1,8,128]{5,4,2,1,3,0:T(8,128)(2,1)S(1)} %collective-permute-done.28), channel_id=1, source_target_pairs={{0,2},{2,0},{4,6},{6,4},{8,10},{10,8},{12,14},{14,12},{16,18},{18,... | collective-permute-start | bytes 442376 | tf_op jit(solution)/shard_map/ppermute | solution.py:319

commit v9 on v8

--- a/solution.py
+++ b/solution.py
@@ -377,8 +377,8 @@
 
     for side, (values, bits) in enumerate(reduced):
         lowest = common_exponent(values, bits)
-        gate = gathers[0][1] if side else sends[-1]
-        kept = later(scaled_sum(values, lowest)[:-1], gate)
+        gates = (gathers[0][1], input_grad[:TILE, :LANES]) if side else (sends[-1],)
+        kept = later(scaled_sum(values, lowest)[:-1], *gates)
         shard = kept.astype(jnp.float16).reshape(taps, shard_tiles, 1, TILE, LANES)
         halves.append(shard)
         exponents.append(later(lowest, shard))
@@ -386,6 +386,23 @@
         for bit in bits_of_depth[::-1]:
             near[bit] = to_level(shard, bit)
         gathers.append((near, to_column(shard)))
+        if side == 0:
+            if chans == 2:
+                cot = jnp.where(
+                    chan == 0,
+                    jnp.concatenate([own_cot, their_cot], 0),
+                    jnp.concatenate([their_cot, own_cot], 0),
+                )
+            input_grad = input_gradient(cot, w, token(shard[0, 0]))
+
+    if chans == 2:
+        mine = lax.dynamic_slice_in_dim(total, chan * own_outs, own_outs, 0)
+        theirs = lax.dynamic_slice_in_dim(total, (1 - chan) * own_outs, own_outs, 0)
+        theirs = jnp.where(token(halves[1][0, 0])[0, 0] > -1e30, theirs, 0.0)
+        result = mine + lax.ppermute(theirs, "chan", [(0, 1), (1, 0)])
+    else:
+        result = lax.psum_scatter(total, "chan", scatter_dimension=0, tiled=True)
+    result = result.astype(jnp.bfloat16)[None]
 
     for side, (near, own) in enumerate(gathers):
         for step in range(1, depth):
@@ -409,6 +426,7 @@
         if side == 0:
             messages = [(pieces, jnp.concatenate(here + there))]
         else:
+            there[-1] = later(there[-1], grad, result.reshape(-1, TILE, LANES))
             messages = [
                 (pieces[:-1], jnp.concatenate(here + there[:-1])),
                 (pieces[-1:], there[-1]),
@@ -431,21 +449,7 @@
     grad = (grad * factor[None, :, None]).reshape(taps, rows // TILE, 2, TILE, LANES)
     weight_grad = jnp.transpose(grad, (1, 3, 0, 2, 4)).reshape(rows, taps, outs)
 
-    if chans == 2:
-        mine = lax.dynamic_slice_in_dim(total, chan * own_outs, own_outs, 0)
-        theirs = lax.dynamic_slice_in_dim(total, (1 - chan) * own_outs, own_outs, 0)
-        theirs = jnp.where(token(halves[1][0, 0])[0, 0] > -1e30, theirs, 0.0)
-        result = mine + lax.ppermute(theirs, "chan", [(0, 1), (1, 0)])
-        cot = jnp.where(
-            chan == 0,
-            jnp.concatenate([own_cot, their_cot], 0),
-            jnp.concatenate([their_cot, own_cot], 0),
-        )
-    else:
-        result = lax.psum_scatter(total, "chan", scatter_dimension=0, tiled=True)
-    result = result.astype(jnp.bfloat16)[None]
-    input_grad = input_gradient(cot, w, token(near[-1][0, 0]))[None]
-    return (result, input_grad, weight_grad)
+    return (result, input_grad[None], weight_grad)
 
 
 def solution(mesh):

time: 95.4 us -> 128 us (1.34)
  local copies, waits for them, and re-layouts: 6.01 us -> 44.4 us
  starting transfers between devices: 39.6 us -> 31.1 us
  other arithmetic: 7.26 us -> 11 us
  waiting for transfers between devices: 17.7 us -> 16 us
    dynamic_update_slice x32, local copies, waits for them, and re-layouts: 2.02 us -> 29.7 us  [on_device(): lax.dynamic_update_slice(grad, value, (0, base * core_tiles + row, lane,...]
    ppermute x29, starting transfers between devices: 35.2 us -> 26.7 us  [to(): lax.ppermute(value, 'dp', [(i, i ^ distance) for i in range(samples)])]
    unnamed x21 -> x25, local copies, waits for them, and re-layouts: 0.59 us -> 8.85 us
    ppermute x29, waiting for transfers between devices: 17.6 us -> 15.1 us  [to(): lax.ppermute(value, 'dp', [(i, i ^ distance) for i in range(samples)])]
    reshape x1, other arithmetic: 4.64 us -> 6.98 us  [on_device(): weight_grad = jnp.transpose(grad, (1, 3, 0, 2, 4)).reshape(rows, taps, outs)]
    gt x11 -> x14, other arithmetic: 0.07 us -> 2.11 us  [later(): gate.astype(jnp.float32) > -1e+30]
  transfers between devices with their start and end apart: 31 -> 31, of which waited for: 10 -> 6; matrix products, arithmetic and copies ran while one was open for 7% -> 36% of each run, Pallas kernels for 23% -> 17%
where the time goes in v9:
time: 128 us; the launch traced here: 127 us
  local copies, waits for them, and re-layouts  44.4 us (35%)
  starting transfers between devices  31.1 us (24%)
  Pallas kernels  22.2 us (17%)
  waiting for transfers between devices  16 us (12%)
  other arithmetic  11 us (9%)
  between operations  2.45 us (2%)
    dynamic_update_slice x32, local copies, waits for them, and re-layouts, on_device(): lax.dynamic_update_slice(grad, value, (0, base * core_tiles + row, lane,...  29.7 us
    ppermute x29, starting transfers between devices, to(): lax.ppermute(value, 'dp', [(i, i ^ distance) for i in range(samples)])  26.7 us
    ppermute x29, waiting for transfers between devices, to(): lax.ppermute(value, 'dp', [(i, i ^ distance) for i in range(samples)])  15.1 us
    pallas_call x2, Pallas kernels, kernel_grad(): pl.pallas_call(functools.partial(kernel_grad_kernel, depth), out_shape=[j...  10.9 us
    unnamed x25, local copies, waits for them, and re-layouts  8.85 us
    reshape x1, other arithmetic, on_device(): weight_grad = jnp.transpose(grad, (1, 3, 0, 2, 4)).reshape(rows, taps, outs)  6.98 us
    pallas_call x1, Pallas kernels, input_gradient(): pl.pallas_call(input_grad_kernel, out_shape=jax.ShapeDtypeStruct((rows, p...  6.54 us
    pallas_call x1, Pallas kernels, forward(): pl.pallas_call(forward_kernel, out_shape=jax.ShapeDtypeStruct((outs, posi...  4.84 us
  transfers between devices with their start and end apart: 31, of which 6 were waited for; matrix products, arithmetic and copies ran while one was open for 36% of the time, Pallas kernels for 17%

profile of v9, /device:TPU:0, one launch (start us, length us, event | category | flops | bytes accessed | tf_op | source)
XLA Modules:
  0.0 127.1 jit_solution(13378332311640131617)
XLA Ops:
  0.7 1.4 %dynamic-slice_bitcast_fusion = bf16[512,1152]{1,0:T(8,128)(2,1)S(1)} fusion(bf16[1,1024,1152]{2,1,0:T(8,128)(2,1)} %param.3, s32[]{:T(128)S(6)} %select_n.233), kind=kLoop, calls=%fused_computation.1 | loop fusion | bytes 2359300 | tf_op jit(solution)/shard_map/dynamic_slice | solution.py:338
  2.6 2.9 %collective-permute-start.5 = (bf16[128,1152]{1,0:T(8,128)(2,1)}, bf16[128,1152]{1,0:T(8,128)(2,1)S(1)}, u32[]{:S(2)}, u32[]{:S(2)}) collective-permute-start(bf16[128,1152]{1,0:T(8,128)(2,1)} %bitcast.426), channel_id=1, source_target_pairs={{0,1},{1,0},{2,3},{3,2},{4,5},{5,4},{6,7},{7,6},{8,9},{9,8},{10,11... | collective-permute-start | bytes 884744 | tf_op jit(solution)/shard_map/ppermute | solution.py:331
  5.7 5.3 %kernel_grad.2 = (f32[73,8,128]{2,1,0:T(8,128)S(1)}, f32[73,8,128]{2,1,0:T(8,128)S(1)}, f32[73,8,128]{2,1,0:T(8,128)S(1)}, f32[73,8,128]{2,1,0:T(8,128)S(1)}, f3...) custom-call(s32[2]{0:T(128)S(1)} %pad_add_fusion.place_ref, bf16[1024,1152]{1,0:T(8,128)(2,1)} %bitcast.397, ...), custom_call_target="tpu_custom_call" | custom-call | flops 1509949440 | bytes 5308416 | tf_op jit(solution)/shard_map/kernel_grad/pallas_call | solution.py:122
  12.2 0.9 collective-permute-done.5
  13.2 2.1 %collective-permute-start.3 = (f16[2,73,8,128]{3,2,1,0:T(8,128)(2,1)S(1)}, f16[2,73,8,128]{3,2,1,0:T(8,128)(2,1)S(1)}, u32[]{:S(2)}, u32[]{:S(2)}) collective-permute-start(f16[2,73,8,128]{3,2,1,0:T(8,128)(2,1)S(1)} %select_convert_fusion.1), channel_id=1, source_target_pairs={{0,4},{2,6},{4,0},{6,2},{8,12},{10,14},{12,8},{14,10},{16,20},{18,... | collective-permute-start | bytes 897032 | tf_op jit(solution)/shard_map/ppermute | solution.py:319
  15.5 5.6 %kernel_grad.3 = (f32[73,8,128]{2,1,0:T(8,128)S(1)}, f32[73,8,128]{2,1,0:T(8,128)S(1)}, f32[73,8,128]{2,1,0:T(8,128)S(1)}, f32[73,8,128]{2,1,0:T(8,128)S(1)}, f3...) custom-call(s32[2]{0:T(128)S(1)} %pad_add_fusion.place_ref, bf16[1024,1152]{1,0:T(8,128)(2,1)} %bitcast.398, ...), custom_call_target="tpu_custom_call" | custom-call | flops 1509949440 | bytes 5308416 | tf_op jit(solution)/shard_map/kernel_grad/pallas_call | solution.py:122
  21.2 2.0 %collective-permute-start.7 = (f16[2,73,8,128]{3,2,1,0:T(8,128)(2,1)S(1)}, f16[2,73,8,128]{3,2,1,0:T(8,128)(2,1)S(1)}, u32[]{:S(2)}, u32[]{:S(2)}) collective-permute-start(f16[2,73,8,128]{3,2,1,0:T(8,128)(2,1)S(1)} %convert_element_type.380), channel_id=1, source_target_pairs={{0,4},{2,6},{4,0},{6,2},{8,12},{10,14},{12,8},{14,10},{16,20},{18,... | collective-permute-start | bytes 897032 | tf_op jit(solution)/shard_map/ppermute | solution.py:319
  23.4 6.2 %collective-permute-done.2 = f16[2,73,8,128]{3,2,1,0:T(8,128)(2,1)S(1)} collective-permute-done((f16[2,73,8,128]{3,2,1,0:T(8,128)(2,1)S(1)}, f16[2,73,8,128]{3,2,1,0:T(8,128)(2,1)S(1)}, u32[]{:S(2)}, u32[]{:S(2)}) %collective-permute-start.2) | collective-permute-done | bytes 299040 | tf_op jit(solution)/shard_map/ppermute | solution.py:319
  29.7 2.2 %collective-permute-start.4 = (f16[73,8,128]{2,1,0:T(8,128)(2,1)S(1)}, f16[73,8,128]{2,1,0:T(8,128)(2,1)S(1)}, u32[]{:S(2)}, u32[]{:S(2)}) collective-permute-start(f16[73,8,128]{2,1,0:T(8,128)(2,1)S(1)} %constant_dynamic-update-slice_fusion.18), channel_id=1, source_target_pairs={{0,8},{2,10},{4,12},{6,14},{8,0},{10,2},{12,4},{14,6},{16,24},{18,... | collective-permute-start | bytes 448520 | tf_op jit(solution)/shard_map/ppermute | solution.py:319
  32.2 4.4 %collective-permute-done.4 = f16[73,8,128]{2,1,0:T(8,128)(2,1)S(1)} collective-permute-done((f16[73,8,128]{2,1,0:T(8,128)(2,1)S(1)}, f16[73,8,128]{2,1,0:T(8,128)(2,1)S(1)}, u32[]{:S(2)}, u32[]{:S(2)}) %collective-permute-start.4) | collective-permute-done | bytes 149536 | tf_op jit(solution)/shard_map/ppermute | solution.py:319
  36.7 2.9 %collective-permute-start.11 = (f16[73,8,128]{2,1,0:T(8,128)(2,1)S(1)}, f16[73,8,128]{2,1,0:T(8,128)(2,1)S(1)}, u32[]{:S(2)}, u32[]{:S(2)}) collective-permute-start(f16[73,8,128]{2,1,0:T(8,128)(2,1)S(1)} %constant_dynamic-update-slice_fusion.16), channel_id=1, source_target_pairs={{0,16},{2,18},{4,20},{6,22},{8,24},{10,26},{12,28},{14,30},{16,0},... | collective-permute-start | bytes 448520 | tf_op jit(solution)/shard_map/ppermute | solution.py:319
  39.8 1.4 %collective-permute-start.9 = (f16[73,8,128]{2,1,0:T(8,128)(2,1)S(1)}, f16[73,8,128]{2,1,0:T(8,128)(2,1)S(1)}, u32[]{:S(2)}, u32[]{:S(2)}) collective-permute-start(f16[73,8,128]{2,1,0:T(8,128)(2,1)S(1)} %constant_dynamic-update-slice_fusion.15), channel_id=1, source_target_pairs={{0,8},{2,10},{4,12},{6,14},{8,0},{10,2},{12,4},{14,6},{16,24},{18,... | collective-permute-start | bytes 448520 | tf_op jit(solution)/shard_map/ppermute | solution.py:319
  41.2 4.8 %forward.1 = f32[256,1152]{1,0:T(8,128)S(1)} custom-call(bf16[1024,1152]{1,0:T(8,128)(2,1)S(1)} %bitcast.399, bf16[9,1024,256]{2,1,0:T(8,128)(2,1)S(1)} %bitcast.402, f32[8,128]{1,0:T(8,128)S(1)} %fusion.147._), custom_call_target="tpu_custom_call" | custom-call | flops 3019898880 | bytes 8257536 | tf_op jit(solution)/shard_map/forward/pallas_call | solution.py:194
  46.2 0.8 collective-permute-start.13
  47.4 1.4 %collective-permute-start.16 = (f16[9,8,1,8,128]{4,3,1,0,2:T(8,128)(2,1)S(1)}, f16[9,8,1,8,128]{4,3,1,0,2:T(8,128)(2,1)S(1)}, u32[]{:S(2)}, u32[]{:S(2)}) collective-permute-start(f16[9,8,1,8,128]{4,3,1,0,2:T(8,128)(2,1)S(1)} %bitcast.413), channel_id=1, source_target_pairs={{0,8},{2,10},{4,12},{6,14},{8,0},{10,2},{12,4},{14,6},{16,24},{18,... | collective-permute-start | bytes 442376 | tf_op jit(solution)/shard_map/ppermute | solution.py:319
  49.2 1.5 %collective-permute-start.12 = (f16[9,8,1,8,128]{4,3,1,0,2:T(8,128)(2,1)S(1)}, f16[9,8,1,8,128]{4,3,1,0,2:T(8,128)(2,1)S(1)}, u32[]{:S(2)}, u32[]{:S(2)}) collective-permute-start(f16[9,8,1,8,128]{4,3,1,0,2:T(8,128)(2,1)S(1)} %bitcast.415), channel_id=1, source_target_pairs={{0,4},{2,6},{4,0},{6,2},{8,12},{10,14},{12,8},{14,10},{16,20},{18,... | collective-permute-start | bytes 442376 | tf_op jit(solution)/shard_map/ppermute | solution.py:319
  50.7 2.5 %collective-permute-start.14 = (f16[73,8,128]{2,1,0:T(8,128)(2,1)S(1)}, f16[73,8,128]{2,1,0:T(8,128)(2,1)S(1)}, u32[]{:S(2)}, u32[]{:S(2)}) collective-permute-start(f16[73,8,128]{2,1,0:T(8,128)(2,1)S(1)} %constant_dynamic-update-slice_fusion.13), channel_id=1, source_target_pairs={{0,16},{2,18},{4,20},{6,22},{8,24},{10,26},{12,28},{14,30},{16,0},... | collective-permute-start | bytes 448520 | tf_op jit(solution)/shard_map/ppermute | solution.py:319
  53.2 6.5 %input_gradient.1 = bf16[1024,1152]{1,0:T(8,128)(2,1)} custom-call(bf16[256,1152]{1,0:T(8,128)(2,1)S(1)} %maximum_select_fusion.cot_ref, bf16[9,1024,256]{2,1,0:T(8,128)(2,1)S(1)} %bitcast.403, f32[8,128]{1,0:T(8,128)S(1)} %convert_bitcast_fusion._), custom_call_target="tpu_custom_call" | custom-call | flops 3019898880 | bytes 7667712 | tf_op jit(solution)/shard_map/input_gradient/pallas_call | solution.py:242
  61.1 0.7 broadcast_in_dim.103
  62.6 0.7 collective-permute-start.18
  63.3 0.8 constant_dynamic-update-slice_fusion.4
  65.5 1.1 collective-permute-start.22
  66.7 1.5 %collective-permute-start.25 = (f16[9,8,1,8,128]{4,3,1,0,2:T(8,128)(2,1)S(1)}, f16[9,8,1,8,128]{4,3,1,0,2:T(8,128)(2,1)S(1)}, u32[]{:S(2)}, u32[]{:S(2)}) collective-permute-start(f16[9,8,1,8,128]{4,3,1,0,2:T(8,128)(2,1)S(1)} %bitcast.408), channel_id=1, source_target_pairs={{0,4},{2,6},{4,0},{6,2},{8,12},{10,14},{12,8},{14,10},{16,20},{18,... | collective-permute-start | bytes 442376 | tf_op jit(solution)/shard_map/ppermute | solution.py:319
  70.1 1.5 %collective-permute-start.15 = (f32[128,1152]{1,0:T(8,128)S(1)}, f32[128,1152]{1,0:T(8,128)S(1)}, u32[]{:S(2)}, u32[]{:S(2)}) collective-permute-start(f32[128,1152]{1,0:T(8,128)S(1)} %dynamic-slice_select_fusion), channel_id=1, source_target_pairs={{0,1},{1,0},{2,3},{3,2},{4,5},{5,4},{6,7},{7,6},{8,9},{9,8},{10,11... | collective-permute-start | bytes 1769480 | tf_op jit(solution)/shard_map/ppermute | solution.py:402
  74.5 1.6 %collective-permute-start.26 = (f16[2,9,8,1,8,128]{5,4,2,1,3,0:T(8,128)(2,1)S(1)}, f16[2,9,8,1,8,128]{5,4,2,1,3,0:T(8,128)(2,1)S(1)}, u32[]{:S(2)}, u32[]{:S(2)}) collective-permute-start(f16[2,9,8,1,8,128]{5,4,2,1,3,0:T(8,128)(2,1)S(1)} %pad_maximum_fusion.1), channel_id=1, source_target_pairs={{0,4},{2,6},{4,0},{6,2},{8,12},{10,14},{12,8},{14,10},{16,20},{18,... | collective-permute-start | bytes 884744 | tf_op jit(solution)/shard_map/ppermute | solution.py:319
  78.0 3.3 %collective-permute-done.24 = f16[9,8,1,8,128]{4,3,1,0,2:T(8,128)(2,1)} collective-permute-done((f16[9,8,1,8,128]{4,3,1,0,2:T(8,128)(2,1)S(1)}, f16[9,8,1,8,128]{4,3,1,0,2:T(8,128)(2,1)}, u32[]{:S(2)}, u32[]{:S(2)}) %collective-permute-start.24) | collective-permute-done | bytes 147488 | tf_op jit(solution)/shard_map/ppermute | solution.py:319
  81.8 1.6 %constant_dynamic-update-slice_fusion.7 = f16[7,9,8,1,8,128]{5,4,2,1,3,0:T(8,128)(2,1)} fusion(f16[7,9,8,1,8,128]{5,4,2,1,3,0:T(8,128)(2,1)} %constant_dynamic-update-slice_fusion.8, f16[9,8,1,8,128]{4,3,1,0,2:T(8,128)(2,1)} %collective-permute-done.24), kind=kLoop, calls=%fused_computation.118 | loop fusion | bytes 294912
  84.2 0.8 constant_dynamic-update-slice_fusion
  86.0 0.8 constant_dynamic-update-slice_fusion.6
  87.6 1.0 reshape_broadcast_in_dim.3
  89.3 0.7 fusion.49
  90.7 0.7 fusion.48
  92.2 0.7 fusion.47
  93.6 0.7 fusion.46
  94.3 0.7 bitcast_dynamic-update-slice_fusion.8
  96.5 0.7 fusion.44
  97.9 0.7 fusion.42
  99.3 0.8 fusion.40
  102.0 1.6 %fusion.39 = f16[9,128,2,8,128]{4,3,2,1,0:T(8,128)(2,1)} fusion(f16[9,128,2,8,128]{4,3,2,1,0:T(8,128)(2,1)} %constant_dynamic-update-slice_fusion.11, s32[]{:T(128)S(6)} %select_n.254, s32[]{:T(128)S(6)} %select_n.269, f16[7,9,8,1,8,128]{5,4,2,1,3,0:T(8,128)(2,1)} %collective-permute-done.27), kind=kLoop, calls=%fused_computation.76 | loop fusion | bytes 294920 | tf_op jit(solution)/shard_map/dynamic_update_slice | solution.py:440
  104.3 1.6 %fusion.38 = f16[9,128,2,8,128]{4,3,2,1,0:T(8,128)(2,1)} fusion(f16[9,128,2,8,128]{4,3,2,1,0:T(8,128)(2,1)} %bitcast_dynamic-update-slice_fusion.6, s32[]{:T(128)S(6)} %select_n.256, s32[]{:T(128)S(6)} %select_n.269, f16[7,9,8,1,8,128]{5,4,2,1,3,0:T(8,128)(2,1)} %collective-permute-done.27), kind=kLoop, calls=%fused_computation.74 | loop fusion | bytes 294920 | tf_op jit(solution)/shard_map/dynamic_update_slice | solution.py:440
  106.7 1.6 %fusion.37 = f16[9,128,2,8,128]{4,3,2,1,0:T(8,128)(2,1)} fusion(f16[9,128,2,8,128]{4,3,2,1,0:T(8,128)(2,1)} %bitcast_dynamic-update-slice_fusion.5, s32[]{:T(128)S(6)} %select_n.258, s32[]{:T(128)S(6)} %select_n.269, f16[7,9,8,1,8,128]{5,4,2,1,3,0:T(8,128)(2,1)} %collective-permute-done.27), kind=kLoop, calls=%fused_computation.72 | loop fusion | bytes 294920 | tf_op jit(solution)/shard_map/dynamic_update_slice | solution.py:440
  108.3 1.6 %bitcast_dynamic-update-slice_fusion.4 = f16[9,128,2,8,128]{4,3,2,1,0:T(8,128)(2,1)} fusion(f16[9,128,2,8,128]{4,3,2,1,0:T(8,128)(2,1)} %fusion.37, s32[]{:T(128)S(6)} %select_n.259, s32[]{:T(128)S(6)} %select_n.269, f16[9,8,1,8,128]{4,3,1,0,2:T(8,128)(2,1)} %collective-permute-done.24), kind=kLoop, calls=%fused_computation.101 | loop fusion | bytes 294920 | tf_op jit(solution)/shard_map/dynamic_update_slice | solution.py:440
  110.0 1.6 %fusion.36 = f16[9,128,2,8,128]{4,3,2,1,0:T(8,128)(2,1)} fusion(f16[9,128,2,8,128]{4,3,2,1,0:T(8,128)(2,1)} %bitcast_dynamic-update-slice_fusion.4, s32[]{:T(128)S(6)} %select_n.260, s32[]{:T(128)S(6)} %select_n.269, f16[7,9,8,1,8,128]{5,4,2,1,3,0:T(8,128)(2,1)} %collective-permute-done.27), kind=kLoop, calls=%fused_computation.70 | loop fusion | bytes 294920 | tf_op jit(solution)/shard_map/dynamic_update_slice | solution.py:440
  112.3 1.6 %fusion.35 = f16[9,128,2,8,128]{4,3,2,1,0:T(8,128)(2,1)} fusion(f16[9,128,2,8,128]{4,3,2,1,0:T(8,128)(2,1)} %bitcast_dynamic-update-slice_fusion.3, s32[]{:T(128)S(6)} %select_n.262, s32[]{:T(128)S(6)} %select_n.269, f16[7,9,8,1,8,128]{5,4,2,1,3,0:T(8,128)(2,1)} %collective-permute-done.27), kind=kLoop, calls=%fused_computation.68 | loop fusion | bytes 294920 | tf_op jit(solution)/shard_map/dynamic_update_slice | solution.py:440
  114.6 1.6 %fusion.33 = f16[9,128,2,8,128]{4,3,2,1,0:T(8,128)(2,1)} fusion(f16[9,128,2,8,128]{4,3,2,1,0:T(8,128)(2,1)} %fusion.34, s32[]{:T(128)S(6)} %select_n.264, s32[]{:T(128)S(6)} %select_n.269, f16[7,9,8,1,8,128]{5,4,2,1,3,0:T(8,128)(2,1)} %collective-permute-done.27), kind=kLoop, calls=%fused_computation.64 | loop fusion | bytes 294920 | tf_op jit(solution)/shard_map/dynamic_update_slice | solution.py:440
  117.0 1.6 %fusion.31 = f16[9,128,2,8,128]{4,3,2,1,0:T(8,128)(2,1)} fusion(f16[9,128,2,8,128]{4,3,2,1,0:T(8,128)(2,1)} %fusion.32, s32[]{:T(128)S(6)} %select_n.266, s32[]{:T(128)S(6)} %select_n.269, f16[7,9,8,1,8,128]{5,4,2,1,3,0:T(8,128)(2,1)} %collective-permute-done.27), kind=kLoop, calls=%fused_computation.60 | loop fusion | bytes 294920 | tf_op jit(solution)/shard_map/dynamic_update_slice | solution.py:440
  119.3 0.7 bitcast_dynamic-update-slice_fusion.2
  120.2 7.0 %multiply_bitcast_fusion = f32[1024,9,256]{2,0,1:T(8,128)} fusion(f16[9,128,2,8,128]{4,3,2,1,0:T(8,128)(2,1)} %bitcast_dynamic-update-slice_fusion.2, f32[128,2,8,128]{3,2,1,0:T(8,128)S(1)} %bitcast.404), kind=kLoop, calls=%fused_computation | loop fusion | flops 4718592 | bytes 15204352 | tf_op jit(solution)/shard_map/reshape | solution.py:450
  (145 shorter events, 27.6 us)
Async XLA Ops:
  2.0 13.4 %copy-start.3 = (bf16[1,128,1152]{2,1,0:T(8,128)(2,1)S(1)}, bf16[1,128,1152]{2,1,0:T(8,128)(2,1)}, u32[]{:S(2)}) copy-start(bf16[1,128,1152]{2,1,0:T(8,128)(2,1)} %param.5) | copy-start | bytes 884740
  2.0 3.6 %collective-permute-start = (bf16[512,1152]{1,0:T(8,128)(2,1)S(1)}, bf16[512,1152]{1,0:T(8,128)(2,1)S(1)}, u32[]{:S(2)}, u32[]{:S(2)}) collective-permute-start(bf16[512,1152]{1,0:T(8,128)(2,1)S(1)} %dynamic-slice_bitcast_fusion), channel_id=1, source_target_pairs={{0,2},{2,0},{4,6},{6,4},{8,10},{10,8},{12,14},{14,12},{16,18},{18,... | collective-permute-start | bytes 3538952 | tf_op jit(solution)/shard_map/ppermute | solution.py:319
  2.5 3.1 %collective-permute-start.1 = (bf16[128,1152]{1,0:T(8,128)(2,1)}, bf16[128,1152]{1,0:T(8,128)(2,1)S(1)}, u32[]{:S(2)}, u32[]{:S(2)}) collective-permute-start(bf16[128,1152]{1,0:T(8,128)(2,1)} %bitcast.425), channel_id=1, source_target_pairs={{0,2},{2,0},{4,6},{6,4},{8,10},{10,8},{12,14},{14,12},{16,18},{18,... | collective-permute-start | bytes 884744 | tf_op jit(solution)/shard_map/ppermute | solution.py:319
  2.6 10.4 %collective-permute-start.5 = (bf16[128,1152]{1,0:T(8,128)(2,1)}, bf16[128,1152]{1,0:T(8,128)(2,1)S(1)}, u32[]{:S(2)}, u32[]{:S(2)}) collective-permute-start(bf16[128,1152]{1,0:T(8,128)(2,1)} %bitcast.426), channel_id=1, source_target_pairs={{0,1},{1,0},{2,3},{3,2},{4,5},{5,4},{6,7},{7,6},{8,9},{9,8},{10,11... | collective-permute-start | bytes 884744 | tf_op jit(solution)/shard_map/ppermute | solution.py:331
  13.1 2.5 %collective-permute-start.6 = (bf16[128,1152]{1,0:T(8,128)(2,1)S(1)}, bf16[128,1152]{1,0:T(8,128)(2,1)S(1)}, u32[]{:S(2)}, u32[]{:S(2)}) collective-permute-start(bf16[128,1152]{1,0:T(8,128)(2,1)S(1)} %broadcast_select_fusion.own_cot), channel_id=1, source_target_pairs={{0,2},{2,0},{4,6},{6,4},{8,10},{10,8},{12,14},{14,12},{16,18},{18,... | collective-permute-start | bytes 884744 | tf_op jit(solution)/shard_map/ppermute | solution.py:319
  13.2 18.7 %collective-permute-start.3 = (f16[2,73,8,128]{3,2,1,0:T(8,128)(2,1)S(1)}, f16[2,73,8,128]{3,2,1,0:T(8,128)(2,1)S(1)}, u32[]{:S(2)}, u32[]{:S(2)}) collective-permute-start(f16[2,73,8,128]{3,2,1,0:T(8,128)(2,1)S(1)} %select_convert_fusion.1), channel_id=1, source_target_pairs={{0,4},{2,6},{4,0},{6,2},{8,12},{10,14},{12,8},{14,10},{16,20},{18,... | collective-permute-start | bytes 897032 | tf_op jit(solution)/shard_map/ppermute | solution.py:319
  15.3 14.3 %collective-permute-start.2 = (f16[2,73,8,128]{3,2,1,0:T(8,128)(2,1)S(1)}, f16[2,73,8,128]{3,2,1,0:T(8,128)(2,1)S(1)}, u32[]{:S(2)}, u32[]{:S(2)}) collective-permute-start(f16[2,73,8,128]{3,2,1,0:T(8,128)(2,1)S(1)} %convert_element_type.352), channel_id=1, source_target_pairs={{0,4},{2,6},{4,0},{6,2},{8,12},{10,14},{12,8},{14,10},{16,20},{18,... | collective-permute-start | bytes 897032 | tf_op jit(solution)/shard_map/ppermute | solution.py:319
  15.4 25.8 %slice-start = ((s8[4718592]{0:T(1024)(128)(4,1)}), s8[4194304]{0:T(1024)(128)(4,1)S(1)}, s32[]{:S(2)}) async-start(s8[4718592]{0:T(1024)(128)(4,1)} %bitcast.400), calls=%async_computation | async-start | bytes 8388608
  15.5 25.7 %copy-start = (bf16[1,1024,1152]{2,1,0:T(8,128)(2,1)S(1)}, bf16[1,1024,1152]{2,1,0:T(8,128)(2,1)}, u32[]{:S(2)}) copy-start(bf16[1,1024,1152]{2,1,0:T(8,128)(2,1)} %param.3) | copy-start | bytes 7077892
  15.5 25.7 %slice-start.1 = ((s8[4718592]{0:T(1024)(128)(4,1)}), s8[524288]{0:T(1024)(128)(4,1)S(1)}, s32[]{:S(2)}) async-start(s8[4718592]{0:T(1024)(128)(4,1)} %bitcast.400), calls=%async_computation.1 | async-start | bytes 1048576
  21.2 18.5 %collective-permute-start.7 = (f16[2,73,8,128]{3,2,1,0:T(8,128)(2,1)S(1)}, f16[2,73,8,128]{3,2,1,0:T(8,128)(2,1)S(1)}, u32[]{:S(2)}, u32[]{:S(2)}) collective-permute-start(f16[2,73,8,128]{3,2,1,0:T(8,128)(2,1)S(1)} %convert_element_type.380), channel_id=1, source_target_pairs={{0,4},{2,6},{4,0},{6,2},{8,12},{10,14},{12,8},{14,10},{16,20},{18,... | collective-permute-start | bytes 897032 | tf_op jit(solution)/shard_map/ppermute | solution.py:319
  23.3 22.8 %collective-permute-start.8 = (f16[2,73,8,128]{3,2,1,0:T(8,128)(2,1)S(1)}, f16[2,73,8,128]{3,2,1,0:T(8,128)(2,1)S(1)}, u32[]{:S(2)}, u32[]{:S(2)}) collective-permute-start(f16[2,73,8,128]{3,2,1,0:T(8,128)(2,1)S(1)} %select_convert_fusion), channel_id=1, source_target_pairs={{0,4},{2,6},{4,0},{6,2},{8,12},{10,14},{12,8},{14,10},{16,20},{18,... | collective-permute-start | bytes 897032 | tf_op jit(solution)/shard_map/ppermute | solution.py:319
  29.7 6.9 %collective-permute-start.4 = (f16[73,8,128]{2,1,0:T(8,128)(2,1)S(1)}, f16[73,8,128]{2,1,0:T(8,128)(2,1)S(1)}, u32[]{:S(2)}, u32[]{:S(2)}) collective-permute-start(f16[73,8,128]{2,1,0:T(8,128)(2,1)S(1)} %constant_dynamic-update-slice_fusion.18), channel_id=1, source_target_pairs={{0,8},{2,10},{4,12},{6,14},{8,0},{10,2},{12,4},{14,6},{16,24},{18,... | collective-permute-start | bytes 448520 | tf_op jit(solution)/shard_map/ppermute | solution.py:319
  32.0 15.0 %collective-permute-start.10 = (f16[73,8,128]{2,1,0:T(8,128)(2,1)S(1)}, f16[73,8,128]{2,1,0:T(8,128)(2,1)S(1)}, u32[]{:S(2)}, u32[]{:S(2)}) collective-permute-start(f16[73,8,128]{2,1,0:T(8,128)(2,1)S(1)} %constant_dynamic-update-slice_fusion.17), channel_id=1, source_target_pairs={{0,8},{2,10},{4,12},{6,14},{8,0},{10,2},{12,4},{14,6},{16,24},{18,... | collective-permute-start | bytes 448520 | tf_op jit(solution)/shard_map/ppermute | solution.py:319
  36.7 10.3 %collective-permute-start.11 = (f16[73,8,128]{2,1,0:T(8,128)(2,1)S(1)}, f16[73,8,128]{2,1,0:T(8,128)(2,1)S(1)}, u32[]{:S(2)}, u32[]{:S(2)}) collective-permute-start(f16[73,8,128]{2,1,0:T(8,128)(2,1)S(1)} %constant_dynamic-update-slice_fusion.16), channel_id=1, source_target_pairs={{0,16},{2,18},{4,20},{6,22},{8,24},{10,26},{12,28},{14,30},{16,0},... | collective-permute-start | bytes 448520 | tf_op jit(solution)/shard_map/ppermute | solution.py:319
  39.8 7.3 %collective-permute-start.9 = (f16[73,8,128]{2,1,0:T(8,128)(2,1)S(1)}, f16[73,8,128]{2,1,0:T(8,128)(2,1)S(1)}, u32[]{:S(2)}, u32[]{:S(2)}) collective-permute-start(f16[73,8,128]{2,1,0:T(8,128)(2,1)S(1)} %constant_dynamic-update-slice_fusion.15), channel_id=1, source_target_pairs={{0,8},{2,10},{4,12},{6,14},{8,0},{10,2},{12,4},{14,6},{16,24},{18,... | collective-permute-start | bytes 448520 | tf_op jit(solution)/shard_map/ppermute | solution.py:319
  46.2 18.7 %collective-permute-start.13 = (f16[73,8,128]{2,1,0:T(8,128)(2,1)S(1)}, f16[73,8,128]{2,1,0:T(8,128)(2,1)S(1)}, u32[]{:S(2)}, u32[]{:S(2)}) collective-permute-start(f16[73,8,128]{2,1,0:T(8,128)(2,1)S(1)} %constant_dynamic-update-slice_fusion.14), channel_id=1, source_target_pairs={{0,8},{2,10},{4,12},{6,14},{8,0},{10,2},{12,4},{14,6},{16,24},{18,... | collective-permute-start | bytes 448520 | tf_op jit(solution)/shard_map/ppermute | solution.py:319
  47.4 14.5 %collective-permute-start.16 = (f16[9,8,1,8,128]{4,3,1,0,2:T(8,128)(2,1)S(1)}, f16[9,8,1,8,128]{4,3,1,0,2:T(8,128)(2,1)S(1)}, u32[]{:S(2)}, u32[]{:S(2)}) collective-permute-start(f16[9,8,1,8,128]{4,3,1,0,2:T(8,128)(2,1)S(1)} %bitcast.413), channel_id=1, source_target_pairs={{0,8},{2,10},{4,12},{6,14},{8,0},{10,2},{12,4},{14,6},{16,24},{18,... | collective-permute-start | bytes 442376 | tf_op jit(solution)/shard_map/ppermute | solution.py:319
  48.8 13.8 %collective-permute-start.17 = (f16[9,8,1,8,128]{4,3,1,0,2:T(8,128)(2,1)S(1)}, f16[9,8,1,8,128]{4,3,1,0,2:T(8,128)(2,1)S(1)}, u32[]{:S(2)}, u32[]{:S(2)}) collective-permute-start(f16[9,8,1,8,128]{4,3,1,0,2:T(8,128)(2,1)S(1)} %bitcast.414), channel_id=1, source_target_pairs={{0,16},{2,18},{4,20},{6,22},{8,24},{10,26},{12,28},{14,30},{16,0},... | collective-permute-start | bytes 442376 | tf_op jit(solution)/shard_map/ppermute | solution.py:319
  49.2 15.7 %collective-permute-start.12 = (f16[9,8,1,8,128]{4,3,1,0,2:T(8,128)(2,1)S(1)}, f16[9,8,1,8,128]{4,3,1,0,2:T(8,128)(2,1)S(1)}, u32[]{:S(2)}, u32[]{:S(2)}) collective-permute-start(f16[9,8,1,8,128]{4,3,1,0,2:T(8,128)(2,1)S(1)} %bitcast.415), channel_id=1, source_target_pairs={{0,4},{2,6},{4,0},{6,2},{8,12},{10,14},{12,8},{14,10},{16,20},{18,... | collective-permute-start | bytes 442376 | tf_op jit(solution)/shard_map/ppermute | solution.py:319
  50.7 14.2 %collective-permute-start.14 = (f16[73,8,128]{2,1,0:T(8,128)(2,1)S(1)}, f16[73,8,128]{2,1,0:T(8,128)(2,1)S(1)}, u32[]{:S(2)}, u32[]{:S(2)}) collective-permute-start(f16[73,8,128]{2,1,0:T(8,128)(2,1)S(1)} %constant_dynamic-update-slice_fusion.13), channel_id=1, source_target_pairs={{0,16},{2,18},{4,20},{6,22},{8,24},{10,26},{12,28},{14,30},{16,0},... | collective-permute-start | bytes 448520 | tf_op jit(solution)/shard_map/ppermute | solution.py:319
  61.9 3.1 %copy-start.1 = (f16[9,128,2,8,128]{4,3,2,1,0:T(8,128)(2,1)}, f16[9,128,2,8,128]{4,3,2,1,0:T(8,128)(2,1)S(1)}, u32[]{:S(2)}) copy-start(f16[9,128,2,8,128]{4,3,2,1,0:T(8,128)(2,1)S(1)} %constant_dynamic-update-slice_fusion.12) | copy-start | bytes 14155780
  62.0 11.1 %collective-permute-start.19 = (f16[1,9,8,1,8,128]{5,4,2,1,3,0:T(8,128)(2,1)S(1)}, f16[1,9,8,1,8,128]{5,4,2,1,3,0:T(8,128)(2,1)S(1)}, u32[]{:S(2)}, u32[]{:S(2)}) collective-permute-start(f16[1,9,8,1,8,128]{5,4,2,1,3,0:T(8,128)(2,1)S(1)} %bitcast.424), channel_id=1, source_target_pairs={{0,4},{2,6},{4,0},{6,2},{8,12},{10,14},{12,8},{14,10},{16,20},{18,... | collective-permute-start | bytes 442376 | tf_op jit(solution)/shard_map/ppermute | solution.py:319
  62.6 7.5 %collective-permute-start.18 = (f16[9,8,1,8,128]{4,3,1,0,2:T(8,128)(2,1)S(1)}, f16[9,8,1,8,128]{4,3,1,0,2:T(8,128)(2,1)S(1)}, u32[]{:S(2)}, u32[]{:S(2)}) collective-permute-start(f16[9,8,1,8,128]{4,3,1,0,2:T(8,128)(2,1)S(1)} %collective-permute-done.17), channel_id=1, source_target_pairs={{0,8},{2,10},{4,12},{6,14},{8,0},{10,2},{12,4},{14,6},{16,24},{18,... | collective-permute-start | bytes 442376 | tf_op jit(solution)/shard_map/ppermute | solution.py:319
  65.1 9.3 %collective-permute-start.23 = (f16[9,8,1,8,128]{4,3,1,0,2:T(8,128)(2,1)S(1)}, f16[9,8,1,8,128]{4,3,1,0,2:T(8,128)(2,1)S(1)}, u32[]{:S(2)}, u32[]{:S(2)}) collective-permute-start(f16[9,8,1,8,128]{4,3,1,0,2:T(8,128)(2,1)S(1)} %bitcast.406), channel_id=1, source_target_pairs={{0,16},{2,18},{4,20},{6,22},{8,24},{10,26},{12,28},{14,30},{16,0},... | collective-permute-start | bytes 442376 | tf_op jit(solution)/shard_map/ppermute | solution.py:319
  65.5 8.9 %collective-permute-start.22 = (f16[9,8,1,8,128]{4,3,1,0,2:T(8,128)(2,1)S(1)}, f16[9,8,1,8,128]{4,3,1,0,2:T(8,128)(2,1)S(1)}, u32[]{:S(2)}, u32[]{:S(2)}) collective-permute-start(f16[9,8,1,8,128]{4,3,1,0,2:T(8,128)(2,1)S(1)} %bitcast.407), channel_id=1, source_target_pairs={{0,8},{2,10},{4,12},{6,14},{8,0},{10,2},{12,4},{14,6},{16,24},{18,... | collective-permute-start | bytes 442376 | tf_op jit(solution)/shard_map/ppermute | solution.py:319
  66.7 16.8 %collective-permute-start.25 = (f16[9,8,1,8,128]{4,3,1,0,2:T(8,128)(2,1)S(1)}, f16[9,8,1,8,128]{4,3,1,0,2:T(8,128)(2,1)S(1)}, u32[]{:S(2)}, u32[]{:S(2)}) collective-permute-start(f16[9,8,1,8,128]{4,3,1,0,2:T(8,128)(2,1)S(1)} %bitcast.408), channel_id=1, source_target_pairs={{0,4},{2,6},{4,0},{6,2},{8,12},{10,14},{12,8},{14,10},{16,20},{18,... | collective-permute-start | bytes 442376 | tf_op jit(solution)/shard_map/ppermute | solution.py:319
  70.1 17.4 %collective-permute-start.15 = (f32[128,1152]{1,0:T(8,128)S(1)}, f32[128,1152]{1,0:T(8,128)S(1)}, u32[]{:S(2)}, u32[]{:S(2)}) collective-permute-start(f32[128,1152]{1,0:T(8,128)S(1)} %dynamic-slice_select_fusion), channel_id=1, source_target_pairs={{0,1},{1,0},{2,3},{3,2},{4,5},{5,4},{6,7},{7,6},{8,9},{9,8},{10,11... | collective-permute-start | bytes 1769480 | tf_op jit(solution)/shard_map/ppermute | solution.py:402
  73.1 11.1 %collective-permute-start.20 = (f16[2,9,8,1,8,128]{5,4,2,1,3,0:T(8,128)(2,1)S(1)}, f16[2,9,8,1,8,128]{5,4,2,1,3,0:T(8,128)(2,1)S(1)}, u32[]{:S(2)}, u32[]{:S(2)}) collective-permute-start(f16[2,9,8,1,8,128]{5,4,2,1,3,0:T(8,128)(2,1)S(1)} %pad_maximum_fusion), channel_id=1, source_target_pairs={{0,4},{2,6},{4,0},{6,2},{8,12},{10,14},{12,8},{14,10},{16,20},{18,... | collective-permute-start | bytes 884744 | tf_op jit(solution)/shard_map/ppermute | solution.py:319
  74.5 11.5 %collective-permute-start.26 = (f16[2,9,8,1,8,128]{5,4,2,1,3,0:T(8,128)(2,1)S(1)}, f16[2,9,8,1,8,128]{5,4,2,1,3,0:T(8,128)(2,1)S(1)}, u32[]{:S(2)}, u32[]{:S(2)}) collective-permute-start(f16[2,9,8,1,8,128]{5,4,2,1,3,0:T(8,128)(2,1)S(1)} %pad_maximum_fusion.1), channel_id=1, source_target_pairs={{0,4},{2,6},{4,0},{6,2},{8,12},{10,14},{12,8},{14,10},{16,20},{18,... | collective-permute-start | bytes 884744 | tf_op jit(solution)/shard_map/ppermute | solution.py:319
  76.1 5.2 %collective-permute-start.24 = (f16[9,8,1,8,128]{4,3,1,0,2:T(8,128)(2,1)S(1)}, f16[9,8,1,8,128]{4,3,1,0,2:T(8,128)(2,1)}, u32[]{:S(2)}, u32[]{:S(2)}) collective-permute-start(f16[9,8,1,8,128]{4,3,1,0,2:T(8,128)(2,1)S(1)} %collective-permute-done.23), channel_id=1, source_target_pairs={{0,8},{2,10},{4,12},{6,14},{8,0},{10,2},{12,4},{14,6},{16,24},{18,... | collective-permute-start | bytes 442376 | tf_op jit(solution)/shard_map/ppermute | solution.py:319
  81.3 19.5 %collective-permute-start.28 = (f16[1,9,8,1,8,128]{5,4,2,1,3,0:T(8,128)(2,1)}, f16[1,9,8,1,8,128]{5,4,2,1,3,0:T(8,128)(2,1)S(1)}, u32[]{:S(2)}, u32[]{:S(2)}) collective-permute-start(f16[1,9,8,1,8,128]{5,4,2,1,3,0:T(8,128)(2,1)} %bitcast.108), channel_id=1, source_target_pairs={{0,4},{2,6},{4,0},{6,2},{8,12},{10,14},{12,8},{14,10},{16,20},{18,... | collective-permute-start | bytes 442376 | tf_op jit(solution)/shard_map/ppermute | solution.py:319
  85.0 4.3 %collective-permute-start.21 = (f16[8,9,8,1,8,128]{5,4,2,1,3,0:T(8,128)(2,1)}, f16[8,9,8,1,8,128]{5,4,2,1,3,0:T(8,128)(2,1)S(1)}, u32[]{:S(2)}, u32[]{:S(2)}) collective-permute-start(f16[8,9,8,1,8,128]{5,4,2,1,3,0:T(8,128)(2,1)} %constant_dynamic-update-slice_fusion), channel_id=1, source_target_pairs={{0,2},{2,0},{4,6},{6,4},{8,10},{10,8},{12,14},{14,12},{16,18},{18,... | collective-permute-start | bytes 3538952 | tf_op jit(solution)/shard_map/ppermute | solution.py:319
  85.0 2.5 %collective-permute-start.30 = (f32[2,8,128]{2,1,0:T(8,128)S(1)}, f32[2,8,128]{2,1,0:T(8,128)S(1)}, u32[]{:S(2)}, u32[]{:S(2)}) collective-permute-start(f32[2,8,128]{2,1,0:T(8,128)S(1)} %fusion.53), channel_id=1, source_target_pairs={{0,2},{2,0},{4,6},{6,4},{8,10},{10,8},{12,14},{14,12},{16,18},{18,... | collective-permute-start | bytes 24584 | tf_op jit(solution)/shard_map/ppermute | solution.py:319
  86.8 15.1 %collective-permute-start.27 = (f16[7,9,8,1,8,128]{5,4,2,1,3,0:T(8,128)(2,1)}, f16[7,9,8,1,8,128]{5,4,2,1,3,0:T(8,128)(2,1)}, u32[]{:S(2)}, u32[]{:S(2)}) collective-permute-start(f16[7,9,8,1,8,128]{5,4,2,1,3,0:T(8,128)(2,1)} %constant_dynamic-update-slice_fusion.6), channel_id=1, source_target_pairs={{0,2},{2,0},{4,6},{6,4},{8,10},{10,8},{12,14},{14,12},{16,18},{18,... | collective-permute-start | bytes 3096584 | tf_op jit(solution)/shard_map/ppermute | solution.py:319
  87.6 31.1 %copy-start.2 = (bf16[128,1152]{1,0:T(8,128)(2,1)}, bf16[128,1152]{1,0:T(8,128)(2,1)S(1)}, u32[]{:S(2)}) copy-start(bf16[128,1152]{1,0:T(8,128)(2,1)S(1)} %add_convert_fusion) | copy-start | bytes 884740
  100.8 18.5 %collective-permute-start.29 = (f16[1,9,8,1,8,128]{5,4,2,1,3,0:T(8,128)(2,1)S(1)}, f16[1,9,8,1,8,128]{5,4,2,1,3,0:T(8,128)(2,1)S(1)}, u32[]{:S(2)}, u32[]{:S(2)}) collective-permute-start(f16[1,9,8,1,8,128]{5,4,2,1,3,0:T(8,128)(2,1)S(1)} %select_select_fusion), channel_id=1, source_target_pairs={{0,2},{2,0},{4,6},{6,4},{8,10},{10,8},{12,14},{14,12},{16,18},{18,... | collective-permute-start | bytes 442376 | tf_op jit(solution)/shard_map/ppermute | solution.py:319

commit v10 on v9

--- a/solution.py
+++ b/solution.py
@@ -395,15 +395,6 @@
                 )
             input_grad = input_gradient(cot, w, token(shard[0, 0]))
 
-    if chans == 2:
-        mine = lax.dynamic_slice_in_dim(total, chan * own_outs, own_outs, 0)
-        theirs = lax.dynamic_slice_in_dim(total, (1 - chan) * own_outs, own_outs, 0)
-        theirs = jnp.where(token(halves[1][0, 0])[0, 0] > -1e30, theirs, 0.0)
-        result = mine + lax.ppermute(theirs, "chan", [(0, 1), (1, 0)])
-    else:
-        result = lax.psum_scatter(total, "chan", scatter_dimension=0, tiled=True)
-    result = result.astype(jnp.bfloat16)[None]
-
     for side, (near, own) in enumerate(gathers):
         for step in range(1, depth):
             if near[step] is None:
@@ -426,7 +417,6 @@
         if side == 0:
             messages = [(pieces, jnp.concatenate(here + there))]
         else:
-            there[-1] = later(there[-1], grad, result.reshape(-1, TILE, LANES))
             messages = [
                 (pieces[:-1], jnp.concatenate(here + there[:-1])),
                 (pieces[-1:], there[-1]),
@@ -449,6 +439,14 @@
     grad = (grad * factor[None, :, None]).reshape(taps, rows // TILE, 2, TILE, LANES)
     weight_grad = jnp.transpose(grad, (1, 3, 0, 2, 4)).reshape(rows, taps, outs)
 
+    if chans == 2:
+        mine = lax.dynamic_slice_in_dim(total, chan * own_outs, own_outs, 0)
+        theirs = lax.dynamic_slice_in_dim(total, (1 - chan) * own_outs, own_outs, 0)
+        theirs = jnp.where(token(halves[1][0, 0])[0, 0] > -1e30, theirs, 0.0)
+        result = mine + lax.ppermute(theirs, "chan", [(0, 1), (1, 0)])
+    else:
+        result = lax.psum_scatter(total, "chan", scatter_dimension=0, tiled=True)
+    result = result.astype(jnp.bfloat16)[None]
     return (result, input_grad[None], weight_grad)
 
 

time: 128 us -> 91.1 us (0.71)
  local copies, waits for them, and re-layouts: 44.4 us -> 6.02 us
  starting transfers between devices: 31.1 us -> 37.1 us
  other arithmetic: 11 us -> 7.98 us
    dynamic_update_slice x32, local copies, waits for them, and re-layouts: 29.7 us -> 2.03 us  [on_device(): lax.dynamic_update_slice(grad, value, (0, base * core_tiles + row, lane,...]
    unnamed x25 -> x21, local copies, waits for them, and re-layouts: 8.85 us -> 0.6 us
    ppermute x29, starting transfers between devices: 26.7 us -> 32.6 us  [to(): lax.ppermute(value, 'dp', [(i, i ^ distance) for i in range(samples)])]
    reshape x1, other arithmetic: 6.98 us -> 4.64 us  [on_device(): weight_grad = jnp.transpose(grad, (1, 3, 0, 2, 4)).reshape(rows, taps, outs)]
    gt x14 -> x12, other arithmetic: 2.11 us -> 0.76 us  [later(): gate.astype(jnp.float32) > -1e+30]
  transfers between devices with their start and end apart: 31 -> 31, of which waited for: 6 -> 8; matrix products, arithmetic and copies ran while one was open for 36% -> 9% of each run, Pallas kernels for 17% -> 24%
where the time goes in v10:
time: 91.1 us; the launch traced here: 90.8 us
  starting transfers between devices  37.1 us (41%)
  Pallas kernels  22.2 us (24%)
  waiting for transfers between devices  14.8 us (16%)
  other arithmetic  7.98 us (9%)
  local copies, waits for them, and re-layouts  6.02 us (7%)
  between operations  2.63 us (3%)
    ppermute x29, starting transfers between devices, to(): lax.ppermute(value, 'dp', [(i, i ^ distance) for i in range(samples)])  32.6 us
    ppermute x29, waiting for transfers between devices, to(): lax.ppermute(value, 'dp', [(i, i ^ distance) for i in range(samples)])  14.8 us
    pallas_call x2, Pallas kernels, kernel_grad(): pl.pallas_call(functools.partial(kernel_grad_kernel, depth), out_shape=[j...  10.8 us
    pallas_call x1, Pallas kernels, input_gradient(): pl.pallas_call(input_grad_kernel, out_shape=jax.ShapeDtypeStruct((rows, p...  6.54 us
    pallas_call x1, Pallas kernels, forward(): pl.pallas_call(forward_kernel, out_shape=jax.ShapeDtypeStruct((outs, posi...  4.84 us
    reshape x1, other arithmetic, on_device(): weight_grad = jnp.transpose(grad, (1, 3, 0, 2, 4)).reshape(rows, taps, outs)  4.64 us
    ppermute x1, starting transfers between devices, on_device(): their_cot = lax.ppermute(own_cot, 'chan', [(0, 1), (1, 0)])  2.95 us
    dynamic_update_slice x32, local copies, waits for them, and re-layouts, on_device(): lax.dynamic_update_slice(grad, value, (0, base * core_tiles + row, lane,...  2.03 us
  transfers between devices with their start and end apart: 31, of which 8 were waited for; matrix products, arithmetic and copies ran while one was open for 9% of the time, Pallas kernels for 24%

profile of v10, /device:TPU:0, one launch (start us, length us, event | category | flops | bytes accessed | tf_op | source)
XLA Modules:
  0.0 90.8 jit_solution(804720607063848815)
XLA Ops:
  0.7 1.4 %dynamic-slice_bitcast_fusion = bf16[512,1152]{1,0:T(8,128)(2,1)S(1)} fusion(bf16[1,1024,1152]{2,1,0:T(8,128)(2,1)} %param.3, s32[]{:T(128)S(6)} %select_n.226), kind=kLoop, calls=%fused_computation.1 | loop fusion | bytes 2359300 | tf_op jit(solution)/shard_map/dynamic_slice | solution.py:338
  2.0 0.5 collective-permute-start
  2.6 2.9 %collective-permute-start.5 = (bf16[128,1152]{1,0:T(8,128)(2,1)}, bf16[128,1152]{1,0:T(8,128)(2,1)S(1)}, u32[]{:S(2)}, u32[]{:S(2)}) collective-permute-start(bf16[128,1152]{1,0:T(8,128)(2,1)} %bitcast.422), channel_id=1, source_target_pairs={{0,1},{1,0},{2,3},{3,2},{4,5},{5,4},{6,7},{7,6},{8,9},{9,8},{10,11... | collective-permute-start | bytes 884744 | tf_op jit(solution)/shard_map/ppermute | solution.py:331
  5.7 5.3 %kernel_grad.2 = (f32[73,8,128]{2,1,0:T(8,128)S(1)}, f32[73,8,128]{2,1,0:T(8,128)S(1)}, f32[73,8,128]{2,1,0:T(8,128)S(1)}, f32[73,8,128]{2,1,0:T(8,128)S(1)}, f3...) custom-call(s32[2]{0:T(128)S(1)} %pad_add_fusion.place_ref, bf16[1024,1152]{1,0:T(8,128)(2,1)} %bitcast.393, ...), custom_call_target="tpu_custom_call" | custom-call | flops 1509949440 | bytes 5308416 | tf_op jit(solution)/shard_map/kernel_grad/pallas_call | solution.py:122
  10.9 0.5 slice.262
  11.5 2.7 %collective-permute-start.2 = (f16[2,73,8,128]{3,2,1,0:T(8,128)(2,1)S(1)}, f16[2,73,8,128]{3,2,1,0:T(8,128)(2,1)S(1)}, u32[]{:S(2)}, u32[]{:S(2)}) collective-permute-start(f16[2,73,8,128]{3,2,1,0:T(8,128)(2,1)S(1)} %convert_element_type.344), channel_id=1, source_target_pairs={{0,4},{2,6},{4,0},{6,2},{8,12},{10,14},{12,8},{14,10},{16,20},{18,... | collective-permute-start | bytes 897032 | tf_op jit(solution)/shard_map/ppermute | solution.py:319
  15.1 0.3 collective-permute-start.3
  15.4 0.1 maximum_select_fusion.cot_ref
  15.5 1.0 %collective-permute-done.6.other_cot = bf16[128,1152]{1,0:T(8,128)(2,1)S(1)} collective-permute-done((bf16[128,1152]{1,0:T(8,128)(2,1)S(1)}, bf16[128,1152]{1,0:T(8,128)(2,1)S(1)}, u32[]{:S(2)}, u32[]{:S(2)}) %collective-permute-start.6) | collective-permute-done | bytes 294944 | tf_op jit(solution)/shard_map/ppermute | solution.py:319
  16.6 5.6 %kernel_grad.3 = (f32[73,8,128]{2,1,0:T(8,128)S(1)}, f32[73,8,128]{2,1,0:T(8,128)S(1)}, f32[73,8,128]{2,1,0:T(8,128)S(1)}, f32[73,8,128]{2,1,0:T(8,128)S(1)}, f3...) custom-call(s32[2]{0:T(128)S(1)} %pad_add_fusion.place_ref, bf16[1024,1152]{1,0:T(8,128)(2,1)} %bitcast.394, ...), custom_call_target="tpu_custom_call" | custom-call | flops 1509949440 | bytes 5308416 | tf_op jit(solution)/shard_map/kernel_grad/pallas_call | solution.py:122
  22.2 0.9 collective-permute-start.7
  23.1 1.3 %collective-permute-start.8 = (f16[2,73,8,128]{3,2,1,0:T(8,128)(2,1)S(1)}, f16[2,73,8,128]{3,2,1,0:T(8,128)(2,1)S(1)}, u32[]{:S(2)}, u32[]{:S(2)}) collective-permute-start(f16[2,73,8,128]{3,2,1,0:T(8,128)(2,1)S(1)} %select_convert_fusion), channel_id=1, source_target_pairs={{0,4},{2,6},{4,0},{6,2},{8,12},{10,14},{12,8},{14,10},{16,20},{18,... | collective-permute-start | bytes 897032 | tf_op jit(solution)/shard_map/ppermute | solution.py:319
  24.5 2.0 %collective-permute-start.4 = (f16[73,8,128]{2,1,0:T(8,128)(2,1)S(1)}, f16[73,8,128]{2,1,0:T(8,128)(2,1)S(1)}, u32[]{:S(2)}, u32[]{:S(2)}) collective-permute-start(f16[73,8,128]{2,1,0:T(8,128)(2,1)S(1)} %constant_dynamic-update-slice_fusion.17), channel_id=1, source_target_pairs={{0,8},{2,10},{4,12},{6,14},{8,0},{10,2},{12,4},{14,6},{16,24},{18,... | collective-permute-start | bytes 448520 | tf_op jit(solution)/shard_map/ppermute | solution.py:319
  26.5 2.0 %collective-permute-done.3 = f16[2,73,8,128]{3,2,1,0:T(8,128)(2,1)S(1)} collective-permute-done((f16[2,73,8,128]{3,2,1,0:T(8,128)(2,1)S(1)}, f16[2,73,8,128]{3,2,1,0:T(8,128)(2,1)S(1)}, u32[]{:S(2)}, u32[]{:S(2)}) %collective-permute-start.3) | collective-permute-done | bytes 299040 | tf_op jit(solution)/shard_map/ppermute | solution.py:319
  28.6 2.2 %collective-permute-start.10 = (f16[73,8,128]{2,1,0:T(8,128)(2,1)S(1)}, f16[73,8,128]{2,1,0:T(8,128)(2,1)S(1)}, u32[]{:S(2)}, u32[]{:S(2)}) collective-permute-start(f16[73,8,128]{2,1,0:T(8,128)(2,1)S(1)} %constant_dynamic-update-slice_fusion.16), channel_id=1, source_target_pairs={{0,8},{2,10},{4,12},{6,14},{8,0},{10,2},{12,4},{14,6},{16,24},{18,... | collective-permute-start | bytes 448520 | tf_op jit(solution)/shard_map/ppermute | solution.py:319
  31.0 2.6 %collective-permute-start.11 = (f16[73,8,128]{2,1,0:T(8,128)(2,1)S(1)}, f16[73,8,128]{2,1,0:T(8,128)(2,1)S(1)}, u32[]{:S(2)}, u32[]{:S(2)}) collective-permute-start(f16[73,8,128]{2,1,0:T(8,128)(2,1)S(1)} %constant_dynamic-update-slice_fusion.15), channel_id=1, source_target_pairs={{0,16},{2,18},{4,20},{6,22},{8,24},{10,26},{12,28},{14,30},{16,0},... | collective-permute-start | bytes 448520 | tf_op jit(solution)/shard_map/ppermute | solution.py:319
  33.7 1.2 %collective-permute-done.7 = f16[2,73,8,128]{3,2,1,0:T(8,128)(2,1)S(1)} collective-permute-done((f16[2,73,8,128]{3,2,1,0:T(8,128)(2,1)S(1)}, f16[2,73,8,128]{3,2,1,0:T(8,128)(2,1)S(1)}, u32[]{:S(2)}, u32[]{:S(2)}) %collective-permute-start.7) | collective-permute-done | bytes 299040 | tf_op jit(solution)/shard_map/ppermute | solution.py:319
  35.0 2.2 %collective-permute-start.9 = (f16[73,8,128]{2,1,0:T(8,128)(2,1)S(1)}, f16[73,8,128]{2,1,0:T(8,128)(2,1)S(1)}, u32[]{:S(2)}, u32[]{:S(2)}) collective-permute-start(f16[73,8,128]{2,1,0:T(8,128)(2,1)S(1)} %constant_dynamic-update-slice_fusion.14), channel_id=1, source_target_pairs={{0,8},{2,10},{4,12},{6,14},{8,0},{10,2},{12,4},{14,6},{16,24},{18,... | collective-permute-start | bytes 448520 | tf_op jit(solution)/shard_map/ppermute | solution.py:319
  37.3 4.8 %forward.1 = f32[256,1152]{1,0:T(8,128)S(1)} custom-call(bf16[1024,1152]{1,0:T(8,128)(2,1)S(1)} %bitcast.395, bf16[9,1024,256]{2,1,0:T(8,128)(2,1)S(1)} %bitcast.398, f32[8,128]{1,0:T(8,128)S(1)} %fusion.146._), custom_call_target="tpu_custom_call" | custom-call | flops 3019898880 | bytes 8257536 | tf_op jit(solution)/shard_map/forward/pallas_call | solution.py:194
  42.3 0.7 collective-permute-start.13
  43.2 2.6 %collective-permute-start.14 = (f16[73,8,128]{2,1,0:T(8,128)(2,1)S(1)}, f16[73,8,128]{2,1,0:T(8,128)(2,1)S(1)}, u32[]{:S(2)}, u32[]{:S(2)}) collective-permute-start(f16[73,8,128]{2,1,0:T(8,128)(2,1)S(1)} %constant_dynamic-update-slice_fusion.12), channel_id=1, source_target_pairs={{0,16},{2,18},{4,20},{6,22},{8,24},{10,26},{12,28},{14,30},{16,0},... | collective-permute-start | bytes 448520 | tf_op jit(solution)/shard_map/ppermute | solution.py:319
  45.9 0.1 fusion.31
  46.0 1.6 %collective-permute-start.12 = (f16[9,8,1,8,128]{4,3,2,1,0:T(8,128)(2,1)S(1)}, f16[9,8,1,8,128]{4,3,2,1,0:T(8,128)(2,1)S(1)}, u32[]{:S(2)}, u32[]{:S(2)}) collective-permute-start(f16[9,8,1,8,128]{4,3,2,1,0:T(8,128)(2,1)S(1)} %bitcast.408), channel_id=1, source_target_pairs={{0,4},{2,6},{4,0},{6,2},{8,12},{10,14},{12,8},{14,10},{16,20},{18,... | collective-permute-start | bytes 442376 | tf_op jit(solution)/shard_map/ppermute | solution.py:319
  47.6 1.4 %collective-permute-start.16 = (f16[9,8,1,8,128]{4,3,1,0,2:T(8,128)(2,1)S(1)}, f16[9,8,1,8,128]{4,3,1,0,2:T(8,128)(2,1)S(1)}, u32[]{:S(2)}, u32[]{:S(2)}) collective-permute-start(f16[9,8,1,8,128]{4,3,1,0,2:T(8,128)(2,1)S(1)} %bitcast.410), channel_id=1, source_target_pairs={{0,8},{2,10},{4,12},{6,14},{8,0},{10,2},{12,4},{14,6},{16,24},{18,... | collective-permute-start | bytes 442376 | tf_op jit(solution)/shard_map/ppermute | solution.py:319
  49.0 0.3 collective-permute-start.17
  49.3 6.5 %input_gradient.1 = bf16[1024,1152]{1,0:T(8,128)(2,1)} custom-call(bf16[256,1152]{1,0:T(8,128)(2,1)S(1)} %maximum_select_fusion.cot_ref, bf16[9,1024,256]{2,1,0:T(8,128)(2,1)S(1)} %bitcast.399, f32[8,128]{1,0:T(8,128)S(1)} %convert_bitcast_fusion._), custom_call_target="tpu_custom_call" | custom-call | flops 3019898880 | bytes 7667712 | tf_op jit(solution)/shard_map/input_gradient/pallas_call | solution.py:242
  55.9 0.7 convert_compare_fusion.4
  56.6 0.7 broadcast_in_dim.96
  57.4 0.6 collective-permute-start.19
  58.1 0.6 collective-permute-done.17
  58.7 0.1 collective-permute-start.18
  59.0 0.2 fusion.26
  59.2 1.9 %collective-permute-start.22 = (f16[9,8,1,8,128]{4,3,1,0,2:T(8,128)(2,1)S(1)}, f16[9,8,1,8,128]{4,3,1,0,2:T(8,128)(2,1)S(1)}, u32[]{:S(2)}, u32[]{:S(2)}) collective-permute-start(f16[9,8,1,8,128]{4,3,1,0,2:T(8,128)(2,1)S(1)} %bitcast.401), channel_id=1, source_target_pairs={{0,8},{2,10},{4,12},{6,14},{8,0},{10,2},{12,4},{14,6},{16,24},{18,... | collective-permute-start | bytes 442376 | tf_op jit(solution)/shard_map/ppermute | solution.py:319
  61.1 2.0 %collective-permute-start.23 = (f16[9,8,1,8,128]{4,3,1,0,2:T(8,128)(2,1)S(1)}, f16[9,8,1,8,128]{4,3,1,0,2:T(8,128)(2,1)S(1)}, u32[]{:S(2)}, u32[]{:S(2)}) collective-permute-start(f16[9,8,1,8,128]{4,3,1,0,2:T(8,128)(2,1)S(1)} %bitcast.402), channel_id=1, source_target_pairs={{0,16},{2,18},{4,20},{6,22},{8,24},{10,26},{12,28},{14,30},{16,0},... | collective-permute-start | bytes 442376 | tf_op jit(solution)/shard_map/ppermute | solution.py:319
  63.1 1.5 %collective-permute-start.25 = (f16[9,8,1,8,128]{4,3,1,0,2:T(8,128)(2,1)S(1)}, f16[9,8,1,8,128]{4,3,1,0,2:T(8,128)(2,1)S(1)}, u32[]{:S(2)}, u32[]{:S(2)}) collective-permute-start(f16[9,8,1,8,128]{4,3,1,0,2:T(8,128)(2,1)S(1)} %bitcast.403), channel_id=1, source_target_pairs={{0,4},{2,6},{4,0},{6,2},{8,12},{10,14},{12,8},{14,10},{16,20},{18,... | collective-permute-start | bytes 442376 | tf_op jit(solution)/shard_map/ppermute | solution.py:319
  64.6 0.5 slice.295
  65.9 1.6 %collective-permute-start.15 = (f32[128,1152]{1,0:T(8,128)S(1)}, f32[128,1152]{1,0:T(8,128)S(1)}, u32[]{:S(2)}, u32[]{:S(2)}) collective-permute-start(f32[128,1152]{1,0:T(8,128)S(1)} %dynamic-slice_select_fusion), channel_id=1, source_target_pairs={{0,1},{1,0},{2,3},{3,2},{4,5},{5,4},{6,7},{7,6},{8,9},{9,8},{10,11... | collective-permute-start | bytes 1769480 | tf_op jit(solution)/shard_map/ppermute | solution.py:446
  67.7 0.6 collective-permute-start.20
  68.5 1.9 %collective-permute-start.26 = (f16[2,9,8,1,8,128]{5,4,2,1,3,0:T(8,128)(2,1)S(1)}, f16[2,9,8,1,8,128]{5,4,2,1,3,0:T(8,128)(2,1)S(1)}, u32[]{:S(2)}, u32[]{:S(2)}) collective-permute-start(f16[2,9,8,1,8,128]{5,4,2,1,3,0:T(8,128)(2,1)S(1)} %pad_maximum_fusion), channel_id=1, source_target_pairs={{0,4},{2,6},{4,0},{6,2},{8,12},{10,14},{12,8},{14,10},{16,20},{18,... | collective-permute-start | bytes 884744 | tf_op jit(solution)/shard_map/ppermute | solution.py:319
  70.4 1.5 %collective-permute-start.24 = (f16[9,8,1,8,128]{4,3,1,0,2:T(8,128)(2,1)S(1)}, f16[9,8,1,8,128]{4,3,1,0,2:T(8,128)(2,1)S(1)}, u32[]{:S(2)}, u32[]{:S(2)}) collective-permute-start(f16[9,8,1,8,128]{4,3,1,0,2:T(8,128)(2,1)S(1)} %collective-permute-done.23), channel_id=1, source_target_pairs={{0,8},{2,10},{4,12},{6,14},{8,0},{10,2},{12,4},{14,6},{16,24},{18,... | collective-permute-start | bytes 442376 | tf_op jit(solution)/shard_map/ppermute | solution.py:319
  72.0 3.6 %collective-permute-done.24 = f16[9,8,1,8,128]{4,3,1,0,2:T(8,128)(2,1)S(1)} collective-permute-done((f16[9,8,1,8,128]{4,3,1,0,2:T(8,128)(2,1)S(1)}, f16[9,8,1,8,128]{4,3,1,0,2:T(8,128)(2,1)S(1)}, u32[]{:S(2)}, u32[]{:S(2)}) %collective-permute-start.24) | collective-permute-done | bytes 147488 | tf_op jit(solution)/shard_map/ppermute | solution.py:319
  75.6 0.2 collective-permute-start.28
  75.9 1.9 %collective-permute-done.20 = f16[2,9,8,1,8,128]{5,4,3,2,1,0:T(8,128)(2,1)S(1)} collective-permute-done((f16[2,9,8,1,8,128]{5,4,3,2,1,0:T(8,128)(2,1)S(1)}, f16[2,9,8,1,8,128]{5,4,3,2,1,0:T(8,128)(2,1)S(1)}, u32[]{:S(2)}, u32[]{:S(2)}) %collective-permute-start.20) | collective-permute-done | bytes 294944 | tf_op jit(solution)/shard_map/ppermute | solution.py:319
  77.9 0.5 collective-permute-start.30
  78.5 3.0 %collective-permute-done.26 = f16[2,9,8,1,8,128]{5,4,2,1,3,0:T(8,128)(2,1)S(1)} collective-permute-done((f16[2,9,8,1,8,128]{5,4,2,1,3,0:T(8,128)(2,1)S(1)}, f16[2,9,8,1,8,128]{5,4,2,1,3,0:T(8,128)(2,1)S(1)}, u32[]{:S(2)}, u32[]{:S(2)}) %collective-permute-start.26) | collective-permute-done | bytes 294944 | tf_op jit(solution)/shard_map/ppermute | solution.py:319
  81.7 1.4 %collective-permute-done.28 = f16[1,9,8,1,8,128]{5,4,2,1,3,0:T(8,128)(2,1)S(1)} collective-permute-done((f16[1,9,8,1,8,128]{5,4,2,1,3,0:T(8,128)(2,1)S(1)}, f16[1,9,8,1,8,128]{5,4,2,1,3,0:T(8,128)(2,1)S(1)}, u32[]{:S(2)}, u32[]{:S(2)}) %collective-permute-start.28) | collective-permute-done | bytes 147488 | tf_op jit(solution)/shard_map/ppermute | solution.py:319
  83.2 0.8 fusion.20
  86.2 4.6 %multiply_bitcast_fusion = f32[1024,9,256]{2,0,1:T(8,128)} fusion(f16[9,128,2,8,128]{4,3,2,1,0:T(8,128)(2,1)S(1)} %bitcast_dynamic-update-slice_fusion, f32[128,2,8,128]{3,2,1,0:T(8,128)S(1)} %bitcast.400), kind=kLoop, calls=%fused_computation | loop fusion | flops 4718592 | bytes 15204352 | tf_op jit(solution)/shard_map/reshape | solution.py:440
  (137 shorter events, 4.7 us)
Async XLA Ops:
  2.0 13.4 %copy-start.1 = (bf16[1,128,1152]{2,1,0:T(8,128)(2,1)S(1)}, bf16[1,128,1152]{2,1,0:T(8,128)(2,1)}, u32[]{:S(2)}) copy-start(bf16[1,128,1152]{2,1,0:T(8,128)(2,1)} %param.5) | copy-start | bytes 884740
  2.0 3.6 %collective-permute-start = (bf16[512,1152]{1,0:T(8,128)(2,1)S(1)}, bf16[512,1152]{1,0:T(8,128)(2,1)S(1)}, u32[]{:S(2)}, u32[]{:S(2)}) collective-permute-start(bf16[512,1152]{1,0:T(8,128)(2,1)S(1)} %dynamic-slice_bitcast_fusion), channel_id=1, source_target_pairs={{0,2},{2,0},{4,6},{6,4},{8,10},{10,8},{12,14},{14,12},{16,18},{18,... | collective-permute-start | bytes 3538952 | tf_op jit(solution)/shard_map/ppermute | solution.py:319
  2.5 3.1 %collective-permute-start.1 = (bf16[128,1152]{1,0:T(8,128)(2,1)}, bf16[128,1152]{1,0:T(8,128)(2,1)S(1)}, u32[]{:S(2)}, u32[]{:S(2)}) collective-permute-start(bf16[128,1152]{1,0:T(8,128)(2,1)} %bitcast.421), channel_id=1, source_target_pairs={{0,2},{2,0},{4,6},{6,4},{8,10},{10,8},{12,14},{14,12},{16,18},{18,... | collective-permute-start | bytes 884744 | tf_op jit(solution)/shard_map/ppermute | solution.py:319
  2.6 12.3 %collective-permute-start.5 = (bf16[128,1152]{1,0:T(8,128)(2,1)}, bf16[128,1152]{1,0:T(8,128)(2,1)S(1)}, u32[]{:S(2)}, u32[]{:S(2)}) collective-permute-start(bf16[128,1152]{1,0:T(8,128)(2,1)} %bitcast.422), channel_id=1, source_target_pairs={{0,1},{1,0},{2,3},{3,2},{4,5},{5,4},{6,7},{7,6},{8,9},{9,8},{10,11... | collective-permute-start | bytes 884744 | tf_op jit(solution)/shard_map/ppermute | solution.py:331
  11.5 12.9 %collective-permute-start.2 = (f16[2,73,8,128]{3,2,1,0:T(8,128)(2,1)S(1)}, f16[2,73,8,128]{3,2,1,0:T(8,128)(2,1)S(1)}, u32[]{:S(2)}, u32[]{:S(2)}) collective-permute-start(f16[2,73,8,128]{3,2,1,0:T(8,128)(2,1)S(1)} %convert_element_type.344), channel_id=1, source_target_pairs={{0,4},{2,6},{4,0},{6,2},{8,12},{10,14},{12,8},{14,10},{16,20},{18,... | collective-permute-start | bytes 897032 | tf_op jit(solution)/shard_map/ppermute | solution.py:319
  14.9 1.6 %collective-permute-start.6 = (bf16[128,1152]{1,0:T(8,128)(2,1)S(1)}, bf16[128,1152]{1,0:T(8,128)(2,1)S(1)}, u32[]{:S(2)}, u32[]{:S(2)}) collective-permute-start(bf16[128,1152]{1,0:T(8,128)(2,1)S(1)} %broadcast_select_fusion.own_cot), channel_id=1, source_target_pairs={{0,2},{2,0},{4,6},{6,4},{8,10},{10,8},{12,14},{14,12},{16,18},{18,... | collective-permute-start | bytes 884744 | tf_op jit(solution)/shard_map/ppermute | solution.py:319
  15.1 13.4 %collective-permute-start.3 = (f16[2,73,8,128]{3,2,1,0:T(8,128)(2,1)S(1)}, f16[2,73,8,128]{3,2,1,0:T(8,128)(2,1)S(1)}, u32[]{:S(2)}, u32[]{:S(2)}) collective-permute-start(f16[2,73,8,128]{3,2,1,0:T(8,128)(2,1)S(1)} %select_convert_fusion.1), channel_id=1, source_target_pairs={{0,4},{2,6},{4,0},{6,2},{8,12},{10,14},{12,8},{14,10},{16,20},{18,... | collective-permute-start | bytes 897032 | tf_op jit(solution)/shard_map/ppermute | solution.py:319
  15.4 21.9 %slice-start = ((s8[4718592]{0:T(1024)(128)(4,1)}), s8[4194304]{0:T(1024)(128)(4,1)S(1)}, s32[]{:S(2)}) async-start(s8[4718592]{0:T(1024)(128)(4,1)} %bitcast.396), calls=%async_computation | async-start | bytes 8388608
  15.5 21.7 %copy-start = (bf16[1,1024,1152]{2,1,0:T(8,128)(2,1)S(1)}, bf16[1,1024,1152]{2,1,0:T(8,128)(2,1)}, u32[]{:S(2)}) copy-start(bf16[1,1024,1152]{2,1,0:T(8,128)(2,1)} %param.3) | copy-start | bytes 7077892
  15.5 21.7 %slice-start.1 = ((s8[4718592]{0:T(1024)(128)(4,1)}), s8[524288]{0:T(1024)(128)(4,1)S(1)}, s32[]{:S(2)}) async-start(s8[4718592]{0:T(1024)(128)(4,1)} %bitcast.396), calls=%async_computation.1 | async-start | bytes 1048576
  22.2 12.7 %collective-permute-start.7 = (f16[2,73,8,128]{3,2,1,0:T(8,128)(2,1)S(1)}, f16[2,73,8,128]{3,2,1,0:T(8,128)(2,1)S(1)}, u32[]{:S(2)}, u32[]{:S(2)}) collective-permute-start(f16[2,73,8,128]{3,2,1,0:T(8,128)(2,1)S(1)} %convert_element_type.372), channel_id=1, source_target_pairs={{0,4},{2,6},{4,0},{6,2},{8,12},{10,14},{12,8},{14,10},{16,20},{18,... | collective-permute-start | bytes 897032 | tf_op jit(solution)/shard_map/ppermute | solution.py:319
  23.1 19.0 %collective-permute-start.8 = (f16[2,73,8,128]{3,2,1,0:T(8,128)(2,1)S(1)}, f16[2,73,8,128]{3,2,1,0:T(8,128)(2,1)S(1)}, u32[]{:S(2)}, u32[]{:S(2)}) collective-permute-start(f16[2,73,8,128]{3,2,1,0:T(8,128)(2,1)S(1)} %select_convert_fusion), channel_id=1, source_target_pairs={{0,4},{2,6},{4,0},{6,2},{8,12},{10,14},{12,8},{14,10},{16,20},{18,... | collective-permute-start | bytes 897032 | tf_op jit(solution)/shard_map/ppermute | solution.py:319
  24.5 6.4 %collective-permute-start.4 = (f16[73,8,128]{2,1,0:T(8,128)(2,1)S(1)}, f16[73,8,128]{2,1,0:T(8,128)(2,1)S(1)}, u32[]{:S(2)}, u32[]{:S(2)}) collective-permute-start(f16[73,8,128]{2,1,0:T(8,128)(2,1)S(1)} %constant_dynamic-update-slice_fusion.17), channel_id=1, source_target_pairs={{0,8},{2,10},{4,12},{6,14},{8,0},{10,2},{12,4},{14,6},{16,24},{18,... | collective-permute-start | bytes 448520 | tf_op jit(solution)/shard_map/ppermute | solution.py:319
  28.6 14.4 %collective-permute-start.10 = (f16[73,8,128]{2,1,0:T(8,128)(2,1)S(1)}, f16[73,8,128]{2,1,0:T(8,128)(2,1)S(1)}, u32[]{:S(2)}, u32[]{:S(2)}) collective-permute-start(f16[73,8,128]{2,1,0:T(8,128)(2,1)S(1)} %constant_dynamic-update-slice_fusion.16), channel_id=1, source_target_pairs={{0,8},{2,10},{4,12},{6,14},{8,0},{10,2},{12,4},{14,6},{16,24},{18,... | collective-permute-start | bytes 448520 | tf_op jit(solution)/shard_map/ppermute | solution.py:319
  31.0 12.0 %collective-permute-start.11 = (f16[73,8,128]{2,1,0:T(8,128)(2,1)S(1)}, f16[73,8,128]{2,1,0:T(8,128)(2,1)S(1)}, u32[]{:S(2)}, u32[]{:S(2)}) collective-permute-start(f16[73,8,128]{2,1,0:T(8,128)(2,1)S(1)} %constant_dynamic-update-slice_fusion.15), channel_id=1, source_target_pairs={{0,16},{2,18},{4,20},{6,22},{8,24},{10,26},{12,28},{14,30},{16,0},... | collective-permute-start | bytes 448520 | tf_op jit(solution)/shard_map/ppermute | solution.py:319
  35.0 8.0 %collective-permute-start.9 = (f16[73,8,128]{2,1,0:T(8,128)(2,1)S(1)}, f16[73,8,128]{2,1,0:T(8,128)(2,1)S(1)}, u32[]{:S(2)}, u32[]{:S(2)}) collective-permute-start(f16[73,8,128]{2,1,0:T(8,128)(2,1)S(1)} %constant_dynamic-update-slice_fusion.14), channel_id=1, source_target_pairs={{0,8},{2,10},{4,12},{6,14},{8,0},{10,2},{12,4},{14,6},{16,24},{18,... | collective-permute-start | bytes 448520 | tf_op jit(solution)/shard_map/ppermute | solution.py:319
  42.3 16.7 %collective-permute-start.13 = (f16[73,8,128]{2,1,0:T(8,128)(2,1)S(1)}, f16[73,8,128]{2,1,0:T(8,128)(2,1)S(1)}, u32[]{:S(2)}, u32[]{:S(2)}) collective-permute-start(f16[73,8,128]{2,1,0:T(8,128)(2,1)S(1)} %constant_dynamic-update-slice_fusion.13), channel_id=1, source_target_pairs={{0,8},{2,10},{4,12},{6,14},{8,0},{10,2},{12,4},{14,6},{16,24},{18,... | collective-permute-start | bytes 448520 | tf_op jit(solution)/shard_map/ppermute | solution.py:319
  43.2 15.7 %collective-permute-start.14 = (f16[73,8,128]{2,1,0:T(8,128)(2,1)S(1)}, f16[73,8,128]{2,1,0:T(8,128)(2,1)S(1)}, u32[]{:S(2)}, u32[]{:S(2)}) collective-permute-start(f16[73,8,128]{2,1,0:T(8,128)(2,1)S(1)} %constant_dynamic-update-slice_fusion.12), channel_id=1, source_target_pairs={{0,16},{2,18},{4,20},{6,22},{8,24},{10,26},{12,28},{14,30},{16,0},... | collective-permute-start | bytes 448520 | tf_op jit(solution)/shard_map/ppermute | solution.py:319
  46.0 12.9 %collective-permute-start.12 = (f16[9,8,1,8,128]{4,3,2,1,0:T(8,128)(2,1)S(1)}, f16[9,8,1,8,128]{4,3,2,1,0:T(8,128)(2,1)S(1)}, u32[]{:S(2)}, u32[]{:S(2)}) collective-permute-start(f16[9,8,1,8,128]{4,3,2,1,0:T(8,128)(2,1)S(1)} %bitcast.408), channel_id=1, source_target_pairs={{0,4},{2,6},{4,0},{6,2},{8,12},{10,14},{12,8},{14,10},{16,20},{18,... | collective-permute-start | bytes 442376 | tf_op jit(solution)/shard_map/ppermute | solution.py:319
  47.6 9.8 %collective-permute-start.16 = (f16[9,8,1,8,128]{4,3,1,0,2:T(8,128)(2,1)S(1)}, f16[9,8,1,8,128]{4,3,1,0,2:T(8,128)(2,1)S(1)}, u32[]{:S(2)}, u32[]{:S(2)}) collective-permute-start(f16[9,8,1,8,128]{4,3,1,0,2:T(8,128)(2,1)S(1)} %bitcast.410), channel_id=1, source_target_pairs={{0,8},{2,10},{4,12},{6,14},{8,0},{10,2},{12,4},{14,6},{16,24},{18,... | collective-permute-start | bytes 442376 | tf_op jit(solution)/shard_map/ppermute | solution.py:319
  49.0 9.7 %collective-permute-start.17 = (f16[9,8,1,8,128]{4,3,1,0,2:T(8,128)(2,1)S(1)}, f16[9,8,1,8,128]{4,3,1,0,2:T(8,128)(2,1)S(1)}, u32[]{:S(2)}, u32[]{:S(2)}) collective-permute-start(f16[9,8,1,8,128]{4,3,1,0,2:T(8,128)(2,1)S(1)} %bitcast.411), channel_id=1, source_target_pairs={{0,16},{2,18},{4,20},{6,22},{8,24},{10,26},{12,28},{14,30},{16,0},... | collective-permute-start | bytes 442376 | tf_op jit(solution)/shard_map/ppermute | solution.py:319
  57.4 10.3 %collective-permute-start.19 = (f16[1,9,8,1,8,128]{5,4,3,2,1,0:T(8,128)(2,1)S(1)}, f16[1,9,8,1,8,128]{5,4,3,2,1,0:T(8,128)(2,1)S(1)}, u32[]{:S(2)}, u32[]{:S(2)}) collective-permute-start(f16[1,9,8,1,8,128]{5,4,3,2,1,0:T(8,128)(2,1)S(1)} %bitcast.419), channel_id=1, source_target_pairs={{0,4},{2,6},{4,0},{6,2},{8,12},{10,14},{12,8},{14,10},{16,20},{18,... | collective-permute-start | bytes 442376 | tf_op jit(solution)/shard_map/ppermute | solution.py:319
  58.7 7.2 %collective-permute-start.18 = (f16[9,8,1,8,128]{4,3,1,0,2:T(8,128)(2,1)S(1)}, f16[9,8,1,8,128]{4,3,1,0,2:T(8,128)(2,1)S(1)}, u32[]{:S(2)}, u32[]{:S(2)}) collective-permute-start(f16[9,8,1,8,128]{4,3,1,0,2:T(8,128)(2,1)S(1)} %collective-permute-done.17), channel_id=1, source_target_pairs={{0,8},{2,10},{4,12},{6,14},{8,0},{10,2},{12,4},{14,6},{16,24},{18,... | collective-permute-start | bytes 442376 | tf_op jit(solution)/shard_map/ppermute | solution.py:319
  59.2 9.2 %collective-permute-start.22 = (f16[9,8,1,8,128]{4,3,1,0,2:T(8,128)(2,1)S(1)}, f16[9,8,1,8,128]{4,3,1,0,2:T(8,128)(2,1)S(1)}, u32[]{:S(2)}, u32[]{:S(2)}) collective-permute-start(f16[9,8,1,8,128]{4,3,1,0,2:T(8,128)(2,1)S(1)} %bitcast.401), channel_id=1, source_target_pairs={{0,8},{2,10},{4,12},{6,14},{8,0},{10,2},{12,4},{14,6},{16,24},{18,... | collective-permute-start | bytes 442376 | tf_op jit(solution)/shard_map/ppermute | solution.py:319
  61.1 7.3 %collective-permute-start.23 = (f16[9,8,1,8,128]{4,3,1,0,2:T(8,128)(2,1)S(1)}, f16[9,8,1,8,128]{4,3,1,0,2:T(8,128)(2,1)S(1)}, u32[]{:S(2)}, u32[]{:S(2)}) collective-permute-start(f16[9,8,1,8,128]{4,3,1,0,2:T(8,128)(2,1)S(1)} %bitcast.402), channel_id=1, source_target_pairs={{0,16},{2,18},{4,20},{6,22},{8,24},{10,26},{12,28},{14,30},{16,0},... | collective-permute-start | bytes 442376 | tf_op jit(solution)/shard_map/ppermute | solution.py:319
  63.1 12.7 %collective-permute-start.25 = (f16[9,8,1,8,128]{4,3,1,0,2:T(8,128)(2,1)S(1)}, f16[9,8,1,8,128]{4,3,1,0,2:T(8,128)(2,1)S(1)}, u32[]{:S(2)}, u32[]{:S(2)}) collective-permute-start(f16[9,8,1,8,128]{4,3,1,0,2:T(8,128)(2,1)S(1)} %bitcast.403), channel_id=1, source_target_pairs={{0,4},{2,6},{4,0},{6,2},{8,12},{10,14},{12,8},{14,10},{16,20},{18,... | collective-permute-start | bytes 442376 | tf_op jit(solution)/shard_map/ppermute | solution.py:319
  65.9 17.2 %collective-permute-start.15 = (f32[128,1152]{1,0:T(8,128)S(1)}, f32[128,1152]{1,0:T(8,128)S(1)}, u32[]{:S(2)}, u32[]{:S(2)}) collective-permute-start(f32[128,1152]{1,0:T(8,128)S(1)} %dynamic-slice_select_fusion), channel_id=1, source_target_pairs={{0,1},{1,0},{2,3},{3,2},{4,5},{5,4},{6,7},{7,6},{8,9},{9,8},{10,11... | collective-permute-start | bytes 1769480 | tf_op jit(solution)/shard_map/ppermute | solution.py:446
  67.7 10.0 %collective-permute-start.20 = (f16[2,9,8,1,8,128]{5,4,3,2,1,0:T(8,128)(2,1)S(1)}, f16[2,9,8,1,8,128]{5,4,3,2,1,0:T(8,128)(2,1)S(1)}, u32[]{:S(2)}, u32[]{:S(2)}) collective-permute-start(f16[2,9,8,1,8,128]{5,4,3,2,1,0:T(8,128)(2,1)S(1)} %maximum_bitcast_fusion), channel_id=1, source_target_pairs={{0,4},{2,6},{4,0},{6,2},{8,12},{10,14},{12,8},{14,10},{16,20},{18,... | collective-permute-start | bytes 884744 | tf_op jit(solution)/shard_map/ppermute | solution.py:319
  68.5 13.0 %collective-permute-start.26 = (f16[2,9,8,1,8,128]{5,4,2,1,3,0:T(8,128)(2,1)S(1)}, f16[2,9,8,1,8,128]{5,4,2,1,3,0:T(8,128)(2,1)S(1)}, u32[]{:S(2)}, u32[]{:S(2)}) collective-permute-start(f16[2,9,8,1,8,128]{5,4,2,1,3,0:T(8,128)(2,1)S(1)} %pad_maximum_fusion), channel_id=1, source_target_pairs={{0,4},{2,6},{4,0},{6,2},{8,12},{10,14},{12,8},{14,10},{16,20},{18,... | collective-permute-start | bytes 884744 | tf_op jit(solution)/shard_map/ppermute | solution.py:319
  70.4 5.1 %collective-permute-start.24 = (f16[9,8,1,8,128]{4,3,1,0,2:T(8,128)(2,1)S(1)}, f16[9,8,1,8,128]{4,3,1,0,2:T(8,128)(2,1)S(1)}, u32[]{:S(2)}, u32[]{:S(2)}) collective-permute-start(f16[9,8,1,8,128]{4,3,1,0,2:T(8,128)(2,1)S(1)} %collective-permute-done.23), channel_id=1, source_target_pairs={{0,8},{2,10},{4,12},{6,14},{8,0},{10,2},{12,4},{14,6},{16,24},{18,... | collective-permute-start | bytes 442376 | tf_op jit(solution)/shard_map/ppermute | solution.py:319
  75.6 7.5 %collective-permute-start.28 = (f16[1,9,8,1,8,128]{5,4,2,1,3,0:T(8,128)(2,1)S(1)}, f16[1,9,8,1,8,128]{5,4,2,1,3,0:T(8,128)(2,1)S(1)}, u32[]{:S(2)}, u32[]{:S(2)}) collective-permute-start(f16[1,9,8,1,8,128]{5,4,2,1,3,0:T(8,128)(2,1)S(1)} %bitcast.420), channel_id=1, source_target_pairs={{0,4},{2,6},{4,0},{6,2},{8,12},{10,14},{12,8},{14,10},{16,20},{18,... | collective-permute-start | bytes 442376 | tf_op jit(solution)/shard_map/ppermute | solution.py:319
  77.8 6.1 %collective-permute-start.21 = (f16[8,9,8,1,8,128]{5,4,3,2,1,0:T(8,128)(2,1)S(1)}, f16[8,9,8,1,8,128]{5,4,3,2,1,0:T(8,128)(2,1)S(1)}, u32[]{:S(2)}, u32[]{:S(2)}) collective-permute-start(f16[8,9,8,1,8,128]{5,4,3,2,1,0:T(8,128)(2,1)S(1)} %constant_dynamic-update-slice_fusion), channel_id=1, source_target_pairs={{0,2},{2,0},{4,6},{6,4},{8,10},{10,8},{12,14},{14,12},{16,18},{18,... | collective-permute-start | bytes 3538952 | tf_op jit(solution)/shard_map/ppermute | solution.py:319
  77.9 5.2 %collective-permute-start.30 = (f32[2,8,128]{2,1,0:T(8,128)S(1)}, f32[2,8,128]{2,1,0:T(8,128)S(1)}, u32[]{:S(2)}, u32[]{:S(2)}) collective-permute-start(f32[2,8,128]{2,1,0:T(8,128)S(1)} %fusion.54), channel_id=1, source_target_pairs={{0,2},{2,0},{4,6},{6,4},{8,10},{10,8},{12,14},{14,12},{16,18},{18,... | collective-permute-start | bytes 24584 | tf_op jit(solution)/shard_map/ppermute | solution.py:319
  81.6 3.4 %collective-permute-start.27 = (f16[7,9,8,1,8,128]{5,4,2,1,3,0:T(8,128)(2,1)S(1)}, f16[7,9,8,1,8,128]{5,4,2,1,3,0:T(8,128)(2,1)S(1)}, u32[]{:S(2)}, u32[]{:S(2)}) collective-permute-start(f16[7,9,8,1,8,128]{5,4,2,1,3,0:T(8,128)(2,1)S(1)} %constant_dynamic-update-slice_fusion.4), channel_id=1, source_target_pairs={{0,2},{2,0},{4,6},{6,4},{8,10},{10,8},{12,14},{14,12},{16,18},{18,... | collective-permute-start | bytes 3096584 | tf_op jit(solution)/shard_map/ppermute | solution.py:319
  83.1 2.9 %collective-permute-start.29 = (f16[1,9,8,1,8,128]{5,4,2,1,3,0:T(8,128)(2,1)S(1)}, f16[1,9,8,1,8,128]{5,4,2,1,3,0:T(8,128)(2,1)S(1)}, u32[]{:S(2)}, u32[]{:S(2)}) collective-permute-start(f16[1,9,8,1,8,128]{5,4,2,1,3,0:T(8,128)(2,1)S(1)} %collective-permute-done.28), channel_id=1, source_target_pairs={{0,2},{2,0},{4,6},{6,4},{8,10},{10,8},{12,14},{14,12},{16,18},{18,... | collective-permute-start | bytes 442376 | tf_op jit(solution)/shard_map/ppermute | solution.py:319

commit v11 on v9

--- a/solution.py
+++ b/solution.py
@@ -385,6 +385,10 @@
         near = [shard] + [None] * (depth - 1)
         for bit in bits_of_depth[::-1]:
             near[bit] = to_level(shard, bit)
+        for step in range(1, depth):
+            if near[step] is None:
+                low = step & -step
+                near[step] = to_level(near[step ^ low], low)
         gathers.append((near, to_column(shard)))
         if side == 0:
             if chans == 2:
@@ -403,19 +407,16 @@
     else:
         result = lax.psum_scatter(total, "chan", scatter_dimension=0, tiled=True)
     result = result.astype(jnp.bfloat16)[None]
-
     for side, (near, own) in enumerate(gathers):
-        for step in range(1, depth):
-            if near[step] is None:
-                low = step & -step
-                near[step] = to_level(near[step ^ low], low)
         steps = list(range(depth))
-        cuts = [steps[1:2], steps[2:]] if side == 0 else [steps[1:-1], steps[-1:]]
+        cuts = [steps[1:-1], steps[-1:]]
         here = [jnp.stack([near[step] for step in cut]) for cut in cuts]
         there = [to_column(values) for values in here]
         if side == 0:
             returned = there[1]
         here, there = [near[0][None]] + here, [own[None]] + there
+        if side == 1:
+            there[-1] = later(there[-1], result[0, :TILE, :LANES])
         pieces = [(column, step, near[step]) for step in steps]
         arrivals = [(steps[0], own)] + [
             (step, values[slot])
@@ -426,7 +427,6 @@
         if side == 0:
             messages = [(pieces, jnp.concatenate(here + there))]
         else:
-            there[-1] = later(there[-1], grad, result.reshape(-1, TILE, LANES))
             messages = [
                 (pieces[:-1], jnp.concatenate(here + there[:-1])),
                 (pieces[-1:], there[-1]),

time: 128 us -> 92.5 us (0.72)
  local copies, waits for them, and re-layouts: 44.4 us -> 5.97 us
  waiting for transfers between devices: 16 us -> 23.5 us
  other arithmetic: 11 us -> 7.35 us
    dynamic_update_slice x32 -> x31, local copies, waits for them, and re-layouts: 29.7 us -> 1.96 us  [on_device(): lax.dynamic_update_slice(grad, value, (0, base * core_tiles + row, lane,...]
    unnamed x25 -> x23, local copies, waits for them, and re-layouts: 8.85 us -> 0.66 us
    ppermute x29, waiting for transfers between devices: 15.1 us -> 22.7 us  [to(): lax.ppermute(value, 'dp', [(i, i ^ distance) for i in range(samples)])]
    reshape x1, other arithmetic: 6.98 us -> 4.64 us  [on_device(): weight_grad = jnp.transpose(grad, (1, 3, 0, 2, 4)).reshape(rows, taps, outs)]
    gt x14 -> x13, other arithmetic: 2.11 us -> 0.77 us  [later(): gate.astype(jnp.float32) > -1e+30]
  transfers between devices with their start and end apart: 31 -> 31, of which waited for: 6 -> 11; matrix products, arithmetic and copies ran while one was open for 36% -> 8% of each run, Pallas kernels for 17% -> 24%
where the time goes in v11:
time: 92.5 us; the launch traced here: 92.3 us
  starting transfers between devices  30.5 us (33%)
  waiting for transfers between devices  23.5 us (25%)
  Pallas kernels  22.2 us (24%)
  other arithmetic  7.35 us (8%)
  local copies, waits for them, and re-layouts  5.97 us (6%)
  between operations  2.64 us (3%)
    ppermute x29, starting transfers between devices, to(): lax.ppermute(value, 'dp', [(i, i ^ distance) for i in range(samples)])  26.1 us
    ppermute x29, waiting for transfers between devices, to(): lax.ppermute(value, 'dp', [(i, i ^ distance) for i in range(samples)])  22.7 us
    pallas_call x2, Pallas kernels, kernel_grad(): pl.pallas_call(functools.partial(kernel_grad_kernel, depth), out_shape=[j...  10.9 us
    pallas_call x1, Pallas kernels, input_gradient(): pl.pallas_call(input_grad_kernel, out_shape=jax.ShapeDtypeStruct((rows, p...  6.54 us
    pallas_call x1, Pallas kernels, forward(): pl.pallas_call(forward_kernel, out_shape=jax.ShapeDtypeStruct((outs, posi...  4.84 us
    reshape x1, other arithmetic, on_device(): weight_grad = jnp.transpose(grad, (1, 3, 0, 2, 4)).reshape(rows, taps, outs)  4.64 us
    ppermute x1, starting transfers between devices, on_device(): their_cot = lax.ppermute(own_cot, 'chan', [(0, 1), (1, 0)])  2.95 us
    dynamic_update_slice x31, local copies, waits for them, and re-layouts, on_device(): lax.dynamic_update_slice(grad, value, (0, base * core_tiles + row, lane,...  1.96 us
  transfers between devices with their start and end apart: 31, of which 11 were waited for; matrix products, arithmetic and copies ran while one was open for 8% of the time, Pallas kernels for 24%

profile of v11, /device:TPU:0, one launch (start us, length us, event | category | flops | bytes accessed | tf_op | source)
XLA Modules:
  0.0 92.3 jit_solution(8555249811949045444)
XLA Ops:
  0.7 1.4 %dynamic-slice_bitcast_fusion = bf16[512,1152]{1,0:T(8,128)(2,1)S(1)} fusion(bf16[1,1024,1152]{2,1,0:T(8,128)(2,1)} %param.3, s32[]{:T(128)S(6)} %select_n.230), kind=kLoop, calls=%fused_computation.1 | loop fusion | bytes 2359300 | tf_op jit(solution)/shard_map/dynamic_slice | solution.py:338
  2.0 0.5 collective-permute-start
  2.6 2.9 %collective-permute-start.5 = (bf16[128,1152]{1,0:T(8,128)(2,1)}, bf16[128,1152]{1,0:T(8,128)(2,1)S(1)}, u32[]{:S(2)}, u32[]{:S(2)}) collective-permute-start(bf16[128,1152]{1,0:T(8,128)(2,1)} %bitcast.418), channel_id=1, source_target_pairs={{0,1},{1,0},{2,3},{3,2},{4,5},{5,4},{6,7},{7,6},{8,9},{9,8},{10,11... | collective-permute-start | bytes 884744 | tf_op jit(solution)/shard_map/ppermute | solution.py:331
  5.7 5.3 %kernel_grad.2 = (f32[73,8,128]{2,1,0:T(8,128)S(1)}, f32[73,8,128]{2,1,0:T(8,128)S(1)}, f32[73,8,128]{2,1,0:T(8,128)S(1)}, f32[73,8,128]{2,1,0:T(8,128)S(1)}, f3...) custom-call(s32[2]{0:T(128)S(1)} %pad_add_fusion.place_ref, bf16[1024,1152]{1,0:T(8,128)(2,1)} %bitcast.389, ...), custom_call_target="tpu_custom_call" | custom-call | flops 1509949440 | bytes 5308416 | tf_op jit(solution)/shard_map/kernel_grad/pallas_call | solution.py:122
  10.9 0.5 slice.265
  12.2 0.9 collective-permute-done.5
  13.2 2.1 %collective-permute-start.3 = (f16[2,73,8,128]{3,2,1,0:T(8,128)(2,1)S(1)}, f16[2,73,8,128]{3,2,1,0:T(8,128)(2,1)S(1)}, u32[]{:S(2)}, u32[]{:S(2)}) collective-permute-start(f16[2,73,8,128]{3,2,1,0:T(8,128)(2,1)S(1)} %select_convert_fusion.1), channel_id=1, source_target_pairs={{0,4},{2,6},{4,0},{6,2},{8,12},{10,14},{12,8},{14,10},{16,20},{18,... | collective-permute-start | bytes 897032 | tf_op jit(solution)/shard_map/ppermute | solution.py:319
  15.4 0.1 maximum_select_fusion.cot_ref
  15.5 5.6 %kernel_grad.3 = (f32[73,8,128]{2,1,0:T(8,128)S(1)}, f32[73,8,128]{2,1,0:T(8,128)S(1)}, f32[73,8,128]{2,1,0:T(8,128)S(1)}, f32[73,8,128]{2,1,0:T(8,128)S(1)}, f3...) custom-call(s32[2]{0:T(128)S(1)} %pad_add_fusion.place_ref, bf16[1024,1152]{1,0:T(8,128)(2,1)} %bitcast.390, ...), custom_call_target="tpu_custom_call" | custom-call | flops 1509949440 | bytes 5308416 | tf_op jit(solution)/shard_map/kernel_grad/pallas_call | solution.py:122
  21.2 2.0 %collective-permute-start.7 = (f16[2,73,8,128]{3,2,1,0:T(8,128)(2,1)S(1)}, f16[2,73,8,128]{3,2,1,0:T(8,128)(2,1)S(1)}, u32[]{:S(2)}, u32[]{:S(2)}) collective-permute-start(f16[2,73,8,128]{3,2,1,0:T(8,128)(2,1)S(1)} %convert_element_type.376), channel_id=1, source_target_pairs={{0,4},{2,6},{4,0},{6,2},{8,12},{10,14},{12,8},{14,10},{16,20},{18,... | collective-permute-start | bytes 897032 | tf_op jit(solution)/shard_map/ppermute | solution.py:319
  23.3 0.1 collective-permute-start.8
  23.4 6.2 %collective-permute-done.2 = f16[2,73,8,128]{3,2,1,0:T(8,128)(2,1)S(1)} collective-permute-done((f16[2,73,8,128]{3,2,1,0:T(8,128)(2,1)S(1)}, f16[2,73,8,128]{3,2,1,0:T(8,128)(2,1)S(1)}, u32[]{:S(2)}, u32[]{:S(2)}) %collective-permute-start.2) | collective-permute-done | bytes 299040 | tf_op jit(solution)/shard_map/ppermute | solution.py:319
  29.7 2.2 %collective-permute-start.4 = (f16[73,8,128]{2,1,0:T(8,128)(2,1)S(1)}, f16[73,8,128]{2,1,0:T(8,128)(2,1)S(1)}, u32[]{:S(2)}, u32[]{:S(2)}) collective-permute-start(f16[73,8,128]{2,1,0:T(8,128)(2,1)S(1)} %constant_dynamic-update-slice_fusion.17), channel_id=1, source_target_pairs={{0,8},{2,10},{4,12},{6,14},{8,0},{10,2},{12,4},{14,6},{16,24},{18,... | collective-permute-start | bytes 448520 | tf_op jit(solution)/shard_map/ppermute | solution.py:319
  32.2 4.4 %collective-permute-done.4 = f16[73,8,128]{2,1,0:T(8,128)(2,1)S(1)} collective-permute-done((f16[73,8,128]{2,1,0:T(8,128)(2,1)S(1)}, f16[73,8,128]{2,1,0:T(8,128)(2,1)S(1)}, u32[]{:S(2)}, u32[]{:S(2)}) %collective-permute-start.4) | collective-permute-done | bytes 149536 | tf_op jit(solution)/shard_map/ppermute | solution.py:319
  36.6 0.1 fusion.14
  36.7 2.9 %collective-permute-start.11 = (f16[73,8,128]{2,1,0:T(8,128)(2,1)S(1)}, f16[73,8,128]{2,1,0:T(8,128)(2,1)S(1)}, u32[]{:S(2)}, u32[]{:S(2)}) collective-permute-start(f16[73,8,128]{2,1,0:T(8,128)(2,1)S(1)} %constant_dynamic-update-slice_fusion.15), channel_id=1, source_target_pairs={{0,16},{2,18},{4,20},{6,22},{8,24},{10,26},{12,28},{14,30},{16,0},... | collective-permute-start | bytes 448520 | tf_op jit(solution)/shard_map/ppermute | solution.py:319
  39.8 1.4 %collective-permute-start.9 = (f16[73,8,128]{2,1,0:T(8,128)(2,1)S(1)}, f16[73,8,128]{2,1,0:T(8,128)(2,1)S(1)}, u32[]{:S(2)}, u32[]{:S(2)}) collective-permute-start(f16[73,8,128]{2,1,0:T(8,128)(2,1)S(1)} %constant_dynamic-update-slice_fusion.14), channel_id=1, source_target_pairs={{0,8},{2,10},{4,12},{6,14},{8,0},{10,2},{12,4},{14,6},{16,24},{18,... | collective-permute-start | bytes 448520 | tf_op jit(solution)/shard_map/ppermute | solution.py:319
  41.2 4.8 %forward.1 = f32[256,1152]{1,0:T(8,128)S(1)} custom-call(bf16[1024,1152]{1,0:T(8,128)(2,1)S(1)} %bitcast.391, bf16[9,1024,256]{2,1,0:T(8,128)(2,1)S(1)} %bitcast.394, f32[8,128]{1,0:T(8,128)S(1)} %fusion.147._), custom_call_target="tpu_custom_call" | custom-call | flops 3019898880 | bytes 8257536 | tf_op jit(solution)/shard_map/forward/pallas_call | solution.py:194
  46.2 0.8 collective-permute-start.13
  47.3 0.1 fusion.31
  47.4 0.1 collective-permute-start.17
  47.6 1.6 %collective-permute-start.16 = (f16[9,8,1,8,128]{4,3,1,0,2:T(8,128)(2,1)S(1)}, f16[9,8,1,8,128]{4,3,1,0,2:T(8,128)(2,1)S(1)}, u32[]{:S(2)}, u32[]{:S(2)}) collective-permute-start(f16[9,8,1,8,128]{4,3,1,0,2:T(8,128)(2,1)S(1)} %bitcast.405), channel_id=1, source_target_pairs={{0,8},{2,10},{4,12},{6,14},{8,0},{10,2},{12,4},{14,6},{16,24},{18,... | collective-permute-start | bytes 442376 | tf_op jit(solution)/shard_map/ppermute | solution.py:319
  49.2 1.5 %collective-permute-start.12 = (f16[9,8,1,8,128]{4,3,2,1,0:T(8,128)(2,1)S(1)}, f16[9,8,1,8,128]{4,3,2,1,0:T(8,128)(2,1)S(1)}, u32[]{:S(2)}, u32[]{:S(2)}) collective-permute-start(f16[9,8,1,8,128]{4,3,2,1,0:T(8,128)(2,1)S(1)} %bitcast.407), channel_id=1, source_target_pairs={{0,4},{2,6},{4,0},{6,2},{8,12},{10,14},{12,8},{14,10},{16,20},{18,... | collective-permute-start | bytes 442376 | tf_op jit(solution)/shard_map/ppermute | solution.py:319
  50.6 2.6 %collective-permute-start.14 = (f16[73,8,128]{2,1,0:T(8,128)(2,1)S(1)}, f16[73,8,128]{2,1,0:T(8,128)(2,1)S(1)}, u32[]{:S(2)}, u32[]{:S(2)}) collective-permute-start(f16[73,8,128]{2,1,0:T(8,128)(2,1)S(1)} %constant_dynamic-update-slice_fusion.12), channel_id=1, source_target_pairs={{0,16},{2,18},{4,20},{6,22},{8,24},{10,26},{12,28},{14,30},{16,0},... | collective-permute-start | bytes 448520 | tf_op jit(solution)/shard_map/ppermute | solution.py:319
  53.2 6.5 %input_gradient.1 = bf16[1024,1152]{1,0:T(8,128)(2,1)} custom-call(bf16[256,1152]{1,0:T(8,128)(2,1)S(1)} %maximum_select_fusion.cot_ref, bf16[9,1024,256]{2,1,0:T(8,128)(2,1)S(1)} %bitcast.395, f32[8,128]{1,0:T(8,128)S(1)} %convert_bitcast_fusion._), custom_call_target="tpu_custom_call" | custom-call | flops 3019898880 | bytes 7667712 | tf_op jit(solution)/shard_map/input_gradient/pallas_call | solution.py:242
  59.7 0.7 convert_compare_fusion.5
  60.5 0.7 broadcast_in_dim.103
  61.4 0.6 collective-permute-start.19
  62.0 0.7 collective-permute-start.18
  62.9 0.2 fusion.26
  63.1 1.4 %collective-permute-start.22 = (f16[9,8,1,8,128]{4,3,1,0,2:T(8,128)(2,1)S(1)}, f16[9,8,1,8,128]{4,3,1,0,2:T(8,128)(2,1)S(1)}, u32[]{:S(2)}, u32[]{:S(2)}) collective-permute-start(f16[9,8,1,8,128]{4,3,1,0,2:T(8,128)(2,1)S(1)} %bitcast.397), channel_id=1, source_target_pairs={{0,8},{2,10},{4,12},{6,14},{8,0},{10,2},{12,4},{14,6},{16,24},{18,... | collective-permute-start | bytes 442376 | tf_op jit(solution)/shard_map/ppermute | solution.py:319
  64.4 1.5 %collective-permute-start.25 = (f16[9,8,1,8,128]{4,3,1,0,2:T(8,128)(2,1)S(1)}, f16[9,8,1,8,128]{4,3,1,0,2:T(8,128)(2,1)S(1)}, u32[]{:S(2)}, u32[]{:S(2)}) collective-permute-start(f16[9,8,1,8,128]{4,3,1,0,2:T(8,128)(2,1)S(1)} %bitcast.398), channel_id=1, source_target_pairs={{0,4},{2,6},{4,0},{6,2},{8,12},{10,14},{12,8},{14,10},{16,20},{18,... | collective-permute-start | bytes 442376 | tf_op jit(solution)/shard_map/ppermute | solution.py:319
  65.9 0.4 collective-permute-start.23
  66.3 0.5 slice.298
  67.6 0.3 collective-permute-done.18
  67.9 1.5 %collective-permute-start.15 = (f32[128,1152]{1,0:T(8,128)S(1)}, f32[128,1152]{1,0:T(8,128)S(1)}, u32[]{:S(2)}, u32[]{:S(2)}) collective-permute-start(f32[128,1152]{1,0:T(8,128)S(1)} %dynamic-slice_select_fusion), channel_id=1, source_target_pairs={{0,1},{1,0},{2,3},{3,2},{4,5},{5,4},{6,7},{7,6},{8,9},{9,8},{10,11... | collective-permute-start | bytes 1769480 | tf_op jit(solution)/shard_map/ppermute | solution.py:406
  69.6 0.7 collective-permute-start.20
  70.3 3.2 %collective-permute-done.23 = f16[9,8,1,8,128]{4,3,1,0,2:T(8,128)(2,1)S(1)} collective-permute-done((f16[9,8,1,8,128]{4,3,1,0,2:T(8,128)(2,1)S(1)}, f16[9,8,1,8,128]{4,3,1,0,2:T(8,128)(2,1)S(1)}, u32[]{:S(2)}, u32[]{:S(2)}) %collective-permute-start.23) | collective-permute-done | bytes 147488 | tf_op jit(solution)/shard_map/ppermute | solution.py:319
  73.6 0.6 collective-permute-start.26
  74.4 0.1 collective-permute-start.24
  74.6 1.5 %collective-permute-done.20 = f16[1,9,8,1,8,128]{5,4,3,2,1,0:T(8,128)(2,1)S(1)} collective-permute-done((f16[1,9,8,1,8,128]{5,4,3,2,1,0:T(8,128)(2,1)S(1)}, f16[1,9,8,1,8,128]{5,4,3,2,1,0:T(8,128)(2,1)S(1)}, u32[]{:S(2)}, u32[]{:S(2)}) %collective-permute-start.20) | collective-permute-done | bytes 147488 | tf_op jit(solution)/shard_map/ppermute | solution.py:319
  76.2 3.3 %collective-permute-done.24 = f16[9,8,1,8,128]{4,3,1,0,2:T(8,128)(2,1)S(1)} collective-permute-done((f16[9,8,1,8,128]{4,3,1,0,2:T(8,128)(2,1)S(1)}, f16[9,8,1,8,128]{4,3,1,0,2:T(8,128)(2,1)S(1)}, u32[]{:S(2)}, u32[]{:S(2)}) %collective-permute-start.24) | collective-permute-done | bytes 147488 | tf_op jit(solution)/shard_map/ppermute | solution.py:319
  79.6 1.5 %collective-permute-start.28 = (f16[1,9,8,1,8,128]{5,4,2,1,3,0:T(8,128)(2,1)S(1)}, f16[1,9,8,1,8,128]{5,4,2,1,3,0:T(8,128)(2,1)S(1)}, u32[]{:S(2)}, u32[]{:S(2)}) collective-permute-start(f16[1,9,8,1,8,128]{5,4,2,1,3,0:T(8,128)(2,1)S(1)} %bitcast.416), channel_id=1, source_target_pairs={{0,4},{2,6},{4,0},{6,2},{8,12},{10,14},{12,8},{14,10},{16,20},{18,... | collective-permute-start | bytes 442376 | tf_op jit(solution)/shard_map/ppermute | solution.py:319
  81.3 0.3 collective-permute-start.27
  82.8 1.2 %collective-permute-done.27 = f16[7,9,8,1,8,128]{5,4,2,1,3,0:T(8,128)(2,1)S(1)} collective-permute-done((f16[7,9,8,1,8,128]{5,4,2,1,3,0:T(8,128)(2,1)S(1)}, f16[7,9,8,1,8,128]{5,4,2,1,3,0:T(8,128)(2,1)S(1)}, u32[]{:S(2)}, u32[]{:S(2)}) %collective-permute-start.27) | collective-permute-done | bytes 1032224 | tf_op jit(solution)/shard_map/ppermute | solution.py:319
  84.9 1.1 %collective-permute-done.28 = f16[1,9,8,1,8,128]{5,4,2,1,3,0:T(8,128)(2,1)S(1)} collective-permute-done((f16[1,9,8,1,8,128]{5,4,2,1,3,0:T(8,128)(2,1)S(1)}, f16[1,9,8,1,8,128]{5,4,2,1,3,0:T(8,128)(2,1)S(1)}, u32[]{:S(2)}, u32[]{:S(2)}) %collective-permute-start.28) | collective-permute-done | bytes 147488 | tf_op jit(solution)/shard_map/ppermute | solution.py:319
  86.2 1.3 %collective-permute-done.29 = f16[1,9,8,1,8,128]{5,4,2,1,3,0:T(8,128)(2,1)S(1)} collective-permute-done((f16[1,9,8,1,8,128]{5,4,2,1,3,0:T(8,128)(2,1)S(1)}, f16[1,9,8,1,8,128]{5,4,2,1,3,0:T(8,128)(2,1)S(1)}, u32[]{:S(2)}, u32[]{:S(2)}) %collective-permute-start.29) | collective-permute-done | bytes 147488 | tf_op jit(solution)/shard_map/ppermute | solution.py:319
  87.6 4.6 %multiply_bitcast_fusion = f32[1024,9,256]{2,0,1:T(8,128)} fusion(f16[9,128,2,8,128]{4,3,2,1,0:T(8,128)(2,1)S(1)} %bitcast_dynamic-update-slice_fusion, f32[128,2,8,128]{3,2,1,0:T(8,128)S(1)} %bitcast.396), kind=kLoop, calls=%fused_computation | loop fusion | flops 4718592 | bytes 15204352 | tf_op jit(solution)/shard_map/reshape | solution.py:450
  (140 shorter events, 4.9 us)
Async XLA Ops:
  2.0 13.4 %copy-start.2 = (bf16[1,128,1152]{2,1,0:T(8,128)(2,1)S(1)}, bf16[1,128,1152]{2,1,0:T(8,128)(2,1)}, u32[]{:S(2)}) copy-start(bf16[1,128,1152]{2,1,0:T(8,128)(2,1)} %param.5) | copy-start | bytes 884740
  2.0 3.6 %collective-permute-start = (bf16[512,1152]{1,0:T(8,128)(2,1)S(1)}, bf16[512,1152]{1,0:T(8,128)(2,1)S(1)}, u32[]{:S(2)}, u32[]{:S(2)}) collective-permute-start(bf16[512,1152]{1,0:T(8,128)(2,1)S(1)} %dynamic-slice_bitcast_fusion), channel_id=1, source_target_pairs={{0,2},{2,0},{4,6},{6,4},{8,10},{10,8},{12,14},{14,12},{16,18},{18,... | collective-permute-start | bytes 3538952 | tf_op jit(solution)/shard_map/ppermute | solution.py:319
  2.5 3.1 %collective-permute-start.1 = (bf16[128,1152]{1,0:T(8,128)(2,1)}, bf16[128,1152]{1,0:T(8,128)(2,1)S(1)}, u32[]{:S(2)}, u32[]{:S(2)}) collective-permute-start(bf16[128,1152]{1,0:T(8,128)(2,1)} %bitcast.417), channel_id=1, source_target_pairs={{0,2},{2,0},{4,6},{6,4},{8,10},{10,8},{12,14},{14,12},{16,18},{18,... | collective-permute-start | bytes 884744 | tf_op jit(solution)/shard_map/ppermute | solution.py:319
  2.6 10.4 %collective-permute-start.5 = (bf16[128,1152]{1,0:T(8,128)(2,1)}, bf16[128,1152]{1,0:T(8,128)(2,1)S(1)}, u32[]{:S(2)}, u32[]{:S(2)}) collective-permute-start(bf16[128,1152]{1,0:T(8,128)(2,1)} %bitcast.418), channel_id=1, source_target_pairs={{0,1},{1,0},{2,3},{3,2},{4,5},{5,4},{6,7},{7,6},{8,9},{9,8},{10,11... | collective-permute-start | bytes 884744 | tf_op jit(solution)/shard_map/ppermute | solution.py:331
  13.1 2.5 %collective-permute-start.6 = (bf16[128,1152]{1,0:T(8,128)(2,1)S(1)}, bf16[128,1152]{1,0:T(8,128)(2,1)S(1)}, u32[]{:S(2)}, u32[]{:S(2)}) collective-permute-start(bf16[128,1152]{1,0:T(8,128)(2,1)S(1)} %broadcast_select_fusion.own_cot), channel_id=1, source_target_pairs={{0,2},{2,0},{4,6},{6,4},{8,10},{10,8},{12,14},{14,12},{16,18},{18,... | collective-permute-start | bytes 884744 | tf_op jit(solution)/shard_map/ppermute | solution.py:319
  13.2 18.7 %collective-permute-start.3 = (f16[2,73,8,128]{3,2,1,0:T(8,128)(2,1)S(1)}, f16[2,73,8,128]{3,2,1,0:T(8,128)(2,1)S(1)}, u32[]{:S(2)}, u32[]{:S(2)}) collective-permute-start(f16[2,73,8,128]{3,2,1,0:T(8,128)(2,1)S(1)} %select_convert_fusion.1), channel_id=1, source_target_pairs={{0,4},{2,6},{4,0},{6,2},{8,12},{10,14},{12,8},{14,10},{16,20},{18,... | collective-permute-start | bytes 897032 | tf_op jit(solution)/shard_map/ppermute | solution.py:319
  15.3 14.3 %collective-permute-start.2 = (f16[2,73,8,128]{3,2,1,0:T(8,128)(2,1)S(1)}, f16[2,73,8,128]{3,2,1,0:T(8,128)(2,1)S(1)}, u32[]{:S(2)}, u32[]{:S(2)}) collective-permute-start(f16[2,73,8,128]{3,2,1,0:T(8,128)(2,1)S(1)} %convert_element_type.348), channel_id=1, source_target_pairs={{0,4},{2,6},{4,0},{6,2},{8,12},{10,14},{12,8},{14,10},{16,20},{18,... | collective-permute-start | bytes 897032 | tf_op jit(solution)/shard_map/ppermute | solution.py:319
  15.4 25.8 %slice-start = ((s8[4718592]{0:T(1024)(128)(4,1)}), s8[4194304]{0:T(1024)(128)(4,1)S(1)}, s32[]{:S(2)}) async-start(s8[4718592]{0:T(1024)(128)(4,1)} %bitcast.392), calls=%async_computation | async-start | bytes 8388608
  15.5 25.7 %copy-start = (bf16[1,1024,1152]{2,1,0:T(8,128)(2,1)S(1)}, bf16[1,1024,1152]{2,1,0:T(8,128)(2,1)}, u32[]{:S(2)}) copy-start(bf16[1,1024,1152]{2,1,0:T(8,128)(2,1)} %param.3) | copy-start | bytes 7077892
  15.5 25.7 %slice-start.1 = ((s8[4718592]{0:T(1024)(128)(4,1)}), s8[524288]{0:T(1024)(128)(4,1)S(1)}, s32[]{:S(2)}) async-start(s8[4718592]{0:T(1024)(128)(4,1)} %bitcast.392), calls=%async_computation.1 | async-start | bytes 1048576
  21.2 18.5 %collective-permute-start.7 = (f16[2,73,8,128]{3,2,1,0:T(8,128)(2,1)S(1)}, f16[2,73,8,128]{3,2,1,0:T(8,128)(2,1)S(1)}, u32[]{:S(2)}, u32[]{:S(2)}) collective-permute-start(f16[2,73,8,128]{3,2,1,0:T(8,128)(2,1)S(1)} %convert_element_type.376), channel_id=1, source_target_pairs={{0,4},{2,6},{4,0},{6,2},{8,12},{10,14},{12,8},{14,10},{16,20},{18,... | collective-permute-start | bytes 897032 | tf_op jit(solution)/shard_map/ppermute | solution.py:319
  23.3 22.8 %collective-permute-start.8 = (f16[2,73,8,128]{3,2,1,0:T(8,128)(2,1)S(1)}, f16[2,73,8,128]{3,2,1,0:T(8,128)(2,1)S(1)}, u32[]{:S(2)}, u32[]{:S(2)}) collective-permute-start(f16[2,73,8,128]{3,2,1,0:T(8,128)(2,1)S(1)} %select_convert_fusion), channel_id=1, source_target_pairs={{0,4},{2,6},{4,0},{6,2},{8,12},{10,14},{12,8},{14,10},{16,20},{18,... | collective-permute-start | bytes 897032 | tf_op jit(solution)/shard_map/ppermute | solution.py:319
  29.7 6.9 %collective-permute-start.4 = (f16[73,8,128]{2,1,0:T(8,128)(2,1)S(1)}, f16[73,8,128]{2,1,0:T(8,128)(2,1)S(1)}, u32[]{:S(2)}, u32[]{:S(2)}) collective-permute-start(f16[73,8,128]{2,1,0:T(8,128)(2,1)S(1)} %constant_dynamic-update-slice_fusion.17), channel_id=1, source_target_pairs={{0,8},{2,10},{4,12},{6,14},{8,0},{10,2},{12,4},{14,6},{16,24},{18,... | collective-permute-start | bytes 448520 | tf_op jit(solution)/shard_map/ppermute | solution.py:319
  32.0 15.0 %collective-permute-start.10 = (f16[73,8,128]{2,1,0:T(8,128)(2,1)S(1)}, f16[73,8,128]{2,1,0:T(8,128)(2,1)S(1)}, u32[]{:S(2)}, u32[]{:S(2)}) collective-permute-start(f16[73,8,128]{2,1,0:T(8,128)(2,1)S(1)} %constant_dynamic-update-slice_fusion.16), channel_id=1, source_target_pairs={{0,8},{2,10},{4,12},{6,14},{8,0},{10,2},{12,4},{14,6},{16,24},{18,... | collective-permute-start | bytes 448520 | tf_op jit(solution)/shard_map/ppermute | solution.py:319
  36.7 10.3 %collective-permute-start.11 = (f16[73,8,128]{2,1,0:T(8,128)(2,1)S(1)}, f16[73,8,128]{2,1,0:T(8,128)(2,1)S(1)}, u32[]{:S(2)}, u32[]{:S(2)}) collective-permute-start(f16[73,8,128]{2,1,0:T(8,128)(2,1)S(1)} %constant_dynamic-update-slice_fusion.15), channel_id=1, source_target_pairs={{0,16},{2,18},{4,20},{6,22},{8,24},{10,26},{12,28},{14,30},{16,0},... | collective-permute-start | bytes 448520 | tf_op jit(solution)/shard_map/ppermute | solution.py:319
  39.8 7.3 %collective-permute-start.9 = (f16[73,8,128]{2,1,0:T(8,128)(2,1)S(1)}, f16[73,8,128]{2,1,0:T(8,128)(2,1)S(1)}, u32[]{:S(2)}, u32[]{:S(2)}) collective-permute-start(f16[73,8,128]{2,1,0:T(8,128)(2,1)S(1)} %constant_dynamic-update-slice_fusion.14), channel_id=1, source_target_pairs={{0,8},{2,10},{4,12},{6,14},{8,0},{10,2},{12,4},{14,6},{16,24},{18,... | collective-permute-start | bytes 448520 | tf_op jit(solution)/shard_map/ppermute | solution.py:319
  46.2 16.7 %collective-permute-start.13 = (f16[73,8,128]{2,1,0:T(8,128)(2,1)S(1)}, f16[73,8,128]{2,1,0:T(8,128)(2,1)S(1)}, u32[]{:S(2)}, u32[]{:S(2)}) collective-permute-start(f16[73,8,128]{2,1,0:T(8,128)(2,1)S(1)} %constant_dynamic-update-slice_fusion.13), channel_id=1, source_target_pairs={{0,8},{2,10},{4,12},{6,14},{8,0},{10,2},{12,4},{14,6},{16,24},{18,... | collective-permute-start | bytes 448520 | tf_op jit(solution)/shard_map/ppermute | solution.py:319
  47.4 13.9 %collective-permute-start.17 = (f16[9,8,1,8,128]{4,3,1,0,2:T(8,128)(2,1)S(1)}, f16[9,8,1,8,128]{4,3,1,0,2:T(8,128)(2,1)S(1)}, u32[]{:S(2)}, u32[]{:S(2)}) collective-permute-start(f16[9,8,1,8,128]{4,3,1,0,2:T(8,128)(2,1)S(1)} %bitcast.404), channel_id=1, source_target_pairs={{0,16},{2,18},{4,20},{6,22},{8,24},{10,26},{12,28},{14,30},{16,0},... | collective-permute-start | bytes 442376 | tf_op jit(solution)/shard_map/ppermute | solution.py:319
  47.6 13.7 %collective-permute-start.16 = (f16[9,8,1,8,128]{4,3,1,0,2:T(8,128)(2,1)S(1)}, f16[9,8,1,8,128]{4,3,1,0,2:T(8,128)(2,1)S(1)}, u32[]{:S(2)}, u32[]{:S(2)}) collective-permute-start(f16[9,8,1,8,128]{4,3,1,0,2:T(8,128)(2,1)S(1)} %bitcast.405), channel_id=1, source_target_pairs={{0,8},{2,10},{4,12},{6,14},{8,0},{10,2},{12,4},{14,6},{16,24},{18,... | collective-permute-start | bytes 442376 | tf_op jit(solution)/shard_map/ppermute | solution.py:319
  49.2 13.7 %collective-permute-start.12 = (f16[9,8,1,8,128]{4,3,2,1,0:T(8,128)(2,1)S(1)}, f16[9,8,1,8,128]{4,3,2,1,0:T(8,128)(2,1)S(1)}, u32[]{:S(2)}, u32[]{:S(2)}) collective-permute-start(f16[9,8,1,8,128]{4,3,2,1,0:T(8,128)(2,1)S(1)} %bitcast.407), channel_id=1, source_target_pairs={{0,4},{2,6},{4,0},{6,2},{8,12},{10,14},{12,8},{14,10},{16,20},{18,... | collective-permute-start | bytes 442376 | tf_op jit(solution)/shard_map/ppermute | solution.py:319
  50.6 12.2 %collective-permute-start.14 = (f16[73,8,128]{2,1,0:T(8,128)(2,1)S(1)}, f16[73,8,128]{2,1,0:T(8,128)(2,1)S(1)}, u32[]{:S(2)}, u32[]{:S(2)}) collective-permute-start(f16[73,8,128]{2,1,0:T(8,128)(2,1)S(1)} %constant_dynamic-update-slice_fusion.12), channel_id=1, source_target_pairs={{0,16},{2,18},{4,20},{6,22},{8,24},{10,26},{12,28},{14,30},{16,0},... | collective-permute-start | bytes 448520 | tf_op jit(solution)/shard_map/ppermute | solution.py:319
  61.4 13.0 %collective-permute-start.19 = (f16[2,9,8,1,8,128]{5,4,2,1,3,0:T(8,128)(2,1)S(1)}, f16[2,9,8,1,8,128]{5,4,2,1,3,0:T(8,128)(2,1)S(1)}, u32[]{:S(2)}, u32[]{:S(2)}) collective-permute-start(f16[2,9,8,1,8,128]{5,4,2,1,3,0:T(8,128)(2,1)S(1)} %pad_maximum_fusion), channel_id=1, source_target_pairs={{0,4},{2,6},{4,0},{6,2},{8,12},{10,14},{12,8},{14,10},{16,20},{18,... | collective-permute-start | bytes 884744 | tf_op jit(solution)/shard_map/ppermute | solution.py:319
  62.0 5.9 %collective-permute-start.18 = (f16[9,8,1,8,128]{4,3,1,0,2:T(8,128)(2,1)S(1)}, f16[9,8,1,8,128]{4,3,1,0,2:T(8,128)(2,1)S(1)}, u32[]{:S(2)}, u32[]{:S(2)}) collective-permute-start(f16[9,8,1,8,128]{4,3,1,0,2:T(8,128)(2,1)S(1)} %collective-permute-done.17), channel_id=1, source_target_pairs={{0,8},{2,10},{4,12},{6,14},{8,0},{10,2},{12,4},{14,6},{16,24},{18,... | collective-permute-start | bytes 442376 | tf_op jit(solution)/shard_map/ppermute | solution.py:319
  63.1 6.5 %collective-permute-start.22 = (f16[9,8,1,8,128]{4,3,1,0,2:T(8,128)(2,1)S(1)}, f16[9,8,1,8,128]{4,3,1,0,2:T(8,128)(2,1)S(1)}, u32[]{:S(2)}, u32[]{:S(2)}) collective-permute-start(f16[9,8,1,8,128]{4,3,1,0,2:T(8,128)(2,1)S(1)} %bitcast.397), channel_id=1, source_target_pairs={{0,8},{2,10},{4,12},{6,14},{8,0},{10,2},{12,4},{14,6},{16,24},{18,... | collective-permute-start | bytes 442376 | tf_op jit(solution)/shard_map/ppermute | solution.py:319
  64.4 15.2 %collective-permute-start.25 = (f16[9,8,1,8,128]{4,3,1,0,2:T(8,128)(2,1)S(1)}, f16[9,8,1,8,128]{4,3,1,0,2:T(8,128)(2,1)S(1)}, u32[]{:S(2)}, u32[]{:S(2)}) collective-permute-start(f16[9,8,1,8,128]{4,3,1,0,2:T(8,128)(2,1)S(1)} %bitcast.398), channel_id=1, source_target_pairs={{0,4},{2,6},{4,0},{6,2},{8,12},{10,14},{12,8},{14,10},{16,20},{18,... | collective-permute-start | bytes 442376 | tf_op jit(solution)/shard_map/ppermute | solution.py:319
  65.9 7.6 %collective-permute-start.23 = (f16[9,8,1,8,128]{4,3,1,0,2:T(8,128)(2,1)S(1)}, f16[9,8,1,8,128]{4,3,1,0,2:T(8,128)(2,1)S(1)}, u32[]{:S(2)}, u32[]{:S(2)}) collective-permute-start(f16[9,8,1,8,128]{4,3,1,0,2:T(8,128)(2,1)S(1)} %bitcast.399), channel_id=1, source_target_pairs={{0,16},{2,18},{4,20},{6,22},{8,24},{10,26},{12,28},{14,30},{16,0},... | collective-permute-start | bytes 442376 | tf_op jit(solution)/shard_map/ppermute | solution.py:319
  67.9 13.7 %collective-permute-start.15 = (f32[128,1152]{1,0:T(8,128)S(1)}, f32[128,1152]{1,0:T(8,128)S(1)}, u32[]{:S(2)}, u32[]{:S(2)}) collective-permute-start(f32[128,1152]{1,0:T(8,128)S(1)} %dynamic-slice_select_fusion), channel_id=1, source_target_pairs={{0,1},{1,0},{2,3},{3,2},{4,5},{5,4},{6,7},{7,6},{8,9},{9,8},{10,11... | collective-permute-start | bytes 1769480 | tf_op jit(solution)/shard_map/ppermute | solution.py:406
  69.6 6.5 %collective-permute-start.20 = (f16[1,9,8,1,8,128]{5,4,3,2,1,0:T(8,128)(2,1)S(1)}, f16[1,9,8,1,8,128]{5,4,3,2,1,0:T(8,128)(2,1)S(1)}, u32[]{:S(2)}, u32[]{:S(2)}) collective-permute-start(f16[1,9,8,1,8,128]{5,4,3,2,1,0:T(8,128)(2,1)S(1)} %bitcast.415), channel_id=1, source_target_pairs={{0,4},{2,6},{4,0},{6,2},{8,12},{10,14},{12,8},{14,10},{16,20},{18,... | collective-permute-start | bytes 442376 | tf_op jit(solution)/shard_map/ppermute | solution.py:319
  73.6 7.6 %collective-permute-start.26 = (f16[2,9,8,1,8,128]{5,4,2,1,3,0:T(8,128)(2,1)S(1)}, f16[2,9,8,1,8,128]{5,4,2,1,3,0:T(8,128)(2,1)S(1)}, u32[]{:S(2)}, u32[]{:S(2)}) collective-permute-start(f16[2,9,8,1,8,128]{5,4,2,1,3,0:T(8,128)(2,1)S(1)} %pad_maximum_fusion.1), channel_id=1, source_target_pairs={{0,4},{2,6},{4,0},{6,2},{8,12},{10,14},{12,8},{14,10},{16,20},{18,... | collective-permute-start | bytes 884744 | tf_op jit(solution)/shard_map/ppermute | solution.py:319
  74.4 5.2 %collective-permute-start.24 = (f16[9,8,1,8,128]{4,3,1,0,2:T(8,128)(2,1)S(1)}, f16[9,8,1,8,128]{4,3,1,0,2:T(8,128)(2,1)S(1)}, u32[]{:S(2)}, u32[]{:S(2)}) collective-permute-start(f16[9,8,1,8,128]{4,3,1,0,2:T(8,128)(2,1)S(1)} %collective-permute-done.23), channel_id=1, source_target_pairs={{0,8},{2,10},{4,12},{6,14},{8,0},{10,2},{12,4},{14,6},{16,24},{18,... | collective-permute-start | bytes 442376 | tf_op jit(solution)/shard_map/ppermute | solution.py:319
  76.1 5.6 %collective-permute-start.21 = (f16[8,9,8,1,8,128]{5,4,2,1,3,0:T(8,128)(2,1)S(1)}, f16[8,9,8,1,8,128]{5,4,2,1,3,0:T(8,128)(2,1)S(1)}, u32[]{:S(2)}, u32[]{:S(2)}) collective-permute-start(f16[8,9,8,1,8,128]{5,4,2,1,3,0:T(8,128)(2,1)S(1)} %bitcast_dynamic-update-slice_fusion.12), channel_id=1, source_target_pairs={{0,2},{2,0},{4,6},{6,4},{8,10},{10,8},{12,14},{14,12},{16,18},{18,... | collective-permute-start | bytes 3538952 | tf_op jit(solution)/shard_map/ppermute | solution.py:319
  79.6 6.6 %collective-permute-start.30 = (f32[2,8,128]{2,1,0:T(8,128)S(1)}, f32[2,8,128]{2,1,0:T(8,128)S(1)}, u32[]{:S(2)}, u32[]{:S(2)}) collective-permute-start(f32[2,8,128]{2,1,0:T(8,128)S(1)} %fusion.54), channel_id=1, source_target_pairs={{0,2},{2,0},{4,6},{6,4},{8,10},{10,8},{12,14},{14,12},{16,18},{18,... | collective-permute-start | bytes 24584 | tf_op jit(solution)/shard_map/ppermute | solution.py:319
  79.6 6.3 %collective-permute-start.28 = (f16[1,9,8,1,8,128]{5,4,2,1,3,0:T(8,128)(2,1)S(1)}, f16[1,9,8,1,8,128]{5,4,2,1,3,0:T(8,128)(2,1)S(1)}, u32[]{:S(2)}, u32[]{:S(2)}) collective-permute-start(f16[1,9,8,1,8,128]{5,4,2,1,3,0:T(8,128)(2,1)S(1)} %bitcast.416), channel_id=1, source_target_pairs={{0,4},{2,6},{4,0},{6,2},{8,12},{10,14},{12,8},{14,10},{16,20},{18,... | collective-permute-start | bytes 442376 | tf_op jit(solution)/shard_map/ppermute | solution.py:319
  81.3 2.7 %collective-permute-start.27 = (f16[7,9,8,1,8,128]{5,4,2,1,3,0:T(8,128)(2,1)S(1)}, f16[7,9,8,1,8,128]{5,4,2,1,3,0:T(8,128)(2,1)S(1)}, u32[]{:S(2)}, u32[]{:S(2)}) collective-permute-start(f16[7,9,8,1,8,128]{5,4,2,1,3,0:T(8,128)(2,1)S(1)} %constant_dynamic-update-slice_fusion.4), channel_id=1, source_target_pairs={{0,2},{2,0},{4,6},{6,4},{8,10},{10,8},{12,14},{14,12},{16,18},{18,... | collective-permute-start | bytes 3096584 | tf_op jit(solution)/shard_map/ppermute | solution.py:319
  81.7 5.9 %copy-start.1 = (bf16[1,128,1152]{2,1,0:T(8,128)(2,1)}, bf16[1,128,1152]{2,1,0:T(8,128)(2,1)S(1)}, u32[]{:S(2)}) copy-start(bf16[1,128,1152]{2,1,0:T(8,128)(2,1)S(1)} %fusion.20) | copy-start | bytes 884740
  86.0 1.4 %collective-permute-start.29 = (f16[1,9,8,1,8,128]{5,4,2,1,3,0:T(8,128)(2,1)S(1)}, f16[1,9,8,1,8,128]{5,4,2,1,3,0:T(8,128)(2,1)S(1)}, u32[]{:S(2)}, u32[]{:S(2)}) collective-permute-start(f16[1,9,8,1,8,128]{5,4,2,1,3,0:T(8,128)(2,1)S(1)} %get-tuple-element.28), channel_id=1, source_target_pairs={{0,2},{2,0},{4,6},{6,4},{8,10},{10,8},{12,14},{14,12},{16,18},{18,... | collective-permute-start | bytes 442376 | tf_op jit(solution)/shard_map/ppermute | solution.py:319

commit v12 on v10

--- a/solution.py
+++ b/solution.py
@@ -385,6 +385,10 @@
         near = [shard] + [None] * (depth - 1)
         for bit in bits_of_depth[::-1]:
             near[bit] = to_level(shard, bit)
+        for step in range(1, depth):
+            if near[step] is None:
+                low = step & -step
+                near[step] = to_level(near[step ^ low], low)
         gathers.append((near, to_column(shard)))
         if side == 0:
             if chans == 2:
@@ -396,12 +400,8 @@
             input_grad = input_gradient(cot, w, token(shard[0, 0]))
 
     for side, (near, own) in enumerate(gathers):
-        for step in range(1, depth):
-            if near[step] is None:
-                low = step & -step
-                near[step] = to_level(near[step ^ low], low)
         steps = list(range(depth))
-        cuts = [steps[1:2], steps[2:]] if side == 0 else [steps[1:-1], steps[-1:]]
+        cuts = [steps[1:-1], steps[-1:]]
         here = [jnp.stack([near[step] for step in cut]) for cut in cuts]
         there = [to_column(values) for values in here]
         if side == 0:
@@ -423,7 +423,10 @@
             ]
         lane = first if side == 0 else 1 - first
         for listed, message in messages:
+            if side == 1 and message is there[-1]:
+                message = later(message, crossed)
             across = to_core(message)
+            crossed = across if side == 0 else crossed
             for slot, (chip, step, piece) in enumerate(listed):
                 row = chip * chip_tiles + (level ^ step) * shard_tiles
                 for base, value in ((core, piece), (1 - core, across[slot])):

time: 91.1 us -> 90.7 us (level)
  starting transfers between devices: 37.1 us -> 34.4 us
  waiting for transfers between devices: 14.8 us -> 17.1 us
    ppermute x29, starting transfers between devices: 32.6 us -> 29.9 us  [to(): lax.ppermute(value, 'dp', [(i, i ^ distance) for i in range(samples)])]
    ppermute x29, waiting for transfers between devices: 14.8 us -> 17.1 us  [to(): lax.ppermute(value, 'dp', [(i, i ^ distance) for i in range(samples)])]
  transfers between devices with their start and end apart: 31 -> 31, of which waited for: 8 -> 12; matrix products, arithmetic and copies ran while one was open for 9% -> 9% of each run, Pallas kernels for 24% -> 25%
where the time goes in v12:
time: 90.7 us; the launch traced here: 90.4 us
  starting transfers between devices  34.4 us (38%)
  Pallas kernels  22.2 us (24%)
  waiting for transfers between devices  17.1 us (19%)
  other arithmetic  8.02 us (9%)
  local copies, waits for them, and re-layouts  6.03 us (7%)
  between operations  2.61 us (3%)
    ppermute x29, starting transfers between devices, to(): lax.ppermute(value, 'dp', [(i, i ^ distance) for i in range(samples)])  29.9 us
    ppermute x29, waiting for transfers between devices, to(): lax.ppermute(value, 'dp', [(i, i ^ distance) for i in range(samples)])  17.1 us
    pallas_call x2, Pallas kernels, kernel_grad(): pl.pallas_call(functools.partial(kernel_grad_kernel, depth), out_shape=[j...  10.8 us
    pallas_call x1, Pallas kernels, input_gradient(): pl.pallas_call(input_grad_kernel, out_shape=jax.ShapeDtypeStruct((rows, p...  6.54 us
    pallas_call x1, Pallas kernels, forward(): pl.pallas_call(forward_kernel, out_shape=jax.ShapeDtypeStruct((outs, posi...  4.84 us
    reshape x1, other arithmetic, on_device(): weight_grad = jnp.transpose(grad, (1, 3, 0, 2, 4)).reshape(rows, taps, outs)  4.64 us
    ppermute x1, starting transfers between devices, on_device(): their_cot = lax.ppermute(own_cot, 'chan', [(0, 1), (1, 0)])  2.95 us
    dynamic_update_slice x32, local copies, waits for them, and re-layouts, on_device(): lax.dynamic_update_slice(grad, value, (0, base * core_tiles + row, lane,...  2.04 us
  transfers between devices with their start and end apart: 31, of which 12 were waited for; matrix products, arithmetic and copies ran while one was open for 9% of the time, Pallas kernels for 25%

profile of v12, /device:TPU:0, one launch (start us, length us, event | category | flops | bytes accessed | tf_op | source)
XLA Modules:
  0.0 90.4 jit_solution(8792649192119134519)
XLA Ops:
  0.7 1.4 %dynamic-slice_bitcast_fusion = bf16[512,1152]{1,0:T(8,128)(2,1)S(1)} fusion(bf16[1,1024,1152]{2,1,0:T(8,128)(2,1)} %param.3, s32[]{:T(128)S(6)} %select_n.230), kind=kLoop, calls=%fused_computation.1 | loop fusion | bytes 2359300 | tf_op jit(solution)/shard_map/dynamic_slice | solution.py:338
  2.0 0.5 collective-permute-start
  2.6 2.9 %collective-permute-start.5 = (bf16[128,1152]{1,0:T(8,128)(2,1)}, bf16[128,1152]{1,0:T(8,128)(2,1)S(1)}, u32[]{:S(2)}, u32[]{:S(2)}) collective-permute-start(bf16[128,1152]{1,0:T(8,128)(2,1)} %bitcast.424), channel_id=1, source_target_pairs={{0,1},{1,0},{2,3},{3,2},{4,5},{5,4},{6,7},{7,6},{8,9},{9,8},{10,11... | collective-permute-start | bytes 884744 | tf_op jit(solution)/shard_map/ppermute | solution.py:331
  5.7 5.3 %kernel_grad.2 = (f32[73,8,128]{2,1,0:T(8,128)S(1)}, f32[73,8,128]{2,1,0:T(8,128)S(1)}, f32[73,8,128]{2,1,0:T(8,128)S(1)}, f32[73,8,128]{2,1,0:T(8,128)S(1)}, f3...) custom-call(s32[2]{0:T(128)S(1)} %pad_add_fusion.place_ref, bf16[1024,1152]{1,0:T(8,128)(2,1)} %bitcast.395, ...), custom_call_target="tpu_custom_call" | custom-call | flops 1509949440 | bytes 5308416 | tf_op jit(solution)/shard_map/kernel_grad/pallas_call | solution.py:122
  10.9 0.5 slice.265
  11.5 2.7 %collective-permute-start.2 = (f16[2,73,8,128]{3,2,1,0:T(8,128)(2,1)S(1)}, f16[2,73,8,128]{3,2,1,0:T(8,128)(2,1)S(1)}, u32[]{:S(2)}, u32[]{:S(2)}) collective-permute-start(f16[2,73,8,128]{3,2,1,0:T(8,128)(2,1)S(1)} %convert_element_type.348), channel_id=1, source_target_pairs={{0,4},{2,6},{4,0},{6,2},{8,12},{10,14},{12,8},{14,10},{16,20},{18,... | collective-permute-start | bytes 897032 | tf_op jit(solution)/shard_map/ppermute | solution.py:319
  15.1 0.3 collective-permute-start.3
  15.5 1.0 %collective-permute-done.6.other_cot = bf16[128,1152]{1,0:T(8,128)(2,1)S(1)} collective-permute-done((bf16[128,1152]{1,0:T(8,128)(2,1)S(1)}, bf16[128,1152]{1,0:T(8,128)(2,1)S(1)}, u32[]{:S(2)}, u32[]{:S(2)}) %collective-permute-start.6) | collective-permute-done | bytes 294944 | tf_op jit(solution)/shard_map/ppermute | solution.py:319
  16.6 5.6 %kernel_grad.3 = (f32[73,8,128]{2,1,0:T(8,128)S(1)}, f32[73,8,128]{2,1,0:T(8,128)S(1)}, f32[73,8,128]{2,1,0:T(8,128)S(1)}, f32[73,8,128]{2,1,0:T(8,128)S(1)}, f3...) custom-call(s32[2]{0:T(128)S(1)} %pad_add_fusion.place_ref, bf16[1024,1152]{1,0:T(8,128)(2,1)} %bitcast.396, ...), custom_call_target="tpu_custom_call" | custom-call | flops 1509949440 | bytes 5308416 | tf_op jit(solution)/shard_map/kernel_grad/pallas_call | solution.py:122
  22.2 0.9 collective-permute-start.7
  23.1 1.3 %collective-permute-start.8 = (f16[2,73,8,128]{3,2,1,0:T(8,128)(2,1)S(1)}, f16[2,73,8,128]{3,2,1,0:T(8,128)(2,1)S(1)}, u32[]{:S(2)}, u32[]{:S(2)}) collective-permute-start(f16[2,73,8,128]{3,2,1,0:T(8,128)(2,1)S(1)} %select_convert_fusion), channel_id=1, source_target_pairs={{0,4},{2,6},{4,0},{6,2},{8,12},{10,14},{12,8},{14,10},{16,20},{18,... | collective-permute-start | bytes 897032 | tf_op jit(solution)/shard_map/ppermute | solution.py:319
  24.5 2.0 %collective-permute-start.4 = (f16[73,8,128]{2,1,0:T(8,128)(2,1)S(1)}, f16[73,8,128]{2,1,0:T(8,128)(2,1)S(1)}, u32[]{:S(2)}, u32[]{:S(2)}) collective-permute-start(f16[73,8,128]{2,1,0:T(8,128)(2,1)S(1)} %constant_dynamic-update-slice_fusion.16), channel_id=1, source_target_pairs={{0,8},{2,10},{4,12},{6,14},{8,0},{10,2},{12,4},{14,6},{16,24},{18,... | collective-permute-start | bytes 448520 | tf_op jit(solution)/shard_map/ppermute | solution.py:319
  26.5 2.0 %collective-permute-done.3 = f16[2,73,8,128]{3,2,1,0:T(8,128)(2,1)S(1)} collective-permute-done((f16[2,73,8,128]{3,2,1,0:T(8,128)(2,1)S(1)}, f16[2,73,8,128]{3,2,1,0:T(8,128)(2,1)S(1)}, u32[]{:S(2)}, u32[]{:S(2)}) %collective-permute-start.3) | collective-permute-done | bytes 299040 | tf_op jit(solution)/shard_map/ppermute | solution.py:319
  28.6 2.2 %collective-permute-start.10 = (f16[73,8,128]{2,1,0:T(8,128)(2,1)S(1)}, f16[73,8,128]{2,1,0:T(8,128)(2,1)S(1)}, u32[]{:S(2)}, u32[]{:S(2)}) collective-permute-start(f16[73,8,128]{2,1,0:T(8,128)(2,1)S(1)} %constant_dynamic-update-slice_fusion.15), channel_id=1, source_target_pairs={{0,8},{2,10},{4,12},{6,14},{8,0},{10,2},{12,4},{14,6},{16,24},{18,... | collective-permute-start | bytes 448520 | tf_op jit(solution)/shard_map/ppermute | solution.py:319
  31.0 2.6 %collective-permute-start.11 = (f16[73,8,128]{2,1,0:T(8,128)(2,1)S(1)}, f16[73,8,128]{2,1,0:T(8,128)(2,1)S(1)}, u32[]{:S(2)}, u32[]{:S(2)}) collective-permute-start(f16[73,8,128]{2,1,0:T(8,128)(2,1)S(1)} %constant_dynamic-update-slice_fusion.14), channel_id=1, source_target_pairs={{0,16},{2,18},{4,20},{6,22},{8,24},{10,26},{12,28},{14,30},{16,0},... | collective-permute-start | bytes 448520 | tf_op jit(solution)/shard_map/ppermute | solution.py:319
  33.7 1.2 %collective-permute-done.7 = f16[2,73,8,128]{3,2,1,0:T(8,128)(2,1)S(1)} collective-permute-done((f16[2,73,8,128]{3,2,1,0:T(8,128)(2,1)S(1)}, f16[2,73,8,128]{3,2,1,0:T(8,128)(2,1)S(1)}, u32[]{:S(2)}, u32[]{:S(2)}) %collective-permute-start.7) | collective-permute-done | bytes 299040 | tf_op jit(solution)/shard_map/ppermute | solution.py:319
  35.0 2.2 %collective-permute-start.9 = (f16[73,8,128]{2,1,0:T(8,128)(2,1)S(1)}, f16[73,8,128]{2,1,0:T(8,128)(2,1)S(1)}, u32[]{:S(2)}, u32[]{:S(2)}) collective-permute-start(f16[73,8,128]{2,1,0:T(8,128)(2,1)S(1)} %constant_dynamic-update-slice_fusion.13), channel_id=1, source_target_pairs={{0,8},{2,10},{4,12},{6,14},{8,0},{10,2},{12,4},{14,6},{16,24},{18,... | collective-permute-start | bytes 448520 | tf_op jit(solution)/shard_map/ppermute | solution.py:319
  37.3 4.8 %forward.1 = f32[256,1152]{1,0:T(8,128)S(1)} custom-call(bf16[1024,1152]{1,0:T(8,128)(2,1)S(1)} %bitcast.397, bf16[9,1024,256]{2,1,0:T(8,128)(2,1)S(1)} %bitcast.400, f32[8,128]{1,0:T(8,128)S(1)} %fusion.147._), custom_call_target="tpu_custom_call" | custom-call | flops 3019898880 | bytes 8257536 | tf_op jit(solution)/shard_map/forward/pallas_call | solution.py:194
  42.3 0.7 collective-permute-start.13
  43.2 2.6 %collective-permute-start.14 = (f16[73,8,128]{2,1,0:T(8,128)(2,1)S(1)}, f16[73,8,128]{2,1,0:T(8,128)(2,1)S(1)}, u32[]{:S(2)}, u32[]{:S(2)}) collective-permute-start(f16[73,8,128]{2,1,0:T(8,128)(2,1)S(1)} %constant_dynamic-update-slice_fusion.11), channel_id=1, source_target_pairs={{0,16},{2,18},{4,20},{6,22},{8,24},{10,26},{12,28},{14,30},{16,0},... | collective-permute-start | bytes 448520 | tf_op jit(solution)/shard_map/ppermute | solution.py:319
  45.9 0.1 fusion.31
  46.0 1.6 %collective-permute-start.12 = (f16[9,8,1,8,128]{4,3,2,1,0:T(8,128)(2,1)S(1)}, f16[9,8,1,8,128]{4,3,2,1,0:T(8,128)(2,1)S(1)}, u32[]{:S(2)}, u32[]{:S(2)}) collective-permute-start(f16[9,8,1,8,128]{4,3,2,1,0:T(8,128)(2,1)S(1)} %bitcast.410), channel_id=1, source_target_pairs={{0,4},{2,6},{4,0},{6,2},{8,12},{10,14},{12,8},{14,10},{16,20},{18,... | collective-permute-start | bytes 442376 | tf_op jit(solution)/shard_map/ppermute | solution.py:319
  47.6 1.4 %collective-permute-start.16 = (f16[9,8,1,8,128]{4,3,1,0,2:T(8,128)(2,1)S(1)}, f16[9,8,1,8,128]{4,3,1,0,2:T(8,128)(2,1)S(1)}, u32[]{:S(2)}, u32[]{:S(2)}) collective-permute-start(f16[9,8,1,8,128]{4,3,1,0,2:T(8,128)(2,1)S(1)} %bitcast.412), channel_id=1, source_target_pairs={{0,8},{2,10},{4,12},{6,14},{8,0},{10,2},{12,4},{14,6},{16,24},{18,... | collective-permute-start | bytes 442376 | tf_op jit(solution)/shard_map/ppermute | solution.py:319
  49.0 0.3 collective-permute-start.17
  49.3 6.5 %input_gradient.1 = bf16[1024,1152]{1,0:T(8,128)(2,1)} custom-call(bf16[256,1152]{1,0:T(8,128)(2,1)S(1)} %maximum_select_fusion.cot_ref, bf16[9,1024,256]{2,1,0:T(8,128)(2,1)S(1)} %bitcast.401, f32[8,128]{1,0:T(8,128)S(1)} %convert_bitcast_fusion._), custom_call_target="tpu_custom_call" | custom-call | flops 3019898880 | bytes 7667712 | tf_op jit(solution)/shard_map/input_gradient/pallas_call | solution.py:242
  55.9 0.7 convert_compare_fusion.5
  56.6 0.7 broadcast_in_dim.103
  57.4 1.3 %collective-permute-done.17 = f16[9,8,1,8,128]{4,3,1,0,2:T(8,128)(2,1)S(1)} collective-permute-done((f16[9,8,1,8,128]{4,3,1,0,2:T(8,128)(2,1)S(1)}, f16[9,8,1,8,128]{4,3,1,0,2:T(8,128)(2,1)S(1)}, u32[]{:S(2)}, u32[]{:S(2)}) %collective-permute-start.17) | collective-permute-done | bytes 147488 | tf_op jit(solution)/shard_map/ppermute | solution.py:319
  58.8 1.5 %collective-permute-start.19 = (f16[2,9,8,1,8,128]{5,4,2,1,3,0:T(8,128)(2,1)S(1)}, f16[2,9,8,1,8,128]{5,4,2,1,3,0:T(8,128)(2,1)S(1)}, u32[]{:S(2)}, u32[]{:S(2)}) collective-permute-start(f16[2,9,8,1,8,128]{5,4,2,1,3,0:T(8,128)(2,1)S(1)} %pad_maximum_fusion), channel_id=1, source_target_pairs={{0,4},{2,6},{4,0},{6,2},{8,12},{10,14},{12,8},{14,10},{16,20},{18,... | collective-permute-start | bytes 884744 | tf_op jit(solution)/shard_map/ppermute | solution.py:319
  60.4 0.2 collective-permute-start.18
  60.7 0.2 fusion.26
  60.9 1.9 %collective-permute-start.22 = (f16[9,8,1,8,128]{4,3,1,0,2:T(8,128)(2,1)S(1)}, f16[9,8,1,8,128]{4,3,1,0,2:T(8,128)(2,1)S(1)}, u32[]{:S(2)}, u32[]{:S(2)}) collective-permute-start(f16[9,8,1,8,128]{4,3,1,0,2:T(8,128)(2,1)S(1)} %bitcast.403), channel_id=1, source_target_pairs={{0,8},{2,10},{4,12},{6,14},{8,0},{10,2},{12,4},{14,6},{16,24},{18,... | collective-permute-start | bytes 442376 | tf_op jit(solution)/shard_map/ppermute | solution.py:319
  62.8 1.1 %collective-permute-start.23 = (f16[9,8,1,8,128]{4,3,1,0,2:T(8,128)(2,1)S(1)}, f16[9,8,1,8,128]{4,3,1,0,2:T(8,128)(2,1)S(1)}, u32[]{:S(2)}, u32[]{:S(2)}) collective-permute-start(f16[9,8,1,8,128]{4,3,1,0,2:T(8,128)(2,1)S(1)} %bitcast.404), channel_id=1, source_target_pairs={{0,16},{2,18},{4,20},{6,22},{8,24},{10,26},{12,28},{14,30},{16,0},... | collective-permute-start | bytes 442376 | tf_op jit(solution)/shard_map/ppermute | solution.py:319
  63.9 0.8 collective-permute-start.25
  64.7 0.5 slice.298
  66.0 0.4 collective-permute-done.18
  66.3 1.6 %collective-permute-start.15 = (f32[128,1152]{1,0:T(8,128)S(1)}, f32[128,1152]{1,0:T(8,128)S(1)}, u32[]{:S(2)}, u32[]{:S(2)}) collective-permute-start(f32[128,1152]{1,0:T(8,128)S(1)} %dynamic-slice_select_fusion), channel_id=1, source_target_pairs={{0,1},{1,0},{2,3},{3,2},{4,5},{5,4},{6,7},{7,6},{8,9},{9,8},{10,11... | collective-permute-start | bytes 1769480 | tf_op jit(solution)/shard_map/ppermute | solution.py:449
  68.0 1.5 %collective-permute-done.22 = f16[9,8,1,8,128]{4,3,1,0,2:T(8,128)(2,1)S(1)} collective-permute-done((f16[9,8,1,8,128]{4,3,1,0,2:T(8,128)(2,1)S(1)}, f16[9,8,1,8,128]{4,3,1,0,2:T(8,128)(2,1)S(1)}, u32[]{:S(2)}, u32[]{:S(2)}) %collective-permute-start.22) | collective-permute-done | bytes 147488 | tf_op jit(solution)/shard_map/ppermute | solution.py:319
  69.5 0.4 collective-permute-start.20
  69.9 0.5 collective-permute-done.23
  70.5 1.3 %collective-permute-start.26 = (f16[2,9,8,1,8,128]{5,4,2,1,3,0:T(8,128)(2,1)S(1)}, f16[2,9,8,1,8,128]{5,4,2,1,3,0:T(8,128)(2,1)S(1)}, u32[]{:S(2)}, u32[]{:S(2)}) collective-permute-start(f16[2,9,8,1,8,128]{5,4,2,1,3,0:T(8,128)(2,1)S(1)} %pad_maximum_fusion.1), channel_id=1, source_target_pairs={{0,4},{2,6},{4,0},{6,2},{8,12},{10,14},{12,8},{14,10},{16,20},{18,... | collective-permute-start | bytes 884744 | tf_op jit(solution)/shard_map/ppermute | solution.py:319
  72.0 3.2 %collective-permute-done.20 = f16[1,9,8,1,8,128]{5,4,3,2,1,0:T(8,128)(2,1)S(1)} collective-permute-done((f16[1,9,8,1,8,128]{5,4,3,2,1,0:T(8,128)(2,1)S(1)}, f16[1,9,8,1,8,128]{5,4,3,2,1,0:T(8,128)(2,1)S(1)}, u32[]{:S(2)}, u32[]{:S(2)}) %collective-permute-start.20) | collective-permute-done | bytes 147488 | tf_op jit(solution)/shard_map/ppermute | solution.py:319
  75.3 1.7 %collective-permute-done.24 = f16[9,8,1,8,128]{4,3,1,0,2:T(8,128)(2,1)S(1)} collective-permute-done((f16[9,8,1,8,128]{4,3,1,0,2:T(8,128)(2,1)S(1)}, f16[9,8,1,8,128]{4,3,1,0,2:T(8,128)(2,1)S(1)}, u32[]{:S(2)}, u32[]{:S(2)}) %collective-permute-start.24) | collective-permute-done | bytes 147488 | tf_op jit(solution)/shard_map/ppermute | solution.py:319
  77.1 0.9 collective-permute-start.28
  78.0 0.2 collective-permute-done.30
  78.6 0.8 fusion.20
  79.4 4.0 %collective-permute-done.28 = f16[1,9,8,1,8,128]{5,4,2,1,3,0:T(8,128)(2,1)S(1)} collective-permute-done((f16[1,9,8,1,8,128]{5,4,2,1,3,0:T(8,128)(2,1)S(1)}, f16[1,9,8,1,8,128]{5,4,2,1,3,0:T(8,128)(2,1)S(1)}, u32[]{:S(2)}, u32[]{:S(2)}) %collective-permute-start.28) | collective-permute-done | bytes 147488 | tf_op jit(solution)/shard_map/ppermute | solution.py:319
  85.8 4.6 %multiply_bitcast_fusion = f32[1024,9,256]{2,0,1:T(8,128)} fusion(f16[9,128,2,8,128]{4,3,2,1,0:T(8,128)(2,1)S(1)} %bitcast_dynamic-update-slice_fusion.1, f32[128,2,8,128]{3,2,1,0:T(8,128)S(1)} %bitcast.402), kind=kLoop, calls=%fused_computation | loop fusion | flops 4718592 | bytes 15204352 | tf_op jit(solution)/shard_map/reshape | solution.py:443
  (139 shorter events, 5.2 us)
Async XLA Ops:
  2.0 13.4 %copy-start.1 = (bf16[1,128,1152]{2,1,0:T(8,128)(2,1)S(1)}, bf16[1,128,1152]{2,1,0:T(8,128)(2,1)}, u32[]{:S(2)}) copy-start(bf16[1,128,1152]{2,1,0:T(8,128)(2,1)} %param.5) | copy-start | bytes 884740
  2.0 3.6 %collective-permute-start = (bf16[512,1152]{1,0:T(8,128)(2,1)S(1)}, bf16[512,1152]{1,0:T(8,128)(2,1)S(1)}, u32[]{:S(2)}, u32[]{:S(2)}) collective-permute-start(bf16[512,1152]{1,0:T(8,128)(2,1)S(1)} %dynamic-slice_bitcast_fusion), channel_id=1, source_target_pairs={{0,2},{2,0},{4,6},{6,4},{8,10},{10,8},{12,14},{14,12},{16,18},{18,... | collective-permute-start | bytes 3538952 | tf_op jit(solution)/shard_map/ppermute | solution.py:319
  2.5 3.1 %collective-permute-start.1 = (bf16[128,1152]{1,0:T(8,128)(2,1)}, bf16[128,1152]{1,0:T(8,128)(2,1)S(1)}, u32[]{:S(2)}, u32[]{:S(2)}) collective-permute-start(bf16[128,1152]{1,0:T(8,128)(2,1)} %bitcast.423), channel_id=1, source_target_pairs={{0,2},{2,0},{4,6},{6,4},{8,10},{10,8},{12,14},{14,12},{16,18},{18,... | collective-permute-start | bytes 884744 | tf_op jit(solution)/shard_map/ppermute | solution.py:319
  2.6 12.3 %collective-permute-start.5 = (bf16[128,1152]{1,0:T(8,128)(2,1)}, bf16[128,1152]{1,0:T(8,128)(2,1)S(1)}, u32[]{:S(2)}, u32[]{:S(2)}) collective-permute-start(bf16[128,1152]{1,0:T(8,128)(2,1)} %bitcast.424), channel_id=1, source_target_pairs={{0,1},{1,0},{2,3},{3,2},{4,5},{5,4},{6,7},{7,6},{8,9},{9,8},{10,11... | collective-permute-start | bytes 884744 | tf_op jit(solution)/shard_map/ppermute | solution.py:331
  11.5 12.9 %collective-permute-start.2 = (f16[2,73,8,128]{3,2,1,0:T(8,128)(2,1)S(1)}, f16[2,73,8,128]{3,2,1,0:T(8,128)(2,1)S(1)}, u32[]{:S(2)}, u32[]{:S(2)}) collective-permute-start(f16[2,73,8,128]{3,2,1,0:T(8,128)(2,1)S(1)} %convert_element_type.348), channel_id=1, source_target_pairs={{0,4},{2,6},{4,0},{6,2},{8,12},{10,14},{12,8},{14,10},{16,20},{18,... | collective-permute-start | bytes 897032 | tf_op jit(solution)/shard_map/ppermute | solution.py:319
  14.9 1.6 %collective-permute-start.6 = (bf16[128,1152]{1,0:T(8,128)(2,1)S(1)}, bf16[128,1152]{1,0:T(8,128)(2,1)S(1)}, u32[]{:S(2)}, u32[]{:S(2)}) collective-permute-start(bf16[128,1152]{1,0:T(8,128)(2,1)S(1)} %broadcast_select_fusion.own_cot), channel_id=1, source_target_pairs={{0,2},{2,0},{4,6},{6,4},{8,10},{10,8},{12,14},{14,12},{16,18},{18,... | collective-permute-start | bytes 884744 | tf_op jit(solution)/shard_map/ppermute | solution.py:319
  15.1 13.4 %collective-permute-start.3 = (f16[2,73,8,128]{3,2,1,0:T(8,128)(2,1)S(1)}, f16[2,73,8,128]{3,2,1,0:T(8,128)(2,1)S(1)}, u32[]{:S(2)}, u32[]{:S(2)}) collective-permute-start(f16[2,73,8,128]{3,2,1,0:T(8,128)(2,1)S(1)} %select_convert_fusion.1), channel_id=1, source_target_pairs={{0,4},{2,6},{4,0},{6,2},{8,12},{10,14},{12,8},{14,10},{16,20},{18,... | collective-permute-start | bytes 897032 | tf_op jit(solution)/shard_map/ppermute | solution.py:319
  15.4 21.9 %slice-start = ((s8[4718592]{0:T(1024)(128)(4,1)}), s8[4194304]{0:T(1024)(128)(4,1)S(1)}, s32[]{:S(2)}) async-start(s8[4718592]{0:T(1024)(128)(4,1)} %bitcast.398), calls=%async_computation | async-start | bytes 8388608
  15.5 21.7 %copy-start = (bf16[1,1024,1152]{2,1,0:T(8,128)(2,1)S(1)}, bf16[1,1024,1152]{2,1,0:T(8,128)(2,1)}, u32[]{:S(2)}) copy-start(bf16[1,1024,1152]{2,1,0:T(8,128)(2,1)} %param.3) | copy-start | bytes 7077892
  15.5 21.7 %slice-start.1 = ((s8[4718592]{0:T(1024)(128)(4,1)}), s8[524288]{0:T(1024)(128)(4,1)S(1)}, s32[]{:S(2)}) async-start(s8[4718592]{0:T(1024)(128)(4,1)} %bitcast.398), calls=%async_computation.1 | async-start | bytes 1048576
  22.2 12.7 %collective-permute-start.7 = (f16[2,73,8,128]{3,2,1,0:T(8,128)(2,1)S(1)}, f16[2,73,8,128]{3,2,1,0:T(8,128)(2,1)S(1)}, u32[]{:S(2)}, u32[]{:S(2)}) collective-permute-start(f16[2,73,8,128]{3,2,1,0:T(8,128)(2,1)S(1)} %convert_element_type.376), channel_id=1, source_target_pairs={{0,4},{2,6},{4,0},{6,2},{8,12},{10,14},{12,8},{14,10},{16,20},{18,... | collective-permute-start | bytes 897032 | tf_op jit(solution)/shard_map/ppermute | solution.py:319
  23.1 19.0 %collective-permute-start.8 = (f16[2,73,8,128]{3,2,1,0:T(8,128)(2,1)S(1)}, f16[2,73,8,128]{3,2,1,0:T(8,128)(2,1)S(1)}, u32[]{:S(2)}, u32[]{:S(2)}) collective-permute-start(f16[2,73,8,128]{3,2,1,0:T(8,128)(2,1)S(1)} %select_convert_fusion), channel_id=1, source_target_pairs={{0,4},{2,6},{4,0},{6,2},{8,12},{10,14},{12,8},{14,10},{16,20},{18,... | collective-permute-start | bytes 897032 | tf_op jit(solution)/shard_map/ppermute | solution.py:319
  24.5 6.3 %collective-permute-start.4 = (f16[73,8,128]{2,1,0:T(8,128)(2,1)S(1)}, f16[73,8,128]{2,1,0:T(8,128)(2,1)S(1)}, u32[]{:S(2)}, u32[]{:S(2)}) collective-permute-start(f16[73,8,128]{2,1,0:T(8,128)(2,1)S(1)} %constant_dynamic-update-slice_fusion.16), channel_id=1, source_target_pairs={{0,8},{2,10},{4,12},{6,14},{8,0},{10,2},{12,4},{14,6},{16,24},{18,... | collective-permute-start | bytes 448520 | tf_op jit(solution)/shard_map/ppermute | solution.py:319
  28.6 14.4 %collective-permute-start.10 = (f16[73,8,128]{2,1,0:T(8,128)(2,1)S(1)}, f16[73,8,128]{2,1,0:T(8,128)(2,1)S(1)}, u32[]{:S(2)}, u32[]{:S(2)}) collective-permute-start(f16[73,8,128]{2,1,0:T(8,128)(2,1)S(1)} %constant_dynamic-update-slice_fusion.15), channel_id=1, source_target_pairs={{0,8},{2,10},{4,12},{6,14},{8,0},{10,2},{12,4},{14,6},{16,24},{18,... | collective-permute-start | bytes 448520 | tf_op jit(solution)/shard_map/ppermute | solution.py:319
  31.0 12.0 %collective-permute-start.11 = (f16[73,8,128]{2,1,0:T(8,128)(2,1)S(1)}, f16[73,8,128]{2,1,0:T(8,128)(2,1)S(1)}, u32[]{:S(2)}, u32[]{:S(2)}) collective-permute-start(f16[73,8,128]{2,1,0:T(8,128)(2,1)S(1)} %constant_dynamic-update-slice_fusion.14), channel_id=1, source_target_pairs={{0,16},{2,18},{4,20},{6,22},{8,24},{10,26},{12,28},{14,30},{16,0},... | collective-permute-start | bytes 448520 | tf_op jit(solution)/shard_map/ppermute | solution.py:319
  35.0 8.0 %collective-permute-start.9 = (f16[73,8,128]{2,1,0:T(8,128)(2,1)S(1)}, f16[73,8,128]{2,1,0:T(8,128)(2,1)S(1)}, u32[]{:S(2)}, u32[]{:S(2)}) collective-permute-start(f16[73,8,128]{2,1,0:T(8,128)(2,1)S(1)} %constant_dynamic-update-slice_fusion.13), channel_id=1, source_target_pairs={{0,8},{2,10},{4,12},{6,14},{8,0},{10,2},{12,4},{14,6},{16,24},{18,... | collective-permute-start | bytes 448520 | tf_op jit(solution)/shard_map/ppermute | solution.py:319
  42.3 18.4 %collective-permute-start.13 = (f16[73,8,128]{2,1,0:T(8,128)(2,1)S(1)}, f16[73,8,128]{2,1,0:T(8,128)(2,1)S(1)}, u32[]{:S(2)}, u32[]{:S(2)}) collective-permute-start(f16[73,8,128]{2,1,0:T(8,128)(2,1)S(1)} %constant_dynamic-update-slice_fusion.12), channel_id=1, source_target_pairs={{0,8},{2,10},{4,12},{6,14},{8,0},{10,2},{12,4},{14,6},{16,24},{18,... | collective-permute-start | bytes 448520 | tf_op jit(solution)/shard_map/ppermute | solution.py:319
  43.2 17.4 %collective-permute-start.14 = (f16[73,8,128]{2,1,0:T(8,128)(2,1)S(1)}, f16[73,8,128]{2,1,0:T(8,128)(2,1)S(1)}, u32[]{:S(2)}, u32[]{:S(2)}) collective-permute-start(f16[73,8,128]{2,1,0:T(8,128)(2,1)S(1)} %constant_dynamic-update-slice_fusion.11), channel_id=1, source_target_pairs={{0,16},{2,18},{4,20},{6,22},{8,24},{10,26},{12,28},{14,30},{16,0},... | collective-permute-start | bytes 448520 | tf_op jit(solution)/shard_map/ppermute | solution.py:319
  46.0 14.6 %collective-permute-start.12 = (f16[9,8,1,8,128]{4,3,2,1,0:T(8,128)(2,1)S(1)}, f16[9,8,1,8,128]{4,3,2,1,0:T(8,128)(2,1)S(1)}, u32[]{:S(2)}, u32[]{:S(2)}) collective-permute-start(f16[9,8,1,8,128]{4,3,2,1,0:T(8,128)(2,1)S(1)} %bitcast.410), channel_id=1, source_target_pairs={{0,4},{2,6},{4,0},{6,2},{8,12},{10,14},{12,8},{14,10},{16,20},{18,... | collective-permute-start | bytes 442376 | tf_op jit(solution)/shard_map/ppermute | solution.py:319
  47.6 9.8 %collective-permute-start.16 = (f16[9,8,1,8,128]{4,3,1,0,2:T(8,128)(2,1)S(1)}, f16[9,8,1,8,128]{4,3,1,0,2:T(8,128)(2,1)S(1)}, u32[]{:S(2)}, u32[]{:S(2)}) collective-permute-start(f16[9,8,1,8,128]{4,3,1,0,2:T(8,128)(2,1)S(1)} %bitcast.412), channel_id=1, source_target_pairs={{0,8},{2,10},{4,12},{6,14},{8,0},{10,2},{12,4},{14,6},{16,24},{18,... | collective-permute-start | bytes 442376 | tf_op jit(solution)/shard_map/ppermute | solution.py:319
  49.0 9.7 %collective-permute-start.17 = (f16[9,8,1,8,128]{4,3,1,0,2:T(8,128)(2,1)S(1)}, f16[9,8,1,8,128]{4,3,1,0,2:T(8,128)(2,1)S(1)}, u32[]{:S(2)}, u32[]{:S(2)}) collective-permute-start(f16[9,8,1,8,128]{4,3,1,0,2:T(8,128)(2,1)S(1)} %bitcast.413), channel_id=1, source_target_pairs={{0,16},{2,18},{4,20},{6,22},{8,24},{10,26},{12,28},{14,30},{16,0},... | collective-permute-start | bytes 442376 | tf_op jit(solution)/shard_map/ppermute | solution.py:319
  58.8 13.0 %collective-permute-start.19 = (f16[2,9,8,1,8,128]{5,4,2,1,3,0:T(8,128)(2,1)S(1)}, f16[2,9,8,1,8,128]{5,4,2,1,3,0:T(8,128)(2,1)S(1)}, u32[]{:S(2)}, u32[]{:S(2)}) collective-permute-start(f16[2,9,8,1,8,128]{5,4,2,1,3,0:T(8,128)(2,1)S(1)} %pad_maximum_fusion), channel_id=1, source_target_pairs={{0,4},{2,6},{4,0},{6,2},{8,12},{10,14},{12,8},{14,10},{16,20},{18,... | collective-permute-start | bytes 884744 | tf_op jit(solution)/shard_map/ppermute | solution.py:319
  60.4 6.0 %collective-permute-start.18 = (f16[9,8,1,8,128]{4,3,1,0,2:T(8,128)(2,1)S(1)}, f16[9,8,1,8,128]{4,3,1,0,2:T(8,128)(2,1)S(1)}, u32[]{:S(2)}, u32[]{:S(2)}) collective-permute-start(f16[9,8,1,8,128]{4,3,1,0,2:T(8,128)(2,1)S(1)} %collective-permute-done.17), channel_id=1, source_target_pairs={{0,8},{2,10},{4,12},{6,14},{8,0},{10,2},{12,4},{14,6},{16,24},{18,... | collective-permute-start | bytes 442376 | tf_op jit(solution)/shard_map/ppermute | solution.py:319
  60.9 8.7 %collective-permute-start.22 = (f16[9,8,1,8,128]{4,3,1,0,2:T(8,128)(2,1)S(1)}, f16[9,8,1,8,128]{4,3,1,0,2:T(8,128)(2,1)S(1)}, u32[]{:S(2)}, u32[]{:S(2)}) collective-permute-start(f16[9,8,1,8,128]{4,3,1,0,2:T(8,128)(2,1)S(1)} %bitcast.403), channel_id=1, source_target_pairs={{0,8},{2,10},{4,12},{6,14},{8,0},{10,2},{12,4},{14,6},{16,24},{18,... | collective-permute-start | bytes 442376 | tf_op jit(solution)/shard_map/ppermute | solution.py:319
  62.8 7.6 %collective-permute-start.23 = (f16[9,8,1,8,128]{4,3,1,0,2:T(8,128)(2,1)S(1)}, f16[9,8,1,8,128]{4,3,1,0,2:T(8,128)(2,1)S(1)}, u32[]{:S(2)}, u32[]{:S(2)}) collective-permute-start(f16[9,8,1,8,128]{4,3,1,0,2:T(8,128)(2,1)S(1)} %bitcast.404), channel_id=1, source_target_pairs={{0,16},{2,18},{4,20},{6,22},{8,24},{10,26},{12,28},{14,30},{16,0},... | collective-permute-start | bytes 442376 | tf_op jit(solution)/shard_map/ppermute | solution.py:319
  63.9 13.2 %collective-permute-start.25 = (f16[9,8,1,8,128]{4,3,1,0,2:T(8,128)(2,1)S(1)}, f16[9,8,1,8,128]{4,3,1,0,2:T(8,128)(2,1)S(1)}, u32[]{:S(2)}, u32[]{:S(2)}) collective-permute-start(f16[9,8,1,8,128]{4,3,1,0,2:T(8,128)(2,1)S(1)} %bitcast.405), channel_id=1, source_target_pairs={{0,4},{2,6},{4,0},{6,2},{8,12},{10,14},{12,8},{14,10},{16,20},{18,... | collective-permute-start | bytes 442376 | tf_op jit(solution)/shard_map/ppermute | solution.py:319
  66.3 12.2 %collective-permute-start.15 = (f32[128,1152]{1,0:T(8,128)S(1)}, f32[128,1152]{1,0:T(8,128)S(1)}, u32[]{:S(2)}, u32[]{:S(2)}) collective-permute-start(f32[128,1152]{1,0:T(8,128)S(1)} %dynamic-slice_select_fusion), channel_id=1, source_target_pairs={{0,1},{1,0},{2,3},{3,2},{4,5},{5,4},{6,7},{7,6},{8,9},{9,8},{10,11... | collective-permute-start | bytes 1769480 | tf_op jit(solution)/shard_map/ppermute | solution.py:449
  69.5 5.6 %collective-permute-start.20 = (f16[1,9,8,1,8,128]{5,4,3,2,1,0:T(8,128)(2,1)S(1)}, f16[1,9,8,1,8,128]{5,4,3,2,1,0:T(8,128)(2,1)S(1)}, u32[]{:S(2)}, u32[]{:S(2)}) collective-permute-start(f16[1,9,8,1,8,128]{5,4,3,2,1,0:T(8,128)(2,1)S(1)} %bitcast.421), channel_id=1, source_target_pairs={{0,4},{2,6},{4,0},{6,2},{8,12},{10,14},{12,8},{14,10},{16,20},{18,... | collective-permute-start | bytes 442376 | tf_op jit(solution)/shard_map/ppermute | solution.py:319
  70.5 7.9 %collective-permute-start.26 = (f16[2,9,8,1,8,128]{5,4,2,1,3,0:T(8,128)(2,1)S(1)}, f16[2,9,8,1,8,128]{5,4,2,1,3,0:T(8,128)(2,1)S(1)}, u32[]{:S(2)}, u32[]{:S(2)}) collective-permute-start(f16[2,9,8,1,8,128]{5,4,2,1,3,0:T(8,128)(2,1)S(1)} %pad_maximum_fusion.1), channel_id=1, source_target_pairs={{0,4},{2,6},{4,0},{6,2},{8,12},{10,14},{12,8},{14,10},{16,20},{18,... | collective-permute-start | bytes 884744 | tf_op jit(solution)/shard_map/ppermute | solution.py:319
  71.8 5.2 %collective-permute-start.24 = (f16[9,8,1,8,128]{4,3,1,0,2:T(8,128)(2,1)S(1)}, f16[9,8,1,8,128]{4,3,1,0,2:T(8,128)(2,1)S(1)}, u32[]{:S(2)}, u32[]{:S(2)}) collective-permute-start(f16[9,8,1,8,128]{4,3,1,0,2:T(8,128)(2,1)S(1)} %collective-permute-done.23), channel_id=1, source_target_pairs={{0,8},{2,10},{4,12},{6,14},{8,0},{10,2},{12,4},{14,6},{16,24},{18,... | collective-permute-start | bytes 442376 | tf_op jit(solution)/shard_map/ppermute | solution.py:319
  75.2 4.1 %collective-permute-start.21 = (f16[8,9,8,1,8,128]{5,4,3,2,1,0:T(8,128)(2,1)S(1)}, f16[8,9,8,1,8,128]{5,4,3,2,1,0:T(8,128)(2,1)S(1)}, u32[]{:S(2)}, u32[]{:S(2)}) collective-permute-start(f16[8,9,8,1,8,128]{5,4,3,2,1,0:T(8,128)(2,1)S(1)} %constant_dynamic-update-slice_fusion), channel_id=1, source_target_pairs={{0,2},{2,0},{4,6},{6,4},{8,10},{10,8},{12,14},{14,12},{16,18},{18,... | collective-permute-start | bytes 3538952 | tf_op jit(solution)/shard_map/ppermute | solution.py:319
  77.0 1.2 %collective-permute-start.30 = (f32[2,8,128]{2,1,0:T(8,128)S(1)}, f32[2,8,128]{2,1,0:T(8,128)S(1)}, u32[]{:S(2)}, u32[]{:S(2)}) collective-permute-start(f32[2,8,128]{2,1,0:T(8,128)S(1)} %fusion.54), channel_id=1, source_target_pairs={{0,2},{2,0},{4,6},{6,4},{8,10},{10,8},{12,14},{14,12},{16,18},{18,... | collective-permute-start | bytes 24584 | tf_op jit(solution)/shard_map/ppermute | solution.py:319
  77.1 6.3 %collective-permute-start.28 = (f16[1,9,8,1,8,128]{5,4,2,1,3,0:T(8,128)(2,1)S(1)}, f16[1,9,8,1,8,128]{5,4,2,1,3,0:T(8,128)(2,1)S(1)}, u32[]{:S(2)}, u32[]{:S(2)}) collective-permute-start(f16[1,9,8,1,8,128]{5,4,2,1,3,0:T(8,128)(2,1)S(1)} %bitcast.422), channel_id=1, source_target_pairs={{0,4},{2,6},{4,0},{6,2},{8,12},{10,14},{12,8},{14,10},{16,20},{18,... | collective-permute-start | bytes 442376 | tf_op jit(solution)/shard_map/ppermute | solution.py:319
  78.4 6.2 %collective-permute-start.27 = (f16[7,9,8,1,8,128]{5,4,2,1,3,0:T(8,128)(2,1)S(1)}, f16[7,9,8,1,8,128]{5,4,2,1,3,0:T(8,128)(2,1)S(1)}, u32[]{:S(2)}, u32[]{:S(2)}) collective-permute-start(f16[7,9,8,1,8,128]{5,4,2,1,3,0:T(8,128)(2,1)S(1)} %constant_dynamic-update-slice_fusion.3), channel_id=1, source_target_pairs={{0,2},{2,0},{4,6},{6,4},{8,10},{10,8},{12,14},{14,12},{16,18},{18,... | collective-permute-start | bytes 3096584 | tf_op jit(solution)/shard_map/ppermute | solution.py:319
  83.5 2.1 %collective-permute-start.29 = (f16[1,9,8,1,8,128]{5,4,2,1,3,0:T(8,128)(2,1)S(1)}, f16[1,9,8,1,8,128]{5,4,2,1,3,0:T(8,128)(2,1)S(1)}, u32[]{:S(2)}, u32[]{:S(2)}) collective-permute-start(f16[1,9,8,1,8,128]{5,4,2,1,3,0:T(8,128)(2,1)S(1)} %broadcast_select_fusion.1), channel_id=1, source_target_pairs={{0,2},{2,0},{4,6},{6,4},{8,10},{10,8},{12,14},{14,12},{16,18},{18,... | collective-permute-start | bytes 442376 | tf_op jit(solution)/shard_map/ppermute | solution.py:319

commit v13 on v12

--- a/solution.py
+++ b/solution.py
@@ -377,14 +377,15 @@
 
     for side, (values, bits) in enumerate(reduced):
         lowest = common_exponent(values, bits)
-        gates = (gathers[0][1], input_grad[:TILE, :LANES]) if side else (sends[-1],)
+        gates = (gathers[0][1],) if side else (sends[-1],)
         kept = later(scaled_sum(values, lowest)[:-1], *gates)
         shard = kept.astype(jnp.float16).reshape(taps, shard_tiles, 1, TILE, LANES)
         halves.append(shard)
         exponents.append(later(lowest, shard))
         near = [shard] + [None] * (depth - 1)
         for bit in bits_of_depth[::-1]:
-            near[bit] = to_level(shard, bit)
+            source = later(shard, gathers[0][0][depth // 2]) if side and bit == 1 else shard
+            near[bit] = to_level(source, bit)
         for step in range(1, depth):
             if near[step] is None:
                 low = step & -step
@@ -427,7 +428,7 @@
                 message = later(message, crossed)
             across = to_core(message)
             crossed = across if side == 0 else crossed
-            for slot, (chip, step, piece) in enumerate(listed):
+            for slot, (chip, step, piece) in reversed(list(enumerate(listed))):
                 row = chip * chip_tiles + (level ^ step) * shard_tiles
                 for base, value in ((core, piece), (1 - core, across[slot])):
                     grad = lax.dynamic_update_slice(

time: 90.7 us -> 91.1 us (level)
  starting transfers between devices: 34.4 us -> 37 us
  waiting for transfers between devices: 17.1 us -> 15.8 us
    ppermute x29, starting transfers between devices: 29.9 us -> 32.5 us  [to(): lax.ppermute(value, 'dp', [(i, i ^ distance) for i in range(samples)])]
    ppermute x29, waiting for transfers between devices: 17.1 us -> 15.8 us  [to(): lax.ppermute(value, 'dp', [(i, i ^ distance) for i in range(samples)])]
  transfers between devices with their start and end apart: 31 -> 31, of which waited for: 12 -> 9; matrix products, arithmetic and copies ran while one was open for 9% -> 8% of each run, Pallas kernels for 25% -> 24%
where the time goes in v13:
time: 91.1 us; the launch traced here: 90.9 us
  starting transfers between devices  37 us (41%)
  Pallas kernels  22 us (24%)
  waiting for transfers between devices  15.8 us (17%)
  other arithmetic  7.34 us (8%)
  local copies, waits for them, and re-layouts  6 us (7%)
  between operations  2.69 us (3%)
    ppermute x29, starting transfers between devices, to(): lax.ppermute(value, 'dp', [(i, i ^ distance) for i in range(samples)])  32.5 us
    ppermute x29, waiting for transfers between devices, to(): lax.ppermute(value, 'dp', [(i, i ^ distance) for i in range(samples)])  15.8 us
    pallas_call x2, Pallas kernels, kernel_grad(): pl.pallas_call(functools.partial(kernel_grad_kernel, depth), out_shape=[j...  10.5 us
    pallas_call x1, Pallas kernels, input_gradient(): pl.pallas_call(input_grad_kernel, out_shape=jax.ShapeDtypeStruct((rows, p...  6.54 us
    pallas_call x1, Pallas kernels, forward(): pl.pallas_call(forward_kernel, out_shape=jax.ShapeDtypeStruct((outs, posi...  4.99 us
    reshape x1, other arithmetic, on_device(): weight_grad = jnp.transpose(grad, (1, 3, 0, 2, 4)).reshape(rows, taps, outs)  4.64 us
    ppermute x1, starting transfers between devices, on_device(): their_cot = lax.ppermute(own_cot, 'chan', [(0, 1), (1, 0)])  2.95 us
    dynamic_update_slice x32, local copies, waits for them, and re-layouts, on_device(): lax.dynamic_update_slice(grad, value, (0, base * core_tiles + row, lane,...  2.02 us
  transfers between devices with their start and end apart: 31, of which 9 were waited for; matrix products, arithmetic and copies ran while one was open for 8% of the time, Pallas kernels for 24%

profile of v13, /device:TPU:0, one launch (start us, length us, event | category | flops | bytes accessed | tf_op | source)
XLA Modules:
  0.0 90.9 jit_solution(4223782612185236848)
XLA Ops:
  0.7 1.4 %dynamic-slice_bitcast_fusion = bf16[512,1152]{1,0:T(8,128)(2,1)S(1)} fusion(bf16[1,1024,1152]{2,1,0:T(8,128)(2,1)} %param.3, s32[]{:T(128)S(6)} %select_n.239), kind=kLoop, calls=%fused_computation.1 | loop fusion | bytes 2359300 | tf_op jit(solution)/shard_map/dynamic_slice | solution.py:338
  2.0 0.5 collective-permute-start
  2.6 2.9 %collective-permute-start.5 = (bf16[128,1152]{1,0:T(8,128)(2,1)}, bf16[128,1152]{1,0:T(8,128)(2,1)S(1)}, u32[]{:S(2)}, u32[]{:S(2)}) collective-permute-start(bf16[128,1152]{1,0:T(8,128)(2,1)} %bitcast.427), channel_id=1, source_target_pairs={{0,1},{1,0},{2,3},{3,2},{4,5},{5,4},{6,7},{7,6},{8,9},{9,8},{10,11... | collective-permute-start | bytes 884744 | tf_op jit(solution)/shard_map/ppermute | solution.py:331
  5.7 5.3 %kernel_grad.2 = (f32[73,8,128]{2,1,0:T(8,128)S(1)}, f32[73,8,128]{2,1,0:T(8,128)S(1)}, f32[73,8,128]{2,1,0:T(8,128)S(1)}, f32[73,8,128]{2,1,0:T(8,128)S(1)}, f3...) custom-call(s32[2]{0:T(128)S(1)} %pad_add_fusion.place_ref, bf16[1024,1152]{1,0:T(8,128)(2,1)} %bitcast.397, ...), custom_call_target="tpu_custom_call" | custom-call | flops 1509949440 | bytes 5308416 | tf_op jit(solution)/shard_map/kernel_grad/pallas_call | solution.py:122
  11.0 2.7 %collective-permute-start.2 = (f16[2,73,8,128]{3,2,1,0:T(8,128)(2,1)S(1)}, f16[2,73,8,128]{3,2,1,0:T(8,128)(2,1)S(1)}, u32[]{:S(2)}, u32[]{:S(2)}) collective-permute-start(f16[2,73,8,128]{3,2,1,0:T(8,128)(2,1)S(1)} %convert_element_type.349), channel_id=1, source_target_pairs={{0,4},{2,6},{4,0},{6,2},{8,12},{10,14},{12,8},{14,10},{16,20},{18,... | collective-permute-start | bytes 897032 | tf_op jit(solution)/shard_map/ppermute | solution.py:319
  13.9 0.5 slice.265
  15.2 0.1 maximum_select_fusion.cot_ref
  15.4 1.4 %collective-permute-done.6.other_cot = bf16[128,1152]{1,0:T(8,128)(2,1)S(1)} collective-permute-done((bf16[128,1152]{1,0:T(8,128)(2,1)S(1)}, bf16[128,1152]{1,0:T(8,128)(2,1)S(1)}, u32[]{:S(2)}, u32[]{:S(2)}) %collective-permute-start.6) | collective-permute-done | bytes 294944 | tf_op jit(solution)/shard_map/ppermute | solution.py:319
  16.7 5.2 %kernel_grad.3 = (f32[73,8,128]{2,1,0:T(8,128)S(1)}, f32[73,8,128]{2,1,0:T(8,128)S(1)}, f32[73,8,128]{2,1,0:T(8,128)S(1)}, f32[73,8,128]{2,1,0:T(8,128)S(1)}, f3...) custom-call(s32[2]{0:T(128)S(1)} %pad_add_fusion.place_ref, bf16[1024,1152]{1,0:T(8,128)(2,1)} %bitcast.398, ...), custom_call_target="tpu_custom_call" | custom-call | flops 1509949440 | bytes 5308416 | tf_op jit(solution)/shard_map/kernel_grad/pallas_call | solution.py:122
  22.1 2.1 %collective-permute-start.7 = (f16[2,73,8,128]{3,2,1,0:T(8,128)(2,1)S(1)}, f16[2,73,8,128]{3,2,1,0:T(8,128)(2,1)S(1)}, u32[]{:S(2)}, u32[]{:S(2)}) collective-permute-start(f16[2,73,8,128]{3,2,1,0:T(8,128)(2,1)S(1)} %convert_element_type.377), channel_id=1, source_target_pairs={{0,4},{2,6},{4,0},{6,2},{8,12},{10,14},{12,8},{14,10},{16,20},{18,... | collective-permute-start | bytes 897032 | tf_op jit(solution)/shard_map/ppermute | solution.py:319
  24.4 2.1 %collective-permute-start.4 = (f16[73,8,128]{2,1,0:T(8,128)(2,1)S(1)}, f16[73,8,128]{2,1,0:T(8,128)(2,1)S(1)}, u32[]{:S(2)}, u32[]{:S(2)}) collective-permute-start(f16[73,8,128]{2,1,0:T(8,128)(2,1)S(1)} %constant_dynamic-update-slice_fusion.19), channel_id=1, source_target_pairs={{0,8},{2,10},{4,12},{6,14},{8,0},{10,2},{12,4},{14,6},{16,24},{18,... | collective-permute-start | bytes 448520 | tf_op jit(solution)/shard_map/ppermute | solution.py:319
  26.5 1.5 %collective-permute-done.3 = f16[2,73,8,128]{3,2,1,0:T(8,128)(2,1)S(1)} collective-permute-done((f16[2,73,8,128]{3,2,1,0:T(8,128)(2,1)S(1)}, f16[2,73,8,128]{3,2,1,0:T(8,128)(2,1)S(1)}, u32[]{:S(2)}, u32[]{:S(2)}) %collective-permute-start.3) | collective-permute-done | bytes 299040 | tf_op jit(solution)/shard_map/ppermute | solution.py:319
  28.1 2.2 %collective-permute-start.10 = (f16[73,8,128]{2,1,0:T(8,128)(2,1)S(1)}, f16[73,8,128]{2,1,0:T(8,128)(2,1)S(1)}, u32[]{:S(2)}, u32[]{:S(2)}) collective-permute-start(f16[73,8,128]{2,1,0:T(8,128)(2,1)S(1)} %constant_dynamic-update-slice_fusion.18), channel_id=1, source_target_pairs={{0,8},{2,10},{4,12},{6,14},{8,0},{10,2},{12,4},{14,6},{16,24},{18,... | collective-permute-start | bytes 448520 | tf_op jit(solution)/shard_map/ppermute | solution.py:319
  30.4 0.4 collective-permute-done.4
  30.8 0.1 fusion.14
  31.0 3.0 %collective-permute-start.11 = (f16[73,8,128]{2,1,0:T(8,128)(2,1)S(1)}, f16[73,8,128]{2,1,0:T(8,128)(2,1)S(1)}, u32[]{:S(2)}, u32[]{:S(2)}) collective-permute-start(f16[73,8,128]{2,1,0:T(8,128)(2,1)S(1)} %constant_dynamic-update-slice_fusion.17), channel_id=1, source_target_pairs={{0,16},{2,18},{4,20},{6,22},{8,24},{10,26},{12,28},{14,30},{16,0},... | collective-permute-start | bytes 448520 | tf_op jit(solution)/shard_map/ppermute | solution.py:319
  34.0 0.4 collective-permute-done.7
  34.5 2.2 %collective-permute-start.9 = (f16[73,8,128]{2,1,0:T(8,128)(2,1)S(1)}, f16[73,8,128]{2,1,0:T(8,128)(2,1)S(1)}, u32[]{:S(2)}, u32[]{:S(2)}) collective-permute-start(f16[73,8,128]{2,1,0:T(8,128)(2,1)S(1)} %constant_dynamic-update-slice_fusion.16), channel_id=1, source_target_pairs={{0,8},{2,10},{4,12},{6,14},{8,0},{10,2},{12,4},{14,6},{16,24},{18,... | collective-permute-start | bytes 448520 | tf_op jit(solution)/shard_map/ppermute | solution.py:319
  36.8 5.0 %forward.1 = f32[256,1152]{1,0:T(8,128)S(1)} custom-call(bf16[1024,1152]{1,0:T(8,128)(2,1)S(1)} %bitcast.399, bf16[9,1024,256]{2,1,0:T(8,128)(2,1)S(1)} %bitcast.402, f32[8,128]{1,0:T(8,128)S(1)} %fusion.147._), custom_call_target="tpu_custom_call" | custom-call | flops 3019898880 | bytes 8257536 | tf_op jit(solution)/shard_map/forward/pallas_call | solution.py:194
  41.9 0.5 collective-permute-start.13
  42.6 0.1 fusion.3
  42.7 2.6 %collective-permute-start.14 = (f16[73,8,128]{2,1,0:T(8,128)(2,1)S(1)}, f16[73,8,128]{2,1,0:T(8,128)(2,1)S(1)}, u32[]{:S(2)}, u32[]{:S(2)}) collective-permute-start(f16[73,8,128]{2,1,0:T(8,128)(2,1)S(1)} %constant_dynamic-update-slice_fusion.14), channel_id=1, source_target_pairs={{0,16},{2,18},{4,20},{6,22},{8,24},{10,26},{12,28},{14,30},{16,0},... | collective-permute-start | bytes 448520 | tf_op jit(solution)/shard_map/ppermute | solution.py:319
  45.4 0.1 fusion.30
  45.5 1.6 %collective-permute-start.12 = (f16[9,8,1,8,128]{4,3,1,0,2:T(8,128)(2,1)S(1)}, f16[9,8,1,8,128]{4,3,1,0,2:T(8,128)(2,1)S(1)}, u32[]{:S(2)}, u32[]{:S(2)}) collective-permute-start(f16[9,8,1,8,128]{4,3,1,0,2:T(8,128)(2,1)S(1)} %bitcast.412), channel_id=1, source_target_pairs={{0,4},{2,6},{4,0},{6,2},{8,12},{10,14},{12,8},{14,10},{16,20},{18,... | collective-permute-start | bytes 442376 | tf_op jit(solution)/shard_map/ppermute | solution.py:319
  47.1 1.6 %collective-permute-start.19 = (f16[9,8,1,8,128]{4,3,1,0,2:T(8,128)(2,1)S(1)}, f16[9,8,1,8,128]{4,3,1,0,2:T(8,128)(2,1)S(1)}, u32[]{:S(2)}, u32[]{:S(2)}) collective-permute-start(f16[9,8,1,8,128]{4,3,1,0,2:T(8,128)(2,1)S(1)} %bitcast.413), channel_id=1, source_target_pairs={{0,8},{2,10},{4,12},{6,14},{8,0},{10,2},{12,4},{14,6},{16,24},{18,... | collective-permute-start | bytes 442376 | tf_op jit(solution)/shard_map/ppermute | solution.py:319
  48.7 0.3 collective-permute-start.16
  49.0 6.5 %input_gradient.1 = bf16[1024,1152]{1,0:T(8,128)(2,1)} custom-call(bf16[256,1152]{1,0:T(8,128)(2,1)S(1)} %maximum_select_fusion.cot_ref, bf16[9,1024,256]{2,1,0:T(8,128)(2,1)S(1)} %bitcast.403, f32[8,128]{1,0:T(8,128)S(1)} %convert_bitcast_fusion._), custom_call_target="tpu_custom_call" | custom-call | flops 3019898880 | bytes 7667712 | tf_op jit(solution)/shard_map/input_gradient/pallas_call | solution.py:242
  55.6 2.6 %collective-permute-done.16 = f16[9,8,1,8,128]{4,3,2,1,0:T(8,128)(2,1)S(1)} collective-permute-done((f16[9,8,1,8,128]{4,3,2,1,0:T(8,128)(2,1)S(1)}, f16[9,8,1,8,128]{4,3,2,1,0:T(8,128)(2,1)S(1)}, u32[]{:S(2)}, u32[]{:S(2)}) %collective-permute-start.16) | collective-permute-done | bytes 147488 | tf_op jit(solution)/shard_map/ppermute | solution.py:319
  58.2 0.3 collective-permute-start.17
  58.6 1.6 %collective-permute-start.20 = (f16[2,9,8,1,8,128]{5,4,2,1,3,0:T(8,128)(2,1)S(1)}, f16[2,9,8,1,8,128]{5,4,2,1,3,0:T(8,128)(2,1)S(1)}, u32[]{:S(2)}, u32[]{:S(2)}) collective-permute-start(f16[2,9,8,1,8,128]{5,4,2,1,3,0:T(8,128)(2,1)S(1)} %pad_maximum_fusion), channel_id=1, source_target_pairs={{0,4},{2,6},{4,0},{6,2},{8,12},{10,14},{12,8},{14,10},{16,20},{18,... | collective-permute-start | bytes 884744 | tf_op jit(solution)/shard_map/ppermute | solution.py:319
  60.4 0.1 fusion.25
  60.5 3.0 %collective-permute-start.23 = (f16[9,8,1,8,128]{4,3,1,0,2:T(8,128)(2,1)S(1)}, f16[9,8,1,8,128]{4,3,1,0,2:T(8,128)(2,1)S(1)}, u32[]{:S(2)}, u32[]{:S(2)}) collective-permute-start(f16[9,8,1,8,128]{4,3,1,0,2:T(8,128)(2,1)S(1)} %bitcast.405), channel_id=1, source_target_pairs={{0,16},{2,18},{4,20},{6,22},{8,24},{10,26},{12,28},{14,30},{16,0},... | collective-permute-start | bytes 442376 | tf_op jit(solution)/shard_map/ppermute | solution.py:319
  63.5 0.5 collective-permute-start.26
  64.1 0.1 collective-permute-start.22
  64.2 0.5 slice.296
  65.5 1.6 %collective-permute-start.15 = (f32[128,1152]{1,0:T(8,128)S(1)}, f32[128,1152]{1,0:T(8,128)S(1)}, u32[]{:S(2)}, u32[]{:S(2)}) collective-permute-start(f32[128,1152]{1,0:T(8,128)S(1)} %dynamic-slice_select_fusion), channel_id=1, source_target_pairs={{0,1},{1,0},{2,3},{3,2},{4,5},{5,4},{6,7},{7,6},{8,9},{9,8},{10,11... | collective-permute-start | bytes 1769480 | tf_op jit(solution)/shard_map/ppermute | solution.py:450
  67.1 2.6 %collective-permute-done.22 = f16[9,8,1,8,128]{4,3,1,0,2:T(8,128)(2,1)S(1)} collective-permute-done((f16[9,8,1,8,128]{4,3,1,0,2:T(8,128)(2,1)S(1)}, f16[9,8,1,8,128]{4,3,1,0,2:T(8,128)(2,1)S(1)}, u32[]{:S(2)}, u32[]{:S(2)}) %collective-permute-start.22) | collective-permute-done | bytes 147488 | tf_op jit(solution)/shard_map/ppermute | solution.py:319
  69.7 1.2 %collective-permute-start.18 = (f16[1,9,8,1,8,128]{5,4,2,1,3,0:T(8,128)(2,1)S(1)}, f16[1,9,8,1,8,128]{5,4,2,1,3,0:T(8,128)(2,1)S(1)}, u32[]{:S(2)}, u32[]{:S(2)}) collective-permute-start(f16[1,9,8,1,8,128]{5,4,2,1,3,0:T(8,128)(2,1)S(1)} %bitcast.424), channel_id=1, source_target_pairs={{0,4},{2,6},{4,0},{6,2},{8,12},{10,14},{12,8},{14,10},{16,20},{18,... | collective-permute-start | bytes 442376 | tf_op jit(solution)/shard_map/ppermute | solution.py:319
  71.0 0.9 %collective-permute-start.24 = (f16[2,9,8,1,8,128]{5,4,2,1,3,0:T(8,128)(2,1)S(1)}, f16[2,9,8,1,8,128]{5,4,2,1,3,0:T(8,128)(2,1)S(1)}, u32[]{:S(2)}, u32[]{:S(2)}) collective-permute-start(f16[2,9,8,1,8,128]{5,4,2,1,3,0:T(8,128)(2,1)S(1)} %pad_maximum_fusion.1), channel_id=1, source_target_pairs={{0,4},{2,6},{4,0},{6,2},{8,12},{10,14},{12,8},{14,10},{16,20},{18,... | collective-permute-start | bytes 884744 | tf_op jit(solution)/shard_map/ppermute | solution.py:319
  72.0 1.0 %collective-permute-start.25 = (f16[9,8,1,8,128]{4,3,1,0,2:T(8,128)(2,1)S(1)}, f16[9,8,1,8,128]{4,3,1,0,2:T(8,128)(2,1)S(1)}, u32[]{:S(2)}, u32[]{:S(2)}) collective-permute-start(f16[9,8,1,8,128]{4,3,1,0,2:T(8,128)(2,1)S(1)} %collective-permute-done.23), channel_id=1, source_target_pairs={{0,8},{2,10},{4,12},{6,14},{8,0},{10,2},{12,4},{14,6},{16,24},{18,... | collective-permute-start | bytes 442376 | tf_op jit(solution)/shard_map/ppermute | solution.py:319
  73.1 3.4 %collective-permute-done.18 = f16[1,9,8,1,8,128]{5,4,2,1,3,0:T(8,128)(2,1)S(1)} collective-permute-done((f16[1,9,8,1,8,128]{5,4,2,1,3,0:T(8,128)(2,1)S(1)}, f16[1,9,8,1,8,128]{5,4,2,1,3,0:T(8,128)(2,1)S(1)}, u32[]{:S(2)}, u32[]{:S(2)}) %collective-permute-start.18) | collective-permute-done | bytes 147488 | tf_op jit(solution)/shard_map/ppermute | solution.py:319
  76.6 0.7 broadcast_in_dim.106
  77.5 0.6 collective-permute-start.21
  78.1 1.2 %collective-permute-start.28 = (f16[1,9,8,1,8,128]{5,4,2,1,3,0:T(8,128)(2,1)S(1)}, f16[1,9,8,1,8,128]{5,4,2,1,3,0:T(8,128)(2,1)S(1)}, u32[]{:S(2)}, u32[]{:S(2)}) collective-permute-start(f16[1,9,8,1,8,128]{5,4,2,1,3,0:T(8,128)(2,1)S(1)} %bitcast.425), channel_id=1, source_target_pairs={{0,4},{2,6},{4,0},{6,2},{8,12},{10,14},{12,8},{14,10},{16,20},{18,... | collective-permute-start | bytes 442376 | tf_op jit(solution)/shard_map/ppermute | solution.py:319
  79.4 1.2 %collective-permute-done.24 = f16[2,9,8,1,8,128]{5,4,2,1,3,0:T(8,128)(2,1)S(1)} collective-permute-done((f16[2,9,8,1,8,128]{5,4,2,1,3,0:T(8,128)(2,1)S(1)}, f16[2,9,8,1,8,128]{5,4,2,1,3,0:T(8,128)(2,1)S(1)}, u32[]{:S(2)}, u32[]{:S(2)}) %collective-permute-start.24) | collective-permute-done | bytes 294944 | tf_op jit(solution)/shard_map/ppermute | solution.py:319
  80.8 0.8 fusion.20
  81.6 2.3 %collective-permute-done.28 = f16[1,9,8,1,8,128]{5,4,2,1,3,0:T(8,128)(2,1)S(1)} collective-permute-done((f16[1,9,8,1,8,128]{5,4,2,1,3,0:T(8,128)(2,1)S(1)}, f16[1,9,8,1,8,128]{5,4,2,1,3,0:T(8,128)(2,1)S(1)}, u32[]{:S(2)}, u32[]{:S(2)}) %collective-permute-start.28) | collective-permute-done | bytes 147488 | tf_op jit(solution)/shard_map/ppermute | solution.py:319
  86.2 4.6 %multiply_bitcast_fusion = f32[1024,9,256]{2,0,1:T(8,128)} fusion(f16[9,128,2,8,128]{4,3,2,1,0:T(8,128)(2,1)S(1)} %bitcast_dynamic-update-slice_fusion, f32[128,2,8,128]{3,2,1,0:T(8,128)S(1)} %bitcast.404), kind=kLoop, calls=%fused_computation | loop fusion | flops 4718592 | bytes 15204352 | tf_op jit(solution)/shard_map/reshape | solution.py:444
  (140 shorter events, 4.7 us)
Async XLA Ops:
  2.0 13.2 %copy-start.1 = (bf16[1,128,1152]{2,1,0:T(8,128)(2,1)S(1)}, bf16[1,128,1152]{2,1,0:T(8,128)(2,1)}, u32[]{:S(2)}) copy-start(bf16[1,128,1152]{2,1,0:T(8,128)(2,1)} %param.5) | copy-start | bytes 884740
  2.0 3.6 %collective-permute-start = (bf16[512,1152]{1,0:T(8,128)(2,1)S(1)}, bf16[512,1152]{1,0:T(8,128)(2,1)S(1)}, u32[]{:S(2)}, u32[]{:S(2)}) collective-permute-start(bf16[512,1152]{1,0:T(8,128)(2,1)S(1)} %dynamic-slice_bitcast_fusion), channel_id=1, source_target_pairs={{0,2},{2,0},{4,6},{6,4},{8,10},{10,8},{12,14},{14,12},{16,18},{18,... | collective-permute-start | bytes 3538952 | tf_op jit(solution)/shard_map/ppermute | solution.py:319
  2.5 3.1 %collective-permute-start.1 = (bf16[128,1152]{1,0:T(8,128)(2,1)}, bf16[128,1152]{1,0:T(8,128)(2,1)S(1)}, u32[]{:S(2)}, u32[]{:S(2)}) collective-permute-start(bf16[128,1152]{1,0:T(8,128)(2,1)} %bitcast.426), channel_id=1, source_target_pairs={{0,2},{2,0},{4,6},{6,4},{8,10},{10,8},{12,14},{14,12},{16,18},{18,... | collective-permute-start | bytes 884744 | tf_op jit(solution)/shard_map/ppermute | solution.py:319
  2.6 12.4 %collective-permute-start.5 = (bf16[128,1152]{1,0:T(8,128)(2,1)}, bf16[128,1152]{1,0:T(8,128)(2,1)S(1)}, u32[]{:S(2)}, u32[]{:S(2)}) collective-permute-start(bf16[128,1152]{1,0:T(8,128)(2,1)} %bitcast.427), channel_id=1, source_target_pairs={{0,1},{1,0},{2,3},{3,2},{4,5},{5,4},{6,7},{7,6},{8,9},{9,8},{10,11... | collective-permute-start | bytes 884744 | tf_op jit(solution)/shard_map/ppermute | solution.py:331
  11.0 13.3 %collective-permute-start.2 = (f16[2,73,8,128]{3,2,1,0:T(8,128)(2,1)S(1)}, f16[2,73,8,128]{3,2,1,0:T(8,128)(2,1)S(1)}, u32[]{:S(2)}, u32[]{:S(2)}) collective-permute-start(f16[2,73,8,128]{3,2,1,0:T(8,128)(2,1)S(1)} %convert_element_type.349), channel_id=1, source_target_pairs={{0,4},{2,6},{4,0},{6,2},{8,12},{10,14},{12,8},{14,10},{16,20},{18,... | collective-permute-start | bytes 897032 | tf_op jit(solution)/shard_map/ppermute | solution.py:319
  13.8 14.2 %collective-permute-start.3 = (f16[2,73,8,128]{3,2,1,0:T(8,128)(2,1)S(1)}, f16[2,73,8,128]{3,2,1,0:T(8,128)(2,1)S(1)}, u32[]{:S(2)}, u32[]{:S(2)}) collective-permute-start(f16[2,73,8,128]{3,2,1,0:T(8,128)(2,1)S(1)} %select_convert_fusion.1), channel_id=1, source_target_pairs={{0,4},{2,6},{4,0},{6,2},{8,12},{10,14},{12,8},{14,10},{16,20},{18,... | collective-permute-start | bytes 897032 | tf_op jit(solution)/shard_map/ppermute | solution.py:319
  15.1 1.6 %collective-permute-start.6 = (bf16[128,1152]{1,0:T(8,128)(2,1)S(1)}, bf16[128,1152]{1,0:T(8,128)(2,1)S(1)}, u32[]{:S(2)}, u32[]{:S(2)}) collective-permute-start(bf16[128,1152]{1,0:T(8,128)(2,1)S(1)} %broadcast_select_fusion.own_cot), channel_id=1, source_target_pairs={{0,2},{2,0},{4,6},{6,4},{8,10},{10,8},{12,14},{14,12},{16,18},{18,... | collective-permute-start | bytes 884744 | tf_op jit(solution)/shard_map/ppermute | solution.py:319
  15.2 21.6 %slice-start = ((s8[4718592]{0:T(1024)(128)(4,1)}), s8[4194304]{0:T(1024)(128)(4,1)S(1)}, s32[]{:S(2)}) async-start(s8[4718592]{0:T(1024)(128)(4,1)} %bitcast.400), calls=%async_computation | async-start | bytes 8388608
  15.3 21.4 %copy-start = (bf16[1,1024,1152]{2,1,0:T(8,128)(2,1)S(1)}, bf16[1,1024,1152]{2,1,0:T(8,128)(2,1)}, u32[]{:S(2)}) copy-start(bf16[1,1024,1152]{2,1,0:T(8,128)(2,1)} %param.3) | copy-start | bytes 7077892
  15.4 21.4 %slice-start.1 = ((s8[4718592]{0:T(1024)(128)(4,1)}), s8[524288]{0:T(1024)(128)(4,1)S(1)}, s32[]{:S(2)}) async-start(s8[4718592]{0:T(1024)(128)(4,1)} %bitcast.400), calls=%async_computation.1 | async-start | bytes 1048576
  22.1 12.3 %collective-permute-start.7 = (f16[2,73,8,128]{3,2,1,0:T(8,128)(2,1)S(1)}, f16[2,73,8,128]{3,2,1,0:T(8,128)(2,1)S(1)}, u32[]{:S(2)}, u32[]{:S(2)}) collective-permute-start(f16[2,73,8,128]{3,2,1,0:T(8,128)(2,1)S(1)} %convert_element_type.377), channel_id=1, source_target_pairs={{0,4},{2,6},{4,0},{6,2},{8,12},{10,14},{12,8},{14,10},{16,20},{18,... | collective-permute-start | bytes 897032 | tf_op jit(solution)/shard_map/ppermute | solution.py:319
  24.2 17.6 %collective-permute-start.8 = (f16[2,73,8,128]{3,2,1,0:T(8,128)(2,1)S(1)}, f16[2,73,8,128]{3,2,1,0:T(8,128)(2,1)S(1)}, u32[]{:S(2)}, u32[]{:S(2)}) collective-permute-start(f16[2,73,8,128]{3,2,1,0:T(8,128)(2,1)S(1)} %select_convert_fusion), channel_id=1, source_target_pairs={{0,4},{2,6},{4,0},{6,2},{8,12},{10,14},{12,8},{14,10},{16,20},{18,... | collective-permute-start | bytes 897032 | tf_op jit(solution)/shard_map/ppermute | solution.py:319
  24.4 6.4 %collective-permute-start.4 = (f16[73,8,128]{2,1,0:T(8,128)(2,1)S(1)}, f16[73,8,128]{2,1,0:T(8,128)(2,1)S(1)}, u32[]{:S(2)}, u32[]{:S(2)}) collective-permute-start(f16[73,8,128]{2,1,0:T(8,128)(2,1)S(1)} %constant_dynamic-update-slice_fusion.19), channel_id=1, source_target_pairs={{0,8},{2,10},{4,12},{6,14},{8,0},{10,2},{12,4},{14,6},{16,24},{18,... | collective-permute-start | bytes 448520 | tf_op jit(solution)/shard_map/ppermute | solution.py:319
  28.1 14.4 %collective-permute-start.10 = (f16[73,8,128]{2,1,0:T(8,128)(2,1)S(1)}, f16[73,8,128]{2,1,0:T(8,128)(2,1)S(1)}, u32[]{:S(2)}, u32[]{:S(2)}) collective-permute-start(f16[73,8,128]{2,1,0:T(8,128)(2,1)S(1)} %constant_dynamic-update-slice_fusion.18), channel_id=1, source_target_pairs={{0,8},{2,10},{4,12},{6,14},{8,0},{10,2},{12,4},{14,6},{16,24},{18,... | collective-permute-start | bytes 448520 | tf_op jit(solution)/shard_map/ppermute | solution.py:319
  31.0 11.5 %collective-permute-start.11 = (f16[73,8,128]{2,1,0:T(8,128)(2,1)S(1)}, f16[73,8,128]{2,1,0:T(8,128)(2,1)S(1)}, u32[]{:S(2)}, u32[]{:S(2)}) collective-permute-start(f16[73,8,128]{2,1,0:T(8,128)(2,1)S(1)} %constant_dynamic-update-slice_fusion.17), channel_id=1, source_target_pairs={{0,16},{2,18},{4,20},{6,22},{8,24},{10,26},{12,28},{14,30},{16,0},... | collective-permute-start | bytes 448520 | tf_op jit(solution)/shard_map/ppermute | solution.py:319
  34.5 8.0 %collective-permute-start.9 = (f16[73,8,128]{2,1,0:T(8,128)(2,1)S(1)}, f16[73,8,128]{2,1,0:T(8,128)(2,1)S(1)}, u32[]{:S(2)}, u32[]{:S(2)}) collective-permute-start(f16[73,8,128]{2,1,0:T(8,128)(2,1)S(1)} %constant_dynamic-update-slice_fusion.16), channel_id=1, source_target_pairs={{0,8},{2,10},{4,12},{6,14},{8,0},{10,2},{12,4},{14,6},{16,24},{18,... | collective-permute-start | bytes 448520 | tf_op jit(solution)/shard_map/ppermute | solution.py:319
  41.9 18.4 %collective-permute-start.13 = (f16[73,8,128]{2,1,0:T(8,128)(2,1)S(1)}, f16[73,8,128]{2,1,0:T(8,128)(2,1)S(1)}, u32[]{:S(2)}, u32[]{:S(2)}) collective-permute-start(f16[73,8,128]{2,1,0:T(8,128)(2,1)S(1)} %constant_dynamic-update-slice_fusion.15), channel_id=1, source_target_pairs={{0,8},{2,10},{4,12},{6,14},{8,0},{10,2},{12,4},{14,6},{16,24},{18,... | collective-permute-start | bytes 448520 | tf_op jit(solution)/shard_map/ppermute | solution.py:319
  42.7 17.6 %collective-permute-start.14 = (f16[73,8,128]{2,1,0:T(8,128)(2,1)S(1)}, f16[73,8,128]{2,1,0:T(8,128)(2,1)S(1)}, u32[]{:S(2)}, u32[]{:S(2)}) collective-permute-start(f16[73,8,128]{2,1,0:T(8,128)(2,1)S(1)} %constant_dynamic-update-slice_fusion.14), channel_id=1, source_target_pairs={{0,16},{2,18},{4,20},{6,22},{8,24},{10,26},{12,28},{14,30},{16,0},... | collective-permute-start | bytes 448520 | tf_op jit(solution)/shard_map/ppermute | solution.py:319
  45.5 14.8 %collective-permute-start.12 = (f16[9,8,1,8,128]{4,3,1,0,2:T(8,128)(2,1)S(1)}, f16[9,8,1,8,128]{4,3,1,0,2:T(8,128)(2,1)S(1)}, u32[]{:S(2)}, u32[]{:S(2)}) collective-permute-start(f16[9,8,1,8,128]{4,3,1,0,2:T(8,128)(2,1)S(1)} %bitcast.412), channel_id=1, source_target_pairs={{0,4},{2,6},{4,0},{6,2},{8,12},{10,14},{12,8},{14,10},{16,20},{18,... | collective-permute-start | bytes 442376 | tf_op jit(solution)/shard_map/ppermute | solution.py:319
  47.1 11.4 %collective-permute-start.19 = (f16[9,8,1,8,128]{4,3,1,0,2:T(8,128)(2,1)S(1)}, f16[9,8,1,8,128]{4,3,1,0,2:T(8,128)(2,1)S(1)}, u32[]{:S(2)}, u32[]{:S(2)}) collective-permute-start(f16[9,8,1,8,128]{4,3,1,0,2:T(8,128)(2,1)S(1)} %bitcast.413), channel_id=1, source_target_pairs={{0,8},{2,10},{4,12},{6,14},{8,0},{10,2},{12,4},{14,6},{16,24},{18,... | collective-permute-start | bytes 442376 | tf_op jit(solution)/shard_map/ppermute | solution.py:319
  48.7 9.5 %collective-permute-start.16 = (f16[9,8,1,8,128]{4,3,2,1,0:T(8,128)(2,1)S(1)}, f16[9,8,1,8,128]{4,3,2,1,0:T(8,128)(2,1)S(1)}, u32[]{:S(2)}, u32[]{:S(2)}) collective-permute-start(f16[9,8,1,8,128]{4,3,2,1,0:T(8,128)(2,1)S(1)} %bitcast.415), channel_id=1, source_target_pairs={{0,16},{2,18},{4,20},{6,22},{8,24},{10,26},{12,28},{14,30},{16,0},... | collective-permute-start | bytes 442376 | tf_op jit(solution)/shard_map/ppermute | solution.py:319
  58.2 7.3 %collective-permute-start.17 = (f16[9,8,1,8,128]{4,3,1,0,2:T(8,128)(2,1)S(1)}, f16[9,8,1,8,128]{4,3,1,0,2:T(8,128)(2,1)S(1)}, u32[]{:S(2)}, u32[]{:S(2)}) collective-permute-start(f16[9,8,1,8,128]{4,3,1,0,2:T(8,128)(2,1)S(1)} %bitcast.419), channel_id=1, source_target_pairs={{0,8},{2,10},{4,12},{6,14},{8,0},{10,2},{12,4},{14,6},{16,24},{18,... | collective-permute-start | bytes 442376 | tf_op jit(solution)/shard_map/ppermute | solution.py:319
  58.6 13.4 %collective-permute-start.20 = (f16[2,9,8,1,8,128]{5,4,2,1,3,0:T(8,128)(2,1)S(1)}, f16[2,9,8,1,8,128]{5,4,2,1,3,0:T(8,128)(2,1)S(1)}, u32[]{:S(2)}, u32[]{:S(2)}) collective-permute-start(f16[2,9,8,1,8,128]{5,4,2,1,3,0:T(8,128)(2,1)S(1)} %pad_maximum_fusion), channel_id=1, source_target_pairs={{0,4},{2,6},{4,0},{6,2},{8,12},{10,14},{12,8},{14,10},{16,20},{18,... | collective-permute-start | bytes 884744 | tf_op jit(solution)/shard_map/ppermute | solution.py:319
  60.5 10.4 %collective-permute-start.23 = (f16[9,8,1,8,128]{4,3,1,0,2:T(8,128)(2,1)S(1)}, f16[9,8,1,8,128]{4,3,1,0,2:T(8,128)(2,1)S(1)}, u32[]{:S(2)}, u32[]{:S(2)}) collective-permute-start(f16[9,8,1,8,128]{4,3,1,0,2:T(8,128)(2,1)S(1)} %bitcast.405), channel_id=1, source_target_pairs={{0,16},{2,18},{4,20},{6,22},{8,24},{10,26},{12,28},{14,30},{16,0},... | collective-permute-start | bytes 442376 | tf_op jit(solution)/shard_map/ppermute | solution.py:319
  63.5 14.6 %collective-permute-start.26 = (f16[9,8,1,8,128]{4,3,1,0,2:T(8,128)(2,1)S(1)}, f16[9,8,1,8,128]{4,3,1,0,2:T(8,128)(2,1)S(1)}, u32[]{:S(2)}, u32[]{:S(2)}) collective-permute-start(f16[9,8,1,8,128]{4,3,1,0,2:T(8,128)(2,1)S(1)} %bitcast.406), channel_id=1, source_target_pairs={{0,4},{2,6},{4,0},{6,2},{8,12},{10,14},{12,8},{14,10},{16,20},{18,... | collective-permute-start | bytes 442376 | tf_op jit(solution)/shard_map/ppermute | solution.py:319
  64.1 5.6 %collective-permute-start.22 = (f16[9,8,1,8,128]{4,3,1,0,2:T(8,128)(2,1)S(1)}, f16[9,8,1,8,128]{4,3,1,0,2:T(8,128)(2,1)S(1)}, u32[]{:S(2)}, u32[]{:S(2)}) collective-permute-start(f16[9,8,1,8,128]{4,3,1,0,2:T(8,128)(2,1)S(1)} %broadcast_select_fusion.2), channel_id=1, source_target_pairs={{0,8},{2,10},{4,12},{6,14},{8,0},{10,2},{12,4},{14,6},{16,24},{18,... | collective-permute-start | bytes 442376 | tf_op jit(solution)/shard_map/ppermute | solution.py:319
  65.5 15.4 %collective-permute-start.15 = (f32[128,1152]{1,0:T(8,128)S(1)}, f32[128,1152]{1,0:T(8,128)S(1)}, u32[]{:S(2)}, u32[]{:S(2)}) collective-permute-start(f32[128,1152]{1,0:T(8,128)S(1)} %dynamic-slice_select_fusion), channel_id=1, source_target_pairs={{0,1},{1,0},{2,3},{3,2},{4,5},{5,4},{6,7},{7,6},{8,9},{9,8},{10,11... | collective-permute-start | bytes 1769480 | tf_op jit(solution)/shard_map/ppermute | solution.py:450
  69.7 6.8 %collective-permute-start.18 = (f16[1,9,8,1,8,128]{5,4,2,1,3,0:T(8,128)(2,1)S(1)}, f16[1,9,8,1,8,128]{5,4,2,1,3,0:T(8,128)(2,1)S(1)}, u32[]{:S(2)}, u32[]{:S(2)}) collective-permute-start(f16[1,9,8,1,8,128]{5,4,2,1,3,0:T(8,128)(2,1)S(1)} %bitcast.424), channel_id=1, source_target_pairs={{0,4},{2,6},{4,0},{6,2},{8,12},{10,14},{12,8},{14,10},{16,20},{18,... | collective-permute-start | bytes 442376 | tf_op jit(solution)/shard_map/ppermute | solution.py:319
  71.0 9.7 %collective-permute-start.24 = (f16[2,9,8,1,8,128]{5,4,2,1,3,0:T(8,128)(2,1)S(1)}, f16[2,9,8,1,8,128]{5,4,2,1,3,0:T(8,128)(2,1)S(1)}, u32[]{:S(2)}, u32[]{:S(2)}) collective-permute-start(f16[2,9,8,1,8,128]{5,4,2,1,3,0:T(8,128)(2,1)S(1)} %pad_maximum_fusion.1), channel_id=1, source_target_pairs={{0,4},{2,6},{4,0},{6,2},{8,12},{10,14},{12,8},{14,10},{16,20},{18,... | collective-permute-start | bytes 884744 | tf_op jit(solution)/shard_map/ppermute | solution.py:319
  72.0 5.4 %collective-permute-start.25 = (f16[9,8,1,8,128]{4,3,1,0,2:T(8,128)(2,1)S(1)}, f16[9,8,1,8,128]{4,3,1,0,2:T(8,128)(2,1)S(1)}, u32[]{:S(2)}, u32[]{:S(2)}) collective-permute-start(f16[9,8,1,8,128]{4,3,1,0,2:T(8,128)(2,1)S(1)} %collective-permute-done.23), channel_id=1, source_target_pairs={{0,8},{2,10},{4,12},{6,14},{8,0},{10,2},{12,4},{14,6},{16,24},{18,... | collective-permute-start | bytes 442376 | tf_op jit(solution)/shard_map/ppermute | solution.py:319
  76.5 2.9 %collective-permute-start.30 = (f32[2,8,128]{2,1,0:T(8,128)S(1)}, f32[2,8,128]{2,1,0:T(8,128)S(1)}, u32[]{:S(2)}, u32[]{:S(2)}) collective-permute-start(f32[2,8,128]{2,1,0:T(8,128)S(1)} %fusion.53), channel_id=1, source_target_pairs={{0,2},{2,0},{4,6},{6,4},{8,10},{10,8},{12,14},{14,12},{16,18},{18,... | collective-permute-start | bytes 24584 | tf_op jit(solution)/shard_map/ppermute | solution.py:319
  77.5 4.2 %collective-permute-start.21 = (f16[8,9,8,1,8,128]{5,4,2,1,3,0:T(8,128)(2,1)S(1)}, f16[8,9,8,1,8,128]{5,4,2,1,3,0:T(8,128)(2,1)S(1)}, u32[]{:S(2)}, u32[]{:S(2)}) collective-permute-start(f16[8,9,8,1,8,128]{5,4,2,1,3,0:T(8,128)(2,1)S(1)} %constant_dynamic-update-slice_fusion), channel_id=1, source_target_pairs={{0,2},{2,0},{4,6},{6,4},{8,10},{10,8},{12,14},{14,12},{16,18},{18,... | collective-permute-start | bytes 3538952 | tf_op jit(solution)/shard_map/ppermute | solution.py:319
  78.1 5.8 %collective-permute-start.28 = (f16[1,9,8,1,8,128]{5,4,2,1,3,0:T(8,128)(2,1)S(1)}, f16[1,9,8,1,8,128]{5,4,2,1,3,0:T(8,128)(2,1)S(1)}, u32[]{:S(2)}, u32[]{:S(2)}) collective-permute-start(f16[1,9,8,1,8,128]{5,4,2,1,3,0:T(8,128)(2,1)S(1)} %bitcast.425), channel_id=1, source_target_pairs={{0,4},{2,6},{4,0},{6,2},{8,12},{10,14},{12,8},{14,10},{16,20},{18,... | collective-permute-start | bytes 442376 | tf_op jit(solution)/shard_map/ppermute | solution.py:319
  80.8 4.4 %collective-permute-start.27 = (f16[7,9,8,1,8,128]{5,4,2,1,3,0:T(8,128)(2,1)S(1)}, f16[7,9,8,1,8,128]{5,4,2,1,3,0:T(8,128)(2,1)S(1)}, u32[]{:S(2)}, u32[]{:S(2)}) collective-permute-start(f16[7,9,8,1,8,128]{5,4,2,1,3,0:T(8,128)(2,1)S(1)} %constant_dynamic-update-slice_fusion.6), channel_id=1, source_target_pairs={{0,2},{2,0},{4,6},{6,4},{8,10},{10,8},{12,14},{14,12},{16,18},{18,... | collective-permute-start | bytes 3096584 | tf_op jit(solution)/shard_map/ppermute | solution.py:319
  84.0 2.1 %collective-permute-start.29 = (f16[1,9,8,1,8,128]{5,4,2,1,3,0:T(8,128)(2,1)S(1)}, f16[1,9,8,1,8,128]{5,4,2,1,3,0:T(8,128)(2,1)S(1)}, u32[]{:S(2)}, u32[]{:S(2)}) collective-permute-start(f16[1,9,8,1,8,128]{5,4,2,1,3,0:T(8,128)(2,1)S(1)} %broadcast_select_fusion.1), channel_id=1, source_target_pairs={{0,2},{2,0},{4,6},{6,4},{8,10},{10,8},{12,14},{14,12},{16,18},{18,... | collective-permute-start | bytes 442376 | tf_op jit(solution)/shard_map/ppermute | solution.py:319

commit v14 on v12

--- a/solution.py
+++ b/solution.py
@@ -55,7 +55,7 @@
 
 def kernel_grad_kernel(depth, place_ref, own_x, other_x, own_cot, other_cot, _, *refs):
     near, far = refs[:depth], refs[depth : depth + 2]
-    sums, peak_ref = refs[depth + 2 :]
+    sums, peak_ref, moved_ref, centre = refs[depth + 2 :]
     step = pl.program_id(0)
     rows, width = own_x.shape[0], own_cot.shape[0]
     shards = 2 * depth
@@ -63,37 +63,54 @@
     tiles = shard_rows // TILE
     lanes = width // LANES
 
+    def products(cots):
+        total = None
+        for x_ref, cot in zip((own_x, other_x), cots):
+            term = lax.dot_general(
+                x_ref[...], cot, (((1,), (1,)), ((), ())), preferred_element_type=jnp.float32
+            )
+            total = term if total is None else total + term
+        return total
+
+    def moved_cotangents(cot_ref, group):
+        cot = cot_ref[...].astype(jnp.float32)
+        return jnp.concatenate(
+            [moved_cotangent(cot, group, shift) for shift in COLUMN_SHIFTS], 0
+        )
+
+    def keep(group, total):
+        peak_ref[...] = jnp.maximum(
+            peak_ref[...], jnp.max(jnp.abs(total), axis=0, keepdims=True)
+        )
+        for column in range(3):
+            for shard in range(shards):
+                for tile in range(tiles):
+                    for lane in range(lanes):
+                        row = shard * shard_rows + tile * TILE
+                        first = column * width + lane * LANES
+                        slot = ((3 * group + column) * tiles + tile) * lanes + lane
+                        sums[shard, slot] = total[row : row + TILE, first : first + LANES]
+
     @pl.when(step == 0)
     def _():
         peak_ref[...] = jnp.zeros(peak_ref.shape, jnp.float32)
-
-    for group in range(3):
-
-        @pl.when(step == group)
-        def _(group=group):
-            where = window(group)
-            total = None
-            for x_ref, cot_ref in ((own_x, own_cot), (other_x, other_cot)):
-                cot = cot_ref[...].astype(jnp.float32)
-                cots = [moved_cotangent(cot, group, shift) for shift in COLUMN_SHIFTS]
-                term = lax.dot_general(
-                    x_ref[:, where],
-                    jnp.concatenate(cots, 0),
-                    (((1,), (1,)), ((), ())),
-                    preferred_element_type=jnp.float32,
-                )
-                total = term if total is None else total + term
-            peak_ref[...] = jnp.maximum(
-                peak_ref[...], jnp.max(jnp.abs(total), axis=0, keepdims=True)
-            )
-            for column in range(3):
-                for shard in range(shards):
-                    for tile in range(tiles):
-                        for lane in range(lanes):
-                            row = shard * shard_rows + tile * TILE
-                            first = column * width + lane * LANES
-                            slot = ((3 * group + column) * tiles + tile) * lanes + lane
-                            sums[shard, slot] = total[row : row + TILE, first : first + LANES]
+        for sample, cot_ref in enumerate((own_cot, other_cot)):
+            moved_ref[sample] = moved_cotangents(cot_ref, 1)
+
+    for part in range(3):
+
+        @pl.when(step == part)
+        def _(part=part):
+            where = slice(part * WINDOW, (part + 1) * WINDOW)
+            middle = products([moved_ref[0, :, where], moved_ref[1, :, where]])
+            if part == 0:
+                centre[...] = middle
+            elif part == 1:
+                centre[...] += middle
+            else:
+                keep(1, centre[...] + middle)
+            if part != 1:
+                keep(part, products([moved_cotangents(ref, part) for ref in (own_cot, other_cot)]))
 
     @pl.when(step == 2)
     def _():
@@ -126,8 +143,8 @@
             num_scalar_prefetch=1,
             grid=(3,),
             in_specs=[
-                pl.BlockSpec((rows, positions), lambda g, h: (h[0], 0), pipeline_mode=once),
-                pl.BlockSpec((rows, positions), whole, pipeline_mode=once),
+                pl.BlockSpec((rows, WINDOW), lambda g, h: (h[0], g)),
+                pl.BlockSpec((rows, WINDOW), lambda g, h: (0, g)),
                 pl.BlockSpec((outs, positions), whole, pipeline_mode=once),
                 pl.BlockSpec((outs, positions), whole, pipeline_mode=once),
                 pl.BlockSpec(memory_space=pl.ANY),
@@ -139,6 +156,8 @@
             scratch_shapes=[
                 pltpu.VMEM((2 * depth, tiles, TILE, LANES), jnp.float32),
                 pltpu.VMEM((1, 3 * outs), jnp.float32),
+                pltpu.VMEM((2, 3 * outs, positions), jnp.bfloat16),
+                pltpu.VMEM((rows, 3 * outs), jnp.float32),
             ],
         ),
         compiler_params=pltpu.CompilerParams(vmem_limit_bytes=VMEM_LIMIT),

time: 90.7 us -> 90.9 us (level)
  waiting for transfers between devices: 17.1 us -> 15.4 us
  starting transfers between devices: 34.4 us -> 36 us
    ppermute x29, waiting for transfers between devices: 17.1 us -> 15.4 us  [to(): lax.ppermute(value, 'dp', [(i, i ^ distance) for i in range(samples)])]
    ppermute x29, starting transfers between devices: 29.9 us -> 31.6 us  [to(): lax.ppermute(value, 'dp', [(i, i ^ distance) for i in range(samples)])]
  transfers between devices with their start and end apart: 31 -> 31, of which waited for: 12 -> 11; matrix products, arithmetic and copies ran while one was open for 9% -> 9% of each run, Pallas kernels for 25% -> 25%
where the time goes in v14:
time: 90.9 us; the launch traced here: 90.6 us
  starting transfers between devices  36 us (40%)
  Pallas kernels  22.5 us (25%)
  waiting for transfers between devices  15.4 us (17%)
  other arithmetic  8.03 us (9%)
  local copies, waits for them, and re-layouts  6.03 us (7%)
  between operations  2.62 us (3%)
    ppermute x29, starting transfers between devices, to(): lax.ppermute(value, 'dp', [(i, i ^ distance) for i in range(samples)])  31.6 us
    ppermute x29, waiting for transfers between devices, to(): lax.ppermute(value, 'dp', [(i, i ^ distance) for i in range(samples)])  15.4 us
    pallas_call x2, Pallas kernels, kernel_grad(): pl.pallas_call(functools.partial(kernel_grad_kernel, depth), out_shape=[j...  11.1 us
    pallas_call x1, Pallas kernels, input_gradient(): pl.pallas_call(input_grad_kernel, out_shape=jax.ShapeDtypeStruct((rows, p...  6.54 us
    pallas_call x1, Pallas kernels, forward(): pl.pallas_call(forward_kernel, out_shape=jax.ShapeDtypeStruct((outs, posi...  4.84 us
    reshape x1, other arithmetic, on_device(): weight_grad = jnp.transpose(grad, (1, 3, 0, 2, 4)).reshape(rows, taps, outs)  4.64 us
    ppermute x1, starting transfers between devices, on_device(): their_cot = lax.ppermute(own_cot, 'chan', [(0, 1), (1, 0)])  2.95 us
    dynamic_update_slice x32, local copies, waits for them, and re-layouts, on_device(): lax.dynamic_update_slice(grad, value, (0, base * core_tiles + row, lane,...  2.04 us
  transfers between devices with their start and end apart: 31, of which 11 were waited for; matrix products, arithmetic and copies ran while one was open for 9% of the time, Pallas kernels for 25%

profile of v14, /device:TPU:0, one launch (start us, length us, event | category | flops | bytes accessed | tf_op | source)
XLA Modules:
  0.0 90.6 jit_solution(17354425764857704609)
XLA Ops:
  0.7 1.4 %dynamic-slice_bitcast_fusion = bf16[512,1152]{1,0:T(8,128)(2,1)S(1)} fusion(bf16[1,1024,1152]{2,1,0:T(8,128)(2,1)} %param.3, s32[]{:T(128)S(6)} %select_n.230), kind=kLoop, calls=%fused_computation.1 | loop fusion | bytes 2359300 | tf_op jit(solution)/shard_map/dynamic_slice | solution.py:357
  2.0 0.5 collective-permute-start
  2.6 2.9 %collective-permute-start.5 = (bf16[128,1152]{1,0:T(8,128)(2,1)}, bf16[128,1152]{1,0:T(8,128)(2,1)S(1)}, u32[]{:S(2)}, u32[]{:S(2)}) collective-permute-start(bf16[128,1152]{1,0:T(8,128)(2,1)} %bitcast.424), channel_id=1, source_target_pairs={{0,1},{1,0},{2,3},{3,2},{4,5},{5,4},{6,7},{7,6},{8,9},{9,8},{10,11... | collective-permute-start | bytes 884744 | tf_op jit(solution)/shard_map/ppermute | solution.py:350
  5.7 5.5 %kernel_grad.2 = (f32[73,8,128]{2,1,0:T(8,128)S(1)}, f32[73,8,128]{2,1,0:T(8,128)S(1)}, f32[73,8,128]{2,1,0:T(8,128)S(1)}, f32[73,8,128]{2,1,0:T(8,128)S(1)}, f3...) custom-call(s32[2]{0:T(128)S(1)} %pad_add_fusion.place_ref, bf16[1024,1152]{1,0:T(8,128)(2,1)} %bitcast.395, ...), custom_call_target="tpu_custom_call" | custom-call | flops 1509949440 | bytes 5308416 | tf_op jit(solution)/shard_map/kernel_grad/pallas_call | solution.py:139
  11.1 0.5 slice.265
  11.7 2.7 %collective-permute-start.2 = (f16[2,73,8,128]{3,2,1,0:T(8,128)(2,1)S(1)}, f16[2,73,8,128]{3,2,1,0:T(8,128)(2,1)S(1)}, u32[]{:S(2)}, u32[]{:S(2)}) collective-permute-start(f16[2,73,8,128]{3,2,1,0:T(8,128)(2,1)S(1)} %convert_element_type.348), channel_id=1, source_target_pairs={{0,4},{2,6},{4,0},{6,2},{8,12},{10,14},{12,8},{14,10},{16,20},{18,... | collective-permute-start | bytes 897032 | tf_op jit(solution)/shard_map/ppermute | solution.py:338
  15.3 0.3 collective-permute-start.3
  15.5 0.1 maximum_select_fusion.cot_ref
  15.7 1.1 %collective-permute-done.6.other_cot = bf16[128,1152]{1,0:T(8,128)(2,1)S(1)} collective-permute-done((bf16[128,1152]{1,0:T(8,128)(2,1)S(1)}, bf16[128,1152]{1,0:T(8,128)(2,1)S(1)}, u32[]{:S(2)}, u32[]{:S(2)}) %collective-permute-start.6) | collective-permute-done | bytes 294944 | tf_op jit(solution)/shard_map/ppermute | solution.py:338
  16.8 5.7 %kernel_grad.3 = (f32[73,8,128]{2,1,0:T(8,128)S(1)}, f32[73,8,128]{2,1,0:T(8,128)S(1)}, f32[73,8,128]{2,1,0:T(8,128)S(1)}, f32[73,8,128]{2,1,0:T(8,128)S(1)}, f3...) custom-call(s32[2]{0:T(128)S(1)} %pad_add_fusion.place_ref, bf16[1024,1152]{1,0:T(8,128)(2,1)} %bitcast.396, ...), custom_call_target="tpu_custom_call" | custom-call | flops 1509949440 | bytes 5308416 | tf_op jit(solution)/shard_map/kernel_grad/pallas_call | solution.py:139
  22.5 0.9 collective-permute-start.7
  23.4 1.3 %collective-permute-start.8 = (f16[2,73,8,128]{3,2,1,0:T(8,128)(2,1)S(1)}, f16[2,73,8,128]{3,2,1,0:T(8,128)(2,1)S(1)}, u32[]{:S(2)}, u32[]{:S(2)}) collective-permute-start(f16[2,73,8,128]{3,2,1,0:T(8,128)(2,1)S(1)} %select_convert_fusion), channel_id=1, source_target_pairs={{0,4},{2,6},{4,0},{6,2},{8,12},{10,14},{12,8},{14,10},{16,20},{18,... | collective-permute-start | bytes 897032 | tf_op jit(solution)/shard_map/ppermute | solution.py:338
  24.8 2.0 %collective-permute-start.4 = (f16[73,8,128]{2,1,0:T(8,128)(2,1)S(1)}, f16[73,8,128]{2,1,0:T(8,128)(2,1)S(1)}, u32[]{:S(2)}, u32[]{:S(2)}) collective-permute-start(f16[73,8,128]{2,1,0:T(8,128)(2,1)S(1)} %constant_dynamic-update-slice_fusion.16), channel_id=1, source_target_pairs={{0,8},{2,10},{4,12},{6,14},{8,0},{10,2},{12,4},{14,6},{16,24},{18,... | collective-permute-start | bytes 448520 | tf_op jit(solution)/shard_map/ppermute | solution.py:338
  26.8 1.9 %collective-permute-done.3 = f16[2,73,8,128]{3,2,1,0:T(8,128)(2,1)S(1)} collective-permute-done((f16[2,73,8,128]{3,2,1,0:T(8,128)(2,1)S(1)}, f16[2,73,8,128]{3,2,1,0:T(8,128)(2,1)S(1)}, u32[]{:S(2)}, u32[]{:S(2)}) %collective-permute-start.3) | collective-permute-done | bytes 299040 | tf_op jit(solution)/shard_map/ppermute | solution.py:338
  28.8 2.2 %collective-permute-start.10 = (f16[73,8,128]{2,1,0:T(8,128)(2,1)S(1)}, f16[73,8,128]{2,1,0:T(8,128)(2,1)S(1)}, u32[]{:S(2)}, u32[]{:S(2)}) collective-permute-start(f16[73,8,128]{2,1,0:T(8,128)(2,1)S(1)} %constant_dynamic-update-slice_fusion.15), channel_id=1, source_target_pairs={{0,8},{2,10},{4,12},{6,14},{8,0},{10,2},{12,4},{14,6},{16,24},{18,... | collective-permute-start | bytes 448520 | tf_op jit(solution)/shard_map/ppermute | solution.py:338
  31.2 2.7 %collective-permute-start.11 = (f16[73,8,128]{2,1,0:T(8,128)(2,1)S(1)}, f16[73,8,128]{2,1,0:T(8,128)(2,1)S(1)}, u32[]{:S(2)}, u32[]{:S(2)}) collective-permute-start(f16[73,8,128]{2,1,0:T(8,128)(2,1)S(1)} %constant_dynamic-update-slice_fusion.14), channel_id=1, source_target_pairs={{0,16},{2,18},{4,20},{6,22},{8,24},{10,26},{12,28},{14,30},{16,0},... | collective-permute-start | bytes 448520 | tf_op jit(solution)/shard_map/ppermute | solution.py:338
  33.9 1.2 %collective-permute-done.7 = f16[2,73,8,128]{3,2,1,0:T(8,128)(2,1)S(1)} collective-permute-done((f16[2,73,8,128]{3,2,1,0:T(8,128)(2,1)S(1)}, f16[2,73,8,128]{3,2,1,0:T(8,128)(2,1)S(1)}, u32[]{:S(2)}, u32[]{:S(2)}) %collective-permute-start.7) | collective-permute-done | bytes 299040 | tf_op jit(solution)/shard_map/ppermute | solution.py:338
  35.2 2.2 %collective-permute-start.9 = (f16[73,8,128]{2,1,0:T(8,128)(2,1)S(1)}, f16[73,8,128]{2,1,0:T(8,128)(2,1)S(1)}, u32[]{:S(2)}, u32[]{:S(2)}) collective-permute-start(f16[73,8,128]{2,1,0:T(8,128)(2,1)S(1)} %constant_dynamic-update-slice_fusion.13), channel_id=1, source_target_pairs={{0,8},{2,10},{4,12},{6,14},{8,0},{10,2},{12,4},{14,6},{16,24},{18,... | collective-permute-start | bytes 448520 | tf_op jit(solution)/shard_map/ppermute | solution.py:338
  37.4 4.8 %forward.1 = f32[256,1152]{1,0:T(8,128)S(1)} custom-call(bf16[1024,1152]{1,0:T(8,128)(2,1)S(1)} %bitcast.397, bf16[9,1024,256]{2,1,0:T(8,128)(2,1)S(1)} %bitcast.400, f32[8,128]{1,0:T(8,128)S(1)} %fusion.147._), custom_call_target="tpu_custom_call" | custom-call | flops 3019898880 | bytes 8257536 | tf_op jit(solution)/shard_map/forward/pallas_call | solution.py:213
  42.4 0.7 collective-permute-start.13
  43.4 2.7 %collective-permute-start.14 = (f16[73,8,128]{2,1,0:T(8,128)(2,1)S(1)}, f16[73,8,128]{2,1,0:T(8,128)(2,1)S(1)}, u32[]{:S(2)}, u32[]{:S(2)}) collective-permute-start(f16[73,8,128]{2,1,0:T(8,128)(2,1)S(1)} %constant_dynamic-update-slice_fusion.11), channel_id=1, source_target_pairs={{0,16},{2,18},{4,20},{6,22},{8,24},{10,26},{12,28},{14,30},{16,0},... | collective-permute-start | bytes 448520 | tf_op jit(solution)/shard_map/ppermute | solution.py:338
  46.0 0.1 fusion.31
  46.2 1.6 %collective-permute-start.12 = (f16[9,8,1,8,128]{4,3,2,1,0:T(8,128)(2,1)S(1)}, f16[9,8,1,8,128]{4,3,2,1,0:T(8,128)(2,1)S(1)}, u32[]{:S(2)}, u32[]{:S(2)}) collective-permute-start(f16[9,8,1,8,128]{4,3,2,1,0:T(8,128)(2,1)S(1)} %bitcast.410), channel_id=1, source_target_pairs={{0,4},{2,6},{4,0},{6,2},{8,12},{10,14},{12,8},{14,10},{16,20},{18,... | collective-permute-start | bytes 442376 | tf_op jit(solution)/shard_map/ppermute | solution.py:338
  47.8 1.4 %collective-permute-start.16 = (f16[9,8,1,8,128]{4,3,1,0,2:T(8,128)(2,1)S(1)}, f16[9,8,1,8,128]{4,3,1,0,2:T(8,128)(2,1)S(1)}, u32[]{:S(2)}, u32[]{:S(2)}) collective-permute-start(f16[9,8,1,8,128]{4,3,1,0,2:T(8,128)(2,1)S(1)} %bitcast.412), channel_id=1, source_target_pairs={{0,8},{2,10},{4,12},{6,14},{8,0},{10,2},{12,4},{14,6},{16,24},{18,... | collective-permute-start | bytes 442376 | tf_op jit(solution)/shard_map/ppermute | solution.py:338
  49.2 0.3 collective-permute-start.17
  49.5 6.5 %input_gradient.1 = bf16[1024,1152]{1,0:T(8,128)(2,1)} custom-call(bf16[256,1152]{1,0:T(8,128)(2,1)S(1)} %maximum_select_fusion.cot_ref, bf16[9,1024,256]{2,1,0:T(8,128)(2,1)S(1)} %bitcast.401, f32[8,128]{1,0:T(8,128)S(1)} %convert_bitcast_fusion._), custom_call_target="tpu_custom_call" | custom-call | flops 3019898880 | bytes 7667712 | tf_op jit(solution)/shard_map/input_gradient/pallas_call | solution.py:261
  56.1 0.7 convert_compare_fusion.5
  56.8 0.7 broadcast_in_dim.103
  57.6 1.2 %collective-permute-done.17 = f16[9,8,1,8,128]{4,3,1,0,2:T(8,128)(2,1)S(1)} collective-permute-done((f16[9,8,1,8,128]{4,3,1,0,2:T(8,128)(2,1)S(1)}, f16[9,8,1,8,128]{4,3,1,0,2:T(8,128)(2,1)S(1)}, u32[]{:S(2)}, u32[]{:S(2)}) %collective-permute-start.17) | collective-permute-done | bytes 147488 | tf_op jit(solution)/shard_map/ppermute | solution.py:338
  58.9 1.6 %collective-permute-start.19 = (f16[2,9,8,1,8,128]{5,4,2,1,3,0:T(8,128)(2,1)S(1)}, f16[2,9,8,1,8,128]{5,4,2,1,3,0:T(8,128)(2,1)S(1)}, u32[]{:S(2)}, u32[]{:S(2)}) collective-permute-start(f16[2,9,8,1,8,128]{5,4,2,1,3,0:T(8,128)(2,1)S(1)} %pad_maximum_fusion), channel_id=1, source_target_pairs={{0,4},{2,6},{4,0},{6,2},{8,12},{10,14},{12,8},{14,10},{16,20},{18,... | collective-permute-start | bytes 884744 | tf_op jit(solution)/shard_map/ppermute | solution.py:338
  60.5 0.1 collective-permute-start.18
  60.9 0.2 fusion.26
  61.0 1.9 %collective-permute-start.22 = (f16[9,8,1,8,128]{4,3,1,0,2:T(8,128)(2,1)S(1)}, f16[9,8,1,8,128]{4,3,1,0,2:T(8,128)(2,1)S(1)}, u32[]{:S(2)}, u32[]{:S(2)}) collective-permute-start(f16[9,8,1,8,128]{4,3,1,0,2:T(8,128)(2,1)S(1)} %bitcast.403), channel_id=1, source_target_pairs={{0,8},{2,10},{4,12},{6,14},{8,0},{10,2},{12,4},{14,6},{16,24},{18,... | collective-permute-start | bytes 442376 | tf_op jit(solution)/shard_map/ppermute | solution.py:338
  63.0 1.0 %collective-permute-start.23 = (f16[9,8,1,8,128]{4,3,1,0,2:T(8,128)(2,1)S(1)}, f16[9,8,1,8,128]{4,3,1,0,2:T(8,128)(2,1)S(1)}, u32[]{:S(2)}, u32[]{:S(2)}) collective-permute-start(f16[9,8,1,8,128]{4,3,1,0,2:T(8,128)(2,1)S(1)} %bitcast.404), channel_id=1, source_target_pairs={{0,16},{2,18},{4,20},{6,22},{8,24},{10,26},{12,28},{14,30},{16,0},... | collective-permute-start | bytes 442376 | tf_op jit(solution)/shard_map/ppermute | solution.py:338
  64.0 0.8 collective-permute-start.25
  64.8 0.5 slice.298
  66.1 0.4 collective-permute-done.18
  66.5 1.5 %collective-permute-start.15 = (f32[128,1152]{1,0:T(8,128)S(1)}, f32[128,1152]{1,0:T(8,128)S(1)}, u32[]{:S(2)}, u32[]{:S(2)}) collective-permute-start(f32[128,1152]{1,0:T(8,128)S(1)} %dynamic-slice_select_fusion), channel_id=1, source_target_pairs={{0,1},{1,0},{2,3},{3,2},{4,5},{5,4},{6,7},{7,6},{8,9},{9,8},{10,11... | collective-permute-start | bytes 1769480 | tf_op jit(solution)/shard_map/ppermute | solution.py:468
  68.1 1.5 %collective-permute-done.22 = f16[9,8,1,8,128]{4,3,1,0,2:T(8,128)(2,1)S(1)} collective-permute-done((f16[9,8,1,8,128]{4,3,1,0,2:T(8,128)(2,1)S(1)}, f16[9,8,1,8,128]{4,3,1,0,2:T(8,128)(2,1)S(1)}, u32[]{:S(2)}, u32[]{:S(2)}) %collective-permute-start.22) | collective-permute-done | bytes 147488 | tf_op jit(solution)/shard_map/ppermute | solution.py:338
  69.8 2.1 %collective-permute-start.26 = (f16[2,9,8,1,8,128]{5,4,2,1,3,0:T(8,128)(2,1)S(1)}, f16[2,9,8,1,8,128]{5,4,2,1,3,0:T(8,128)(2,1)S(1)}, u32[]{:S(2)}, u32[]{:S(2)}) collective-permute-start(f16[2,9,8,1,8,128]{5,4,2,1,3,0:T(8,128)(2,1)S(1)} %pad_maximum_fusion.1), channel_id=1, source_target_pairs={{0,4},{2,6},{4,0},{6,2},{8,12},{10,14},{12,8},{14,10},{16,20},{18,... | collective-permute-start | bytes 884744 | tf_op jit(solution)/shard_map/ppermute | solution.py:338
  72.0 2.1 %collective-permute-start.24 = (f16[9,8,1,8,128]{4,3,1,0,2:T(8,128)(2,1)S(1)}, f16[9,8,1,8,128]{4,3,1,0,2:T(8,128)(2,1)S(1)}, u32[]{:S(2)}, u32[]{:S(2)}) collective-permute-start(f16[9,8,1,8,128]{4,3,1,0,2:T(8,128)(2,1)S(1)} %collective-permute-done.23), channel_id=1, source_target_pairs={{0,8},{2,10},{4,12},{6,14},{8,0},{10,2},{12,4},{14,6},{16,24},{18,... | collective-permute-start | bytes 442376 | tf_op jit(solution)/shard_map/ppermute | solution.py:338
  74.2 1.3 %collective-permute-done.20 = f16[1,9,8,1,8,128]{5,4,3,2,1,0:T(8,128)(2,1)S(1)} collective-permute-done((f16[1,9,8,1,8,128]{5,4,3,2,1,0:T(8,128)(2,1)S(1)}, f16[1,9,8,1,8,128]{5,4,3,2,1,0:T(8,128)(2,1)S(1)}, u32[]{:S(2)}, u32[]{:S(2)}) %collective-permute-start.20) | collective-permute-done | bytes 147488 | tf_op jit(solution)/shard_map/ppermute | solution.py:338
  75.6 1.6 %collective-permute-done.24 = f16[9,8,1,8,128]{4,3,1,0,2:T(8,128)(2,1)S(1)} collective-permute-done((f16[9,8,1,8,128]{4,3,1,0,2:T(8,128)(2,1)S(1)}, f16[9,8,1,8,128]{4,3,1,0,2:T(8,128)(2,1)S(1)}, u32[]{:S(2)}, u32[]{:S(2)}) %collective-permute-start.24) | collective-permute-done | bytes 147488 | tf_op jit(solution)/shard_map/ppermute | solution.py:338
  77.4 1.0 %collective-permute-done.30 = f32[2,8,128]{2,1,0:T(8,128)S(1)} collective-permute-done((f32[2,8,128]{2,1,0:T(8,128)S(1)}, f32[2,8,128]{2,1,0:T(8,128)S(1)}, u32[]{:S(2)}, u32[]{:S(2)}) %collective-permute-start.30) | collective-permute-done | bytes 8224 | tf_op jit(solution)/shard_map/ppermute | solution.py:338
  78.5 0.2 collective-permute-done.26
  78.8 0.8 fusion.20
  79.7 4.0 %collective-permute-done.28 = f16[1,9,8,1,8,128]{5,4,2,1,3,0:T(8,128)(2,1)S(1)} collective-permute-done((f16[1,9,8,1,8,128]{5,4,2,1,3,0:T(8,128)(2,1)S(1)}, f16[1,9,8,1,8,128]{5,4,2,1,3,0:T(8,128)(2,1)S(1)}, u32[]{:S(2)}, u32[]{:S(2)}) %collective-permute-start.28) | collective-permute-done | bytes 147488 | tf_op jit(solution)/shard_map/ppermute | solution.py:338
  85.9 4.6 %multiply_bitcast_fusion = f32[1024,9,256]{2,0,1:T(8,128)} fusion(f16[9,128,2,8,128]{4,3,2,1,0:T(8,128)(2,1)S(1)} %bitcast_dynamic-update-slice_fusion.1, f32[128,2,8,128]{3,2,1,0:T(8,128)S(1)} %bitcast.402), kind=kLoop, calls=%fused_computation | loop fusion | flops 4718592 | bytes 15204352 | tf_op jit(solution)/shard_map/reshape | solution.py:462
  (139 shorter events, 4.9 us)
Async XLA Ops:
  2.0 13.5 %copy-start.1 = (bf16[1,128,1152]{2,1,0:T(8,128)(2,1)S(1)}, bf16[1,128,1152]{2,1,0:T(8,128)(2,1)}, u32[]{:S(2)}) copy-start(bf16[1,128,1152]{2,1,0:T(8,128)(2,1)} %param.5) | copy-start | bytes 884740
  2.0 3.6 %collective-permute-start = (bf16[512,1152]{1,0:T(8,128)(2,1)S(1)}, bf16[512,1152]{1,0:T(8,128)(2,1)S(1)}, u32[]{:S(2)}, u32[]{:S(2)}) collective-permute-start(bf16[512,1152]{1,0:T(8,128)(2,1)S(1)} %dynamic-slice_bitcast_fusion), channel_id=1, source_target_pairs={{0,2},{2,0},{4,6},{6,4},{8,10},{10,8},{12,14},{14,12},{16,18},{18,... | collective-permute-start | bytes 3538952 | tf_op jit(solution)/shard_map/ppermute | solution.py:338
  2.5 3.1 %collective-permute-start.1 = (bf16[128,1152]{1,0:T(8,128)(2,1)}, bf16[128,1152]{1,0:T(8,128)(2,1)S(1)}, u32[]{:S(2)}, u32[]{:S(2)}) collective-permute-start(bf16[128,1152]{1,0:T(8,128)(2,1)} %bitcast.423), channel_id=1, source_target_pairs={{0,2},{2,0},{4,6},{6,4},{8,10},{10,8},{12,14},{14,12},{16,18},{18,... | collective-permute-start | bytes 884744 | tf_op jit(solution)/shard_map/ppermute | solution.py:338
  2.6 12.4 %collective-permute-start.5 = (bf16[128,1152]{1,0:T(8,128)(2,1)}, bf16[128,1152]{1,0:T(8,128)(2,1)S(1)}, u32[]{:S(2)}, u32[]{:S(2)}) collective-permute-start(bf16[128,1152]{1,0:T(8,128)(2,1)} %bitcast.424), channel_id=1, source_target_pairs={{0,1},{1,0},{2,3},{3,2},{4,5},{5,4},{6,7},{7,6},{8,9},{9,8},{10,11... | collective-permute-start | bytes 884744 | tf_op jit(solution)/shard_map/ppermute | solution.py:350
  11.7 13.0 %collective-permute-start.2 = (f16[2,73,8,128]{3,2,1,0:T(8,128)(2,1)S(1)}, f16[2,73,8,128]{3,2,1,0:T(8,128)(2,1)S(1)}, u32[]{:S(2)}, u32[]{:S(2)}) collective-permute-start(f16[2,73,8,128]{3,2,1,0:T(8,128)(2,1)S(1)} %convert_element_type.348), channel_id=1, source_target_pairs={{0,4},{2,6},{4,0},{6,2},{8,12},{10,14},{12,8},{14,10},{16,20},{18,... | collective-permute-start | bytes 897032 | tf_op jit(solution)/shard_map/ppermute | solution.py:338
  15.1 1.6 %collective-permute-start.6 = (bf16[128,1152]{1,0:T(8,128)(2,1)S(1)}, bf16[128,1152]{1,0:T(8,128)(2,1)S(1)}, u32[]{:S(2)}, u32[]{:S(2)}) collective-permute-start(bf16[128,1152]{1,0:T(8,128)(2,1)S(1)} %broadcast_select_fusion.own_cot), channel_id=1, source_target_pairs={{0,2},{2,0},{4,6},{6,4},{8,10},{10,8},{12,14},{14,12},{16,18},{18,... | collective-permute-start | bytes 884744 | tf_op jit(solution)/shard_map/ppermute | solution.py:338
  15.3 13.4 %collective-permute-start.3 = (f16[2,73,8,128]{3,2,1,0:T(8,128)(2,1)S(1)}, f16[2,73,8,128]{3,2,1,0:T(8,128)(2,1)S(1)}, u32[]{:S(2)}, u32[]{:S(2)}) collective-permute-start(f16[2,73,8,128]{3,2,1,0:T(8,128)(2,1)S(1)} %select_convert_fusion.1), channel_id=1, source_target_pairs={{0,4},{2,6},{4,0},{6,2},{8,12},{10,14},{12,8},{14,10},{16,20},{18,... | collective-permute-start | bytes 897032 | tf_op jit(solution)/shard_map/ppermute | solution.py:338
  15.5 21.9 %slice-start = ((s8[4718592]{0:T(1024)(128)(4,1)}), s8[4194304]{0:T(1024)(128)(4,1)S(1)}, s32[]{:S(2)}) async-start(s8[4718592]{0:T(1024)(128)(4,1)} %bitcast.398), calls=%async_computation | async-start | bytes 8388608
  15.7 21.7 %copy-start = (bf16[1,1024,1152]{2,1,0:T(8,128)(2,1)S(1)}, bf16[1,1024,1152]{2,1,0:T(8,128)(2,1)}, u32[]{:S(2)}) copy-start(bf16[1,1024,1152]{2,1,0:T(8,128)(2,1)} %param.3) | copy-start | bytes 7077892
  15.7 21.7 %slice-start.1 = ((s8[4718592]{0:T(1024)(128)(4,1)}), s8[524288]{0:T(1024)(128)(4,1)S(1)}, s32[]{:S(2)}) async-start(s8[4718592]{0:T(1024)(128)(4,1)} %bitcast.398), calls=%async_computation.1 | async-start | bytes 1048576
  22.5 12.6 %collective-permute-start.7 = (f16[2,73,8,128]{3,2,1,0:T(8,128)(2,1)S(1)}, f16[2,73,8,128]{3,2,1,0:T(8,128)(2,1)S(1)}, u32[]{:S(2)}, u32[]{:S(2)}) collective-permute-start(f16[2,73,8,128]{3,2,1,0:T(8,128)(2,1)S(1)} %convert_element_type.376), channel_id=1, source_target_pairs={{0,4},{2,6},{4,0},{6,2},{8,12},{10,14},{12,8},{14,10},{16,20},{18,... | collective-permute-start | bytes 897032 | tf_op jit(solution)/shard_map/ppermute | solution.py:338
  23.4 18.9 %collective-permute-start.8 = (f16[2,73,8,128]{3,2,1,0:T(8,128)(2,1)S(1)}, f16[2,73,8,128]{3,2,1,0:T(8,128)(2,1)S(1)}, u32[]{:S(2)}, u32[]{:S(2)}) collective-permute-start(f16[2,73,8,128]{3,2,1,0:T(8,128)(2,1)S(1)} %select_convert_fusion), channel_id=1, source_target_pairs={{0,4},{2,6},{4,0},{6,2},{8,12},{10,14},{12,8},{14,10},{16,20},{18,... | collective-permute-start | bytes 897032 | tf_op jit(solution)/shard_map/ppermute | solution.py:338
  24.8 6.2 %collective-permute-start.4 = (f16[73,8,128]{2,1,0:T(8,128)(2,1)S(1)}, f16[73,8,128]{2,1,0:T(8,128)(2,1)S(1)}, u32[]{:S(2)}, u32[]{:S(2)}) collective-permute-start(f16[73,8,128]{2,1,0:T(8,128)(2,1)S(1)} %constant_dynamic-update-slice_fusion.16), channel_id=1, source_target_pairs={{0,8},{2,10},{4,12},{6,14},{8,0},{10,2},{12,4},{14,6},{16,24},{18,... | collective-permute-start | bytes 448520 | tf_op jit(solution)/shard_map/ppermute | solution.py:338
  28.8 14.4 %collective-permute-start.10 = (f16[73,8,128]{2,1,0:T(8,128)(2,1)S(1)}, f16[73,8,128]{2,1,0:T(8,128)(2,1)S(1)}, u32[]{:S(2)}, u32[]{:S(2)}) collective-permute-start(f16[73,8,128]{2,1,0:T(8,128)(2,1)S(1)} %constant_dynamic-update-slice_fusion.15), channel_id=1, source_target_pairs={{0,8},{2,10},{4,12},{6,14},{8,0},{10,2},{12,4},{14,6},{16,24},{18,... | collective-permute-start | bytes 448520 | tf_op jit(solution)/shard_map/ppermute | solution.py:338
  31.2 12.0 %collective-permute-start.11 = (f16[73,8,128]{2,1,0:T(8,128)(2,1)S(1)}, f16[73,8,128]{2,1,0:T(8,128)(2,1)S(1)}, u32[]{:S(2)}, u32[]{:S(2)}) collective-permute-start(f16[73,8,128]{2,1,0:T(8,128)(2,1)S(1)} %constant_dynamic-update-slice_fusion.14), channel_id=1, source_target_pairs={{0,16},{2,18},{4,20},{6,22},{8,24},{10,26},{12,28},{14,30},{16,0},... | collective-permute-start | bytes 448520 | tf_op jit(solution)/shard_map/ppermute | solution.py:338
  35.2 8.0 %collective-permute-start.9 = (f16[73,8,128]{2,1,0:T(8,128)(2,1)S(1)}, f16[73,8,128]{2,1,0:T(8,128)(2,1)S(1)}, u32[]{:S(2)}, u32[]{:S(2)}) collective-permute-start(f16[73,8,128]{2,1,0:T(8,128)(2,1)S(1)} %constant_dynamic-update-slice_fusion.13), channel_id=1, source_target_pairs={{0,8},{2,10},{4,12},{6,14},{8,0},{10,2},{12,4},{14,6},{16,24},{18,... | collective-permute-start | bytes 448520 | tf_op jit(solution)/shard_map/ppermute | solution.py:338
  42.4 18.4 %collective-permute-start.13 = (f16[73,8,128]{2,1,0:T(8,128)(2,1)S(1)}, f16[73,8,128]{2,1,0:T(8,128)(2,1)S(1)}, u32[]{:S(2)}, u32[]{:S(2)}) collective-permute-start(f16[73,8,128]{2,1,0:T(8,128)(2,1)S(1)} %constant_dynamic-update-slice_fusion.12), channel_id=1, source_target_pairs={{0,8},{2,10},{4,12},{6,14},{8,0},{10,2},{12,4},{14,6},{16,24},{18,... | collective-permute-start | bytes 448520 | tf_op jit(solution)/shard_map/ppermute | solution.py:338
  43.4 17.4 %collective-permute-start.14 = (f16[73,8,128]{2,1,0:T(8,128)(2,1)S(1)}, f16[73,8,128]{2,1,0:T(8,128)(2,1)S(1)}, u32[]{:S(2)}, u32[]{:S(2)}) collective-permute-start(f16[73,8,128]{2,1,0:T(8,128)(2,1)S(1)} %constant_dynamic-update-slice_fusion.11), channel_id=1, source_target_pairs={{0,16},{2,18},{4,20},{6,22},{8,24},{10,26},{12,28},{14,30},{16,0},... | collective-permute-start | bytes 448520 | tf_op jit(solution)/shard_map/ppermute | solution.py:338
  46.2 14.6 %collective-permute-start.12 = (f16[9,8,1,8,128]{4,3,2,1,0:T(8,128)(2,1)S(1)}, f16[9,8,1,8,128]{4,3,2,1,0:T(8,128)(2,1)S(1)}, u32[]{:S(2)}, u32[]{:S(2)}) collective-permute-start(f16[9,8,1,8,128]{4,3,2,1,0:T(8,128)(2,1)S(1)} %bitcast.410), channel_id=1, source_target_pairs={{0,4},{2,6},{4,0},{6,2},{8,12},{10,14},{12,8},{14,10},{16,20},{18,... | collective-permute-start | bytes 442376 | tf_op jit(solution)/shard_map/ppermute | solution.py:338
  47.8 9.8 %collective-permute-start.16 = (f16[9,8,1,8,128]{4,3,1,0,2:T(8,128)(2,1)S(1)}, f16[9,8,1,8,128]{4,3,1,0,2:T(8,128)(2,1)S(1)}, u32[]{:S(2)}, u32[]{:S(2)}) collective-permute-start(f16[9,8,1,8,128]{4,3,1,0,2:T(8,128)(2,1)S(1)} %bitcast.412), channel_id=1, source_target_pairs={{0,8},{2,10},{4,12},{6,14},{8,0},{10,2},{12,4},{14,6},{16,24},{18,... | collective-permute-start | bytes 442376 | tf_op jit(solution)/shard_map/ppermute | solution.py:338
  49.2 9.7 %collective-permute-start.17 = (f16[9,8,1,8,128]{4,3,1,0,2:T(8,128)(2,1)S(1)}, f16[9,8,1,8,128]{4,3,1,0,2:T(8,128)(2,1)S(1)}, u32[]{:S(2)}, u32[]{:S(2)}) collective-permute-start(f16[9,8,1,8,128]{4,3,1,0,2:T(8,128)(2,1)S(1)} %bitcast.413), channel_id=1, source_target_pairs={{0,16},{2,18},{4,20},{6,22},{8,24},{10,26},{12,28},{14,30},{16,0},... | collective-permute-start | bytes 442376 | tf_op jit(solution)/shard_map/ppermute | solution.py:338
  58.9 13.0 %collective-permute-start.19 = (f16[2,9,8,1,8,128]{5,4,2,1,3,0:T(8,128)(2,1)S(1)}, f16[2,9,8,1,8,128]{5,4,2,1,3,0:T(8,128)(2,1)S(1)}, u32[]{:S(2)}, u32[]{:S(2)}) collective-permute-start(f16[2,9,8,1,8,128]{5,4,2,1,3,0:T(8,128)(2,1)S(1)} %pad_maximum_fusion), channel_id=1, source_target_pairs={{0,4},{2,6},{4,0},{6,2},{8,12},{10,14},{12,8},{14,10},{16,20},{18,... | collective-permute-start | bytes 884744 | tf_op jit(solution)/shard_map/ppermute | solution.py:338
  60.5 6.0 %collective-permute-start.18 = (f16[9,8,1,8,128]{4,3,1,0,2:T(8,128)(2,1)S(1)}, f16[9,8,1,8,128]{4,3,1,0,2:T(8,128)(2,1)S(1)}, u32[]{:S(2)}, u32[]{:S(2)}) collective-permute-start(f16[9,8,1,8,128]{4,3,1,0,2:T(8,128)(2,1)S(1)} %collective-permute-done.17), channel_id=1, source_target_pairs={{0,8},{2,10},{4,12},{6,14},{8,0},{10,2},{12,4},{14,6},{16,24},{18,... | collective-permute-start | bytes 442376 | tf_op jit(solution)/shard_map/ppermute | solution.py:338
  61.0 8.6 %collective-permute-start.22 = (f16[9,8,1,8,128]{4,3,1,0,2:T(8,128)(2,1)S(1)}, f16[9,8,1,8,128]{4,3,1,0,2:T(8,128)(2,1)S(1)}, u32[]{:S(2)}, u32[]{:S(2)}) collective-permute-start(f16[9,8,1,8,128]{4,3,1,0,2:T(8,128)(2,1)S(1)} %bitcast.403), channel_id=1, source_target_pairs={{0,8},{2,10},{4,12},{6,14},{8,0},{10,2},{12,4},{14,6},{16,24},{18,... | collective-permute-start | bytes 442376 | tf_op jit(solution)/shard_map/ppermute | solution.py:338
  63.0 6.7 %collective-permute-start.23 = (f16[9,8,1,8,128]{4,3,1,0,2:T(8,128)(2,1)S(1)}, f16[9,8,1,8,128]{4,3,1,0,2:T(8,128)(2,1)S(1)}, u32[]{:S(2)}, u32[]{:S(2)}) collective-permute-start(f16[9,8,1,8,128]{4,3,1,0,2:T(8,128)(2,1)S(1)} %bitcast.404), channel_id=1, source_target_pairs={{0,16},{2,18},{4,20},{6,22},{8,24},{10,26},{12,28},{14,30},{16,0},... | collective-permute-start | bytes 442376 | tf_op jit(solution)/shard_map/ppermute | solution.py:338
  64.0 13.3 %collective-permute-start.25 = (f16[9,8,1,8,128]{4,3,1,0,2:T(8,128)(2,1)S(1)}, f16[9,8,1,8,128]{4,3,1,0,2:T(8,128)(2,1)S(1)}, u32[]{:S(2)}, u32[]{:S(2)}) collective-permute-start(f16[9,8,1,8,128]{4,3,1,0,2:T(8,128)(2,1)S(1)} %bitcast.405), channel_id=1, source_target_pairs={{0,4},{2,6},{4,0},{6,2},{8,12},{10,14},{12,8},{14,10},{16,20},{18,... | collective-permute-start | bytes 442376 | tf_op jit(solution)/shard_map/ppermute | solution.py:338
  66.5 12.3 %collective-permute-start.15 = (f32[128,1152]{1,0:T(8,128)S(1)}, f32[128,1152]{1,0:T(8,128)S(1)}, u32[]{:S(2)}, u32[]{:S(2)}) collective-permute-start(f32[128,1152]{1,0:T(8,128)S(1)} %dynamic-slice_select_fusion), channel_id=1, source_target_pairs={{0,1},{1,0},{2,3},{3,2},{4,5},{5,4},{6,7},{7,6},{8,9},{9,8},{10,11... | collective-permute-start | bytes 1769480 | tf_op jit(solution)/shard_map/ppermute | solution.py:468
  69.7 5.8 %collective-permute-start.20 = (f16[1,9,8,1,8,128]{5,4,3,2,1,0:T(8,128)(2,1)S(1)}, f16[1,9,8,1,8,128]{5,4,3,2,1,0:T(8,128)(2,1)S(1)}, u32[]{:S(2)}, u32[]{:S(2)}) collective-permute-start(f16[1,9,8,1,8,128]{5,4,3,2,1,0:T(8,128)(2,1)S(1)} %bitcast.421), channel_id=1, source_target_pairs={{0,4},{2,6},{4,0},{6,2},{8,12},{10,14},{12,8},{14,10},{16,20},{18,... | collective-permute-start | bytes 442376 | tf_op jit(solution)/shard_map/ppermute | solution.py:338
  69.8 8.9 %collective-permute-start.26 = (f16[2,9,8,1,8,128]{5,4,2,1,3,0:T(8,128)(2,1)S(1)}, f16[2,9,8,1,8,128]{5,4,2,1,3,0:T(8,128)(2,1)S(1)}, u32[]{:S(2)}, u32[]{:S(2)}) collective-permute-start(f16[2,9,8,1,8,128]{5,4,2,1,3,0:T(8,128)(2,1)S(1)} %pad_maximum_fusion.1), channel_id=1, source_target_pairs={{0,4},{2,6},{4,0},{6,2},{8,12},{10,14},{12,8},{14,10},{16,20},{18,... | collective-permute-start | bytes 884744 | tf_op jit(solution)/shard_map/ppermute | solution.py:338
  72.0 5.3 %collective-permute-start.24 = (f16[9,8,1,8,128]{4,3,1,0,2:T(8,128)(2,1)S(1)}, f16[9,8,1,8,128]{4,3,1,0,2:T(8,128)(2,1)S(1)}, u32[]{:S(2)}, u32[]{:S(2)}) collective-permute-start(f16[9,8,1,8,128]{4,3,1,0,2:T(8,128)(2,1)S(1)} %collective-permute-done.23), channel_id=1, source_target_pairs={{0,8},{2,10},{4,12},{6,14},{8,0},{10,2},{12,4},{14,6},{16,24},{18,... | collective-permute-start | bytes 442376 | tf_op jit(solution)/shard_map/ppermute | solution.py:338
  75.5 4.1 %collective-permute-start.21 = (f16[8,9,8,1,8,128]{5,4,3,2,1,0:T(8,128)(2,1)S(1)}, f16[8,9,8,1,8,128]{5,4,3,2,1,0:T(8,128)(2,1)S(1)}, u32[]{:S(2)}, u32[]{:S(2)}) collective-permute-start(f16[8,9,8,1,8,128]{5,4,3,2,1,0:T(8,128)(2,1)S(1)} %constant_dynamic-update-slice_fusion), channel_id=1, source_target_pairs={{0,2},{2,0},{4,6},{6,4},{8,10},{10,8},{12,14},{14,12},{16,18},{18,... | collective-permute-start | bytes 3538952 | tf_op jit(solution)/shard_map/ppermute | solution.py:338
  77.2 1.2 %collective-permute-start.30 = (f32[2,8,128]{2,1,0:T(8,128)S(1)}, f32[2,8,128]{2,1,0:T(8,128)S(1)}, u32[]{:S(2)}, u32[]{:S(2)}) collective-permute-start(f32[2,8,128]{2,1,0:T(8,128)S(1)} %fusion.54), channel_id=1, source_target_pairs={{0,2},{2,0},{4,6},{6,4},{8,10},{10,8},{12,14},{14,12},{16,18},{18,... | collective-permute-start | bytes 24584 | tf_op jit(solution)/shard_map/ppermute | solution.py:338
  77.3 6.3 %collective-permute-start.28 = (f16[1,9,8,1,8,128]{5,4,2,1,3,0:T(8,128)(2,1)S(1)}, f16[1,9,8,1,8,128]{5,4,2,1,3,0:T(8,128)(2,1)S(1)}, u32[]{:S(2)}, u32[]{:S(2)}) collective-permute-start(f16[1,9,8,1,8,128]{5,4,2,1,3,0:T(8,128)(2,1)S(1)} %bitcast.422), channel_id=1, source_target_pairs={{0,4},{2,6},{4,0},{6,2},{8,12},{10,14},{12,8},{14,10},{16,20},{18,... | collective-permute-start | bytes 442376 | tf_op jit(solution)/shard_map/ppermute | solution.py:338
  78.7 6.1 %collective-permute-start.27 = (f16[7,9,8,1,8,128]{5,4,2,1,3,0:T(8,128)(2,1)S(1)}, f16[7,9,8,1,8,128]{5,4,2,1,3,0:T(8,128)(2,1)S(1)}, u32[]{:S(2)}, u32[]{:S(2)}) collective-permute-start(f16[7,9,8,1,8,128]{5,4,2,1,3,0:T(8,128)(2,1)S(1)} %constant_dynamic-update-slice_fusion.3), channel_id=1, source_target_pairs={{0,2},{2,0},{4,6},{6,4},{8,10},{10,8},{12,14},{14,12},{16,18},{18,... | collective-permute-start | bytes 3096584 | tf_op jit(solution)/shard_map/ppermute | solution.py:338
  83.7 2.1 %collective-permute-start.29 = (f16[1,9,8,1,8,128]{5,4,2,1,3,0:T(8,128)(2,1)S(1)}, f16[1,9,8,1,8,128]{5,4,2,1,3,0:T(8,128)(2,1)S(1)}, u32[]{:S(2)}, u32[]{:S(2)}) collective-permute-start(f16[1,9,8,1,8,128]{5,4,2,1,3,0:T(8,128)(2,1)S(1)} %broadcast_select_fusion.1), channel_id=1, source_target_pairs={{0,2},{2,0},{4,6},{6,4},{8,10},{10,8},{12,14},{14,12},{16,18},{18,... | collective-permute-start | bytes 442376 | tf_op jit(solution)/shard_map/ppermute | solution.py:338

commit v15 on v12

--- a/solution.py
+++ b/solution.py
@@ -427,7 +427,7 @@
                 message = later(message, crossed)
             across = to_core(message)
             crossed = across if side == 0 else crossed
-            for slot, (chip, step, piece) in enumerate(listed):
+            for slot, (chip, step, piece) in reversed(list(enumerate(listed))):
                 row = chip * chip_tiles + (level ^ step) * shard_tiles
                 for base, value in ((core, piece), (1 - core, across[slot])):
                     grad = lax.dynamic_update_slice(

time: 90.7 us -> 92 us (1.014)
  transfers between devices with their start and end apart: 31 -> 31, of which waited for: 12 -> 10; matrix products, arithmetic and copies ran while one was open for 9% -> 9% of each run, Pallas kernels for 25% -> 24%
where the time goes in v15:
time: 92 us; the launch traced here: 91.7 us
  starting transfers between devices  35.1 us (38%)
  Pallas kernels  22.4 us (24%)
  waiting for transfers between devices  17.6 us (19%)
  other arithmetic  8 us (9%)
  local copies, waits for them, and re-layouts  6.01 us (7%)
  between operations  2.65 us (3%)
    ppermute x29, starting transfers between devices, to(): lax.ppermute(value, 'dp', [(i, i ^ distance) for i in range(samples)])  30.6 us
    ppermute x29, waiting for transfers between devices, to(): lax.ppermute(value, 'dp', [(i, i ^ distance) for i in range(samples)])  17.6 us
    pallas_call x2, Pallas kernels, kernel_grad(): pl.pallas_call(functools.partial(kernel_grad_kernel, depth), out_shape=[j...  10.8 us
    pallas_call x1, Pallas kernels, input_gradient(): pl.pallas_call(input_grad_kernel, out_shape=jax.ShapeDtypeStruct((rows, p...  6.55 us
    pallas_call x1, Pallas kernels, forward(): pl.pallas_call(forward_kernel, out_shape=jax.ShapeDtypeStruct((outs, posi...  4.97 us
    reshape x1, other arithmetic, on_device(): weight_grad = jnp.transpose(grad, (1, 3, 0, 2, 4)).reshape(rows, taps, outs)  4.64 us
    ppermute x1, starting transfers between devices, on_device(): their_cot = lax.ppermute(own_cot, 'chan', [(0, 1), (1, 0)])  2.95 us
    dynamic_update_slice x32, local copies, waits for them, and re-layouts, on_device(): lax.dynamic_update_slice(grad, value, (0, base * core_tiles + row, lane,...  2.02 us
  transfers between devices with their start and end apart: 31, of which 10 were waited for; matrix products, arithmetic and copies ran while one was open for 9% of the time, Pallas kernels for 24%

profile of v15, /device:TPU:0, one launch (start us, length us, event | category | flops | bytes accessed | tf_op | source)
XLA Modules:
  0.0 91.7 jit_solution(12181984386394896203)
XLA Ops:
  0.7 1.4 %dynamic-slice_bitcast_fusion = bf16[512,1152]{1,0:T(8,128)(2,1)S(1)} fusion(bf16[1,1024,1152]{2,1,0:T(8,128)(2,1)} %param.3, s32[]{:T(128)S(6)} %select_n.230), kind=kLoop, calls=%fused_computation.1 | loop fusion | bytes 2359300 | tf_op jit(solution)/shard_map/dynamic_slice | solution.py:338
  2.0 0.5 collective-permute-start
  2.6 2.9 %collective-permute-start.5 = (bf16[128,1152]{1,0:T(8,128)(2,1)}, bf16[128,1152]{1,0:T(8,128)(2,1)S(1)}, u32[]{:S(2)}, u32[]{:S(2)}) collective-permute-start(bf16[128,1152]{1,0:T(8,128)(2,1)} %bitcast.424), channel_id=1, source_target_pairs={{0,1},{1,0},{2,3},{3,2},{4,5},{5,4},{6,7},{7,6},{8,9},{9,8},{10,11... | collective-permute-start | bytes 884744 | tf_op jit(solution)/shard_map/ppermute | solution.py:331
  5.7 5.3 %kernel_grad.2 = (f32[73,8,128]{2,1,0:T(8,128)S(1)}, f32[73,8,128]{2,1,0:T(8,128)S(1)}, f32[73,8,128]{2,1,0:T(8,128)S(1)}, f32[73,8,128]{2,1,0:T(8,128)S(1)}, f3...) custom-call(s32[2]{0:T(128)S(1)} %pad_add_fusion.place_ref, bf16[1024,1152]{1,0:T(8,128)(2,1)} %bitcast.395, ...), custom_call_target="tpu_custom_call" | custom-call | flops 1509949440 | bytes 5308416 | tf_op jit(solution)/shard_map/kernel_grad/pallas_call | solution.py:122
  10.9 0.5 slice.265
  11.5 2.7 %collective-permute-start.2 = (f16[2,73,8,128]{3,2,1,0:T(8,128)(2,1)S(1)}, f16[2,73,8,128]{3,2,1,0:T(8,128)(2,1)S(1)}, u32[]{:S(2)}, u32[]{:S(2)}) collective-permute-start(f16[2,73,8,128]{3,2,1,0:T(8,128)(2,1)S(1)} %convert_element_type.348), channel_id=1, source_target_pairs={{0,4},{2,6},{4,0},{6,2},{8,12},{10,14},{12,8},{14,10},{16,20},{18,... | collective-permute-start | bytes 897032 | tf_op jit(solution)/shard_map/ppermute | solution.py:319
  15.1 0.3 collective-permute-start.3
  15.4 0.1 maximum_select_fusion.cot_ref
  15.5 1.0 %collective-permute-done.6.other_cot = bf16[128,1152]{1,0:T(8,128)(2,1)S(1)} collective-permute-done((bf16[128,1152]{1,0:T(8,128)(2,1)S(1)}, bf16[128,1152]{1,0:T(8,128)(2,1)S(1)}, u32[]{:S(2)}, u32[]{:S(2)}) %collective-permute-start.6) | collective-permute-done | bytes 294944 | tf_op jit(solution)/shard_map/ppermute | solution.py:319
  16.6 5.6 %kernel_grad.3 = (f32[73,8,128]{2,1,0:T(8,128)S(1)}, f32[73,8,128]{2,1,0:T(8,128)S(1)}, f32[73,8,128]{2,1,0:T(8,128)S(1)}, f32[73,8,128]{2,1,0:T(8,128)S(1)}, f3...) custom-call(s32[2]{0:T(128)S(1)} %pad_add_fusion.place_ref, bf16[1024,1152]{1,0:T(8,128)(2,1)} %bitcast.396, ...), custom_call_target="tpu_custom_call" | custom-call | flops 1509949440 | bytes 5308416 | tf_op jit(solution)/shard_map/kernel_grad/pallas_call | solution.py:122
  22.2 0.9 collective-permute-start.7
  23.2 1.3 %collective-permute-start.8 = (f16[2,73,8,128]{3,2,1,0:T(8,128)(2,1)S(1)}, f16[2,73,8,128]{3,2,1,0:T(8,128)(2,1)S(1)}, u32[]{:S(2)}, u32[]{:S(2)}) collective-permute-start(f16[2,73,8,128]{3,2,1,0:T(8,128)(2,1)S(1)} %select_convert_fusion), channel_id=1, source_target_pairs={{0,4},{2,6},{4,0},{6,2},{8,12},{10,14},{12,8},{14,10},{16,20},{18,... | collective-permute-start | bytes 897032 | tf_op jit(solution)/shard_map/ppermute | solution.py:319
  24.5 2.0 %collective-permute-start.4 = (f16[73,8,128]{2,1,0:T(8,128)(2,1)S(1)}, f16[73,8,128]{2,1,0:T(8,128)(2,1)S(1)}, u32[]{:S(2)}, u32[]{:S(2)}) collective-permute-start(f16[73,8,128]{2,1,0:T(8,128)(2,1)S(1)} %constant_dynamic-update-slice_fusion.16), channel_id=1, source_target_pairs={{0,8},{2,10},{4,12},{6,14},{8,0},{10,2},{12,4},{14,6},{16,24},{18,... | collective-permute-start | bytes 448520 | tf_op jit(solution)/shard_map/ppermute | solution.py:319
  26.5 2.0 %collective-permute-done.3 = f16[2,73,8,128]{3,2,1,0:T(8,128)(2,1)S(1)} collective-permute-done((f16[2,73,8,128]{3,2,1,0:T(8,128)(2,1)S(1)}, f16[2,73,8,128]{3,2,1,0:T(8,128)(2,1)S(1)}, u32[]{:S(2)}, u32[]{:S(2)}) %collective-permute-start.3) | collective-permute-done | bytes 299040 | tf_op jit(solution)/shard_map/ppermute | solution.py:319
  28.6 2.2 %collective-permute-start.10 = (f16[73,8,128]{2,1,0:T(8,128)(2,1)S(1)}, f16[73,8,128]{2,1,0:T(8,128)(2,1)S(1)}, u32[]{:S(2)}, u32[]{:S(2)}) collective-permute-start(f16[73,8,128]{2,1,0:T(8,128)(2,1)S(1)} %constant_dynamic-update-slice_fusion.15), channel_id=1, source_target_pairs={{0,8},{2,10},{4,12},{6,14},{8,0},{10,2},{12,4},{14,6},{16,24},{18,... | collective-permute-start | bytes 448520 | tf_op jit(solution)/shard_map/ppermute | solution.py:319
  31.0 2.6 %collective-permute-start.11 = (f16[73,8,128]{2,1,0:T(8,128)(2,1)S(1)}, f16[73,8,128]{2,1,0:T(8,128)(2,1)S(1)}, u32[]{:S(2)}, u32[]{:S(2)}) collective-permute-start(f16[73,8,128]{2,1,0:T(8,128)(2,1)S(1)} %constant_dynamic-update-slice_fusion.14), channel_id=1, source_target_pairs={{0,16},{2,18},{4,20},{6,22},{8,24},{10,26},{12,28},{14,30},{16,0},... | collective-permute-start | bytes 448520 | tf_op jit(solution)/shard_map/ppermute | solution.py:319
  33.7 1.2 %collective-permute-done.7 = f16[2,73,8,128]{3,2,1,0:T(8,128)(2,1)S(1)} collective-permute-done((f16[2,73,8,128]{3,2,1,0:T(8,128)(2,1)S(1)}, f16[2,73,8,128]{3,2,1,0:T(8,128)(2,1)S(1)}, u32[]{:S(2)}, u32[]{:S(2)}) %collective-permute-start.7) | collective-permute-done | bytes 299040 | tf_op jit(solution)/shard_map/ppermute | solution.py:319
  35.0 2.2 %collective-permute-start.9 = (f16[73,8,128]{2,1,0:T(8,128)(2,1)S(1)}, f16[73,8,128]{2,1,0:T(8,128)(2,1)S(1)}, u32[]{:S(2)}, u32[]{:S(2)}) collective-permute-start(f16[73,8,128]{2,1,0:T(8,128)(2,1)S(1)} %constant_dynamic-update-slice_fusion.13), channel_id=1, source_target_pairs={{0,8},{2,10},{4,12},{6,14},{8,0},{10,2},{12,4},{14,6},{16,24},{18,... | collective-permute-start | bytes 448520 | tf_op jit(solution)/shard_map/ppermute | solution.py:319
  37.3 5.0 %forward.1 = f32[256,1152]{1,0:T(8,128)S(1)} custom-call(bf16[1024,1152]{1,0:T(8,128)(2,1)S(1)} %bitcast.397, bf16[9,1024,256]{2,1,0:T(8,128)(2,1)S(1)} %bitcast.400, f32[8,128]{1,0:T(8,128)S(1)} %fusion.147._), custom_call_target="tpu_custom_call" | custom-call | flops 3019898880 | bytes 8257536 | tf_op jit(solution)/shard_map/forward/pallas_call | solution.py:194
  42.4 0.5 collective-permute-start.13
  43.1 0.1 fusion.3
  43.2 2.6 %collective-permute-start.14 = (f16[73,8,128]{2,1,0:T(8,128)(2,1)S(1)}, f16[73,8,128]{2,1,0:T(8,128)(2,1)S(1)}, u32[]{:S(2)}, u32[]{:S(2)}) collective-permute-start(f16[73,8,128]{2,1,0:T(8,128)(2,1)S(1)} %constant_dynamic-update-slice_fusion.11), channel_id=1, source_target_pairs={{0,16},{2,18},{4,20},{6,22},{8,24},{10,26},{12,28},{14,30},{16,0},... | collective-permute-start | bytes 448520 | tf_op jit(solution)/shard_map/ppermute | solution.py:319
  45.9 0.1 fusion.31
  46.0 1.6 %collective-permute-start.12 = (f16[9,8,1,8,128]{4,3,2,1,0:T(8,128)(2,1)S(1)}, f16[9,8,1,8,128]{4,3,2,1,0:T(8,128)(2,1)S(1)}, u32[]{:S(2)}, u32[]{:S(2)}) collective-permute-start(f16[9,8,1,8,128]{4,3,2,1,0:T(8,128)(2,1)S(1)} %bitcast.410), channel_id=1, source_target_pairs={{0,4},{2,6},{4,0},{6,2},{8,12},{10,14},{12,8},{14,10},{16,20},{18,... | collective-permute-start | bytes 442376 | tf_op jit(solution)/shard_map/ppermute | solution.py:319
  47.6 0.3 collective-permute-start.16
  47.9 1.5 %collective-permute-start.19 = (f16[9,8,1,8,128]{4,3,1,0,2:T(8,128)(2,1)S(1)}, f16[9,8,1,8,128]{4,3,1,0,2:T(8,128)(2,1)S(1)}, u32[]{:S(2)}, u32[]{:S(2)}) collective-permute-start(f16[9,8,1,8,128]{4,3,1,0,2:T(8,128)(2,1)S(1)} %bitcast.413), channel_id=1, source_target_pairs={{0,8},{2,10},{4,12},{6,14},{8,0},{10,2},{12,4},{14,6},{16,24},{18,... | collective-permute-start | bytes 442376 | tf_op jit(solution)/shard_map/ppermute | solution.py:319
  49.4 6.5 %input_gradient.1 = bf16[1024,1152]{1,0:T(8,128)(2,1)} custom-call(bf16[256,1152]{1,0:T(8,128)(2,1)S(1)} %maximum_select_fusion.cot_ref, bf16[9,1024,256]{2,1,0:T(8,128)(2,1)S(1)} %bitcast.401, f32[8,128]{1,0:T(8,128)S(1)} %convert_bitcast_fusion._), custom_call_target="tpu_custom_call" | custom-call | flops 3019898880 | bytes 7667712 | tf_op jit(solution)/shard_map/input_gradient/pallas_call | solution.py:242
  56.0 0.7 convert_compare_fusion.5
  56.7 1.9 %collective-permute-done.16 = f16[9,8,1,8,128]{4,3,1,0,2:T(8,128)(2,1)S(1)} collective-permute-done((f16[9,8,1,8,128]{4,3,1,0,2:T(8,128)(2,1)S(1)}, f16[9,8,1,8,128]{4,3,1,0,2:T(8,128)(2,1)S(1)}, u32[]{:S(2)}, u32[]{:S(2)}) %collective-permute-start.16) | collective-permute-done | bytes 147488 | tf_op jit(solution)/shard_map/ppermute | solution.py:319
  58.7 1.5 %collective-permute-start.20 = (f16[2,9,8,1,8,128]{5,4,2,1,3,0:T(8,128)(2,1)S(1)}, f16[2,9,8,1,8,128]{5,4,2,1,3,0:T(8,128)(2,1)S(1)}, u32[]{:S(2)}, u32[]{:S(2)}) collective-permute-start(f16[2,9,8,1,8,128]{5,4,2,1,3,0:T(8,128)(2,1)S(1)} %pad_maximum_fusion), channel_id=1, source_target_pairs={{0,4},{2,6},{4,0},{6,2},{8,12},{10,14},{12,8},{14,10},{16,20},{18,... | collective-permute-start | bytes 884744 | tf_op jit(solution)/shard_map/ppermute | solution.py:319
  60.5 0.1 fusion.26
  60.6 3.2 %collective-permute-start.23 = (f16[9,8,1,8,128]{4,3,1,0,2:T(8,128)(2,1)S(1)}, f16[9,8,1,8,128]{4,3,1,0,2:T(8,128)(2,1)S(1)}, u32[]{:S(2)}, u32[]{:S(2)}) collective-permute-start(f16[9,8,1,8,128]{4,3,1,0,2:T(8,128)(2,1)S(1)} %bitcast.403), channel_id=1, source_target_pairs={{0,16},{2,18},{4,20},{6,22},{8,24},{10,26},{12,28},{14,30},{16,0},... | collective-permute-start | bytes 442376 | tf_op jit(solution)/shard_map/ppermute | solution.py:319
  63.8 0.8 collective-permute-start.26
  64.6 0.5 slice.298
  65.9 3.2 %collective-permute-done.17 = f16[9,8,1,8,128]{4,3,1,0,2:T(8,128)(2,1)S(1)} collective-permute-done((f16[9,8,1,8,128]{4,3,1,0,2:T(8,128)(2,1)S(1)}, f16[9,8,1,8,128]{4,3,1,0,2:T(8,128)(2,1)S(1)}, u32[]{:S(2)}, u32[]{:S(2)}) %collective-permute-start.17) | collective-permute-done | bytes 147488 | tf_op jit(solution)/shard_map/ppermute | solution.py:319
  69.1 1.6 %collective-permute-start.15 = (f32[128,1152]{1,0:T(8,128)S(1)}, f32[128,1152]{1,0:T(8,128)S(1)}, u32[]{:S(2)}, u32[]{:S(2)}) collective-permute-start(f32[128,1152]{1,0:T(8,128)S(1)} %dynamic-slice_select_fusion), channel_id=1, source_target_pairs={{0,1},{1,0},{2,3},{3,2},{4,5},{5,4},{6,7},{7,6},{8,9},{9,8},{10,11... | collective-permute-start | bytes 1769480 | tf_op jit(solution)/shard_map/ppermute | solution.py:449
  70.8 0.9 %collective-permute-start.18 = (f16[1,9,8,1,8,128]{5,4,3,2,1,0:T(8,128)(2,1)S(1)}, f16[1,9,8,1,8,128]{5,4,3,2,1,0:T(8,128)(2,1)S(1)}, u32[]{:S(2)}, u32[]{:S(2)}) collective-permute-start(f16[1,9,8,1,8,128]{5,4,3,2,1,0:T(8,128)(2,1)S(1)} %bitcast.421), channel_id=1, source_target_pairs={{0,4},{2,6},{4,0},{6,2},{8,12},{10,14},{12,8},{14,10},{16,20},{18,... | collective-permute-start | bytes 442376 | tf_op jit(solution)/shard_map/ppermute | solution.py:319
  71.8 1.2 %collective-permute-start.24 = (f16[2,9,8,1,8,128]{5,4,2,1,3,0:T(8,128)(2,1)S(1)}, f16[2,9,8,1,8,128]{5,4,2,1,3,0:T(8,128)(2,1)S(1)}, u32[]{:S(2)}, u32[]{:S(2)}) collective-permute-start(f16[2,9,8,1,8,128]{5,4,2,1,3,0:T(8,128)(2,1)S(1)} %pad_maximum_fusion.1), channel_id=1, source_target_pairs={{0,4},{2,6},{4,0},{6,2},{8,12},{10,14},{12,8},{14,10},{16,20},{18,... | collective-permute-start | bytes 884744 | tf_op jit(solution)/shard_map/ppermute | solution.py:319
  73.3 3.6 %collective-permute-done.18 = f16[1,9,8,1,8,128]{5,4,3,2,1,0:T(8,128)(2,1)S(1)} collective-permute-done((f16[1,9,8,1,8,128]{5,4,3,2,1,0:T(8,128)(2,1)S(1)}, f16[1,9,8,1,8,128]{5,4,3,2,1,0:T(8,128)(2,1)S(1)}, u32[]{:S(2)}, u32[]{:S(2)}) %collective-permute-start.18) | collective-permute-done | bytes 147488 | tf_op jit(solution)/shard_map/ppermute | solution.py:319
  77.1 0.7 broadcast_in_dim.103
  77.9 0.4 collective-permute-done.25
  78.4 0.1 collective-permute-start.30
  78.6 1.0 %collective-permute-start.28 = (f16[1,9,8,1,8,128]{5,4,2,1,3,0:T(8,128)(2,1)S(1)}, f16[1,9,8,1,8,128]{5,4,2,1,3,0:T(8,128)(2,1)S(1)}, u32[]{:S(2)}, u32[]{:S(2)}) collective-permute-start(f16[1,9,8,1,8,128]{5,4,2,1,3,0:T(8,128)(2,1)S(1)} %bitcast.422), channel_id=1, source_target_pairs={{0,4},{2,6},{4,0},{6,2},{8,12},{10,14},{12,8},{14,10},{16,20},{18,... | collective-permute-start | bytes 442376 | tf_op jit(solution)/shard_map/ppermute | solution.py:319
  79.6 0.4 collective-permute-done.30
  80.0 0.2 collective-permute-done.24
  80.3 0.8 fusion.20
  81.1 3.7 %collective-permute-done.28 = f16[1,9,8,1,8,128]{5,4,2,1,3,0:T(8,128)(2,1)S(1)} collective-permute-done((f16[1,9,8,1,8,128]{5,4,2,1,3,0:T(8,128)(2,1)S(1)}, f16[1,9,8,1,8,128]{5,4,2,1,3,0:T(8,128)(2,1)S(1)}, u32[]{:S(2)}, u32[]{:S(2)}) %collective-permute-start.28) | collective-permute-done | bytes 147488 | tf_op jit(solution)/shard_map/ppermute | solution.py:319
  87.1 4.6 %multiply_bitcast_fusion = f32[1024,9,256]{2,0,1:T(8,128)} fusion(f16[9,128,2,8,128]{4,3,2,1,0:T(8,128)(2,1)S(1)} %bitcast_dynamic-update-slice_fusion.1, f32[128,2,8,128]{3,2,1,0:T(8,128)S(1)} %bitcast.402), kind=kLoop, calls=%fused_computation | loop fusion | flops 4718592 | bytes 15204352 | tf_op jit(solution)/shard_map/reshape | solution.py:443
  (139 shorter events, 4.7 us)
Async XLA Ops:
  2.0 13.4 %copy-start.1 = (bf16[1,128,1152]{2,1,0:T(8,128)(2,1)S(1)}, bf16[1,128,1152]{2,1,0:T(8,128)(2,1)}, u32[]{:S(2)}) copy-start(bf16[1,128,1152]{2,1,0:T(8,128)(2,1)} %param.5) | copy-start | bytes 884740
  2.0 3.6 %collective-permute-start = (bf16[512,1152]{1,0:T(8,128)(2,1)S(1)}, bf16[512,1152]{1,0:T(8,128)(2,1)S(1)}, u32[]{:S(2)}, u32[]{:S(2)}) collective-permute-start(bf16[512,1152]{1,0:T(8,128)(2,1)S(1)} %dynamic-slice_bitcast_fusion), channel_id=1, source_target_pairs={{0,2},{2,0},{4,6},{6,4},{8,10},{10,8},{12,14},{14,12},{16,18},{18,... | collective-permute-start | bytes 3538952 | tf_op jit(solution)/shard_map/ppermute | solution.py:319
  2.5 3.1 %collective-permute-start.1 = (bf16[128,1152]{1,0:T(8,128)(2,1)}, bf16[128,1152]{1,0:T(8,128)(2,1)S(1)}, u32[]{:S(2)}, u32[]{:S(2)}) collective-permute-start(bf16[128,1152]{1,0:T(8,128)(2,1)} %bitcast.423), channel_id=1, source_target_pairs={{0,2},{2,0},{4,6},{6,4},{8,10},{10,8},{12,14},{14,12},{16,18},{18,... | collective-permute-start | bytes 884744 | tf_op jit(solution)/shard_map/ppermute | solution.py:319
  2.6 12.3 %collective-permute-start.5 = (bf16[128,1152]{1,0:T(8,128)(2,1)}, bf16[128,1152]{1,0:T(8,128)(2,1)S(1)}, u32[]{:S(2)}, u32[]{:S(2)}) collective-permute-start(bf16[128,1152]{1,0:T(8,128)(2,1)} %bitcast.424), channel_id=1, source_target_pairs={{0,1},{1,0},{2,3},{3,2},{4,5},{5,4},{6,7},{7,6},{8,9},{9,8},{10,11... | collective-permute-start | bytes 884744 | tf_op jit(solution)/shard_map/ppermute | solution.py:331
  11.5 12.9 %collective-permute-start.2 = (f16[2,73,8,128]{3,2,1,0:T(8,128)(2,1)S(1)}, f16[2,73,8,128]{3,2,1,0:T(8,128)(2,1)S(1)}, u32[]{:S(2)}, u32[]{:S(2)}) collective-permute-start(f16[2,73,8,128]{3,2,1,0:T(8,128)(2,1)S(1)} %convert_element_type.348), channel_id=1, source_target_pairs={{0,4},{2,6},{4,0},{6,2},{8,12},{10,14},{12,8},{14,10},{16,20},{18,... | collective-permute-start | bytes 897032 | tf_op jit(solution)/shard_map/ppermute | solution.py:319
  14.9 1.6 %collective-permute-start.6 = (bf16[128,1152]{1,0:T(8,128)(2,1)S(1)}, bf16[128,1152]{1,0:T(8,128)(2,1)S(1)}, u32[]{:S(2)}, u32[]{:S(2)}) collective-permute-start(bf16[128,1152]{1,0:T(8,128)(2,1)S(1)} %broadcast_select_fusion.own_cot), channel_id=1, source_target_pairs={{0,2},{2,0},{4,6},{6,4},{8,10},{10,8},{12,14},{14,12},{16,18},{18,... | collective-permute-start | bytes 884744 | tf_op jit(solution)/shard_map/ppermute | solution.py:319
  15.1 13.4 %collective-permute-start.3 = (f16[2,73,8,128]{3,2,1,0:T(8,128)(2,1)S(1)}, f16[2,73,8,128]{3,2,1,0:T(8,128)(2,1)S(1)}, u32[]{:S(2)}, u32[]{:S(2)}) collective-permute-start(f16[2,73,8,128]{3,2,1,0:T(8,128)(2,1)S(1)} %select_convert_fusion.1), channel_id=1, source_target_pairs={{0,4},{2,6},{4,0},{6,2},{8,12},{10,14},{12,8},{14,10},{16,20},{18,... | collective-permute-start | bytes 897032 | tf_op jit(solution)/shard_map/ppermute | solution.py:319
  15.4 21.9 %slice-start = ((s8[4718592]{0:T(1024)(128)(4,1)}), s8[4194304]{0:T(1024)(128)(4,1)S(1)}, s32[]{:S(2)}) async-start(s8[4718592]{0:T(1024)(128)(4,1)} %bitcast.398), calls=%async_computation | async-start | bytes 8388608
  15.5 21.7 %copy-start = (bf16[1,1024,1152]{2,1,0:T(8,128)(2,1)S(1)}, bf16[1,1024,1152]{2,1,0:T(8,128)(2,1)}, u32[]{:S(2)}) copy-start(bf16[1,1024,1152]{2,1,0:T(8,128)(2,1)} %param.3) | copy-start | bytes 7077892
  15.5 21.7 %slice-start.1 = ((s8[4718592]{0:T(1024)(128)(4,1)}), s8[524288]{0:T(1024)(128)(4,1)S(1)}, s32[]{:S(2)}) async-start(s8[4718592]{0:T(1024)(128)(4,1)} %bitcast.398), calls=%async_computation.1 | async-start | bytes 1048576
  22.2 12.7 %collective-permute-start.7 = (f16[2,73,8,128]{3,2,1,0:T(8,128)(2,1)S(1)}, f16[2,73,8,128]{3,2,1,0:T(8,128)(2,1)S(1)}, u32[]{:S(2)}, u32[]{:S(2)}) collective-permute-start(f16[2,73,8,128]{3,2,1,0:T(8,128)(2,1)S(1)} %convert_element_type.376), channel_id=1, source_target_pairs={{0,4},{2,6},{4,0},{6,2},{8,12},{10,14},{12,8},{14,10},{16,20},{18,... | collective-permute-start | bytes 897032 | tf_op jit(solution)/shard_map/ppermute | solution.py:319
  23.2 19.1 %collective-permute-start.8 = (f16[2,73,8,128]{3,2,1,0:T(8,128)(2,1)S(1)}, f16[2,73,8,128]{3,2,1,0:T(8,128)(2,1)S(1)}, u32[]{:S(2)}, u32[]{:S(2)}) collective-permute-start(f16[2,73,8,128]{3,2,1,0:T(8,128)(2,1)S(1)} %select_convert_fusion), channel_id=1, source_target_pairs={{0,4},{2,6},{4,0},{6,2},{8,12},{10,14},{12,8},{14,10},{16,20},{18,... | collective-permute-start | bytes 897032 | tf_op jit(solution)/shard_map/ppermute | solution.py:319
  24.5 6.3 %collective-permute-start.4 = (f16[73,8,128]{2,1,0:T(8,128)(2,1)S(1)}, f16[73,8,128]{2,1,0:T(8,128)(2,1)S(1)}, u32[]{:S(2)}, u32[]{:S(2)}) collective-permute-start(f16[73,8,128]{2,1,0:T(8,128)(2,1)S(1)} %constant_dynamic-update-slice_fusion.16), channel_id=1, source_target_pairs={{0,8},{2,10},{4,12},{6,14},{8,0},{10,2},{12,4},{14,6},{16,24},{18,... | collective-permute-start | bytes 448520 | tf_op jit(solution)/shard_map/ppermute | solution.py:319
  28.6 14.4 %collective-permute-start.10 = (f16[73,8,128]{2,1,0:T(8,128)(2,1)S(1)}, f16[73,8,128]{2,1,0:T(8,128)(2,1)S(1)}, u32[]{:S(2)}, u32[]{:S(2)}) collective-permute-start(f16[73,8,128]{2,1,0:T(8,128)(2,1)S(1)} %constant_dynamic-update-slice_fusion.15), channel_id=1, source_target_pairs={{0,8},{2,10},{4,12},{6,14},{8,0},{10,2},{12,4},{14,6},{16,24},{18,... | collective-permute-start | bytes 448520 | tf_op jit(solution)/shard_map/ppermute | solution.py:319
  31.0 12.0 %collective-permute-start.11 = (f16[73,8,128]{2,1,0:T(8,128)(2,1)S(1)}, f16[73,8,128]{2,1,0:T(8,128)(2,1)S(1)}, u32[]{:S(2)}, u32[]{:S(2)}) collective-permute-start(f16[73,8,128]{2,1,0:T(8,128)(2,1)S(1)} %constant_dynamic-update-slice_fusion.14), channel_id=1, source_target_pairs={{0,16},{2,18},{4,20},{6,22},{8,24},{10,26},{12,28},{14,30},{16,0},... | collective-permute-start | bytes 448520 | tf_op jit(solution)/shard_map/ppermute | solution.py:319
  35.0 8.0 %collective-permute-start.9 = (f16[73,8,128]{2,1,0:T(8,128)(2,1)S(1)}, f16[73,8,128]{2,1,0:T(8,128)(2,1)S(1)}, u32[]{:S(2)}, u32[]{:S(2)}) collective-permute-start(f16[73,8,128]{2,1,0:T(8,128)(2,1)S(1)} %constant_dynamic-update-slice_fusion.13), channel_id=1, source_target_pairs={{0,8},{2,10},{4,12},{6,14},{8,0},{10,2},{12,4},{14,6},{16,24},{18,... | collective-permute-start | bytes 448520 | tf_op jit(solution)/shard_map/ppermute | solution.py:319
  42.4 18.0 %collective-permute-start.13 = (f16[73,8,128]{2,1,0:T(8,128)(2,1)S(1)}, f16[73,8,128]{2,1,0:T(8,128)(2,1)S(1)}, u32[]{:S(2)}, u32[]{:S(2)}) collective-permute-start(f16[73,8,128]{2,1,0:T(8,128)(2,1)S(1)} %constant_dynamic-update-slice_fusion.12), channel_id=1, source_target_pairs={{0,8},{2,10},{4,12},{6,14},{8,0},{10,2},{12,4},{14,6},{16,24},{18,... | collective-permute-start | bytes 448520 | tf_op jit(solution)/shard_map/ppermute | solution.py:319
  43.2 17.2 %collective-permute-start.14 = (f16[73,8,128]{2,1,0:T(8,128)(2,1)S(1)}, f16[73,8,128]{2,1,0:T(8,128)(2,1)S(1)}, u32[]{:S(2)}, u32[]{:S(2)}) collective-permute-start(f16[73,8,128]{2,1,0:T(8,128)(2,1)S(1)} %constant_dynamic-update-slice_fusion.11), channel_id=1, source_target_pairs={{0,16},{2,18},{4,20},{6,22},{8,24},{10,26},{12,28},{14,30},{16,0},... | collective-permute-start | bytes 448520 | tf_op jit(solution)/shard_map/ppermute | solution.py:319
  46.0 14.4 %collective-permute-start.12 = (f16[9,8,1,8,128]{4,3,2,1,0:T(8,128)(2,1)S(1)}, f16[9,8,1,8,128]{4,3,2,1,0:T(8,128)(2,1)S(1)}, u32[]{:S(2)}, u32[]{:S(2)}) collective-permute-start(f16[9,8,1,8,128]{4,3,2,1,0:T(8,128)(2,1)S(1)} %bitcast.410), channel_id=1, source_target_pairs={{0,4},{2,6},{4,0},{6,2},{8,12},{10,14},{12,8},{14,10},{16,20},{18,... | collective-permute-start | bytes 442376 | tf_op jit(solution)/shard_map/ppermute | solution.py:319
  47.6 11.0 %collective-permute-start.16 = (f16[9,8,1,8,128]{4,3,1,0,2:T(8,128)(2,1)S(1)}, f16[9,8,1,8,128]{4,3,1,0,2:T(8,128)(2,1)S(1)}, u32[]{:S(2)}, u32[]{:S(2)}) collective-permute-start(f16[9,8,1,8,128]{4,3,1,0,2:T(8,128)(2,1)S(1)} %bitcast.412), channel_id=1, source_target_pairs={{0,16},{2,18},{4,20},{6,22},{8,24},{10,26},{12,28},{14,30},{16,0},... | collective-permute-start | bytes 442376 | tf_op jit(solution)/shard_map/ppermute | solution.py:319
  47.9 10.7 %collective-permute-start.19 = (f16[9,8,1,8,128]{4,3,1,0,2:T(8,128)(2,1)S(1)}, f16[9,8,1,8,128]{4,3,1,0,2:T(8,128)(2,1)S(1)}, u32[]{:S(2)}, u32[]{:S(2)}) collective-permute-start(f16[9,8,1,8,128]{4,3,1,0,2:T(8,128)(2,1)S(1)} %bitcast.413), channel_id=1, source_target_pairs={{0,8},{2,10},{4,12},{6,14},{8,0},{10,2},{12,4},{14,6},{16,24},{18,... | collective-permute-start | bytes 442376 | tf_op jit(solution)/shard_map/ppermute | solution.py:319
  58.7 14.4 %collective-permute-start.20 = (f16[2,9,8,1,8,128]{5,4,2,1,3,0:T(8,128)(2,1)S(1)}, f16[2,9,8,1,8,128]{5,4,2,1,3,0:T(8,128)(2,1)S(1)}, u32[]{:S(2)}, u32[]{:S(2)}) collective-permute-start(f16[2,9,8,1,8,128]{5,4,2,1,3,0:T(8,128)(2,1)S(1)} %pad_maximum_fusion), channel_id=1, source_target_pairs={{0,4},{2,6},{4,0},{6,2},{8,12},{10,14},{12,8},{14,10},{16,20},{18,... | collective-permute-start | bytes 884744 | tf_op jit(solution)/shard_map/ppermute | solution.py:319
  60.3 8.8 %collective-permute-start.17 = (f16[9,8,1,8,128]{4,3,1,0,2:T(8,128)(2,1)S(1)}, f16[9,8,1,8,128]{4,3,1,0,2:T(8,128)(2,1)S(1)}, u32[]{:S(2)}, u32[]{:S(2)}) collective-permute-start(f16[9,8,1,8,128]{4,3,1,0,2:T(8,128)(2,1)S(1)} %collective-permute-done.16), channel_id=1, source_target_pairs={{0,8},{2,10},{4,12},{6,14},{8,0},{10,2},{12,4},{14,6},{16,24},{18,... | collective-permute-start | bytes 442376 | tf_op jit(solution)/shard_map/ppermute | solution.py:319
  60.6 10.2 %collective-permute-start.23 = (f16[9,8,1,8,128]{4,3,1,0,2:T(8,128)(2,1)S(1)}, f16[9,8,1,8,128]{4,3,1,0,2:T(8,128)(2,1)S(1)}, u32[]{:S(2)}, u32[]{:S(2)}) collective-permute-start(f16[9,8,1,8,128]{4,3,1,0,2:T(8,128)(2,1)S(1)} %bitcast.403), channel_id=1, source_target_pairs={{0,16},{2,18},{4,20},{6,22},{8,24},{10,26},{12,28},{14,30},{16,0},... | collective-permute-start | bytes 442376 | tf_op jit(solution)/shard_map/ppermute | solution.py:319
  63.8 7.9 %collective-permute-start.22 = (f16[9,8,1,8,128]{4,3,1,0,2:T(8,128)(2,1)S(1)}, f16[9,8,1,8,128]{4,3,1,0,2:T(8,128)(2,1)S(1)}, u32[]{:S(2)}, u32[]{:S(2)}) collective-permute-start(f16[9,8,1,8,128]{4,3,1,0,2:T(8,128)(2,1)S(1)} %bitcast.404), channel_id=1, source_target_pairs={{0,8},{2,10},{4,12},{6,14},{8,0},{10,2},{12,4},{14,6},{16,24},{18,... | collective-permute-start | bytes 442376 | tf_op jit(solution)/shard_map/ppermute | solution.py:319
  63.8 14.7 %collective-permute-start.26 = (f16[9,8,1,8,128]{4,3,1,0,2:T(8,128)(2,1)S(1)}, f16[9,8,1,8,128]{4,3,1,0,2:T(8,128)(2,1)S(1)}, u32[]{:S(2)}, u32[]{:S(2)}) collective-permute-start(f16[9,8,1,8,128]{4,3,1,0,2:T(8,128)(2,1)S(1)} %bitcast.405), channel_id=1, source_target_pairs={{0,4},{2,6},{4,0},{6,2},{8,12},{10,14},{12,8},{14,10},{16,20},{18,... | collective-permute-start | bytes 442376 | tf_op jit(solution)/shard_map/ppermute | solution.py:319
  69.1 11.2 %collective-permute-start.15 = (f32[128,1152]{1,0:T(8,128)S(1)}, f32[128,1152]{1,0:T(8,128)S(1)}, u32[]{:S(2)}, u32[]{:S(2)}) collective-permute-start(f32[128,1152]{1,0:T(8,128)S(1)} %dynamic-slice_select_fusion), channel_id=1, source_target_pairs={{0,1},{1,0},{2,3},{3,2},{4,5},{5,4},{6,7},{7,6},{8,9},{9,8},{10,11... | collective-permute-start | bytes 1769480 | tf_op jit(solution)/shard_map/ppermute | solution.py:449
  70.8 6.2 %collective-permute-start.18 = (f16[1,9,8,1,8,128]{5,4,3,2,1,0:T(8,128)(2,1)S(1)}, f16[1,9,8,1,8,128]{5,4,3,2,1,0:T(8,128)(2,1)S(1)}, u32[]{:S(2)}, u32[]{:S(2)}) collective-permute-start(f16[1,9,8,1,8,128]{5,4,3,2,1,0:T(8,128)(2,1)S(1)} %bitcast.421), channel_id=1, source_target_pairs={{0,4},{2,6},{4,0},{6,2},{8,12},{10,14},{12,8},{14,10},{16,20},{18,... | collective-permute-start | bytes 442376 | tf_op jit(solution)/shard_map/ppermute | solution.py:319
  71.8 8.3 %collective-permute-start.24 = (f16[2,9,8,1,8,128]{5,4,2,1,3,0:T(8,128)(2,1)S(1)}, f16[2,9,8,1,8,128]{5,4,2,1,3,0:T(8,128)(2,1)S(1)}, u32[]{:S(2)}, u32[]{:S(2)}) collective-permute-start(f16[2,9,8,1,8,128]{5,4,2,1,3,0:T(8,128)(2,1)S(1)} %pad_maximum_fusion.1), channel_id=1, source_target_pairs={{0,4},{2,6},{4,0},{6,2},{8,12},{10,14},{12,8},{14,10},{16,20},{18,... | collective-permute-start | bytes 884744 | tf_op jit(solution)/shard_map/ppermute | solution.py:319
  73.2 5.2 %collective-permute-start.25 = (f16[9,8,1,8,128]{4,3,1,0,2:T(8,128)(2,1)S(1)}, f16[9,8,1,8,128]{4,3,1,0,2:T(8,128)(2,1)S(1)}, u32[]{:S(2)}, u32[]{:S(2)}) collective-permute-start(f16[9,8,1,8,128]{4,3,1,0,2:T(8,128)(2,1)S(1)} %collective-permute-done.23), channel_id=1, source_target_pairs={{0,8},{2,10},{4,12},{6,14},{8,0},{10,2},{12,4},{14,6},{16,24},{18,... | collective-permute-start | bytes 442376 | tf_op jit(solution)/shard_map/ppermute | solution.py:319
  77.0 4.1 %collective-permute-start.21 = (f16[8,9,8,1,8,128]{5,4,3,2,1,0:T(8,128)(2,1)S(1)}, f16[8,9,8,1,8,128]{5,4,3,2,1,0:T(8,128)(2,1)S(1)}, u32[]{:S(2)}, u32[]{:S(2)}) collective-permute-start(f16[8,9,8,1,8,128]{5,4,3,2,1,0:T(8,128)(2,1)S(1)} %constant_dynamic-update-slice_fusion), channel_id=1, source_target_pairs={{0,2},{2,0},{4,6},{6,4},{8,10},{10,8},{12,14},{14,12},{16,18},{18,... | collective-permute-start | bytes 3538952 | tf_op jit(solution)/shard_map/ppermute | solution.py:319
  78.4 1.6 %collective-permute-start.30 = (f32[2,8,128]{2,1,0:T(8,128)S(1)}, f32[2,8,128]{2,1,0:T(8,128)S(1)}, u32[]{:S(2)}, u32[]{:S(2)}) collective-permute-start(f32[2,8,128]{2,1,0:T(8,128)S(1)} %fusion.54), channel_id=1, source_target_pairs={{0,2},{2,0},{4,6},{6,4},{8,10},{10,8},{12,14},{14,12},{16,18},{18,... | collective-permute-start | bytes 24584 | tf_op jit(solution)/shard_map/ppermute | solution.py:319
  78.6 6.2 %collective-permute-start.28 = (f16[1,9,8,1,8,128]{5,4,2,1,3,0:T(8,128)(2,1)S(1)}, f16[1,9,8,1,8,128]{5,4,2,1,3,0:T(8,128)(2,1)S(1)}, u32[]{:S(2)}, u32[]{:S(2)}) collective-permute-start(f16[1,9,8,1,8,128]{5,4,2,1,3,0:T(8,128)(2,1)S(1)} %bitcast.422), channel_id=1, source_target_pairs={{0,4},{2,6},{4,0},{6,2},{8,12},{10,14},{12,8},{14,10},{16,20},{18,... | collective-permute-start | bytes 442376 | tf_op jit(solution)/shard_map/ppermute | solution.py:319
  80.2 5.7 %collective-permute-start.27 = (f16[7,9,8,1,8,128]{5,4,2,1,3,0:T(8,128)(2,1)S(1)}, f16[7,9,8,1,8,128]{5,4,2,1,3,0:T(8,128)(2,1)S(1)}, u32[]{:S(2)}, u32[]{:S(2)}) collective-permute-start(f16[7,9,8,1,8,128]{5,4,2,1,3,0:T(8,128)(2,1)S(1)} %constant_dynamic-update-slice_fusion.3), channel_id=1, source_target_pairs={{0,2},{2,0},{4,6},{6,4},{8,10},{10,8},{12,14},{14,12},{16,18},{18,... | collective-permute-start | bytes 3096584 | tf_op jit(solution)/shard_map/ppermute | solution.py:319
  84.8 2.1 %collective-permute-start.29 = (f16[1,9,8,1,8,128]{5,4,2,1,3,0:T(8,128)(2,1)S(1)}, f16[1,9,8,1,8,128]{5,4,2,1,3,0:T(8,128)(2,1)S(1)}, u32[]{:S(2)}, u32[]{:S(2)}) collective-permute-start(f16[1,9,8,1,8,128]{5,4,2,1,3,0:T(8,128)(2,1)S(1)} %broadcast_select_fusion.1), channel_id=1, source_target_pairs={{0,2},{2,0},{4,6},{6,4},{8,10},{10,8},{12,14},{14,12},{16,18},{18,... | collective-permute-start | bytes 442376 | tf_op jit(solution)/shard_map/ppermute | solution.py:319

commit v16 on v15

--- a/solution.py
+++ b/solution.py
@@ -377,7 +377,7 @@
 
     for side, (values, bits) in enumerate(reduced):
         lowest = common_exponent(values, bits)
-        gates = (gathers[0][1], input_grad[:TILE, :LANES]) if side else (sends[-1],)
+        gates = (gathers[0][1],) if side else (sends[-1],)
         kept = later(scaled_sum(values, lowest)[:-1], *gates)
         shard = kept.astype(jnp.float16).reshape(taps, shard_tiles, 1, TILE, LANES)
         halves.append(shard)
@@ -385,10 +385,6 @@
         near = [shard] + [None] * (depth - 1)
         for bit in bits_of_depth[::-1]:
             near[bit] = to_level(shard, bit)
-        for step in range(1, depth):
-            if near[step] is None:
-                low = step & -step
-                near[step] = to_level(near[step ^ low], low)
         gathers.append((near, to_column(shard)))
         if side == 0:
             if chans == 2:
@@ -400,9 +396,16 @@
             input_grad = input_gradient(cot, w, token(shard[0, 0]))
 
     for side, (near, own) in enumerate(gathers):
+        for step in range(1, depth):
+            if near[step] is None:
+                low = step & -step
+                source = near[step ^ low] if side else later(near[step ^ low], halves[1])
+                near[step] = to_level(source, low)
         steps = list(range(depth))
         cuts = [steps[1:-1], steps[-1:]]
         here = [jnp.stack([near[step] for step in cut]) for cut in cuts]
+        if side == 0:
+            here[0] = later(here[0], halves[1])
         there = [to_column(values) for values in here]
         if side == 0:
             returned = there[1]

time: 92 us -> 90.1 us (0.979)
  waiting for transfers between devices: 17.6 us -> 15 us
  starting transfers between devices: 35.1 us -> 36.9 us
    ppermute x29, waiting for transfers between devices: 17.6 us -> 13.3 us  [to(): lax.ppermute(value, 'dp', [(i, i ^ distance) for i in range(samples)])]
    ppermute x29, starting transfers between devices: 30.6 us -> 32.4 us  [to(): lax.ppermute(value, 'dp', [(i, i ^ distance) for i in range(samples)])]
    ppermute x1, waiting for transfers between devices: 0.01 us -> 1.71 us  [on_device(): result = mine + lax.ppermute(theirs, 'chan', [(0, 1), (1, 0)])]
  transfers between devices with their start and end apart: 31 -> 31, of which waited for: 10 -> 11; matrix products, arithmetic and copies ran while one was open for 9% -> 8% of each run, Pallas kernels for 24% -> 25%
where the time goes in v16:
time: 90.1 us; the launch traced here: 89.9 us
  starting transfers between devices  36.9 us (41%)
  Pallas kernels  22 us (24%)
  waiting for transfers between devices  15 us (17%)
  other arithmetic  7.44 us (8%)
  local copies, waits for them, and re-layouts  5.89 us (7%)
  between operations  2.66 us (3%)
    ppermute x29, starting transfers between devices, to(): lax.ppermute(value, 'dp', [(i, i ^ distance) for i in range(samples)])  32.4 us
    ppermute x29, waiting for transfers between devices, to(): lax.ppermute(value, 'dp', [(i, i ^ distance) for i in range(samples)])  13.3 us
    pallas_call x2, Pallas kernels, kernel_grad(): pl.pallas_call(functools.partial(kernel_grad_kernel, depth), out_shape=[j...  10.5 us
    pallas_call x1, Pallas kernels, input_gradient(): pl.pallas_call(input_grad_kernel, out_shape=jax.ShapeDtypeStruct((rows, p...  6.54 us
    pallas_call x1, Pallas kernels, forward(): pl.pallas_call(forward_kernel, out_shape=jax.ShapeDtypeStruct((outs, posi...  4.99 us
    reshape x1, other arithmetic, on_device(): weight_grad = jnp.transpose(grad, (1, 3, 0, 2, 4)).reshape(rows, taps, outs)  4.64 us
    ppermute x1, starting transfers between devices, on_device(): their_cot = lax.ppermute(own_cot, 'chan', [(0, 1), (1, 0)])  2.95 us
    dynamic_update_slice x32, local copies, waits for them, and re-layouts, on_device(): lax.dynamic_update_slice(grad, value, (0, base * core_tiles + row, lane,...  2.01 us
  transfers between devices with their start and end apart: 31, of which 11 were waited for; matrix products, arithmetic and copies ran while one was open for 8% of the time, Pallas kernels for 25%

profile of v16, /device:TPU:0, one launch (start us, length us, event | category | flops | bytes accessed | tf_op | source)
XLA Modules:
  0.0 89.9 jit_solution(10025506829531868993)
XLA Ops:
  0.7 1.4 %dynamic-slice_bitcast_fusion = bf16[512,1152]{1,0:T(8,128)(2,1)S(1)} fusion(bf16[1,1024,1152]{2,1,0:T(8,128)(2,1)} %param.3, s32[]{:T(128)S(6)} %select_n.243), kind=kLoop, calls=%fused_computation.1 | loop fusion | bytes 2359300 | tf_op jit(solution)/shard_map/dynamic_slice | solution.py:338
  2.0 0.5 collective-permute-start
  2.6 2.9 %collective-permute-start.5 = (bf16[128,1152]{1,0:T(8,128)(2,1)}, bf16[128,1152]{1,0:T(8,128)(2,1)S(1)}, u32[]{:S(2)}, u32[]{:S(2)}) collective-permute-start(bf16[128,1152]{1,0:T(8,128)(2,1)} %bitcast.423), channel_id=1, source_target_pairs={{0,1},{1,0},{2,3},{3,2},{4,5},{5,4},{6,7},{7,6},{8,9},{9,8},{10,11... | collective-permute-start | bytes 884744 | tf_op jit(solution)/shard_map/ppermute | solution.py:331
  5.7 5.3 %kernel_grad.2 = (f32[73,8,128]{2,1,0:T(8,128)S(1)}, f32[73,8,128]{2,1,0:T(8,128)S(1)}, f32[73,8,128]{2,1,0:T(8,128)S(1)}, f32[73,8,128]{2,1,0:T(8,128)S(1)}, f3...) custom-call(s32[2]{0:T(128)S(1)} %pad_add_fusion.place_ref, bf16[1024,1152]{1,0:T(8,128)(2,1)} %bitcast.393, ...), custom_call_target="tpu_custom_call" | custom-call | flops 1509949440 | bytes 5308416 | tf_op jit(solution)/shard_map/kernel_grad/pallas_call | solution.py:122
  11.0 2.7 %collective-permute-start.2 = (f16[2,73,8,128]{3,2,1,0:T(8,128)(2,1)S(1)}, f16[2,73,8,128]{3,2,1,0:T(8,128)(2,1)S(1)}, u32[]{:S(2)}, u32[]{:S(2)}) collective-permute-start(f16[2,73,8,128]{3,2,1,0:T(8,128)(2,1)S(1)} %convert_element_type.349), channel_id=1, source_target_pairs={{0,4},{2,6},{4,0},{6,2},{8,12},{10,14},{12,8},{14,10},{16,20},{18,... | collective-permute-start | bytes 897032 | tf_op jit(solution)/shard_map/ppermute | solution.py:319
  13.9 0.5 slice.261
  15.2 0.1 maximum_select_fusion.cot_ref
  15.4 1.4 %collective-permute-done.6.other_cot = bf16[128,1152]{1,0:T(8,128)(2,1)S(1)} collective-permute-done((bf16[128,1152]{1,0:T(8,128)(2,1)S(1)}, bf16[128,1152]{1,0:T(8,128)(2,1)S(1)}, u32[]{:S(2)}, u32[]{:S(2)}) %collective-permute-start.6) | collective-permute-done | bytes 294944 | tf_op jit(solution)/shard_map/ppermute | solution.py:319
  16.7 5.2 %kernel_grad.3 = (f32[73,8,128]{2,1,0:T(8,128)S(1)}, f32[73,8,128]{2,1,0:T(8,128)S(1)}, f32[73,8,128]{2,1,0:T(8,128)S(1)}, f32[73,8,128]{2,1,0:T(8,128)S(1)}, f3...) custom-call(s32[2]{0:T(128)S(1)} %pad_add_fusion.place_ref, bf16[1024,1152]{1,0:T(8,128)(2,1)} %bitcast.394, ...), custom_call_target="tpu_custom_call" | custom-call | flops 1509949440 | bytes 5308416 | tf_op jit(solution)/shard_map/kernel_grad/pallas_call | solution.py:122
  22.1 2.1 %collective-permute-start.7 = (f16[2,73,8,128]{3,2,1,0:T(8,128)(2,1)S(1)}, f16[2,73,8,128]{3,2,1,0:T(8,128)(2,1)S(1)}, u32[]{:S(2)}, u32[]{:S(2)}) collective-permute-start(f16[2,73,8,128]{3,2,1,0:T(8,128)(2,1)S(1)} %convert_element_type.377), channel_id=1, source_target_pairs={{0,4},{2,6},{4,0},{6,2},{8,12},{10,14},{12,8},{14,10},{16,20},{18,... | collective-permute-start | bytes 897032 | tf_op jit(solution)/shard_map/ppermute | solution.py:319
  24.4 2.1 %collective-permute-start.4 = (f16[73,8,128]{2,1,0:T(8,128)(2,1)S(1)}, f16[73,8,128]{2,1,0:T(8,128)(2,1)S(1)}, u32[]{:S(2)}, u32[]{:S(2)}) collective-permute-start(f16[73,8,128]{2,1,0:T(8,128)(2,1)S(1)} %constant_dynamic-update-slice_fusion.16), channel_id=1, source_target_pairs={{0,8},{2,10},{4,12},{6,14},{8,0},{10,2},{12,4},{14,6},{16,24},{18,... | collective-permute-start | bytes 448520 | tf_op jit(solution)/shard_map/ppermute | solution.py:319
  26.5 1.4 %collective-permute-done.3 = f16[2,73,8,128]{3,2,1,0:T(8,128)(2,1)S(1)} collective-permute-done((f16[2,73,8,128]{3,2,1,0:T(8,128)(2,1)S(1)}, f16[2,73,8,128]{3,2,1,0:T(8,128)(2,1)S(1)}, u32[]{:S(2)}, u32[]{:S(2)}) %collective-permute-start.3) | collective-permute-done | bytes 299040 | tf_op jit(solution)/shard_map/ppermute | solution.py:319
  28.1 2.2 %collective-permute-start.10 = (f16[73,8,128]{2,1,0:T(8,128)(2,1)S(1)}, f16[73,8,128]{2,1,0:T(8,128)(2,1)S(1)}, u32[]{:S(2)}, u32[]{:S(2)}) collective-permute-start(f16[73,8,128]{2,1,0:T(8,128)(2,1)S(1)} %constant_dynamic-update-slice_fusion.15), channel_id=1, source_target_pairs={{0,8},{2,10},{4,12},{6,14},{8,0},{10,2},{12,4},{14,6},{16,24},{18,... | collective-permute-start | bytes 448520 | tf_op jit(solution)/shard_map/ppermute | solution.py:319
  30.4 0.4 collective-permute-done.4
  31.0 3.0 %collective-permute-start.11 = (f16[73,8,128]{2,1,0:T(8,128)(2,1)S(1)}, f16[73,8,128]{2,1,0:T(8,128)(2,1)S(1)}, u32[]{:S(2)}, u32[]{:S(2)}) collective-permute-start(f16[73,8,128]{2,1,0:T(8,128)(2,1)S(1)} %constant_dynamic-update-slice_fusion.14), channel_id=1, source_target_pairs={{0,16},{2,18},{4,20},{6,22},{8,24},{10,26},{12,28},{14,30},{16,0},... | collective-permute-start | bytes 448520 | tf_op jit(solution)/shard_map/ppermute | solution.py:319
  34.0 0.4 collective-permute-done.7
  34.5 2.2 %collective-permute-start.9 = (f16[73,8,128]{2,1,0:T(8,128)(2,1)S(1)}, f16[73,8,128]{2,1,0:T(8,128)(2,1)S(1)}, u32[]{:S(2)}, u32[]{:S(2)}) collective-permute-start(f16[73,8,128]{2,1,0:T(8,128)(2,1)S(1)} %constant_dynamic-update-slice_fusion.13), channel_id=1, source_target_pairs={{0,8},{2,10},{4,12},{6,14},{8,0},{10,2},{12,4},{14,6},{16,24},{18,... | collective-permute-start | bytes 448520 | tf_op jit(solution)/shard_map/ppermute | solution.py:319
  36.8 5.0 %forward.1 = f32[256,1152]{1,0:T(8,128)S(1)} custom-call(bf16[1024,1152]{1,0:T(8,128)(2,1)S(1)} %bitcast.395, bf16[9,1024,256]{2,1,0:T(8,128)(2,1)S(1)} %bitcast.398, f32[8,128]{1,0:T(8,128)S(1)} %fusion.146._), custom_call_target="tpu_custom_call" | custom-call | flops 3019898880 | bytes 8257536 | tf_op jit(solution)/shard_map/forward/pallas_call | solution.py:194
  41.9 0.5 collective-permute-start.13
  42.6 0.1 fusion.3
  42.7 2.6 %collective-permute-start.14 = (f16[73,8,128]{2,1,0:T(8,128)(2,1)S(1)}, f16[73,8,128]{2,1,0:T(8,128)(2,1)S(1)}, u32[]{:S(2)}, u32[]{:S(2)}) collective-permute-start(f16[73,8,128]{2,1,0:T(8,128)(2,1)S(1)} %constant_dynamic-update-slice_fusion.11), channel_id=1, source_target_pairs={{0,16},{2,18},{4,20},{6,22},{8,24},{10,26},{12,28},{14,30},{16,0},... | collective-permute-start | bytes 448520 | tf_op jit(solution)/shard_map/ppermute | solution.py:319
  45.4 0.1 fusion.30
  45.5 0.4 collective-permute-start.16
  45.9 1.6 %collective-permute-start.19 = (f16[9,8,1,8,128]{4,3,1,0,2:T(8,128)(2,1)S(1)}, f16[9,8,1,8,128]{4,3,1,0,2:T(8,128)(2,1)S(1)}, u32[]{:S(2)}, u32[]{:S(2)}) collective-permute-start(f16[9,8,1,8,128]{4,3,1,0,2:T(8,128)(2,1)S(1)} %bitcast.410), channel_id=1, source_target_pairs={{0,8},{2,10},{4,12},{6,14},{8,0},{10,2},{12,4},{14,6},{16,24},{18,... | collective-permute-start | bytes 442376 | tf_op jit(solution)/shard_map/ppermute | solution.py:319
  47.5 1.5 %collective-permute-start.12 = (f16[9,8,1,8,128]{4,3,2,1,0:T(8,128)(2,1)S(1)}, f16[9,8,1,8,128]{4,3,2,1,0:T(8,128)(2,1)S(1)}, u32[]{:S(2)}, u32[]{:S(2)}) collective-permute-start(f16[9,8,1,8,128]{4,3,2,1,0:T(8,128)(2,1)S(1)} %bitcast.411), channel_id=1, source_target_pairs={{0,4},{2,6},{4,0},{6,2},{8,12},{10,14},{12,8},{14,10},{16,20},{18,... | collective-permute-start | bytes 442376 | tf_op jit(solution)/shard_map/ppermute | solution.py:319
  49.0 6.5 %input_gradient.1 = bf16[1024,1152]{1,0:T(8,128)(2,1)} custom-call(bf16[256,1152]{1,0:T(8,128)(2,1)S(1)} %maximum_select_fusion.cot_ref, bf16[9,1024,256]{2,1,0:T(8,128)(2,1)S(1)} %bitcast.399, f32[8,128]{1,0:T(8,128)S(1)} %convert_bitcast_fusion._), custom_call_target="tpu_custom_call" | custom-call | flops 3019898880 | bytes 7667712 | tf_op jit(solution)/shard_map/input_gradient/pallas_call | solution.py:242
  55.6 0.8 collective-permute-done.14
  56.5 0.1 fusion.25
  56.7 3.3 %collective-permute-start.23 = (f16[9,8,1,8,128]{4,3,1,0,2:T(8,128)(2,1)S(1)}, f16[9,8,1,8,128]{4,3,1,0,2:T(8,128)(2,1)S(1)}, u32[]{:S(2)}, u32[]{:S(2)}) collective-permute-start(f16[9,8,1,8,128]{4,3,1,0,2:T(8,128)(2,1)S(1)} %bitcast.402), channel_id=1, source_target_pairs={{0,16},{2,18},{4,20},{6,22},{8,24},{10,26},{12,28},{14,30},{16,0},... | collective-permute-start | bytes 442376 | tf_op jit(solution)/shard_map/ppermute | solution.py:319
  60.0 1.6 %collective-permute-start.26 = (f16[9,8,1,8,128]{4,3,1,0,2:T(8,128)(2,1)S(1)}, f16[9,8,1,8,128]{4,3,1,0,2:T(8,128)(2,1)S(1)}, u32[]{:S(2)}, u32[]{:S(2)}) collective-permute-start(f16[9,8,1,8,128]{4,3,1,0,2:T(8,128)(2,1)S(1)} %bitcast.403), channel_id=1, source_target_pairs={{0,4},{2,6},{4,0},{6,2},{8,12},{10,14},{12,8},{14,10},{16,20},{18,... | collective-permute-start | bytes 442376 | tf_op jit(solution)/shard_map/ppermute | solution.py:319
  61.6 0.1 collective-permute-start.17
  61.8 0.2 bitcast_dynamic-update-slice_fusion.1
  62.0 1.1 %collective-permute-start.20 = (f16[2,9,8,1,8,128]{5,4,2,1,3,0:T(8,128)(2,1)S(1)}, f16[2,9,8,1,8,128]{5,4,2,1,3,0:T(8,128)(2,1)S(1)}, u32[]{:S(2)}, u32[]{:S(2)}) collective-permute-start(f16[2,9,8,1,8,128]{5,4,2,1,3,0:T(8,128)(2,1)S(1)} %get-tuple-element.28), channel_id=1, source_target_pairs={{0,4},{2,6},{4,0},{6,2},{8,12},{10,14},{12,8},{14,10},{16,20},{18,... | collective-permute-start | bytes 884744 | tf_op jit(solution)/shard_map/ppermute | solution.py:319
  63.0 0.5 slice.292
  64.3 2.8 %collective-permute-done.17 = f16[9,8,1,8,128]{4,3,1,0,2:T(8,128)(2,1)S(1)} collective-permute-done((f16[9,8,1,8,128]{4,3,1,0,2:T(8,128)(2,1)S(1)}, f16[9,8,1,8,128]{4,3,1,0,2:T(8,128)(2,1)S(1)}, u32[]{:S(2)}, u32[]{:S(2)}) %collective-permute-start.17) | collective-permute-done | bytes 147488 | tf_op jit(solution)/shard_map/ppermute | solution.py:319
  67.1 1.5 %collective-permute-start.15 = (f32[128,1152]{1,0:T(8,128)S(1)}, f32[128,1152]{1,0:T(8,128)S(1)}, u32[]{:S(2)}, u32[]{:S(2)}) collective-permute-start(f32[128,1152]{1,0:T(8,128)S(1)} %dynamic-slice_select_fusion), channel_id=1, source_target_pairs={{0,1},{1,0},{2,3},{3,2},{4,5},{5,4},{6,7},{7,6},{8,9},{9,8},{10,11... | collective-permute-start | bytes 1769480 | tf_op jit(solution)/shard_map/ppermute | solution.py:452
  68.6 0.8 collective-permute-start.18
  69.5 1.3 %collective-permute-start.24 = (f16[2,9,8,1,8,128]{5,4,2,1,3,0:T(8,128)(2,1)S(1)}, f16[2,9,8,1,8,128]{5,4,2,1,3,0:T(8,128)(2,1)S(1)}, u32[]{:S(2)}, u32[]{:S(2)}) collective-permute-start(f16[2,9,8,1,8,128]{5,4,2,1,3,0:T(8,128)(2,1)S(1)} %pad_maximum_fusion), channel_id=1, source_target_pairs={{0,4},{2,6},{4,0},{6,2},{8,12},{10,14},{12,8},{14,10},{16,20},{18,... | collective-permute-start | bytes 884744 | tf_op jit(solution)/shard_map/ppermute | solution.py:319
  71.0 1.2 %collective-permute-start.25 = (f16[9,8,1,8,128]{4,3,1,0,2:T(8,128)(2,1)S(1)}, f16[9,8,1,8,128]{4,3,1,0,2:T(8,128)(2,1)S(1)}, u32[]{:S(2)}, u32[]{:S(2)}) collective-permute-start(f16[9,8,1,8,128]{4,3,1,0,2:T(8,128)(2,1)S(1)} %collective-permute-done.23), channel_id=1, source_target_pairs={{0,8},{2,10},{4,12},{6,14},{8,0},{10,2},{12,4},{14,6},{16,24},{18,... | collective-permute-start | bytes 442376 | tf_op jit(solution)/shard_map/ppermute | solution.py:319
  72.3 3.1 %collective-permute-done.18 = f16[1,9,8,1,8,128]{5,4,3,2,1,0:T(8,128)(2,1)S(1)} collective-permute-done((f16[1,9,8,1,8,128]{5,4,3,2,1,0:T(8,128)(2,1)S(1)}, f16[1,9,8,1,8,128]{5,4,3,2,1,0:T(8,128)(2,1)S(1)}, u32[]{:S(2)}, u32[]{:S(2)}) %collective-permute-start.18) | collective-permute-done | bytes 147488 | tf_op jit(solution)/shard_map/ppermute | solution.py:319
  75.5 0.7 collective-permute-done.25
  76.3 0.8 collective-permute-start.28
  77.2 0.7 broadcast_in_dim.113
  78.0 1.0 %collective-permute-done.24 = f16[2,9,8,1,8,128]{5,4,2,1,3,0:T(8,128)(2,1)S(1)} collective-permute-done((f16[2,9,8,1,8,128]{5,4,2,1,3,0:T(8,128)(2,1)S(1)}, f16[2,9,8,1,8,128]{5,4,2,1,3,0:T(8,128)(2,1)S(1)}, u32[]{:S(2)}, u32[]{:S(2)}) %collective-permute-start.24) | collective-permute-done | bytes 294944 | tf_op jit(solution)/shard_map/ppermute | solution.py:319
  79.2 1.7 %collective-permute-done.15 = f32[128,1152]{1,0:T(8,128)S(1)} collective-permute-done((f32[128,1152]{1,0:T(8,128)S(1)}, f32[128,1152]{1,0:T(8,128)S(1)}, u32[]{:S(2)}, u32[]{:S(2)}) %collective-permute-start.15) | collective-permute-done | bytes 589856 | tf_op jit(solution)/shard_map/ppermute | solution.py:452
  80.9 0.8 fusion.20
  83.9 1.2 %collective-permute-done.29 = f16[1,9,8,1,8,128]{5,4,2,1,3,0:T(8,128)(2,1)S(1)} collective-permute-done((f16[1,9,8,1,8,128]{5,4,2,1,3,0:T(8,128)(2,1)S(1)}, f16[1,9,8,1,8,128]{5,4,2,1,3,0:T(8,128)(2,1)S(1)}, u32[]{:S(2)}, u32[]{:S(2)}) %collective-permute-start.29) | collective-permute-done | bytes 147488 | tf_op jit(solution)/shard_map/ppermute | solution.py:319
  85.3 4.6 %multiply_bitcast_fusion = f32[1024,9,256]{2,0,1:T(8,128)} fusion(f16[9,128,2,8,128]{4,3,2,1,0:T(8,128)(2,1)S(1)} %bitcast_dynamic-update-slice_fusion.2, f32[128,2,8,128]{3,2,1,0:T(8,128)S(1)} %bitcast.400), kind=kLoop, calls=%fused_computation | loop fusion | flops 4718592 | bytes 15204352 | tf_op jit(solution)/shard_map/reshape | solution.py:446
  (138 shorter events, 4.7 us)
Async XLA Ops:
  2.0 13.2 %copy-start.1 = (bf16[1,128,1152]{2,1,0:T(8,128)(2,1)S(1)}, bf16[1,128,1152]{2,1,0:T(8,128)(2,1)}, u32[]{:S(2)}) copy-start(bf16[1,128,1152]{2,1,0:T(8,128)(2,1)} %param.5) | copy-start | bytes 884740
  2.0 3.6 %collective-permute-start = (bf16[512,1152]{1,0:T(8,128)(2,1)S(1)}, bf16[512,1152]{1,0:T(8,128)(2,1)S(1)}, u32[]{:S(2)}, u32[]{:S(2)}) collective-permute-start(bf16[512,1152]{1,0:T(8,128)(2,1)S(1)} %dynamic-slice_bitcast_fusion), channel_id=1, source_target_pairs={{0,2},{2,0},{4,6},{6,4},{8,10},{10,8},{12,14},{14,12},{16,18},{18,... | collective-permute-start | bytes 3538952 | tf_op jit(solution)/shard_map/ppermute | solution.py:319
  2.5 3.1 %collective-permute-start.1 = (bf16[128,1152]{1,0:T(8,128)(2,1)}, bf16[128,1152]{1,0:T(8,128)(2,1)S(1)}, u32[]{:S(2)}, u32[]{:S(2)}) collective-permute-start(bf16[128,1152]{1,0:T(8,128)(2,1)} %bitcast.422), channel_id=1, source_target_pairs={{0,2},{2,0},{4,6},{6,4},{8,10},{10,8},{12,14},{14,12},{16,18},{18,... | collective-permute-start | bytes 884744 | tf_op jit(solution)/shard_map/ppermute | solution.py:319
  2.6 12.4 %collective-permute-start.5 = (bf16[128,1152]{1,0:T(8,128)(2,1)}, bf16[128,1152]{1,0:T(8,128)(2,1)S(1)}, u32[]{:S(2)}, u32[]{:S(2)}) collective-permute-start(bf16[128,1152]{1,0:T(8,128)(2,1)} %bitcast.423), channel_id=1, source_target_pairs={{0,1},{1,0},{2,3},{3,2},{4,5},{5,4},{6,7},{7,6},{8,9},{9,8},{10,11... | collective-permute-start | bytes 884744 | tf_op jit(solution)/shard_map/ppermute | solution.py:331
  11.0 13.3 %collective-permute-start.2 = (f16[2,73,8,128]{3,2,1,0:T(8,128)(2,1)S(1)}, f16[2,73,8,128]{3,2,1,0:T(8,128)(2,1)S(1)}, u32[]{:S(2)}, u32[]{:S(2)}) collective-permute-start(f16[2,73,8,128]{3,2,1,0:T(8,128)(2,1)S(1)} %convert_element_type.349), channel_id=1, source_target_pairs={{0,4},{2,6},{4,0},{6,2},{8,12},{10,14},{12,8},{14,10},{16,20},{18,... | collective-permute-start | bytes 897032 | tf_op jit(solution)/shard_map/ppermute | solution.py:319
  13.8 14.2 %collective-permute-start.3 = (f16[2,73,8,128]{3,2,1,0:T(8,128)(2,1)S(1)}, f16[2,73,8,128]{3,2,1,0:T(8,128)(2,1)S(1)}, u32[]{:S(2)}, u32[]{:S(2)}) collective-permute-start(f16[2,73,8,128]{3,2,1,0:T(8,128)(2,1)S(1)} %select_convert_fusion.1), channel_id=1, source_target_pairs={{0,4},{2,6},{4,0},{6,2},{8,12},{10,14},{12,8},{14,10},{16,20},{18,... | collective-permute-start | bytes 897032 | tf_op jit(solution)/shard_map/ppermute | solution.py:319
  15.1 1.6 %collective-permute-start.6 = (bf16[128,1152]{1,0:T(8,128)(2,1)S(1)}, bf16[128,1152]{1,0:T(8,128)(2,1)S(1)}, u32[]{:S(2)}, u32[]{:S(2)}) collective-permute-start(bf16[128,1152]{1,0:T(8,128)(2,1)S(1)} %broadcast_select_fusion.own_cot), channel_id=1, source_target_pairs={{0,2},{2,0},{4,6},{6,4},{8,10},{10,8},{12,14},{14,12},{16,18},{18,... | collective-permute-start | bytes 884744 | tf_op jit(solution)/shard_map/ppermute | solution.py:319
  15.2 21.6 %slice-start = ((s8[4718592]{0:T(1024)(128)(4,1)}), s8[4194304]{0:T(1024)(128)(4,1)S(1)}, s32[]{:S(2)}) async-start(s8[4718592]{0:T(1024)(128)(4,1)} %bitcast.396), calls=%async_computation | async-start | bytes 8388608
  15.3 21.4 %copy-start = (bf16[1,1024,1152]{2,1,0:T(8,128)(2,1)S(1)}, bf16[1,1024,1152]{2,1,0:T(8,128)(2,1)}, u32[]{:S(2)}) copy-start(bf16[1,1024,1152]{2,1,0:T(8,128)(2,1)} %param.3) | copy-start | bytes 7077892
  15.4 21.4 %slice-start.1 = ((s8[4718592]{0:T(1024)(128)(4,1)}), s8[524288]{0:T(1024)(128)(4,1)S(1)}, s32[]{:S(2)}) async-start(s8[4718592]{0:T(1024)(128)(4,1)} %bitcast.396), calls=%async_computation.1 | async-start | bytes 1048576
  22.1 12.3 %collective-permute-start.7 = (f16[2,73,8,128]{3,2,1,0:T(8,128)(2,1)S(1)}, f16[2,73,8,128]{3,2,1,0:T(8,128)(2,1)S(1)}, u32[]{:S(2)}, u32[]{:S(2)}) collective-permute-start(f16[2,73,8,128]{3,2,1,0:T(8,128)(2,1)S(1)} %convert_element_type.377), channel_id=1, source_target_pairs={{0,4},{2,6},{4,0},{6,2},{8,12},{10,14},{12,8},{14,10},{16,20},{18,... | collective-permute-start | bytes 897032 | tf_op jit(solution)/shard_map/ppermute | solution.py:319
  24.2 17.6 %collective-permute-start.8 = (f16[2,73,8,128]{3,2,1,0:T(8,128)(2,1)S(1)}, f16[2,73,8,128]{3,2,1,0:T(8,128)(2,1)S(1)}, u32[]{:S(2)}, u32[]{:S(2)}) collective-permute-start(f16[2,73,8,128]{3,2,1,0:T(8,128)(2,1)S(1)} %select_convert_fusion), channel_id=1, source_target_pairs={{0,4},{2,6},{4,0},{6,2},{8,12},{10,14},{12,8},{14,10},{16,20},{18,... | collective-permute-start | bytes 897032 | tf_op jit(solution)/shard_map/ppermute | solution.py:319
  24.4 6.4 %collective-permute-start.4 = (f16[73,8,128]{2,1,0:T(8,128)(2,1)S(1)}, f16[73,8,128]{2,1,0:T(8,128)(2,1)S(1)}, u32[]{:S(2)}, u32[]{:S(2)}) collective-permute-start(f16[73,8,128]{2,1,0:T(8,128)(2,1)S(1)} %constant_dynamic-update-slice_fusion.16), channel_id=1, source_target_pairs={{0,8},{2,10},{4,12},{6,14},{8,0},{10,2},{12,4},{14,6},{16,24},{18,... | collective-permute-start | bytes 448520 | tf_op jit(solution)/shard_map/ppermute | solution.py:319
  28.1 14.4 %collective-permute-start.10 = (f16[73,8,128]{2,1,0:T(8,128)(2,1)S(1)}, f16[73,8,128]{2,1,0:T(8,128)(2,1)S(1)}, u32[]{:S(2)}, u32[]{:S(2)}) collective-permute-start(f16[73,8,128]{2,1,0:T(8,128)(2,1)S(1)} %constant_dynamic-update-slice_fusion.15), channel_id=1, source_target_pairs={{0,8},{2,10},{4,12},{6,14},{8,0},{10,2},{12,4},{14,6},{16,24},{18,... | collective-permute-start | bytes 448520 | tf_op jit(solution)/shard_map/ppermute | solution.py:319
  31.0 11.6 %collective-permute-start.11 = (f16[73,8,128]{2,1,0:T(8,128)(2,1)S(1)}, f16[73,8,128]{2,1,0:T(8,128)(2,1)S(1)}, u32[]{:S(2)}, u32[]{:S(2)}) collective-permute-start(f16[73,8,128]{2,1,0:T(8,128)(2,1)S(1)} %constant_dynamic-update-slice_fusion.14), channel_id=1, source_target_pairs={{0,16},{2,18},{4,20},{6,22},{8,24},{10,26},{12,28},{14,30},{16,0},... | collective-permute-start | bytes 448520 | tf_op jit(solution)/shard_map/ppermute | solution.py:319
  34.5 8.0 %collective-permute-start.9 = (f16[73,8,128]{2,1,0:T(8,128)(2,1)S(1)}, f16[73,8,128]{2,1,0:T(8,128)(2,1)S(1)}, u32[]{:S(2)}, u32[]{:S(2)}) collective-permute-start(f16[73,8,128]{2,1,0:T(8,128)(2,1)S(1)} %constant_dynamic-update-slice_fusion.13), channel_id=1, source_target_pairs={{0,8},{2,10},{4,12},{6,14},{8,0},{10,2},{12,4},{14,6},{16,24},{18,... | collective-permute-start | bytes 448520 | tf_op jit(solution)/shard_map/ppermute | solution.py:319
  41.9 13.7 %collective-permute-start.13 = (f16[73,8,128]{2,1,0:T(8,128)(2,1)S(1)}, f16[73,8,128]{2,1,0:T(8,128)(2,1)S(1)}, u32[]{:S(2)}, u32[]{:S(2)}) collective-permute-start(f16[73,8,128]{2,1,0:T(8,128)(2,1)S(1)} %constant_dynamic-update-slice_fusion.12), channel_id=1, source_target_pairs={{0,8},{2,10},{4,12},{6,14},{8,0},{10,2},{12,4},{14,6},{16,24},{18,... | collective-permute-start | bytes 448520 | tf_op jit(solution)/shard_map/ppermute | solution.py:319
  42.7 13.7 %collective-permute-start.14 = (f16[73,8,128]{2,1,0:T(8,128)(2,1)S(1)}, f16[73,8,128]{2,1,0:T(8,128)(2,1)S(1)}, u32[]{:S(2)}, u32[]{:S(2)}) collective-permute-start(f16[73,8,128]{2,1,0:T(8,128)(2,1)S(1)} %constant_dynamic-update-slice_fusion.11), channel_id=1, source_target_pairs={{0,16},{2,18},{4,20},{6,22},{8,24},{10,26},{12,28},{14,30},{16,0},... | collective-permute-start | bytes 448520 | tf_op jit(solution)/shard_map/ppermute | solution.py:319
  45.5 16.0 %collective-permute-start.16 = (f16[9,8,1,8,128]{4,3,1,0,2:T(8,128)(2,1)S(1)}, f16[9,8,1,8,128]{4,3,1,0,2:T(8,128)(2,1)S(1)}, u32[]{:S(2)}, u32[]{:S(2)}) collective-permute-start(f16[9,8,1,8,128]{4,3,1,0,2:T(8,128)(2,1)S(1)} %bitcast.409), channel_id=1, source_target_pairs={{0,16},{2,18},{4,20},{6,22},{8,24},{10,26},{12,28},{14,30},{16,0},... | collective-permute-start | bytes 442376 | tf_op jit(solution)/shard_map/ppermute | solution.py:319
  45.9 15.8 %collective-permute-start.19 = (f16[9,8,1,8,128]{4,3,1,0,2:T(8,128)(2,1)S(1)}, f16[9,8,1,8,128]{4,3,1,0,2:T(8,128)(2,1)S(1)}, u32[]{:S(2)}, u32[]{:S(2)}) collective-permute-start(f16[9,8,1,8,128]{4,3,1,0,2:T(8,128)(2,1)S(1)} %bitcast.410), channel_id=1, source_target_pairs={{0,8},{2,10},{4,12},{6,14},{8,0},{10,2},{12,4},{14,6},{16,24},{18,... | collective-permute-start | bytes 442376 | tf_op jit(solution)/shard_map/ppermute | solution.py:319
  47.5 8.1 %collective-permute-start.12 = (f16[9,8,1,8,128]{4,3,2,1,0:T(8,128)(2,1)S(1)}, f16[9,8,1,8,128]{4,3,2,1,0:T(8,128)(2,1)S(1)}, u32[]{:S(2)}, u32[]{:S(2)}) collective-permute-start(f16[9,8,1,8,128]{4,3,2,1,0:T(8,128)(2,1)S(1)} %bitcast.411), channel_id=1, source_target_pairs={{0,4},{2,6},{4,0},{6,2},{8,12},{10,14},{12,8},{14,10},{16,20},{18,... | collective-permute-start | bytes 442376 | tf_op jit(solution)/shard_map/ppermute | solution.py:319
  56.6 12.0 %collective-permute-start.22 = (f16[9,8,1,8,128]{4,3,1,0,2:T(8,128)(2,1)S(1)}, f16[9,8,1,8,128]{4,3,1,0,2:T(8,128)(2,1)S(1)}, u32[]{:S(2)}, u32[]{:S(2)}) collective-permute-start(f16[9,8,1,8,128]{4,3,1,0,2:T(8,128)(2,1)S(1)} %bitcast.401), channel_id=1, source_target_pairs={{0,8},{2,10},{4,12},{6,14},{8,0},{10,2},{12,4},{14,6},{16,24},{18,... | collective-permute-start | bytes 442376 | tf_op jit(solution)/shard_map/ppermute | solution.py:319
  56.7 12.7 %collective-permute-start.23 = (f16[9,8,1,8,128]{4,3,1,0,2:T(8,128)(2,1)S(1)}, f16[9,8,1,8,128]{4,3,1,0,2:T(8,128)(2,1)S(1)}, u32[]{:S(2)}, u32[]{:S(2)}) collective-permute-start(f16[9,8,1,8,128]{4,3,1,0,2:T(8,128)(2,1)S(1)} %bitcast.402), channel_id=1, source_target_pairs={{0,16},{2,18},{4,20},{6,22},{8,24},{10,26},{12,28},{14,30},{16,0},... | collective-permute-start | bytes 442376 | tf_op jit(solution)/shard_map/ppermute | solution.py:319
  60.0 16.3 %collective-permute-start.26 = (f16[9,8,1,8,128]{4,3,1,0,2:T(8,128)(2,1)S(1)}, f16[9,8,1,8,128]{4,3,1,0,2:T(8,128)(2,1)S(1)}, u32[]{:S(2)}, u32[]{:S(2)}) collective-permute-start(f16[9,8,1,8,128]{4,3,1,0,2:T(8,128)(2,1)S(1)} %bitcast.403), channel_id=1, source_target_pairs={{0,4},{2,6},{4,0},{6,2},{8,12},{10,14},{12,8},{14,10},{16,20},{18,... | collective-permute-start | bytes 442376 | tf_op jit(solution)/shard_map/ppermute | solution.py:319
  61.6 5.4 %collective-permute-start.17 = (f16[9,8,1,8,128]{4,3,1,0,2:T(8,128)(2,1)S(1)}, f16[9,8,1,8,128]{4,3,1,0,2:T(8,128)(2,1)S(1)}, u32[]{:S(2)}, u32[]{:S(2)}) collective-permute-start(f16[9,8,1,8,128]{4,3,1,0,2:T(8,128)(2,1)S(1)} %broadcast_select_fusion.2), channel_id=1, source_target_pairs={{0,8},{2,10},{4,12},{6,14},{8,0},{10,2},{12,4},{14,6},{16,24},{18,... | collective-permute-start | bytes 442376 | tf_op jit(solution)/shard_map/ppermute | solution.py:319
  62.0 9.0 %collective-permute-start.20 = (f16[2,9,8,1,8,128]{5,4,2,1,3,0:T(8,128)(2,1)S(1)}, f16[2,9,8,1,8,128]{5,4,2,1,3,0:T(8,128)(2,1)S(1)}, u32[]{:S(2)}, u32[]{:S(2)}) collective-permute-start(f16[2,9,8,1,8,128]{5,4,2,1,3,0:T(8,128)(2,1)S(1)} %get-tuple-element.28), channel_id=1, source_target_pairs={{0,4},{2,6},{4,0},{6,2},{8,12},{10,14},{12,8},{14,10},{16,20},{18,... | collective-permute-start | bytes 884744 | tf_op jit(solution)/shard_map/ppermute | solution.py:319
  67.1 13.9 %collective-permute-start.15 = (f32[128,1152]{1,0:T(8,128)S(1)}, f32[128,1152]{1,0:T(8,128)S(1)}, u32[]{:S(2)}, u32[]{:S(2)}) collective-permute-start(f32[128,1152]{1,0:T(8,128)S(1)} %dynamic-slice_select_fusion), channel_id=1, source_target_pairs={{0,1},{1,0},{2,3},{3,2},{4,5},{5,4},{6,7},{7,6},{8,9},{9,8},{10,11... | collective-permute-start | bytes 1769480 | tf_op jit(solution)/shard_map/ppermute | solution.py:452
  68.6 6.8 %collective-permute-start.18 = (f16[1,9,8,1,8,128]{5,4,3,2,1,0:T(8,128)(2,1)S(1)}, f16[1,9,8,1,8,128]{5,4,3,2,1,0:T(8,128)(2,1)S(1)}, u32[]{:S(2)}, u32[]{:S(2)}) collective-permute-start(f16[1,9,8,1,8,128]{5,4,3,2,1,0:T(8,128)(2,1)S(1)} %bitcast.420), channel_id=1, source_target_pairs={{0,4},{2,6},{4,0},{6,2},{8,12},{10,14},{12,8},{14,10},{16,20},{18,... | collective-permute-start | bytes 442376 | tf_op jit(solution)/shard_map/ppermute | solution.py:319
  69.5 9.6 %collective-permute-start.24 = (f16[2,9,8,1,8,128]{5,4,2,1,3,0:T(8,128)(2,1)S(1)}, f16[2,9,8,1,8,128]{5,4,2,1,3,0:T(8,128)(2,1)S(1)}, u32[]{:S(2)}, u32[]{:S(2)}) collective-permute-start(f16[2,9,8,1,8,128]{5,4,2,1,3,0:T(8,128)(2,1)S(1)} %pad_maximum_fusion), channel_id=1, source_target_pairs={{0,4},{2,6},{4,0},{6,2},{8,12},{10,14},{12,8},{14,10},{16,20},{18,... | collective-permute-start | bytes 884744 | tf_op jit(solution)/shard_map/ppermute | solution.py:319
  71.0 5.2 %collective-permute-start.25 = (f16[9,8,1,8,128]{4,3,1,0,2:T(8,128)(2,1)S(1)}, f16[9,8,1,8,128]{4,3,1,0,2:T(8,128)(2,1)S(1)}, u32[]{:S(2)}, u32[]{:S(2)}) collective-permute-start(f16[9,8,1,8,128]{4,3,1,0,2:T(8,128)(2,1)S(1)} %collective-permute-done.23), channel_id=1, source_target_pairs={{0,8},{2,10},{4,12},{6,14},{8,0},{10,2},{12,4},{14,6},{16,24},{18,... | collective-permute-start | bytes 442376 | tf_op jit(solution)/shard_map/ppermute | solution.py:319
  75.4 2.6 %collective-permute-start.30 = (f32[2,8,128]{2,1,0:T(8,128)S(1)}, f32[2,8,128]{2,1,0:T(8,128)S(1)}, u32[]{:S(2)}, u32[]{:S(2)}) collective-permute-start(f32[2,8,128]{2,1,0:T(8,128)S(1)} %fusion.53), channel_id=1, source_target_pairs={{0,2},{2,0},{4,6},{6,4},{8,10},{10,8},{12,14},{14,12},{16,18},{18,... | collective-permute-start | bytes 24584 | tf_op jit(solution)/shard_map/ppermute | solution.py:319
  76.2 5.5 %collective-permute-start.21 = (f16[8,9,8,1,8,128]{5,4,3,2,1,0:T(8,128)(2,1)S(1)}, f16[8,9,8,1,8,128]{5,4,3,2,1,0:T(8,128)(2,1)S(1)}, u32[]{:S(2)}, u32[]{:S(2)}) collective-permute-start(f16[8,9,8,1,8,128]{5,4,3,2,1,0:T(8,128)(2,1)S(1)} %constant_dynamic-update-slice_fusion), channel_id=1, source_target_pairs={{0,2},{2,0},{4,6},{6,4},{8,10},{10,8},{12,14},{14,12},{16,18},{18,... | collective-permute-start | bytes 3538952 | tf_op jit(solution)/shard_map/ppermute | solution.py:319
  76.3 7.3 %collective-permute-start.28 = (f16[1,9,8,1,8,128]{5,4,2,1,3,0:T(8,128)(2,1)S(1)}, f16[1,9,8,1,8,128]{5,4,2,1,3,0:T(8,128)(2,1)S(1)}, u32[]{:S(2)}, u32[]{:S(2)}) collective-permute-start(f16[1,9,8,1,8,128]{5,4,2,1,3,0:T(8,128)(2,1)S(1)} %bitcast.419), channel_id=1, source_target_pairs={{0,4},{2,6},{4,0},{6,2},{8,12},{10,14},{12,8},{14,10},{16,20},{18,... | collective-permute-start | bytes 442376 | tf_op jit(solution)/shard_map/ppermute | solution.py:319
  79.2 3.6 %collective-permute-start.27 = (f16[7,9,8,1,8,128]{5,4,2,1,3,0:T(8,128)(2,1)S(1)}, f16[7,9,8,1,8,128]{5,4,2,1,3,0:T(8,128)(2,1)S(1)}, u32[]{:S(2)}, u32[]{:S(2)}) collective-permute-start(f16[7,9,8,1,8,128]{5,4,2,1,3,0:T(8,128)(2,1)S(1)} %constant_dynamic-update-slice_fusion.3), channel_id=1, source_target_pairs={{0,2},{2,0},{4,6},{6,4},{8,10},{10,8},{12,14},{14,12},{16,18},{18,... | collective-permute-start | bytes 3096584 | tf_op jit(solution)/shard_map/ppermute | solution.py:319
  83.7 1.4 %collective-permute-start.29 = (f16[1,9,8,1,8,128]{5,4,2,1,3,0:T(8,128)(2,1)S(1)}, f16[1,9,8,1,8,128]{5,4,2,1,3,0:T(8,128)(2,1)S(1)}, u32[]{:S(2)}, u32[]{:S(2)}) collective-permute-start(f16[1,9,8,1,8,128]{5,4,2,1,3,0:T(8,128)(2,1)S(1)} %broadcast_select_fusion.1), channel_id=1, source_target_pairs={{0,2},{2,0},{4,6},{6,4},{8,10},{10,8},{12,14},{14,12},{16,18},{18,... | collective-permute-start | bytes 442376 | tf_op jit(solution)/shard_map/ppermute | solution.py:319
